TPU v7x, 512 devices: a whole 4x8x8 slice. The times are simulated.
512 devices in a mesh: tm: 16 (over z_hi, y), height: 32 (over z_lo, x, core).
Axes of the slice: x: 4, y: 8, z: 8 (z_hi: 2, z_lo: 4; z = z_hi * 4 + z_lo), core: 2. Of those that a mesh axis runs over, the one named last changes fastest.
Arguments:
- features: bfloat16 [32, 64, 16, 192], P('tm', 'height'), may hold values from -6 to 6
- cotangent: bfloat16 [32, 128, 32, 96], P('tm', 'height'), may hold values from -6 to 6
- weight_one: bfloat16 [3, 3, 3, 192, 96], replicated, may hold values from -0.078125 to 0.078125
- weight_two: bfloat16 [3, 3, 3, 96, 96], replicated, may hold values from -0.125 to 0.125
- norm_gain: float32 [96], replicated, may hold values from 0.5 to 1.5
- norm_shift: float32 [96], replicated, may hold values from -3 to 3
Outputs:
- decoded: bfloat16 [32, 128, 32, 96], P('tm', 'height')
- grad_features: float32 [32, 64, 16, 192], P('tm', 'height')
- grad_one: float32 [3, 3, 3, 192, 96], replicated
- grad_two: float32 [3, 3, 3, 96, 96], replicated
All inputs are finite; a program needn't handle non-finite values.
Results may differ from a plain program's by a relative error of at most 0.0055.
Values may be sent and summed in bfloat16 or wider, within the bound.
No kernel may reach another device: no remote copies, remote signals or barrier semaphores. Data moves between devices by JAX's collectives and lax.ppermute only.
A program may use at most 64 MiB of HBM per device.

v0:
```python
import jax
import jax.numpy as jnp
from jax import lax
from jax.sharding import PartitionSpec as P

GROUPS = 32


EPSILON = 1e-05


def shifted_2(value, axis, steps):
    count = lax.axis_size(axis)
    first, last = (max(0, -steps), min(count, count - steps))
    return lax.ppermute(value, axis, [(source, source + steps) for source in range(first, last)])


def padded_2(cells, sides, width):
    for axis, dim in sides:
        count = lax.axis_size(axis)
        ends = count - 1
        head = lax.slice_in_dim(cells, 0, width, axis=dim)
        tail = lax.slice_in_dim(cells, cells.shape[dim] - width, cells.shape[dim], axis=dim)
        cells = jnp.concatenate(
            [
                lax.ppermute(tail, axis, [(i, (i + 1) % count) for i in range(ends)]),
                cells,
                lax.ppermute(head, axis, [((i + 1) % count, i) for i in range(ends)]),
            ],
            axis=dim,
        )
    return cells


def convolve(padded, weight):
    result = lax.conv_general_dilated(
        padded[None],
        weight,
        (1, 1, 1),
        "VALID",
        dimension_numbers=("NDHWC", "DHWIO", "NDHWC"),
        preferred_element_type=jnp.float32,
    )
    return result[0]


def flipped(weight):
    return jnp.transpose(jnp.flip(weight, (0, 1, 2)), (0, 1, 2, 4, 3))


def taps(padded, grad):
    frames, rows, cols, outs = grad.shape
    flat_grad = grad.reshape(-1, outs)
    pieces = []
    for time_tap in range(3):
        for row_tap in range(3):
            for col_tap in range(3):
                patch = padded[
                    time_tap : time_tap + frames, row_tap : row_tap + rows, col_tap : col_tap + cols
                ]
                patch = patch.reshape(-1, padded.shape[-1])
                pieces.append(
                    lax.dot_general(
                        patch,
                        flat_grad,
                        (((0,), (0,)), ((), ())),
                        preferred_element_type=jnp.float32,
                    )
                )
    return jnp.stack(pieces).reshape(3, 3, 3, padded.shape[-1], outs)


def upsample(field):
    return jnp.repeat(jnp.repeat(field, 2, 1), 2, 2)


def pad_cols(field):
    return jnp.pad(field, ((0, 0), (0, 0), (1, 1), (0, 0)))


def body(features, cotangent, weight_one, weight_two, norm_gain, norm_shift):
    frames = features.shape[0]
    devices_all = lax.axis_size("tm") * lax.axis_size("height")
    cache_in = shifted_2(features, "tm", 1)
    timed = jnp.concatenate([cache_in, features], 0)
    rowed = padded_2(timed, (("height", 1),), 1)
    padded_in = pad_cols(upsample(rowed)[:, 1:-1])
    pre_norm = convolve(padded_in, weight_one)
    shape = pre_norm.shape
    grouped = pre_norm.reshape(shape[0], shape[1], shape[2], GROUPS, -1)
    count = shape[0] * shape[1] * shape[2] * (shape[3] // GROUPS) * devices_all
    total_one, total_two = lax.psum(
        (jnp.sum(grouped, (0, 1, 2, 4)), jnp.sum(grouped * grouped, (0, 1, 2, 4))), ("tm", "height")
    )
    mean = total_one / count
    rstd = lax.rsqrt(total_two / count - mean * mean + EPSILON)
    normed = ((grouped - mean[:, None]) * rstd[:, None]).reshape(shape)
    shifted = normed * norm_gain + norm_shift
    hidden = jax.nn.silu(shifted).astype(jnp.bfloat16)
    cache_mid = shifted_2(hidden[frames - 2 :], "tm", 1)
    mid_rowed = padded_2(jnp.concatenate([cache_mid, hidden], 0), (("height", 1),), 1)
    padded_mid = pad_cols(mid_rowed)
    decoded = convolve(padded_mid, weight_two).astype(jnp.bfloat16)
    scale = 1.0 / (shape[0] * shape[1] * shape[2] * devices_all) ** 0.5
    local_two = taps(padded_mid, cotangent)
    later_cot = shifted_2(cotangent, "tm", -1)
    cot_rowed = padded_2(jnp.concatenate([cotangent, later_cot], 0), (("height", 1),), 1)
    grad_hidden = convolve(pad_cols(cot_rowed), flipped(weight_two))
    sigma = jax.nn.sigmoid(shifted)
    grad_normed = grad_hidden * sigma * (1.0 + shifted * (1.0 - sigma)) * norm_gain
    grad_grouped = grad_normed.reshape(grouped.shape)
    normed_grouped = normed.reshape(grouped.shape)
    sum_first, sum_second = lax.psum(
        (jnp.sum(grad_grouped, (0, 1, 2, 4)), jnp.sum(grad_grouped * normed_grouped, (0, 1, 2, 4))),
        ("tm", "height"),
    )
    first = sum_first / count
    second = sum_second / count
    grad_pre = (
        ((grad_grouped - first[:, None] - normed_grouped * second[:, None]) * rstd[:, None])
        .reshape(shape)
        .astype(jnp.bfloat16)
    )
    local_one = taps(padded_in, grad_pre)
    full_pad = jnp.pad(grad_pre, ((2, 2), (2, 2), (2, 2), (0, 0)))
    spread = convolve(full_pad, flipped(weight_one))[:, :, 1:-1]
    from_below = shifted_2(spread[:, 0].astype(jnp.bfloat16), "height", -1).astype(jnp.float32)
    from_above = shifted_2(spread[:, -1].astype(jnp.bfloat16), "height", 1).astype(jnp.float32)
    inner = spread[:, 1:-1]
    inner = inner.at[:, -1].add(from_below).at[:, 0].add(from_above)
    later_terms = shifted_2(inner[:2].astype(jnp.bfloat16), "tm", -1).astype(jnp.float32)
    grad_upsampled = inner[2:].at[frames - 2 :].add(later_terms)
    rows, cols, chans = (features.shape[1], features.shape[2], features.shape[3])
    grad_features = grad_upsampled.reshape(frames, rows, 2, cols, 2, chans).sum((2, 4))
    summed_one, summed_two = lax.psum((local_one, local_two), ("tm", "height"))
    grad_one = summed_one * scale
    grad_two = summed_two * scale
    return (decoded, grad_features, grad_one, grad_two)


def solution(mesh):
    return jax.shard_map(
        body,
        mesh=mesh,
        in_specs=(P("tm", "height", None, None), P("tm", "height", None, None), P(), P(), P(), P()),
        out_specs=(P("tm", "height", None, None), P("tm", "height", None, None), P(), P()),
        check_vma=False,
    )
```

profile of v0, /device:TPU:1, one launch (start us, length us, event | category | flops | bytes accessed | tf_op | source)
XLA Modules:
  0.0 580.2 jit_solution(15161080337047814239)
XLA Ops:
  7.2 4.2 collective-permute-start
  11.4 1.3 collective-permute-start.6
  12.7 0.8 constant_dynamic-update-slice_fusion.3
  14.3 4.0 collective-permute-start.1
  18.3 3.4 collective-permute-start.2
  21.7 2.2 collective-permute-start.7
  25.9 1.1 select_reduce_fusion.3
  27.4 2.1 collective-permute-start.8
  29.6 111.9 %all-reduce.5 = (f32[32]{0:T(128)S(1)}, f32[32]{0:T(128)S(1)}) all-reduce(f32[32]{0:T(128)S(1)} %reduce_sum.62, f32[32]{0:T(128)S(1)} %reduce_sum.59), channel_id=1, replica_groups=mesh['tm'=16,'height'=32] {'tm','height'}, use_global_device_ids=true, to_apply=%region_5.6 | all-reduce | flops 64 | bytes 512 | tf_op jit(solution)/shard_map/psum | solution.py:92
  142.3 1.9 select_reduce_fusion.1
  144.7 94.3 %all-reduce.4 = (f32[32]{0:T(128)S(1)}, f32[32]{0:T(128)S(1)}) all-reduce(f32[32]{0:T(128)S(1)} %reduce_sum.84, f32[32]{0:T(128)S(1)} %reduce_sum.81), channel_id=1, replica_groups=mesh['tm'=16,'height'=32] {'tm','height'}, use_global_device_ids=true, to_apply=%region_11.12 | all-reduce | flops 64 | bytes 512 | tf_op jit(solution)/shard_map/psum | solution.py:113
  239.8 2.4 collective-permute-start.3
  242.9 2.0 convolution_select_fusion
  245.8 3.0 collective-permute-start.9
  254.3 2.8 collective-permute-start.4
  257.1 1.9 collective-permute-start.5
  259.3 3.1 collective-permute-done.5
  263.3 0.8 fusion.36
  268.1 0.8 fusion.35
  268.9 0.8 fusion.50
  270.6 0.8 fusion.34
  273.8 0.8 fusion.46
  275.4 0.8 fusion.32
  281.1 0.8 fusion.39
  282.7 0.8 fusion.30
  284.5 1.9 collective-permute-start.10
  286.6 1.2 collective-permute-done.10
  287.9 1.3 collective-permute-start.11
  291.0 3.8 collective-permute-done.11
  295.8 272.6 %all-reduce.9.cloned.1.call-done = (f32[3,3,3,192,96]{4,3,2,1,0:T(8,128)}, f32[3,3,3,96,96]{4,3,2,1,0:T(8,128)}) async-done(((f32[3,3,3,192,96]{4,3,2,1,0:T(8,128)}, f32[3,3,3,96,96]{4,3,2,1,0:T(8,128)}), (f32[3,3,3,192,96]{4,3,2,1,0:T(8,128)}, f32[3,3,3,96,96]{4,3,2,1,0:T(8,128)})) %all-reduce.9.cloned.1.call-update) | async-done | bytes 2986000 | tf_op jit(solution)/shard_map/psum | solution.py:135
  568.4 3.7 broadcast_multiply_fusion
  572.1 1.2 broadcast_multiply_fusion.1
  (147 shorter events, 30.8 us)
Async XLA Ops:
  7.2 18.6 %copy-start = (bf16[3,3,3,192,96]{4,3,2,1,0:T(8,128)(2,1)S(1)}, bf16[3,3,3,192,96]{4,3,2,1,0:T(8,128)(2,1)}, u32[]{:S(2)}) copy-start(bf16[3,3,3,192,96]{4,3,2,1,0:T(8,128)(2,1)} %param.16) | copy-start | bytes 2985988
  7.2 561.2 %all-reduce.9.cloned.1.call-start = ((), (), s32[]{:S(2)}) async-start(), calls=%async_computation | async-start | bytes 7962624 | tf_op jit(solution)/shard_map/psum | solution.py:135
  7.2 6.3 %collective-permute-start = (bf16[2,2,16,192]{3,2,1,0:T(8,128)(2,1)}, bf16[2,2,16,192]{3,2,1,0:T(8,128)(2,1)S(1)}, u32[]{:S(2)}, u32[]{:S(2)}) collective-permute-start(bf16[2,2,16,192]{3,2,1,0:T(8,128)(2,1)} %param.14), channel_id=1, source_target_pairs={{0,32},{32,64},{64,96},{96,128},{128,160},{160,192},{192,224},{224... | collective-permute-start | bytes 73736 | tf_op jit(solution)/shard_map/ppermute | solution.py:15
  11.4 10.3 %collective-permute-start.6 = (bf16[2,4,32,96]{3,2,1,0:T(8,128)(2,1)}, bf16[2,4,32,96]{3,2,1,0:T(8,128)(2,1)S(1)}, u32[]{:S(2)}, u32[]{:S(2)}) collective-permute-start(bf16[2,4,32,96]{3,2,1,0:T(8,128)(2,1)} %param.15), channel_id=1, source_target_pairs={{32,0},{64,32},{96,64},{128,96},{160,128},{192,160},{224,192},{256... | collective-permute-start | bytes 147464 | tf_op jit(solution)/shard_map/ppermute | solution.py:15
  14.3 9.6 %collective-permute-start.1 = (bf16[4,1,16,192]{3,2,1,0:T(8,128)(2,1)S(1)}, bf16[4,1,16,192]{3,2,1,0:T(8,128)(2,1)S(1)}, u32[]{:S(2)}, u32[]{:S(2)}) collective-permute-start(bf16[4,1,16,192]{3,2,1,0:T(8,128)(2,1)S(1)} %get-tuple-element.74), channel_id=1, source_target_pairs={{0,1},{1,2},{2,3},{3,4},{4,5},{5,6},{6,7},{7,8},{8,9},{9,10},{10,1... | collective-permute-start | bytes 73736 | tf_op jit(solution)/shard_map/ppermute | solution.py:26
  18.3 5.6 collective-permute-start.2
  21.7 120.2 %collective-permute-start.7 = (bf16[4,1,32,96]{3,2,1,0:T(8,128)(2,1)S(1)}, bf16[4,1,32,96]{3,2,1,0:T(8,128)(2,1)S(1)}, u32[]{:S(2)}, u32[]{:S(2)}) collective-permute-start(bf16[4,1,32,96]{3,2,1,0:T(8,128)(2,1)S(1)} %get-tuple-element.70), channel_id=1, source_target_pairs={{0,1},{1,2},{2,3},{3,4},{4,5},{5,6},{6,7},{7,8},{8,9},{9,10},{10,1... | collective-permute-start | bytes 73736 | tf_op jit(solution)/shard_map/ppermute | solution.py:26
  25.2 0.7 copy-start.7
  27.0 115.3 %copy-start.4 = (f32[96]{0:T(128)S(1)}, f32[96]{0:T(128)}, u32[]{:S(2)}) copy-start(f32[96]{0:T(128)} %param.19) | copy-start | bytes 1156
  27.0 115.3 %copy-start.5 = (f32[96]{0:T(128)S(1)}, f32[96]{0:T(128)}, u32[]{:S(2)}) copy-start(f32[96]{0:T(128)} %param.18) | copy-start | bytes 1156
  27.4 114.5 %collective-permute-start.8 = (bf16[4,1,32,96]{3,2,1,0:T(8,128)(2,1)S(1)}, bf16[4,1,32,96]{3,2,1,0:T(8,128)(2,1)S(1)}, u32[]{:S(2)}, u32[]{:S(2)}) collective-permute-start(bf16[4,1,32,96]{3,2,1,0:T(8,128)(2,1)S(1)} %get-tuple-element.71), channel_id=1, source_target_pairs={{1,0},{2,1},{3,2},{4,3},{5,4},{6,5},{7,6},{8,7},{9,8},{10,9},{11,1... | collective-permute-start | bytes 73736 | tf_op jit(solution)/shard_map/ppermute | solution.py:28
  239.8 14.5 %collective-permute-start.3 = (bf16[2,4,32,96]{3,2,1,0:T(8,128)(2,1)S(1)}, bf16[2,4,32,96]{3,2,1,0:T(8,128)(2,1)S(1)}, u32[]{:S(2)}, u32[]{:S(2)}) collective-permute-start(bf16[2,4,32,96]{3,2,1,0:T(8,128)(2,1)S(1)} %get-tuple-element.69), channel_id=1, source_target_pairs={{0,32},{32,64},{64,96},{96,128},{128,160},{160,192},{192,224},{224... | collective-permute-start | bytes 147464 | tf_op jit(solution)/shard_map/ppermute | solution.py:15
  242.2 0.7 copy-start.9
  245.8 40.7 %collective-permute-start.9 = (bf16[4,32,192]{2,0,1:T(4,128)(2,1)S(1)}, bf16[4,32,192]{2,0,1:T(4,128)(2,1)S(1)}, u32[]{:S(2)}, u32[]{:S(2)}) collective-permute-start(bf16[4,32,192]{2,0,1:T(4,128)(2,1)S(1)} %get-tuple-element.67), channel_id=1, source_target_pairs={{1,0},{2,1},{3,2},{4,3},{5,4},{6,5},{7,6},{8,7},{9,8},{10,9},{11,1... | collective-permute-start | bytes 147464 | tf_op jit(solution)/shard_map/ppermute | solution.py:15
  253.6 8.8 %copy-start.3 = (bf16[2,4,32,96]{3,2,1,0:T(8,128)(2,1)S(1)}, bf16[2,4,32,96]{3,2,1,0:T(8,128)(2,1)}, u32[]{:S(2)}) copy-start(bf16[2,4,32,96]{3,2,1,0:T(8,128)(2,1)} %param.15) | copy-start | bytes 147460
  254.3 4.9 collective-permute-start.4
  257.1 5.2 collective-permute-start.5
  259.3 9.7 %copy-start.1 = (f32[27,192,96]{2,1,0:T(8,128)}, f32[27,192,96]{2,1,0:T(8,128)S(1)}, u32[]{:S(2)}) copy-start(f32[27,192,96]{2,1,0:T(8,128)S(1)} %fusion.3) | copy-start | bytes 5971972
  284.5 3.2 collective-permute-start.10
  286.5 3.1 copy-start.6
  286.5 3.1 copy-start.8
  287.9 6.9 %collective-permute-start.11 = (bf16[2,4,32,192]{3,0,2,1:T(2,128)(2,1)S(1)}, bf16[2,4,32,192]{3,0,2,1:T(2,128)(2,1)S(1)}, u32[]{:S(2)}, u32[]{:S(2)}) collective-permute-start(bf16[2,4,32,192]{3,0,2,1:T(2,128)(2,1)S(1)} %slice.514), channel_id=1, source_target_pairs={{32,0},{64,32},{96,64},{128,96},{160,128},{192,160},{224,192},{256... | collective-permute-start | bytes 294920 | tf_op jit(solution)/shard_map/ppermute | solution.py:15
  568.4 3.7 copy-start.2
Sparse Core Ops, SparseCore 0:
  284.5 283.9 all-reduce.8
where the time goes:
time: 581 us; the launch traced here: 580 us
  waiting for transfers between devices  281 us (48%)
  blocking collectives  206 us (35%)
  matrix products  33.2 us (6%)
  starting transfers between devices  30.5 us (5%)
  between operations  14.9 us (3%)
  local copies, waits for them, and re-layouts  8.48 us (1%)
  other arithmetic  6.23 us (1%)
    psum x1, waiting for transfers between devices, body(): summed_one, summed_two = lax.psum((local_one, local_two), ('tm', 'height'))  273 us
    psum x1, blocking collectives, body(): lax.psum((jnp.sum(grouped, (0, 1, 2, 4)), jnp.sum(grouped * grouped, (0,...  112 us
    psum x1, blocking collectives, body(): lax.psum((jnp.sum(grad_grouped, (0, 1, 2, 4)), jnp.sum(grad_grouped * nor...  94.3 us
    dot_general x54, matrix products, taps(): lax.dot_general(patch, flat_grad, (((0,), (0,)), ((), ())), preferred_ele...  27.5 us
    ppermute x6, starting transfers between devices, shifted_2(): lax.ppermute(value, axis, [(source, source + steps) for source in range(f...  14.1 us
  transfers between devices with their start and end apart: 13, of which 4 were waited for; matrix products, arithmetic and copies ran while one was open for 7% of the time, Pallas kernels for 0%

commit v1 on v0

v1 whole, which is shorter than its diff:
```python
import functools

import jax
import jax.numpy as jnp
from jax import lax
from jax.sharding import Mesh
from jax.sharding import PartitionSpec as P

GROUPS = 32
EPSILON = 1e-05

TM = ("zh", "y")
HEIGHT = ("zl", "x", "c")
REST = ("zh", "y", "zl")


def fine_mesh(mesh):
    tm, height = mesh.shape["tm"], mesh.shape["height"]
    zh = 2 if tm % 2 == 0 else 1
    core = 2
    x = 4 if height % 8 == 0 else height // 2
    return Mesh(mesh.devices.reshape(zh, tm // zh, height // (core * x), x, core), TM + HEIGHT)


def neighbour(value, axis, steps):
    count = lax.axis_size(axis)
    first, last = max(0, -steps), min(count, count - steps)
    return lax.ppermute(value, axis, [(i, i + steps) for i in range(first, last)])


def row_halo(cells):
    return jnp.concatenate(
        [neighbour(cells[:, -1:], HEIGHT, 1), cells, neighbour(cells[:, :1], HEIGHT, -1)], axis=1
    )


def sum_everywhere(value, stages):
    for axes in stages:
        count = lax.axis_size(axes)
        value = lax.all_to_all(jnp.broadcast_to(value[None], (count,) + value.shape), axes, 0, 0).sum(0)
    return value


def conv(padded, weight):
    return lax.conv_general_dilated(
        padded[None],
        weight,
        (1, 1, 1),
        "VALID",
        dimension_numbers=("NDHWC", "DHWIO", "NDHWC"),
        preferred_element_type=jnp.float32,
    )[0]


def flipped(weight):
    return jnp.transpose(jnp.flip(weight, (0, 1, 2)), (0, 1, 2, 4, 3))


def pad_cols(field):
    return jnp.pad(field, ((0, 0), (0, 0), (1, 1), (0, 0)))


def upsample(field):
    return jnp.repeat(jnp.repeat(field, 2, 1), 2, 2)


def pooled(grad):
    frames, rows, cols, outs = grad.shape
    row_sets = []
    for b in range(3):
        part = grad[:, 2 - b : 2 - b + rows - 2]
        row_sets.append(part.reshape(frames, (rows - 2) // 2, 2, cols, outs).sum(2))
    pieces = []
    for part in row_sets:
        wide = jnp.pad(part, ((0, 0), (0, 0), (1, 1), (0, 0)))
        for e in range(3):
            cell = wide[:, :, 2 - e : 2 - e + cols].reshape(frames, (rows - 2) // 2, cols // 2, 2, outs)
            pieces.append(cell.sum(3))
    return jnp.concatenate(pieces, -1)


def pack(local_one, local_two):
    both = jnp.concatenate([local_one.reshape(-1, 864), local_two.reshape(-1, 864)], 0)
    both = jnp.pad(both, ((0, 0), (0, 32)))
    rows = both.shape[0]
    return jnp.transpose(both.reshape(rows, 7, 128), (1, 0, 2)).reshape(7 * rows, 128)


def unpack(packed, ins, mids):
    rows = 3 * (ins + mids)
    both = jnp.transpose(packed[: 7 * rows].reshape(7, rows, 128), (1, 0, 2)).reshape(rows, 896)
    both = both[:, : 9 * mids]
    one, two = both[: 3 * ins], both[3 * ins :]
    one = jnp.transpose(one.reshape(3, ins, 3, 3, mids), (0, 2, 3, 1, 4))
    two = jnp.transpose(two.reshape(3, mids, 3, 3, mids), (0, 2, 3, 1, 4))
    return one, two


def sum_large(packed):
    core, xs, rest = lax.axis_size("c"), lax.axis_size("x"), lax.axis_size(REST)
    rows = packed.shape[0]
    unit = core * xs * rest
    piece = -(-rows // unit)
    packed = jnp.pad(packed, ((0, piece * unit - rows), (0, 0)))
    swap = [(0, 1), (1, 0)]
    mine = lax.axis_index("c")
    halves = packed.reshape(2, -1, 128)
    away = lax.dynamic_index_in_dim(halves, 1 - mine, 0, False).astype(jnp.bfloat16)
    kept = lax.dynamic_index_in_dim(halves, mine, 0, False)
    part = kept + lax.ppermute(away, "c", swap).astype(jnp.float32)
    part = part.astype(jnp.bfloat16).reshape(xs, -1, 128)
    part = lax.all_to_all(part, "x", 0, 0).astype(jnp.float32).sum(0)
    part = lax.all_to_all(part.reshape(rest, piece, 128), REST, 0, 0).sum(0)
    part = part.astype(jnp.bfloat16)
    part = lax.all_to_all(jnp.broadcast_to(part[None], (rest, piece, 128)), REST, 0, 0)
    part = part.reshape(rest * piece, 128)
    part = lax.all_to_all(jnp.broadcast_to(part[None], (xs,) + part.shape), "x", 0, 0)
    part = part.reshape(-1, 128)
    other = lax.ppermute(part, "c", swap)
    low = jnp.where(mine == 0, part, other)
    high = jnp.where(mine == 0, other, part)
    return jnp.concatenate([low, high], 0)


def body(features, cotangent, weight_one, weight_two, norm_gain, norm_shift):
    frames, ins = features.shape[0], features.shape[-1]
    mids = cotangent.shape[-1]
    devices_all = lax.axis_size(TM) * lax.axis_size(HEIGHT)
    per_group = mids // GROUPS
    member = jnp.arange(mids) // per_group
    same_group = (member[:, None] == member[None]).astype(jnp.float32)

    def group_sums(first, second, stages):
        both = jnp.stack([first, second])
        both = jnp.dot(both, same_group, precision=lax.Precision.HIGHEST)
        return sum_everywhere(both, stages)

    timed = jnp.concatenate([neighbour(features, TM, 1), features], 0)
    rowed = row_halo(timed)
    padded_in = pad_cols(upsample(rowed)[:, 1:-1])
    pre_norm = conv(padded_in, weight_one)
    shape = pre_norm.shape
    count = shape[0] * shape[1] * shape[2] * per_group * devices_all
    total_one, total_two = group_sums(
        jnp.sum(pre_norm, (0, 1, 2)), jnp.sum(pre_norm * pre_norm, (0, 1, 2)), (HEIGHT, TM)
    )
    cot_rowed = row_halo(jnp.concatenate([cotangent, neighbour(cotangent, TM, -1)], 0))
    grad_hidden = conv(pad_cols(cot_rowed), flipped(weight_two))

    mean = total_one / count
    rstd = lax.rsqrt(total_two / count - mean * mean + EPSILON)
    normed = (pre_norm - mean) * rstd
    shifted = normed * norm_gain + norm_shift
    sigma = jax.nn.sigmoid(shifted)
    hidden = (shifted * sigma).astype(jnp.bfloat16)
    grad_normed = grad_hidden * sigma * (1.0 + shifted * (1.0 - sigma)) * norm_gain
    sum_first, sum_second = group_sums(
        jnp.sum(grad_normed, (0, 1, 2)),
        jnp.sum(grad_normed * normed, (0, 1, 2)),
        (("y", "c"), ("zh", "zl", "x")),
    )
    mid_rowed = row_halo(jnp.concatenate([neighbour(hidden[frames - 2 :], TM, 1), hidden], 0))
    decoded = conv(pad_cols(mid_rowed), weight_two).astype(jnp.bfloat16)

    scale = 1.0 / (shape[0] * shape[1] * shape[2] * devices_all) ** 0.5
    wide_cot = pad_cols(cot_rowed)
    shifted_cot = jnp.concatenate(
        [
            wide_cot[:, 2 - b : 2 - b + shape[1], 2 - e : 2 - e + shape[2]]
            for b in range(3)
            for e in range(3)
        ],
        -1,
    )
    flat_hidden = hidden.reshape(-1, mids)
    local_two = jnp.stack(
        [
            lax.dot_general(
                flat_hidden,
                shifted_cot[2 - a : 2 - a + frames].reshape(-1, 9 * mids),
                (((0,), (0,)), ((), ())),
                preferred_element_type=jnp.float32,
            )
            for a in range(3)
        ]
    )

    first = sum_first / count
    second = sum_second / count
    grad_pre = ((grad_normed - first - normed * second) * rstd).astype(jnp.bfloat16)
    local = pooled(jnp.pad(grad_pre, ((0, 0), (3, 3), (0, 0), (0, 0))).astype(jnp.float32))
    local = local.astype(jnp.bfloat16).reshape(-1, 9 * mids)
    local_one = jnp.stack(
        [
            lax.dot_general(
                rowed[a : a + frames].reshape(-1, ins),
                local,
                (((0,), (0,)), ((), ())),
                preferred_element_type=jnp.float32,
            )
            for a in range(3)
        ]
    )
    summed_one, summed_two = unpack(sum_large(pack(local_one, local_two)), ins, mids)
    grad_one = summed_one.astype(jnp.float32) * scale
    grad_two = summed_two.astype(jnp.float32) * scale

    grad_rowed = row_halo(jnp.concatenate([grad_pre, neighbour(grad_pre, TM, -1)], 0))
    cells = pooled(grad_rowed.astype(jnp.float32)).astype(jnp.bfloat16)
    back = jnp.transpose(weight_one, (0, 1, 2, 4, 3)).reshape(3, 9 * mids, ins)
    grad_features = sum(
        lax.dot_general(
            cells[2 - a : 2 - a + frames],
            back[a],
            (((3,), (0,)), ((), ())),
            preferred_element_type=jnp.float32,
        )
        for a in range(3)
    )
    return decoded, grad_features, grad_one, grad_two


def solution(mesh):
    split = P(TM, HEIGHT, None, None)
    return jax.shard_map(
        body,
        mesh=fine_mesh(mesh),
        in_specs=(split, split, P(), P(), P(), P()),
        out_specs=(split, split, P(), P()),
        check_vma=False,
    )
```

time: 581 us -> 247 us (0.43)
  waiting for transfers between devices: 281 us -> 49.5 us
  blocking collectives: 206 us -> 14.4 us
  starting transfers between devices: 30.5 us -> 105 us
  local copies, waits for them, and re-layouts: 8.48 us -> 46.4 us
  matrix products: 33.2 us -> 5.71 us
  other arithmetic: 6.23 us -> 22.9 us
  between operations: 14.9 us -> 1.65 us
    psum x1 -> x0, waiting for transfers between devices: 273 us -> none  [body(): summed_one, summed_two = lax.psum((local_one, local_two), ('tm', 'height'))]
    psum x2 -> x0, blocking collectives: 206 us -> none  [the longest x1 112 us: body(): lax.psum((jnp.sum(grouped, (0, 1, 2, 4)), jnp.sum(grouped * grouped, (0,...]
    all_to_all x0 -> x7, starting transfers between devices: none -> 61.5 us  [the longest x4 35.7 us: sum_everywhere(): lax.all_to_all(jnp.broadcast_to(value[None], (count,) + value.shape), axe...]
    all_to_all x0 -> x7, waiting for transfers between devices: none -> 39.1 us  [the longest x4 31 us: sum_everywhere(): lax.all_to_all(jnp.broadcast_to(value[None], (count,) + value.shape), axe...]
    dot_general x54 -> x11, matrix products: 27.5 us -> 3.18 us  [the longest x3 1.25 us: body(): lax.dot_general(cells[2 - a:2 - a + frames], back[a], (((3,), (0,)), ((),...]
    all_to_all x0 -> x1, blocking collectives: none -> 14.4 us  [sum_large(): part = lax.all_to_all(part, 'x', 0, 0).astype(jnp.float32).sum(0)]
    ppermute x12 -> x14, starting transfers between devices: 30.4 us -> 43.5 us  [the longest x12 35 us: neighbour(): lax.ppermute(value, axis, [(i, i + steps) for i in range(first, last)])]
    reduce_sum x5 -> x32, other arithmetic: 0.59 us -> 10.8 us  [the longest x18 5.86 us: pooled(): pieces.append(cell.sum(3))]
  transfers between devices with their start and end apart: 13 -> 21, of which waited for: 4 -> 9; matrix products, arithmetic and copies ran while one was open for 7% -> 12% of each run, Pallas kernels for 0% -> 0%
where the time goes in v1:
time: 247 us; the launch traced here: 246 us
  starting transfers between devices  105 us (43%)
  waiting for transfers between devices  49.5 us (20%)
  local copies, waits for them, and re-layouts  46.4 us (19%)
  other arithmetic  22.9 us (9%)
  blocking collectives  14.4 us (6%)
  matrix products  5.71 us (2%)
    all_to_all x4, starting transfers between devices, sum_everywhere(): lax.all_to_all(jnp.broadcast_to(value[None], (count,) + value.shape), axe...  35.7 us
    ppermute x12, starting transfers between devices, neighbour(): lax.ppermute(value, axis, [(i, i + steps) for i in range(first, last)])  35 us
    all_to_all x4, waiting for transfers between devices, sum_everywhere(): lax.all_to_all(jnp.broadcast_to(value[None], (count,) + value.shape), axe...  31 us
    all_to_all x1, starting transfers between devices, sum_large(): lax.all_to_all(jnp.broadcast_to(part[None], (rest, piece, 128)), REST, 0, 0)  14.9 us
    all_to_all x1, blocking collectives, sum_large(): part = lax.all_to_all(part, 'x', 0, 0).astype(jnp.float32).sum(0)  14.4 us
    unnamed x29, local copies, waits for them, and re-layouts  13 us
    ppermute x12, waiting for transfers between devices, neighbour(): lax.ppermute(value, axis, [(i, i + steps) for i in range(first, last)])  8.46 us
    all_to_all x1, starting transfers between devices, sum_large(): lax.all_to_all(jnp.broadcast_to(part[None], (xs,) + part.shape), 'x', 0, 0)  6.33 us
  transfers between devices with their start and end apart: 21, of which 9 were waited for; matrix products, arithmetic and copies ran while one was open for 12% of the time, Pallas kernels for 0%

profile of v1, /device:TPU:1, one launch (start us, length us, event | category | flops | bytes accessed | tf_op | source)
XLA Modules:
  0.0 245.6 jit_solution(9639642550023463645)
XLA Ops:
  0.6 4.2 %collective-permute-start = (bf16[2,2,16,192]{3,2,1,0:T(8,128)(2,1)}, bf16[2,2,16,192]{3,2,1,0:T(8,128)(2,1)S(1)}, u32[]{:S(2)}, u32[]{:S(2)}) collective-permute-start(bf16[2,2,16,192]{3,2,1,0:T(8,128)(2,1)} %param.6), channel_id=1, source_target_pairs={{0,32},{32,64},{64,96},{96,128},{128,160},{160,192},{192,224},{224... | collective-permute-start | bytes 73736 | tf_op jit(solution)/shard_map/ppermute | solution.py:28
  7.7 4.0 %collective-permute-start.1 = (bf16[4,1,16,192]{3,2,1,0:T(8,128)(2,1)S(1)}, bf16[4,1,16,192]{3,2,1,0:T(8,128)(2,1)S(1)}, u32[]{:S(2)}, u32[]{:S(2)}) collective-permute-start(bf16[4,1,16,192]{3,2,1,0:T(8,128)(2,1)S(1)} %get-tuple-element.73), channel_id=1, source_target_pairs={{0,1},{1,2},{2,3},{3,4},{4,5},{5,6},{6,7},{7,8},{8,9},{9,10},{10,1... | collective-permute-start | bytes 73736 | tf_op jit(solution)/shard_map/ppermute | solution.py:28
  11.7 3.4 %collective-permute-start.2 = (bf16[4,1,16,192]{3,2,1,0:T(8,128)(2,1)S(1)}, bf16[4,1,16,192]{3,2,1,0:T(8,128)(2,1)S(1)}, u32[]{:S(2)}, u32[]{:S(2)}) collective-permute-start(bf16[4,1,16,192]{3,2,1,0:T(8,128)(2,1)S(1)} %get-tuple-element.74), channel_id=1, source_target_pairs={{1,0},{2,1},{3,2},{4,3},{5,4},{6,5},{7,6},{8,7},{9,8},{10,9},{11,1... | collective-permute-start | bytes 73736 | tf_op jit(solution)/shard_map/ppermute | solution.py:28
  19.1 2.4 collective-permute-start.8
  25.1 11.8 %all-to-all-start = ((f32[32,2,96]{2,1,0:T(2,128)}), f32[32,2,96]{2,1,0:T(2,128)S(1)}, u32[]{:S(2)}, u32[]{:S(2)}) async-start(f32[32,2,96]{2,1,0:T(2,128)} %broadcast_in_dim.27), calls=%async_computation | async-start | bytes 65536 | tf_op jit(solution)/shard_map/all_to_all | solution.py:40
  37.6 7.0 %all-to-all-done = f32[32,2,96]{2,1,0:T(2,128)S(1)} async-done(((f32[32,2,96]{2,1,0:T(2,128)}), f32[32,2,96]{2,1,0:T(2,128)S(1)}, u32[]{:S(2)}, u32[]{:S(2)}) %all-to-all-start) | async-done | bytes 24608 | tf_op jit(solution)/shard_map/all_to_all | solution.py:40
  45.2 15.0 %all-to-all-start.1 = ((f32[16,2,96]{2,1,0:T(2,128)}), f32[16,2,96]{2,1,0:T(2,128)S(1)}, u32[]{:S(2)}, u32[]{:S(2)}) async-start(f32[16,2,96]{2,1,0:T(2,128)} %broadcast_in_dim.28), calls=%async_computation.1 | async-start | bytes 32768 | tf_op jit(solution)/shard_map/all_to_all | solution.py:40
  61.8 9.7 %all-to-all-done.1 = f32[16,2,96]{2,1,0:T(2,128)S(1)} async-done(((f32[16,2,96]{2,1,0:T(2,128)}), f32[16,2,96]{2,1,0:T(2,128)S(1)}, u32[]{:S(2)}, u32[]{:S(2)}) %all-to-all-start.1) | async-done | bytes 12320 | tf_op jit(solution)/shard_map/all_to_all | solution.py:40
  73.0 5.1 %all-to-all-start.2 = ((f32[16,2,96]{2,1,0:T(2,128)}), f32[16,2,96]{2,1,0:T(2,128)S(1)}, u32[]{:S(2)}, u32[]{:S(2)}) async-start(f32[16,2,96]{2,1,0:T(2,128)} %broadcast_in_dim.31), calls=%async_computation.2 | async-start | bytes 32768 | tf_op jit(solution)/shard_map/all_to_all | solution.py:40
  78.4 7.2 %all-to-all-done.2 = f32[16,2,96]{2,1,0:T(2,128)S(1)} async-done(((f32[16,2,96]{2,1,0:T(2,128)}), f32[16,2,96]{2,1,0:T(2,128)S(1)}, u32[]{:S(2)}, u32[]{:S(2)}) %all-to-all-start.2) | async-done | bytes 12320 | tf_op jit(solution)/shard_map/all_to_all | solution.py:40
  86.2 3.9 %all-to-all-start.3 = ((f32[32,2,96]{2,1,0:T(2,128)}), f32[32,2,96]{2,1,0:T(2,128)S(1)}, u32[]{:S(2)}, u32[]{:S(2)}) async-start(f32[32,2,96]{2,1,0:T(2,128)} %broadcast_in_dim.32), calls=%async_computation.3 | async-start | bytes 65536 | tf_op jit(solution)/shard_map/all_to_all | solution.py:40
  91.6 7.2 %all-to-all-done.3 = f32[32,2,96]{2,1,0:T(2,128)S(1)} async-done(((f32[32,2,96]{2,1,0:T(2,128)}), f32[32,2,96]{2,1,0:T(2,128)S(1)}, u32[]{:S(2)}, u32[]{:S(2)}) %all-to-all-start.3) | async-done | bytes 24608 | tf_op jit(solution)/shard_map/all_to_all | solution.py:40
  103.5 2.3 copy.293
  105.8 3.5 %select_maximum_fusion = f32[864,896]{0,1:T(8,128)} fusion(f32[288,864]{0,1:T(8,128)} %copy.294, f32[576,864]{0,1:T(8,128)S(1)} %copy.293), kind=kLoop, calls=%fused_computation | loop fusion | flops 3096576 | bytes 6082560 | tf_op jit(solution)/shard_map/concatenate | solution.py:83
  109.3 4.3 %copy.295 = f32[7,864,128]{2,1,0:T(8,128)} copy(f32[7,864,128]{1,2,0:T(8,128)} %bitcast.175) | data formatting | bytes 6193152 | tf_op jit(solution)/shard_map/transpose | solution.py:86
  113.6 2.1 pad.55
  117.4 3.4 %collective-permute-start.12 = (bf16[3072,128]{1,0:T(8,128)(2,1)S(1)}, bf16[3072,128]{1,0:T(8,128)(2,1)S(1)}, u32[]{:S(2)}, u32[]{:S(2)}) collective-permute-start(bf16[3072,128]{1,0:T(8,128)(2,1)S(1)} %fusion.3), channel_id=1, source_target_pairs={{0,1},{1,0},{2,3},{3,2},{4,5},{5,4},{6,7},{7,6},{8,9},{9,8},{10,11... | collective-permute-start | bytes 2359304 | tf_op jit(solution)/shard_map/ppermute | solution.py:110
  124.3 14.4 %all_to_all.40 = bf16[4,768,128]{2,1,0:T(8,128)(2,1)S(1)} all-to-all(bf16[4,768,128]{2,1,0:T(8,128)(2,1)S(1)} %bitcast.186), channel_id=1, replica_groups=mesh['zh'=2,'y'=8,'zl'=4,'x'=4,'c'=2] {'x'}, dimensions={0} | all-to-all | bytes 1572864 | tf_op jit(solution)/shard_map/all_to_all | solution.py:112
  139.6 4.6 %all-to-all-start.5 = ((f32[64,12,128]{2,1,0:T(8,128)}), f32[64,12,128]{2,1,0:T(8,128)S(1)}, u32[]{:S(2)}, u32[]{:S(2)}) async-start(f32[64,12,128]{2,1,0:T(8,128)} %reshape.244), calls=%async_computation.5 | async-start | bytes 1048576 | tf_op jit(solution)/shard_map/all_to_all | solution.py:113
  144.3 2.8 %collective-permute-start.3 = (bf16[2,4,32,96]{3,1,2,0:T(4,128)(2,1)S(1)}, bf16[2,4,32,96]{3,1,2,0:T(4,128)(2,1)S(1)}, u32[]{:S(2)}, u32[]{:S(2)}) collective-permute-start(bf16[2,4,32,96]{3,1,2,0:T(4,128)(2,1)S(1)} %get-tuple-element.52), channel_id=1, source_target_pairs={{0,32},{32,64},{64,96},{96,128},{128,160},{160,192},{192,224},{224... | collective-permute-start | bytes 147464 | tf_op jit(solution)/shard_map/ppermute | solution.py:28
  147.1 6.6 %collective-permute-done.3 = bf16[2,4,32,96]{3,1,2,0:T(4,128)(2,1)S(1)} collective-permute-done((bf16[2,4,32,96]{3,1,2,0:T(4,128)(2,1)S(1)}, bf16[2,4,32,96]{3,1,2,0:T(4,128)(2,1)S(1)}, u32[]{:S(2)}, u32[]{:S(2)}) %collective-permute-start.3) | collective-permute-done | bytes 49184 | tf_op jit(solution)/shard_map/ppermute | solution.py:28
  153.9 5.3 %collective-permute-start.4 = (bf16[4,1,32,96]{3,1,2,0:T(2,128)(2,1)S(1)}, bf16[4,1,32,96]{3,1,2,0:T(2,128)(2,1)S(1)}, u32[]{:S(2)}, u32[]{:S(2)}) collective-permute-start(bf16[4,1,32,96]{3,1,2,0:T(2,128)(2,1)S(1)} %get-tuple-element.71), channel_id=1, source_target_pairs={{0,1},{1,2},{2,3},{3,4},{4,5},{5,6},{6,7},{7,8},{8,9},{9,10},{10,1... | collective-permute-start | bytes 73736 | tf_op jit(solution)/shard_map/ppermute | solution.py:28
  167.4 14.9 %all-to-all-start.6 = ((bf16[64,12,128]{2,1,0:T(8,128)(2,1)}), bf16[64,12,128]{2,1,0:T(8,128)(2,1)S(1)}, u32[]{:S(2)}, u32[]{:S(2)}) async-start(bf16[64,12,128]{2,1,0:T(8,128)(2,1)} %broadcast_in_dim.33), calls=%async_computation.6 | async-start | bytes 524288 | tf_op jit(solution)/shard_map/all_to_all | solution.py:115
  183.8 4.2 %collective-permute-start.10 = (bf16[4,1,32,96]{3,1,2,0:T(2,128)(2,1)}, bf16[4,1,32,96]{3,1,2,0:T(2,128)(2,1)S(1)}, u32[]{:S(2)}, u32[]{:S(2)}) collective-permute-start(bf16[4,1,32,96]{3,1,2,0:T(2,128)(2,1)} %get-tuple-element.67), channel_id=1, source_target_pairs={{0,1},{1,2},{2,3},{3,4},{4,5},{5,6},{6,7},{7,8},{8,9},{9,10},{10,1... | collective-permute-start | bytes 73736 | tf_op jit(solution)/shard_map/ppermute | solution.py:28
  188.0 2.4 collective-permute-start.11
  191.1 3.7 %all-to-all-done.6 = bf16[64,12,128]{2,1,0:T(8,128)(2,1)S(1)} async-done(((bf16[64,12,128]{2,1,0:T(8,128)(2,1)}), bf16[64,12,128]{2,1,0:T(8,128)(2,1)S(1)}, u32[]{:S(2)}, u32[]{:S(2)}) %all-to-all-start.6) | async-done | bytes 196640 | tf_op jit(solution)/shard_map/all_to_all | solution.py:115
  195.8 6.3 %all-to-all-start.7 = ((bf16[4,768,128]{2,1,0:T(8,128)(2,1)}), bf16[4,768,128]{2,1,0:T(8,128)(2,1)S(1)}, u32[]{:S(2)}, u32[]{:S(2)}) async-start(bf16[4,768,128]{2,1,0:T(8,128)(2,1)} %broadcast_in_dim.35), calls=%async_computation.7 | async-start | bytes 1572864 | tf_op jit(solution)/shard_map/all_to_all | solution.py:117
  208.0 4.4 %all-to-all-done.7 = bf16[4,768,128]{2,1,0:T(8,128)(2,1)S(1)} async-done(((bf16[4,768,128]{2,1,0:T(8,128)(2,1)}), bf16[4,768,128]{2,1,0:T(8,128)(2,1)S(1)}, u32[]{:S(2)}, u32[]{:S(2)}) %all-to-all-start.7) | async-done | bytes 786464 | tf_op jit(solution)/shard_map/all_to_all | solution.py:117
  212.4 5.2 %collective-permute-start.13 = (bf16[3072,128]{1,0:T(8,128)(2,1)S(1)}, bf16[3072,128]{1,0:T(8,128)(2,1)}, u32[]{:S(2)}, u32[]{:S(2)}) collective-permute-start(bf16[3072,128]{1,0:T(8,128)(2,1)S(1)} %bitcast.185), channel_id=1, source_target_pairs={{0,1},{1,0},{2,3},{3,2},{4,5},{5,4},{6,7},{7,6},{8,9},{9,8},{10,11... | collective-permute-start | bytes 2359304 | tf_op jit(solution)/shard_map/ppermute | solution.py:119
  227.9 2.9 %copy.296 = bf16[864,7,128]{0,2,1:T(8,128)(2,1)S(1)} copy(bf16[864,7,128]{2,0,1:T(8,128)(2,1)} %bitcast.183) | data formatting | bytes 3096576 | tf_op jit(solution)/shard_map/transpose | solution.py:91
  238.1 3.7 %mul.102 = f32[3,192,3,3,96]{4,3,2,1,0:T(4,128)} reshape(f32[576,864]{1,0:T(8,128)S(1)} %convert_multiply_fusion) | data formatting | bytes 3981312 | tf_op jit(solution)/shard_map/mul | solution.py:205
  241.8 3.8 %copy.300 = f32[3,3,3,192,96]{4,3,2,1,0:T(8,128)} copy(f32[3,3,3,192,96]{4,2,1,3,0:T(4,128)} %bitcast.174) | data formatting | bytes 3981312
  (181 shorter events, 62.6 us)
Async XLA Ops:
  0.6 59.6 %copy-start = (bf16[3,3,3,96,96]{4,3,2,1,0:T(8,128)(2,1)S(1)}, bf16[3,3,3,96,96]{4,3,2,1,0:T(8,128)(2,1)}, u32[]{:S(2)}) copy-start(bf16[3,3,3,96,96]{4,3,2,1,0:T(8,128)(2,1)} %param.9) | copy-start | bytes 1492996
  0.6 6.3 %collective-permute-start = (bf16[2,2,16,192]{3,2,1,0:T(8,128)(2,1)}, bf16[2,2,16,192]{3,2,1,0:T(8,128)(2,1)S(1)}, u32[]{:S(2)}, u32[]{:S(2)}) collective-permute-start(bf16[2,2,16,192]{3,2,1,0:T(8,128)(2,1)} %param.6), channel_id=1, source_target_pairs={{0,32},{32,64},{64,96},{96,128},{128,160},{160,192},{192,224},{224... | collective-permute-start | bytes 73736 | tf_op jit(solution)/shard_map/ppermute | solution.py:28
  4.8 12.3 %collective-permute-start.6 = (bf16[2,4,32,96]{3,2,1,0:T(8,128)(2,1)}, bf16[2,4,32,96]{3,2,1,0:T(8,128)(2,1)S(1)}, u32[]{:S(2)}, u32[]{:S(2)}) collective-permute-start(bf16[2,4,32,96]{3,2,1,0:T(8,128)(2,1)} %param.7), channel_id=1, source_target_pairs={{32,0},{64,32},{96,64},{128,96},{160,128},{192,160},{224,192},{256... | collective-permute-start | bytes 147464 | tf_op jit(solution)/shard_map/ppermute | solution.py:28
  7.7 7.4 %collective-permute-start.1 = (bf16[4,1,16,192]{3,2,1,0:T(8,128)(2,1)S(1)}, bf16[4,1,16,192]{3,2,1,0:T(8,128)(2,1)S(1)}, u32[]{:S(2)}, u32[]{:S(2)}) collective-permute-start(bf16[4,1,16,192]{3,2,1,0:T(8,128)(2,1)S(1)} %get-tuple-element.73), channel_id=1, source_target_pairs={{0,1},{1,2},{2,3},{3,4},{4,5},{5,6},{6,7},{7,8},{8,9},{9,10},{10,1... | collective-permute-start | bytes 73736 | tf_op jit(solution)/shard_map/ppermute | solution.py:28
  11.7 5.2 %collective-permute-start.2 = (bf16[4,1,16,192]{3,2,1,0:T(8,128)(2,1)S(1)}, bf16[4,1,16,192]{3,2,1,0:T(8,128)(2,1)S(1)}, u32[]{:S(2)}, u32[]{:S(2)}) collective-permute-start(bf16[4,1,16,192]{3,2,1,0:T(8,128)(2,1)S(1)} %get-tuple-element.74), channel_id=1, source_target_pairs={{1,0},{2,1},{3,2},{4,3},{5,4},{6,5},{7,6},{8,7},{9,8},{10,9},{11,1... | collective-permute-start | bytes 73736 | tf_op jit(solution)/shard_map/ppermute | solution.py:28
  17.0 5.3 %copy-start.5 = (bf16[4,1,16,192]{3,2,1,0:T(8,128)(2,1)}, bf16[4,1,16,192]{3,2,1,0:T(8,128)(2,1)S(1)}, u32[]{:S(2)}) copy-start(bf16[4,1,16,192]{3,2,1,0:T(8,128)(2,1)S(1)} %collective-permute-done.2) | copy-start | bytes 73732
  17.1 19.8 %collective-permute-start.7 = (bf16[4,1,32,96]{3,2,1,0:T(8,128)(2,1)S(1)}, bf16[4,1,32,96]{3,2,1,0:T(8,128)(2,1)S(1)}, u32[]{:S(2)}, u32[]{:S(2)}) collective-permute-start(bf16[4,1,32,96]{3,2,1,0:T(8,128)(2,1)S(1)} %get-tuple-element.69), channel_id=1, source_target_pairs={{0,1},{1,2},{2,3},{3,4},{4,5},{5,6},{6,7},{7,8},{8,9},{9,10},{10,1... | collective-permute-start | bytes 73736 | tf_op jit(solution)/shard_map/ppermute | solution.py:28
  19.1 17.9 %collective-permute-start.8 = (bf16[4,1,32,96]{3,2,1,0:T(8,128)(2,1)S(1)}, bf16[4,1,32,96]{3,2,1,0:T(8,128)(2,1)S(1)}, u32[]{:S(2)}, u32[]{:S(2)}) collective-permute-start(bf16[4,1,32,96]{3,2,1,0:T(8,128)(2,1)S(1)} %get-tuple-element.70), channel_id=1, source_target_pairs={{1,0},{2,1},{3,2},{4,3},{5,4},{6,5},{7,6},{8,7},{9,8},{10,9},{11,1... | collective-permute-start | bytes 73736 | tf_op jit(solution)/shard_map/ppermute | solution.py:28
  21.7 1.3 copy-start.3
  21.7 1.3 copy-start.9
  25.1 19.4 %all-to-all-start = ((f32[32,2,96]{2,1,0:T(2,128)}), f32[32,2,96]{2,1,0:T(2,128)S(1)}, u32[]{:S(2)}, u32[]{:S(2)}) async-start(f32[32,2,96]{2,1,0:T(2,128)} %broadcast_in_dim.27), calls=%async_computation | async-start | bytes 65536 | tf_op jit(solution)/shard_map/all_to_all | solution.py:40
  45.2 26.2 %all-to-all-start.1 = ((f32[16,2,96]{2,1,0:T(2,128)}), f32[16,2,96]{2,1,0:T(2,128)S(1)}, u32[]{:S(2)}, u32[]{:S(2)}) async-start(f32[16,2,96]{2,1,0:T(2,128)} %broadcast_in_dim.28), calls=%async_computation.1 | async-start | bytes 32768 | tf_op jit(solution)/shard_map/all_to_all | solution.py:40
  60.2 11.3 %copy-start.7 = (f32[96]{0:T(128)S(1)}, f32[96]{0:T(128)}, u32[]{:S(2)}) copy-start(f32[96]{0:T(128)} %param.11) | copy-start | bytes 1156
  60.2 11.3 %copy-start.8 = (f32[96]{0:T(128)S(1)}, f32[96]{0:T(128)}, u32[]{:S(2)}) copy-start(f32[96]{0:T(128)} %param.10) | copy-start | bytes 1156
  73.0 12.5 %all-to-all-start.2 = ((f32[16,2,96]{2,1,0:T(2,128)}), f32[16,2,96]{2,1,0:T(2,128)S(1)}, u32[]{:S(2)}, u32[]{:S(2)}) async-start(f32[16,2,96]{2,1,0:T(2,128)} %broadcast_in_dim.31), calls=%async_computation.2 | async-start | bytes 32768 | tf_op jit(solution)/shard_map/all_to_all | solution.py:40
  86.2 12.6 %all-to-all-start.3 = ((f32[32,2,96]{2,1,0:T(2,128)}), f32[32,2,96]{2,1,0:T(2,128)S(1)}, u32[]{:S(2)}, u32[]{:S(2)}) async-start(f32[32,2,96]{2,1,0:T(2,128)} %broadcast_in_dim.32), calls=%async_computation.3 | async-start | bytes 65536 | tf_op jit(solution)/shard_map/all_to_all | solution.py:40
  99.8 1.3 copy-start.6
  115.7 1.7 copy-start.1
  117.4 5.3 %collective-permute-start.12 = (bf16[3072,128]{1,0:T(8,128)(2,1)S(1)}, bf16[3072,128]{1,0:T(8,128)(2,1)S(1)}, u32[]{:S(2)}, u32[]{:S(2)}) collective-permute-start(bf16[3072,128]{1,0:T(8,128)(2,1)S(1)} %fusion.3), channel_id=1, source_target_pairs={{0,1},{1,0},{2,3},{3,2},{4,5},{5,4},{6,7},{7,6},{8,9},{9,8},{10,11... | collective-permute-start | bytes 2359304 | tf_op jit(solution)/shard_map/ppermute | solution.py:110
  139.6 27.0 %all-to-all-start.5 = ((f32[64,12,128]{2,1,0:T(8,128)}), f32[64,12,128]{2,1,0:T(8,128)S(1)}, u32[]{:S(2)}, u32[]{:S(2)}) async-start(f32[64,12,128]{2,1,0:T(8,128)} %reshape.244), calls=%async_computation.5 | async-start | bytes 1048576 | tf_op jit(solution)/shard_map/all_to_all | solution.py:113
  144.3 9.5 %collective-permute-start.3 = (bf16[2,4,32,96]{3,1,2,0:T(4,128)(2,1)S(1)}, bf16[2,4,32,96]{3,1,2,0:T(4,128)(2,1)S(1)}, u32[]{:S(2)}, u32[]{:S(2)}) collective-permute-start(bf16[2,4,32,96]{3,1,2,0:T(4,128)(2,1)S(1)} %get-tuple-element.52), channel_id=1, source_target_pairs={{0,32},{32,64},{64,96},{96,128},{128,160},{160,192},{192,224},{224... | collective-permute-start | bytes 147464 | tf_op jit(solution)/shard_map/ppermute | solution.py:28
  153.9 10.7 %collective-permute-start.4 = (bf16[4,1,32,96]{3,1,2,0:T(2,128)(2,1)S(1)}, bf16[4,1,32,96]{3,1,2,0:T(2,128)(2,1)S(1)}, u32[]{:S(2)}, u32[]{:S(2)}) collective-permute-start(bf16[4,1,32,96]{3,1,2,0:T(2,128)(2,1)S(1)} %get-tuple-element.71), channel_id=1, source_target_pairs={{0,1},{1,2},{2,3},{3,4},{4,5},{5,6},{6,7},{7,8},{8,9},{9,10},{10,1... | collective-permute-start | bytes 73736 | tf_op jit(solution)/shard_map/ppermute | solution.py:28
  159.1 6.0 %collective-permute-start.5 = (bf16[4,1,32,96]{3,1,2,0:T(2,128)(2,1)S(1)}, bf16[4,1,32,96]{3,1,2,0:T(2,128)(2,1)}, u32[]{:S(2)}, u32[]{:S(2)}) collective-permute-start(bf16[4,1,32,96]{3,1,2,0:T(2,128)(2,1)S(1)} %get-tuple-element.72), channel_id=1, source_target_pairs={{1,0},{2,1},{3,2},{4,3},{5,4},{6,5},{7,6},{8,7},{9,8},{10,9},{11,1... | collective-permute-start | bytes 73736 | tf_op jit(solution)/shard_map/ppermute | solution.py:28
  163.2 19.8 %collective-permute-start.9 = (bf16[2,4,32,96]{3,1,2,0:T(4,128)(2,1)S(1)}, bf16[2,4,32,96]{3,1,2,0:T(4,128)(2,1)S(1)}, u32[]{:S(2)}, u32[]{:S(2)}) collective-permute-start(bf16[2,4,32,96]{3,1,2,0:T(4,128)(2,1)S(1)} %multiply_convert_fusion), channel_id=1, source_target_pairs={{32,0},{64,32},{96,64},{128,96},{160,128},{192,160},{224,192},{256... | collective-permute-start | bytes 147464 | tf_op jit(solution)/shard_map/ppermute | solution.py:28
  164.5 0.6 copy-start.4
  167.4 27.4 %all-to-all-start.6 = ((bf16[64,12,128]{2,1,0:T(8,128)(2,1)}), bf16[64,12,128]{2,1,0:T(8,128)(2,1)S(1)}, u32[]{:S(2)}, u32[]{:S(2)}) async-start(bf16[64,12,128]{2,1,0:T(8,128)(2,1)} %broadcast_in_dim.33), calls=%async_computation.6 | async-start | bytes 524288 | tf_op jit(solution)/shard_map/all_to_all | solution.py:115
  183.8 18.4 %collective-permute-start.10 = (bf16[4,1,32,96]{3,1,2,0:T(2,128)(2,1)}, bf16[4,1,32,96]{3,1,2,0:T(2,128)(2,1)S(1)}, u32[]{:S(2)}, u32[]{:S(2)}) collective-permute-start(bf16[4,1,32,96]{3,1,2,0:T(2,128)(2,1)} %get-tuple-element.67), channel_id=1, source_target_pairs={{0,1},{1,2},{2,3},{3,4},{4,5},{5,6},{6,7},{7,8},{8,9},{9,10},{10,1... | collective-permute-start | bytes 73736 | tf_op jit(solution)/shard_map/ppermute | solution.py:28
  188.0 14.2 %collective-permute-start.11 = (bf16[4,1,32,96]{3,1,2,0:T(2,128)(2,1)}, bf16[4,1,32,96]{3,1,2,0:T(2,128)(2,1)S(1)}, u32[]{:S(2)}, u32[]{:S(2)}) collective-permute-start(bf16[4,1,32,96]{3,1,2,0:T(2,128)(2,1)} %get-tuple-element.68), channel_id=1, source_target_pairs={{1,0},{2,1},{3,2},{4,3},{5,4},{6,5},{7,6},{8,7},{9,8},{10,9},{11,1... | collective-permute-start | bytes 73736 | tf_op jit(solution)/shard_map/ppermute | solution.py:28
  195.8 16.5 %all-to-all-start.7 = ((bf16[4,768,128]{2,1,0:T(8,128)(2,1)}), bf16[4,768,128]{2,1,0:T(8,128)(2,1)S(1)}, u32[]{:S(2)}, u32[]{:S(2)}) async-start(bf16[4,768,128]{2,1,0:T(8,128)(2,1)} %broadcast_in_dim.35), calls=%async_computation.7 | async-start | bytes 1572864 | tf_op jit(solution)/shard_map/all_to_all | solution.py:117
  212.4 13.0 %collective-permute-start.13 = (bf16[3072,128]{1,0:T(8,128)(2,1)S(1)}, bf16[3072,128]{1,0:T(8,128)(2,1)}, u32[]{:S(2)}, u32[]{:S(2)}) collective-permute-start(bf16[3072,128]{1,0:T(8,128)(2,1)S(1)} %bitcast.185), channel_id=1, source_target_pairs={{0,1},{1,0},{2,3},{3,2},{4,5},{5,4},{6,7},{7,6},{8,9},{9,8},{10,11... | collective-permute-start | bytes 2359304 | tf_op jit(solution)/shard_map/ppermute | solution.py:119
  236.4 1.5 copy-start.2

commit v2 on v1

v2 whole, which is shorter than its diff:
```python
import functools

import jax
import jax.numpy as jnp
from jax import lax
from jax.experimental import pallas as pl
from jax.experimental.pallas import tpu as pltpu
from jax.sharding import Mesh
from jax.sharding import PartitionSpec as P

GROUPS = 32
EPSILON = 1e-05

TM = ("zh", "y")
HEIGHT = ("zl", "x", "c")
REST = ("zh", "y", "zl")

VMEM_LIMIT = 32 * 2**20


def fine_mesh(mesh):
    tm, height = mesh.shape["tm"], mesh.shape["height"]
    zh = 2 if tm % 2 == 0 else 1
    core = 2
    x = 4 if height % 8 == 0 else height // 2
    return Mesh(mesh.devices.reshape(zh, tm // zh, height // (core * x), x, core), TM + HEIGHT)


def neighbour(value, axis, steps):
    count = lax.axis_size(axis)
    first, last = max(0, -steps), min(count, count - steps)
    return lax.ppermute(value, axis, [(i, i + steps) for i in range(first, last)])


def row_halo(cells):
    return jnp.concatenate(
        [neighbour(cells[:, -1:], HEIGHT, 1), cells, neighbour(cells[:, :1], HEIGHT, -1)], axis=1
    )


def stage_sum(value, axes):
    count = lax.axis_size(axes)
    return lax.all_to_all(jnp.broadcast_to(value[None], (count,) + value.shape), axes, 0, 0).sum(0)


def conv(padded, weight):
    return lax.conv_general_dilated(
        padded[None],
        weight,
        (1, 1, 1),
        "VALID",
        dimension_numbers=("NDHWC", "DHWIO", "NDHWC"),
        preferred_element_type=jnp.float32,
    )[0]


def flipped(weight):
    return jnp.transpose(jnp.flip(weight, (0, 1, 2)), (0, 1, 2, 4, 3))


def pad_cols(field):
    return jnp.pad(field, ((0, 0), (0, 0), (1, 1), (0, 0)))


def upsample(field):
    return jnp.repeat(jnp.repeat(field, 2, 1), 2, 2)


def col_sums(wide, cells):
    half = cells.shape[1] // 2
    wide[...] = jnp.zeros_like(wide)
    wide[:, 8 : 8 + cells.shape[1], : cells.shape[2]] = cells

    def every_second(start):
        return wide[:, pl.ds(start, half, stride=2), : cells.shape[2]]

    before, even, odd, after = (every_second(7 + k) for k in range(4))
    return odd + after, even + odd, before + even


def weight_grads_kernel(core, rows_in, grad_normed, normed, vectors, two, grad_pre, away, kept, wide):
    frames, rows, cols, outs = grad_normed.shape
    ins, mids = rows_in.shape[-1], two.shape[1]
    first, second, rstd = (vectors[k : k + 1] for k in range(3))
    merged = (frames * rows * cols, outs)
    grad = grad_normed[...].reshape(merged) - first - normed[...].reshape(merged) * second
    grad = (grad * rstd).astype(jnp.bfloat16)
    grad_pre[...] = grad.reshape(grad_pre.shape)
    by_tap = col_sums(wide, grad.astype(jnp.float32).reshape(frames * rows, cols, outs))
    pieces = []
    for b in range(3):
        for e in range(3):
            part = by_tap[e].reshape(frames, rows, cols // 2, outs)
            none = jnp.zeros_like(part[:, 0])
            r = [part[:, k] for k in range(rows)]
            stacked = (
                [r[0], r[1] + r[2], r[3], none],
                [none, r[0] + r[1], r[2] + r[3], none],
                [none, r[0], r[1] + r[2], r[3]],
            )[b]
            cells = jnp.stack(stacked, 1).astype(jnp.bfloat16)
            pieces.append(cells.reshape(-1, outs))
    pieces.append(jnp.zeros((pieces[0].shape[0], 32), jnp.bfloat16))
    cells = jnp.concatenate(pieces, 1)
    lower = core[0] == 0

    def write(at, low, high):
        away[at : at + low.shape[0]] = jnp.where(lower, high, low).astype(jnp.bfloat16)
        kept[at : at + low.shape[0]] = jnp.where(lower, low, high)

    at = 0
    for a in range(3):
        product = lax.dot_general(
            rows_in[a : a + frames].reshape(-1, ins),
            cells,
            (((0,), (0,)), ((), ())),
            preferred_element_type=jnp.float32,
        )
        for j in range(7):
            block = product[:, 128 * j : 128 * j + 128]
            write(at, block[: ins // 2], block[ins // 2 :])
            at += ins // 2
    for a in range(3):
        product = two[a]
        for j in range(7):
            block = product[:, 128 * j : 128 * j + 128]
            write(at, block[: mids // 2], block[mids // 2 :])
            at += mids // 2
    if at < kept.shape[0]:
        tail = jnp.zeros((kept.shape[0] - at, 128), jnp.float32)
        away[at:] = tail.astype(jnp.bfloat16)
        kept[at:] = tail


def weight_grads(core, rows_in, grad_normed, normed, vectors, two, half_rows):
    frames, rows, cols, outs = grad_normed.shape
    whole = pl.BlockSpec(memory_space=pltpu.VMEM)
    return pl.pallas_call(
        weight_grads_kernel,
        out_shape=(
            jax.ShapeDtypeStruct(grad_normed.shape, jnp.bfloat16),
            jax.ShapeDtypeStruct((half_rows, 128), jnp.bfloat16),
            jax.ShapeDtypeStruct((half_rows, 128), jnp.float32),
        ),
        in_specs=[pl.BlockSpec(memory_space=pltpu.SMEM)] + [whole] * 5,
        out_specs=[whole] * 3,
        scratch_shapes=[pltpu.VMEM((frames * rows, cols + 16, 128), jnp.float32)],
        compiler_params=pltpu.CompilerParams(vmem_limit_bytes=VMEM_LIMIT),
        name="weight_grads",
    )(core, rows_in, grad_normed, normed, vectors, two)


def unpack_kernel(scale, core, mine_one, other_one, mine_two, other_two, one, two):
    lower = core[0] == 0
    for mine, other, out in ((mine_one, other_one, one), (mine_two, other_two, two)):
        taps, rows, outs = out.shape
        half = rows // 2
        own = jnp.concatenate([mine[half * j : half * j + half] for j in range(7)], 1)
        far = jnp.concatenate([other[half * j : half * j + half] for j in range(7)], 1)
        own, far = own.astype(jnp.float32) * scale, far.astype(jnp.float32) * scale
        low, high = jnp.where(lower, own, far), jnp.where(lower, far, own)
        for k in range(taps):
            out[k, :half] = low[:, outs * k : outs * k + outs]
            out[k, half:] = high[:, outs * k : outs * k + outs]


def unpack(core, mine, other, ins, mids, scale):
    half_one, half_two = 7 * ins // 2, 7 * mids // 2
    skip = 3 * half_one // half_two
    block_one = pl.BlockSpec((half_one, 128), lambda a: (a, 0))
    block_two = pl.BlockSpec((half_two, 128), lambda a: (a + skip, 0))
    return pl.pallas_call(
        functools.partial(unpack_kernel, scale),
        grid=(3,),
        out_shape=(
            jax.ShapeDtypeStruct((27, ins, mids), jnp.float32),
            jax.ShapeDtypeStruct((27, mids, mids), jnp.float32),
        ),
        in_specs=[pl.BlockSpec(memory_space=pltpu.SMEM), block_one, block_one, block_two, block_two],
        out_specs=[
            pl.BlockSpec((9, ins, mids), lambda a: (a, 0, 0)),
            pl.BlockSpec((9, mids, mids), lambda a: (a, 0, 0)),
        ],
        compiler_params=pltpu.CompilerParams(vmem_limit_bytes=VMEM_LIMIT),
        name="unpack",
    )(core, mine, other, mine, other)


def feature_grads_kernel(grad_pre, weight, out, wide):
    frames, rows, cols, outs = grad_pre.shape
    own, cells_in, cols_in, ins = out.shape
    by_tap = col_sums(wide, grad_pre[...].astype(jnp.float32).reshape(frames * rows, cols, outs))
    total = jnp.zeros((own * cells_in * cols_in, ins), jnp.float32)
    for b in range(3):
        for e in range(3):
            part = by_tap[e].reshape(frames, rows, cols // 2, outs)
            cells = jnp.stack(
                [part[:, 2 * k + 2 - b] + part[:, 2 * k + 3 - b] for k in range(cells_in)], 1
            ).astype(jnp.bfloat16)
            for a in range(3):
                total += lax.dot_general(
                    cells[2 - a : 2 - a + own].reshape(-1, outs),
                    weight[a, b, e],
                    (((1,), (1,)), ((), ())),
                    preferred_element_type=jnp.float32,
                )
    out[...] = total.reshape(out.shape)


def feature_grads(grad_rowed, weight, shape):
    frames, rows, cols, _ = grad_rowed.shape
    whole = pl.BlockSpec(memory_space=pltpu.VMEM)
    return pl.pallas_call(
        feature_grads_kernel,
        out_shape=jax.ShapeDtypeStruct(shape, jnp.float32),
        in_specs=[whole] * 2,
        out_specs=whole,
        scratch_shapes=[pltpu.VMEM((frames * rows, cols + 16, 128), jnp.float32)],
        compiler_params=pltpu.CompilerParams(vmem_limit_bytes=VMEM_LIMIT),
        cost_estimate=pl.CostEstimate(flops=2**28, bytes_accessed=2**21, transcendentals=0),
        name="feature_grads",
    )(grad_rowed, weight)


def half_rows(ins, mids):
    unit = lax.axis_size("x") * lax.axis_size(REST)
    return -(-(21 * (ins + mids) // 2) // unit) * unit


SWAP = [(0, 1), (1, 0)]


def body(features, cotangent, weight_one, weight_two, norm_gain, norm_shift):
    frames, ins = features.shape[0], features.shape[-1]
    mids = cotangent.shape[-1]
    xs, rest = lax.axis_size("x"), lax.axis_size(REST)
    devices_all = 2 * xs * rest
    per_group = mids // GROUPS
    member = jnp.arange(mids) // per_group
    same_group = (member[:, None] == member[None]).astype(jnp.float32)
    core = lax.axis_index("c").astype(jnp.int32).reshape(1)
    barrier = lax.optimization_barrier

    def group_sums(first, second):
        both = jnp.stack([first, second])
        return jnp.dot(both, same_group, precision=lax.Precision.HIGHEST)

    timed = jnp.concatenate([neighbour(features, TM, 1), features], 0)
    rowed = row_halo(timed)
    padded_in = pad_cols(upsample(rowed)[:, 1:-1])
    pre_norm = conv(padded_in, weight_one)
    shape = pre_norm.shape
    count = shape[0] * shape[1] * shape[2] * per_group * devices_all
    sums = group_sums(jnp.sum(pre_norm, (0, 1, 2)), jnp.sum(pre_norm * pre_norm, (0, 1, 2)))
    sums, cotangent = barrier((sums, cotangent))
    sums = stage_sum(sums, HEIGHT)
    cot_timed = jnp.concatenate([cotangent, neighbour(cotangent, TM, -1)], 0)
    sums, cot_timed = barrier((sums, cot_timed))
    sums = stage_sum(sums, TM)
    wide_cot = pad_cols(row_halo(cot_timed))
    grad_hidden = conv(wide_cot, flipped(weight_two))
    shifted_cot = jnp.concatenate(
        [
            wide_cot[:, 2 - b : 2 - b + shape[1], 2 - e : 2 - e + shape[2]]
            for b in range(3)
            for e in range(3)
        ],
        -1,
    )
    (total_one, total_two), grad_hidden, shifted_cot = barrier((sums, grad_hidden, shifted_cot))

    mean = total_one / count
    rstd = lax.rsqrt(total_two / count - mean * mean + EPSILON)
    normed = (pre_norm - mean) * rstd
    shifted = normed * norm_gain + norm_shift
    sigma = jax.nn.sigmoid(shifted)
    hidden = (shifted * sigma).astype(jnp.bfloat16)
    grad_normed = grad_hidden * sigma * (1.0 + shifted * (1.0 - sigma)) * norm_gain
    sums = group_sums(jnp.sum(grad_normed, (0, 1, 2)), jnp.sum(grad_normed * normed, (0, 1, 2)))
    sums, hidden = barrier((sums, hidden))
    sums = stage_sum(sums, ("y", "c"))
    mid_timed = jnp.concatenate([neighbour(hidden[frames - 2 :], TM, 1), hidden], 0)
    flat_hidden = hidden.reshape(-1, mids)
    local_two = jnp.stack(
        [
            lax.dot_general(
                flat_hidden,
                shifted_cot[2 - a : 2 - a + frames].reshape(-1, 9 * mids),
                (((0,), (0,)), ((), ())),
                preferred_element_type=jnp.float32,
            )
            for a in range(3)
        ]
    )
    sums, mid_timed, local_two = barrier((sums, mid_timed, local_two))
    sums = stage_sum(sums, ("zh", "zl", "x"))
    mid_rowed = row_halo(mid_timed)
    sums, mid_rowed = barrier((sums, mid_rowed))

    scale = 1.0 / (shape[0] * shape[1] * shape[2] * devices_all) ** 0.5
    vectors = jnp.concatenate([sums / count, rstd[None]], 0)
    local_two = jnp.pad(local_two, ((0, 0), (0, 0), (0, 32)))
    grad_pre, away, kept = weight_grads(
        core, rowed, grad_normed, normed, vectors, local_two, half_rows(ins, mids)
    )

    part = kept + lax.ppermute(away, "c", SWAP).astype(jnp.float32)
    part = part.astype(jnp.bfloat16).reshape(xs, -1, 128)
    part, grad_pre, mid_rowed = barrier((part, grad_pre, mid_rowed))
    part = lax.all_to_all(part, "x", 0, 0).astype(jnp.float32).sum(0)
    grad_timed = jnp.concatenate([grad_pre, neighbour(grad_pre, TM, -1)], 0)
    part, grad_timed = barrier((part, grad_timed))
    part = lax.all_to_all(part.reshape(rest, -1, 128), REST, 0, 0).sum(0).astype(jnp.bfloat16)
    grad_rowed = row_halo(grad_timed)
    part, grad_rowed = barrier((part, grad_rowed))
    part = lax.all_to_all(jnp.broadcast_to(part[None], (rest,) + part.shape), REST, 0, 0)
    decoded = conv(pad_cols(mid_rowed), weight_two).astype(jnp.bfloat16)
    part, decoded, grad_rowed = barrier((part.reshape(-1, 128), decoded, grad_rowed))
    part = lax.all_to_all(jnp.broadcast_to(part[None], (xs,) + part.shape), "x", 0, 0)
    grad_features = feature_grads(grad_rowed, weight_one, features.shape)
    part, grad_features = barrier((part.reshape(-1, 128), grad_features))
    grad_one, grad_two = unpack(core, part, lax.ppermute(part, "c", SWAP), ins, mids, scale)
    return decoded, grad_features, grad_one.reshape(weight_one.shape), grad_two.reshape(weight_two.shape)


def solution(mesh):
    split = P(TM, HEIGHT, None, None)
    return jax.shard_map(
        body,
        mesh=fine_mesh(mesh),
        in_specs=(split, split, P(), P(), P(), P()),
        out_specs=(split, split, P(), P()),
        check_vma=False,
    )
```

time: 247 us -> 222 us (0.90)
  local copies, waits for them, and re-layouts: 46.4 us -> 13.4 us
  blocking collectives: 14.4 us -> 45.2 us
  starting transfers between devices: 105 us -> 74.5 us
  other arithmetic: 22.9 us -> 8.27 us
  waiting for transfers between devices: 49.5 us -> 61.6 us
  matrix products: 5.71 us -> 11.3 us
  Pallas kernels: 0 us -> 5.07 us
    all_to_all x1 -> x2, blocking collectives: 14.4 us -> 45.2 us  [stage_sum(): lax.all_to_all(jnp.broadcast_to(value[None], (count,) + value.shape), axe...]
    all_to_all x7 -> x6, starting transfers between devices: 61.5 us -> 32.5 us  [the longest x2 10.9 us: stage_sum(): lax.all_to_all(jnp.broadcast_to(value[None], (count,) + value.shape), axe...]
    unnamed x29 -> x20, local copies, waits for them, and re-layouts: 13 us -> 2.61 us
    reduce_sum x30 -> x6, other arithmetic: 10.5 us -> 1.08 us  [the longest x1 0.85 us: body(): part = lax.all_to_all(part, 'x', 0, 0).astype(jnp.float32).sum(0)]
    all_to_all x7 -> x6, waiting for transfers between devices: 39.1 us -> 47.1 us  [the longest x2 11.7 us: stage_sum(): lax.all_to_all(jnp.broadcast_to(value[None], (count,) + value.shape), axe...]
    transpose x2 -> x0, local copies, waits for them, and re-layouts: 7.19 us -> none  [the longest x1 4.3 us: pack(): jnp.transpose(both.reshape(rows, 7, 128), (1, 0, 2)).reshape(7 * rows, 128)]
    slice x14 -> x1, local copies, waits for them, and re-layouts: 6.74 us -> 0.88 us  [body(): wide_cot[:, 2 - b:2 - b + shape[1], 2 - e:2 - e + shape[2]]]
    conv_general_dilated x3, matrix products: 2.53 us -> 7.99 us  [conv(): lax.conv_general_dilated(padded[None], weight, (1, 1, 1), 'VALID', dimens...]
  transfers between devices with their start and end apart: 21 -> 20, of which waited for: 9 -> 12; matrix products, arithmetic and copies ran while one was open for 12% -> 5% of each run, Pallas kernels for 0% -> 1%
where the time goes in v2:
time: 222 us; the launch traced here: 220 us
  starting transfers between devices  74.5 us (34%)
  waiting for transfers between devices  61.6 us (28%)
  blocking collectives  45.2 us (20%)
  local copies, waits for them, and re-layouts  13.4 us (6%)
  matrix products  11.3 us (5%)
  other arithmetic  8.27 us (4%)
  Pallas kernels  5.07 us (2%)
    all_to_all x2, blocking collectives, stage_sum(): lax.all_to_all(jnp.broadcast_to(value[None], (count,) + value.shape), axe...  45.2 us
    ppermute x12, starting transfers between devices, neighbour(): lax.ppermute(value, axis, [(i, i + steps) for i in range(first, last)])  33.4 us
    all_to_all x2, waiting for transfers between devices, stage_sum(): lax.all_to_all(jnp.broadcast_to(value[None], (count,) + value.shape), axe...  11.7 us
    all_to_all x2, starting transfers between devices, stage_sum(): lax.all_to_all(jnp.broadcast_to(value[None], (count,) + value.shape), axe...  10.9 us
    ppermute x12, waiting for transfers between devices, neighbour(): lax.ppermute(value, axis, [(i, i + steps) for i in range(first, last)])  10.8 us
    all_to_all x1, waiting for transfers between devices, body(): lax.all_to_all(jnp.broadcast_to(part[None], (rest,) + part.shape), REST,...  10.2 us
    all_to_all x1, waiting for transfers between devices, body(): lax.all_to_all(jnp.broadcast_to(part[None], (xs,) + part.shape), 'x', 0, 0)  9.82 us
    all_to_all x1, waiting for transfers between devices, body(): lax.all_to_all(part.reshape(rest, -1, 128), REST, 0, 0).sum(0)  8.63 us
  transfers between devices with their start and end apart: 20, of which 12 were waited for; matrix products, arithmetic and copies ran while one was open for 5% of the time, Pallas kernels for 1%

profile of v2, /device:TPU:1, one launch (start us, length us, event | category | flops | bytes accessed | tf_op | source)
XLA Modules:
  0.0 220.4 jit_solution(11526505078691027592)
XLA Ops:
  0.6 4.2 %collective-permute-start = (bf16[2,2,16,192]{3,2,1,0:T(8,128)(2,1)}, bf16[2,2,16,192]{3,2,1,0:T(8,128)(2,1)S(1)}, u32[]{:S(2)}, u32[]{:S(2)}) collective-permute-start(bf16[2,2,16,192]{3,2,1,0:T(8,128)(2,1)} %param.6), channel_id=1, source_target_pairs={{0,32},{32,64},{64,96},{96,128},{128,160},{160,192},{192,224},{224... | collective-permute-start | bytes 73736 | tf_op jit(solution)/shard_map/ppermute | solution.py:32
  6.9 4.5 %collective-permute-start.1 = (bf16[4,1,16,192]{3,2,1,0:T(8,128)(2,1)S(1)}, bf16[4,1,16,192]{3,2,1,0:T(8,128)(2,1)S(1)}, u32[]{:S(2)}, u32[]{:S(2)}) collective-permute-start(bf16[4,1,16,192]{3,2,1,0:T(8,128)(2,1)S(1)} %get-tuple-element.85), channel_id=1, source_target_pairs={{0,1},{1,2},{2,3},{3,4},{4,5},{5,6},{6,7},{7,8},{8,9},{9,10},{10,1... | collective-permute-start | bytes 73736 | tf_op jit(solution)/shard_map/ppermute | solution.py:32
  11.5 3.4 %collective-permute-start.2 = (bf16[4,1,16,192]{3,2,1,0:T(8,128)(2,1)S(1)}, bf16[4,1,16,192]{3,2,1,0:T(8,128)(2,1)S(1)}, u32[]{:S(2)}, u32[]{:S(2)}) collective-permute-start(bf16[4,1,16,192]{3,2,1,0:T(8,128)(2,1)S(1)} %get-tuple-element.86), channel_id=1, source_target_pairs={{1,0},{2,1},{3,2},{4,3},{5,4},{6,5},{7,6},{8,7},{9,8},{10,9},{11,1... | collective-permute-start | bytes 73736 | tf_op jit(solution)/shard_map/ppermute | solution.py:32
  18.0 3.1 %fusion.39 = (f32[96]{0:T(128)S(1)}, f32[1,2,4,32,96]{4,0,3,2,1:T(1,128)S(1)}) fusion(bf16[3,3,3,192,96]{4,3,2,1,0:T(8,128)(2,1)S(1)} %copy-done.1, bf16[1,4,6,34,192]{4,1,3,2,0:T(4,128)(2,1)S(1)} %pad_bitcast_fusion), kind=kOutput, calls=%fused_computation.78 | convolution fusion | flops 254828448 | bytes 1407360 | tf_op jit(solution)/shard_map/conv_general_dilated | solution.py:47
  23.4 18.3 %all_to_all.40 = f32[32,2,96]{2,1,0:T(2,128)S(1)} all-to-all(f32[32,2,96]{2,1,0:T(2,128)S(1)} %broadcast_in_dim.25), channel_id=1, replica_groups=mesh['zh'=2,'y'=8,'zl'=4,'x'=4,'c'=2] {'zl','x','c'}, dimensions={0} | all-to-all | bytes 49152 | tf_op jit(solution)/shard_map/all_to_all | solution.py:43
  41.8 2.5 %collective-permute-start.4 = (bf16[4,1,32,96]{3,2,1,0:T(8,128)(2,1)S(1)}, bf16[4,1,32,96]{3,2,1,0:T(8,128)(2,1)S(1)}, u32[]{:S(2)}, u32[]{:S(2)}) collective-permute-start(bf16[4,1,32,96]{3,2,1,0:T(8,128)(2,1)S(1)} %get-tuple-element.83), channel_id=1, source_target_pairs={{0,1},{1,2},{2,3},{3,4},{4,5},{5,6},{6,7},{7,8},{8,9},{9,10},{10,1... | collective-permute-start | bytes 73736 | tf_op jit(solution)/shard_map/ppermute | solution.py:32
  44.2 1.9 collective-permute-start.5
  46.2 26.9 %all_to_all.41 = f32[16,2,96]{2,1,0:T(2,128)S(1)} all-to-all(f32[16,2,96]{2,1,0:T(2,128)S(1)} %broadcast_in_dim.26), channel_id=1, replica_groups=mesh['zh'=2,'y'=8,'zl'=4,'x'=4,'c'=2] {'zh','y'}, dimensions={0} | all-to-all | bytes 24576 | tf_op jit(solution)/shard_map/all_to_all | solution.py:43
  74.3 3.3 %fusion.6 = f32[1,2,4,32,96]{4,0,3,2,1:T(1,128)} fusion(bf16[3,3,3,96,96]{4,3,2,1,0:T(8,128)(2,1)S(1)} %copy-done, bf16[1,4,6,34,96]{4,3,2,1,0:T(8,128)(2,1)S(1)} %fusion.46), kind=kOutput, calls=%fused_computation.16 | convolution fusion | flops 127401984 | bytes 752640 | tf_op jit(solution)/shard_map/conv_general_dilated | solution.py:47
  82.2 2.5 %collective-permute-start.6 = (bf16[2,4,32,96]{3,2,1,0:T(8,128)(2,1)S(1)}, bf16[2,4,32,96]{3,2,1,0:T(8,128)(2,1)S(1)}, u32[]{:S(2)}, u32[]{:S(2)}) collective-permute-start(bf16[2,4,32,96]{3,2,1,0:T(8,128)(2,1)S(1)} %get-tuple-element.42), channel_id=1, source_target_pairs={{0,32},{32,64},{64,96},{96,128},{128,160},{160,192},{192,224},{224... | collective-permute-start | bytes 147464 | tf_op jit(solution)/shard_map/ppermute | solution.py:32
  88.3 4.7 %all-to-all-start.2 = ((f32[16,2,96]{2,1,0:T(2,128)}), f32[16,2,96]{2,1,0:T(2,128)S(1)}, u32[]{:S(2)}, u32[]{:S(2)}) async-start(f32[16,2,96]{2,1,0:T(2,128)} %broadcast_in_dim.28), calls=%async_computation.2 | async-start | bytes 32768 | tf_op jit(solution)/shard_map/all_to_all | solution.py:43
  93.0 2.2 %pad_maximum_fusion = f32[3,96,864]{2,1,0:T(8,128)} fusion(f32[1,96,864]{2,1,0:T(8,128)} %convolution_bitcast_fusion, f32[1,96,864]{2,1,0:T(8,128)} %convolution_bitcast_fusion.1, f32[1,96,864]{2,1,0:T(8,128)} %convolution_bitcast_fusion.2), kind=kLoop, calls=%fused_computation.6 | loop fusion | flops 497664 | bytes 1990656 | tf_op jit(solution)/shard_map/stack | solution.py:284
  95.2 5.1 %all-to-all-done.2 = f32[16,2,96]{2,1,0:T(2,128)S(1)} async-done(((f32[16,2,96]{2,1,0:T(2,128)}), f32[16,2,96]{2,1,0:T(2,128)S(1)}, u32[]{:S(2)}, u32[]{:S(2)}) %all-to-all-start.2) | async-done | bytes 12320 | tf_op jit(solution)/shard_map/all_to_all | solution.py:43
  101.6 4.7 %collective-permute-start.7 = (bf16[4,1,32,96]{3,2,1,0:T(8,128)(2,1)}, bf16[4,1,32,96]{3,2,1,0:T(8,128)(2,1)S(1)}, u32[]{:S(2)}, u32[]{:S(2)}) collective-permute-start(bf16[4,1,32,96]{3,2,1,0:T(8,128)(2,1)} %get-tuple-element.79), channel_id=1, source_target_pairs={{0,1},{1,2},{2,3},{3,4},{4,5},{5,6},{6,7},{7,8},{8,9},{9,10},{10,1... | collective-permute-start | bytes 73736 | tf_op jit(solution)/shard_map/ppermute | solution.py:32
  106.3 1.9 collective-permute-start.8
  108.9 6.2 %all-to-all-start.3 = ((f32[32,2,96]{2,1,0:T(2,128)}), f32[32,2,96]{2,1,0:T(2,128)S(1)}, u32[]{:S(2)}, u32[]{:S(2)}) async-start(f32[32,2,96]{2,1,0:T(2,128)} %broadcast_in_dim.29), calls=%async_computation.3 | async-start | bytes 65536 | tf_op jit(solution)/shard_map/all_to_all | solution.py:43
  117.2 6.6 %all-to-all-done.3 = f32[32,2,96]{2,1,0:T(2,128)S(1)} async-done(((f32[32,2,96]{2,1,0:T(2,128)}), f32[32,2,96]{2,1,0:T(2,128)S(1)}, u32[]{:S(2)}, u32[]{:S(2)}) %all-to-all-start.3) | async-done | bytes 24608 | tf_op jit(solution)/shard_map/all_to_all | solution.py:43
  124.5 4.8 %collective-permute-start.9 = (bf16[3072,128]{1,0:T(8,128)(2,1)S(1)}, bf16[3072,128]{1,0:T(8,128)(2,1)S(1)}, u32[]{:S(2)}, u32[]{:S(2)}) collective-permute-start(bf16[3072,128]{1,0:T(8,128)(2,1)S(1)} %get-tuple-element.49), channel_id=1, source_target_pairs={{0,1},{1,0},{2,3},{3,2},{4,5},{5,4},{6,7},{7,6},{8,9},{9,8},{10,11... | collective-permute-start | bytes 2359304 | tf_op jit(solution)/shard_map/ppermute | solution.py:307
  132.3 3.5 %all-to-all-start.4 = ((bf16[4,768,128]{2,1,0:T(8,128)(2,1)}), bf16[4,768,128]{2,1,0:T(8,128)(2,1)S(1)}, u32[]{:S(2)}, u32[]{:S(2)}) async-start(bf16[4,768,128]{2,1,0:T(8,128)(2,1)} %bitcast.59), calls=%async_computation.4 | async-start | bytes 1572864 | tf_op jit(solution)/shard_map/all_to_all | solution.py:310
  137.1 4.0 %collective-permute-done.10 = bf16[2,4,32,96]{3,2,1,0:T(8,128)(2,1)S(1)} collective-permute-done((bf16[2,4,32,96]{3,2,1,0:T(8,128)(2,1)S(1)}, bf16[2,4,32,96]{3,2,1,0:T(8,128)(2,1)S(1)}, u32[]{:S(2)}, u32[]{:S(2)}) %collective-permute-start.10) | collective-permute-done | bytes 49184 | tf_op jit(solution)/shard_map/ppermute | solution.py:32
  141.1 6.7 %all-to-all-done.4 = bf16[4,768,128]{2,1,0:T(8,128)(2,1)S(1)} async-done(((bf16[4,768,128]{2,1,0:T(8,128)(2,1)}), bf16[4,768,128]{2,1,0:T(8,128)(2,1)S(1)}, u32[]{:S(2)}, u32[]{:S(2)}) %all-to-all-start.4) | async-done | bytes 786464 | tf_op jit(solution)/shard_map/all_to_all | solution.py:310
  150.5 4.9 %all-to-all-start.5 = ((f32[64,12,128]{2,1,0:T(8,128)}), f32[64,12,128]{2,1,0:T(8,128)S(1)}, u32[]{:S(2)}, u32[]{:S(2)}) async-start(f32[64,12,128]{2,1,0:T(8,128)} %reshape.99), calls=%async_computation.5 | async-start | bytes 1048576 | tf_op jit(solution)/shard_map/all_to_all | solution.py:313
  155.5 3.3 %collective-permute-start.11 = (bf16[4,1,32,96]{3,2,1,0:T(8,128)(2,1)S(1)}, bf16[4,1,32,96]{3,2,1,0:T(8,128)(2,1)S(1)}, u32[]{:S(2)}, u32[]{:S(2)}) collective-permute-start(bf16[4,1,32,96]{3,2,1,0:T(8,128)(2,1)S(1)} %get-tuple-element.77), channel_id=1, source_target_pairs={{0,1},{1,2},{2,3},{3,4},{4,5},{5,6},{6,7},{7,8},{8,9},{9,10},{10,1... | collective-permute-start | bytes 73736 | tf_op jit(solution)/shard_map/ppermute | solution.py:32
  158.7 1.9 collective-permute-start.12
  160.7 3.6 %collective-permute-done.12 = bf16[4,1,32,96]{3,2,1,0:T(8,128)(2,1)S(1)} collective-permute-done((bf16[4,1,32,96]{3,2,1,0:T(8,128)(2,1)S(1)}, bf16[4,1,32,96]{3,2,1,0:T(8,128)(2,1)S(1)}, u32[]{:S(2)}, u32[]{:S(2)}) %collective-permute-start.12) | collective-permute-done | bytes 24608 | tf_op jit(solution)/shard_map/ppermute | solution.py:32
  164.3 8.6 %all-to-all-done.5 = f32[64,12,128]{2,1,0:T(8,128)S(1)} async-done(((f32[64,12,128]{2,1,0:T(8,128)}), f32[64,12,128]{2,1,0:T(8,128)S(1)}, u32[]{:S(2)}, u32[]{:S(2)}) %all-to-all-start.5) | async-done | bytes 393248 | tf_op jit(solution)/shard_map/all_to_all | solution.py:313
  173.8 6.8 %all-to-all-start.6 = ((bf16[64,12,128]{2,1,0:T(8,128)(2,1)}), bf16[64,12,128]{2,1,0:T(8,128)(2,1)S(1)}, u32[]{:S(2)}, u32[]{:S(2)}) async-start(bf16[64,12,128]{2,1,0:T(8,128)(2,1)} %broadcast_in_dim.30), calls=%async_computation.6 | async-start | bytes 524288 | tf_op jit(solution)/shard_map/all_to_all | solution.py:316
  182.8 10.2 %all-to-all-done.6 = bf16[64,12,128]{2,1,0:T(8,128)(2,1)S(1)} async-done(((bf16[64,12,128]{2,1,0:T(8,128)(2,1)}), bf16[64,12,128]{2,1,0:T(8,128)(2,1)S(1)}, u32[]{:S(2)}, u32[]{:S(2)}) %all-to-all-start.6) | async-done | bytes 196640 | tf_op jit(solution)/shard_map/all_to_all | solution.py:316
  194.1 6.4 %all-to-all-start.7 = ((bf16[4,768,128]{2,1,0:T(8,128)(2,1)}), bf16[4,768,128]{2,1,0:T(8,128)(2,1)S(1)}, u32[]{:S(2)}, u32[]{:S(2)}) async-start(bf16[4,768,128]{2,1,0:T(8,128)(2,1)} %broadcast_in_dim.32), calls=%async_computation.7 | async-start | bytes 1572864 | tf_op jit(solution)/shard_map/all_to_all | solution.py:319
  202.1 9.8 %all-to-all-done.7 = bf16[4,768,128]{2,1,0:T(8,128)(2,1)S(1)} async-done(((bf16[4,768,128]{2,1,0:T(8,128)(2,1)}), bf16[4,768,128]{2,1,0:T(8,128)(2,1)S(1)}, u32[]{:S(2)}, u32[]{:S(2)}) %all-to-all-start.7) | async-done | bytes 786464 | tf_op jit(solution)/shard_map/all_to_all | solution.py:319
  211.9 3.7 %collective-permute-start.13 = (bf16[3072,128]{1,0:T(8,128)(2,1)S(1)}, bf16[3072,128]{1,0:T(8,128)(2,1)S(1)}, u32[]{:S(2)}, u32[]{:S(2)}) collective-permute-start(bf16[3072,128]{1,0:T(8,128)(2,1)S(1)} %bitcast.56), channel_id=1, source_target_pairs={{0,1},{1,0},{2,3},{3,2},{4,5},{5,4},{6,7},{7,6},{8,9},{9,8},{10,11... | collective-permute-start | bytes 2359304 | tf_op jit(solution)/shard_map/ppermute | solution.py:322
  217.5 2.9 %unpack.1 = (f32[27,192,96]{2,1,0:T(8,128)}, f32[27,96,96]{2,1,0:T(8,128)}) custom-call(s32[1]{0:T(128)} %bitcast.core, bf16[3072,128]{1,0:T(8,128)(2,1)S(1)} %bitcast.57, bf16[3072,128]{1,0:T(8,128)(2,1)S(1)} %collective-permute-done.13.other_one.other_two, bf16[3072,128]{1,0:T(8,128)(2,1)S(1)} %bitcast.58, ...), custom_call_target="tpu_custom_call" | custom-call | tf_op jit(solution)/shard_map/unpack/pallas_call | solution.py:172
  (88 shorter events, 36.0 us)
Async XLA Ops:
  0.6 73.6 %copy-start = (bf16[3,3,3,96,96]{4,3,2,1,0:T(8,128)(2,1)S(1)}, bf16[3,3,3,96,96]{4,3,2,1,0:T(8,128)(2,1)}, u32[]{:S(2)}) copy-start(bf16[3,3,3,96,96]{4,3,2,1,0:T(8,128)(2,1)} %param.9) | copy-start | bytes 1492996
  0.6 5.5 %collective-permute-start = (bf16[2,2,16,192]{3,2,1,0:T(8,128)(2,1)}, bf16[2,2,16,192]{3,2,1,0:T(8,128)(2,1)S(1)}, u32[]{:S(2)}, u32[]{:S(2)}) collective-permute-start(bf16[2,2,16,192]{3,2,1,0:T(8,128)(2,1)} %param.6), channel_id=1, source_target_pairs={{0,32},{32,64},{64,96},{96,128},{128,160},{160,192},{192,224},{224... | collective-permute-start | bytes 73736 | tf_op jit(solution)/shard_map/ppermute | solution.py:32
  6.9 7.9 %collective-permute-start.1 = (bf16[4,1,16,192]{3,2,1,0:T(8,128)(2,1)S(1)}, bf16[4,1,16,192]{3,2,1,0:T(8,128)(2,1)S(1)}, u32[]{:S(2)}, u32[]{:S(2)}) collective-permute-start(bf16[4,1,16,192]{3,2,1,0:T(8,128)(2,1)S(1)} %get-tuple-element.85), channel_id=1, source_target_pairs={{0,1},{1,2},{2,3},{3,4},{4,5},{5,6},{6,7},{7,8},{8,9},{9,10},{10,1... | collective-permute-start | bytes 73736 | tf_op jit(solution)/shard_map/ppermute | solution.py:32
  11.5 5.2 %collective-permute-start.2 = (bf16[4,1,16,192]{3,2,1,0:T(8,128)(2,1)S(1)}, bf16[4,1,16,192]{3,2,1,0:T(8,128)(2,1)S(1)}, u32[]{:S(2)}, u32[]{:S(2)}) collective-permute-start(bf16[4,1,16,192]{3,2,1,0:T(8,128)(2,1)S(1)} %get-tuple-element.86), channel_id=1, source_target_pairs={{1,0},{2,1},{3,2},{4,3},{5,4},{6,5},{7,6},{8,7},{9,8},{10,9},{11,1... | collective-permute-start | bytes 73736 | tf_op jit(solution)/shard_map/ppermute | solution.py:32
  16.7 1.3 copy-start.1
  18.0 4.0 %copy-start.6 = (bf16[2,4,32,96]{3,2,1,0:T(8,128)(2,1)S(1)}, bf16[2,4,32,96]{3,2,1,0:T(8,128)(2,1)}, u32[]{:S(2)}) copy-start(bf16[2,4,32,96]{3,2,1,0:T(8,128)(2,1)} %param.7) | copy-start | bytes 147460
  21.2 0.7 copy-start.5
  22.1 19.6 %collective-permute-start.3 = (bf16[2,4,32,96]{3,2,1,0:T(8,128)(2,1)S(1)}, bf16[2,4,32,96]{3,2,1,0:T(8,128)(2,1)S(1)}, u32[]{:S(2)}, u32[]{:S(2)}) collective-permute-start(bf16[2,4,32,96]{3,2,1,0:T(8,128)(2,1)S(1)} %copy-done.6), channel_id=1, source_target_pairs={{32,0},{64,32},{96,64},{128,96},{160,128},{192,160},{224,192},{256... | collective-permute-start | bytes 147464 | tf_op jit(solution)/shard_map/ppermute | solution.py:32
  41.8 31.4 %collective-permute-start.4 = (bf16[4,1,32,96]{3,2,1,0:T(8,128)(2,1)S(1)}, bf16[4,1,32,96]{3,2,1,0:T(8,128)(2,1)S(1)}, u32[]{:S(2)}, u32[]{:S(2)}) collective-permute-start(bf16[4,1,32,96]{3,2,1,0:T(8,128)(2,1)S(1)} %get-tuple-element.83), channel_id=1, source_target_pairs={{0,1},{1,2},{2,3},{3,4},{4,5},{5,6},{6,7},{7,8},{8,9},{9,10},{10,1... | collective-permute-start | bytes 73736 | tf_op jit(solution)/shard_map/ppermute | solution.py:32
  44.2 28.9 %collective-permute-start.5 = (bf16[4,1,32,96]{3,2,1,0:T(8,128)(2,1)S(1)}, bf16[4,1,32,96]{3,2,1,0:T(8,128)(2,1)S(1)}, u32[]{:S(2)}, u32[]{:S(2)}) collective-permute-start(bf16[4,1,32,96]{3,2,1,0:T(8,128)(2,1)S(1)} %get-tuple-element.84), channel_id=1, source_target_pairs={{1,0},{2,1},{3,2},{4,3},{5,4},{6,5},{7,6},{8,7},{9,8},{10,9},{11,1... | collective-permute-start | bytes 73736 | tf_op jit(solution)/shard_map/ppermute | solution.py:32
  77.6 2.4 %copy-start.7 = (f32[96]{0:T(128)S(1)}, f32[96]{0:T(128)}, u32[]{:S(2)}) copy-start(f32[96]{0:T(128)} %param.11) | copy-start | bytes 1156
  77.6 2.4 %copy-start.8 = (f32[96]{0:T(128)S(1)}, f32[96]{0:T(128)}, u32[]{:S(2)}) copy-start(f32[96]{0:T(128)} %param.10) | copy-start | bytes 1156
  82.2 18.1 %collective-permute-start.6 = (bf16[2,4,32,96]{3,2,1,0:T(8,128)(2,1)S(1)}, bf16[2,4,32,96]{3,2,1,0:T(8,128)(2,1)S(1)}, u32[]{:S(2)}, u32[]{:S(2)}) collective-permute-start(bf16[2,4,32,96]{3,2,1,0:T(8,128)(2,1)S(1)} %get-tuple-element.42), channel_id=1, source_target_pairs={{0,32},{32,64},{64,96},{96,128},{128,160},{160,192},{192,224},{224... | collective-permute-start | bytes 147464 | tf_op jit(solution)/shard_map/ppermute | solution.py:32
  88.3 12.0 %all-to-all-start.2 = ((f32[16,2,96]{2,1,0:T(2,128)}), f32[16,2,96]{2,1,0:T(2,128)S(1)}, u32[]{:S(2)}, u32[]{:S(2)}) async-start(f32[16,2,96]{2,1,0:T(2,128)} %broadcast_in_dim.28), calls=%async_computation.2 | async-start | bytes 32768 | tf_op jit(solution)/shard_map/all_to_all | solution.py:43
  100.4 0.7 copy-start.2
  101.6 14.8 %collective-permute-start.7 = (bf16[4,1,32,96]{3,2,1,0:T(8,128)(2,1)}, bf16[4,1,32,96]{3,2,1,0:T(8,128)(2,1)S(1)}, u32[]{:S(2)}, u32[]{:S(2)}) collective-permute-start(bf16[4,1,32,96]{3,2,1,0:T(8,128)(2,1)} %get-tuple-element.79), channel_id=1, source_target_pairs={{0,1},{1,2},{2,3},{3,4},{4,5},{5,6},{6,7},{7,8},{8,9},{9,10},{10,1... | collective-permute-start | bytes 73736 | tf_op jit(solution)/shard_map/ppermute | solution.py:32
  106.3 10.2 %collective-permute-start.8 = (bf16[4,1,32,96]{3,2,1,0:T(8,128)(2,1)S(1)}, bf16[4,1,32,96]{3,2,1,0:T(8,128)(2,1)S(1)}, u32[]{:S(2)}, u32[]{:S(2)}) collective-permute-start(bf16[4,1,32,96]{3,2,1,0:T(8,128)(2,1)S(1)} %get-tuple-element.80), channel_id=1, source_target_pairs={{1,0},{2,1},{3,2},{4,3},{5,4},{6,5},{7,6},{8,7},{9,8},{10,9},{11,1... | collective-permute-start | bytes 73736 | tf_op jit(solution)/shard_map/ppermute | solution.py:32
  108.9 14.9 %all-to-all-start.3 = ((f32[32,2,96]{2,1,0:T(2,128)}), f32[32,2,96]{2,1,0:T(2,128)S(1)}, u32[]{:S(2)}, u32[]{:S(2)}) async-start(f32[32,2,96]{2,1,0:T(2,128)} %broadcast_in_dim.29), calls=%async_computation.3 | async-start | bytes 65536 | tf_op jit(solution)/shard_map/all_to_all | solution.py:43
  115.2 1.4 copy-start.3
  124.5 6.7 %collective-permute-start.9 = (bf16[3072,128]{1,0:T(8,128)(2,1)S(1)}, bf16[3072,128]{1,0:T(8,128)(2,1)S(1)}, u32[]{:S(2)}, u32[]{:S(2)}) collective-permute-start(bf16[3072,128]{1,0:T(8,128)(2,1)S(1)} %get-tuple-element.49), channel_id=1, source_target_pairs={{0,1},{1,0},{2,3},{3,2},{4,5},{5,4},{6,7},{7,6},{8,9},{9,8},{10,11... | collective-permute-start | bytes 2359304 | tf_op jit(solution)/shard_map/ppermute | solution.py:307
  132.3 15.5 %all-to-all-start.4 = ((bf16[4,768,128]{2,1,0:T(8,128)(2,1)}), bf16[4,768,128]{2,1,0:T(8,128)(2,1)S(1)}, u32[]{:S(2)}, u32[]{:S(2)}) async-start(bf16[4,768,128]{2,1,0:T(8,128)(2,1)} %bitcast.59), calls=%async_computation.4 | async-start | bytes 1572864 | tf_op jit(solution)/shard_map/all_to_all | solution.py:310
  135.8 5.3 %collective-permute-start.10 = (bf16[2,4,32,96]{3,2,1,0:T(8,128)(2,1)S(1)}, bf16[2,4,32,96]{3,2,1,0:T(8,128)(2,1)S(1)}, u32[]{:S(2)}, u32[]{:S(2)}) collective-permute-start(bf16[2,4,32,96]{3,2,1,0:T(8,128)(2,1)S(1)} %get-tuple-element.53), channel_id=1, source_target_pairs={{32,0},{64,32},{96,64},{128,96},{160,128},{192,160},{224,192},{256... | collective-permute-start | bytes 147464 | tf_op jit(solution)/shard_map/ppermute | solution.py:32
  150.5 30.1 %copy-start.4 = (bf16[4,6,32,96]{3,2,1,0:T(8,128)(2,1)S(1)}, bf16[4,6,32,96]{3,2,1,0:T(8,128)(2,1)}, u32[]{:S(2)}) copy-start(bf16[4,6,32,96]{3,2,1,0:T(8,128)(2,1)} %pad_maximum_fusion.1) | copy-start | bytes 442372
  150.5 22.5 %all-to-all-start.5 = ((f32[64,12,128]{2,1,0:T(8,128)}), f32[64,12,128]{2,1,0:T(8,128)S(1)}, u32[]{:S(2)}, u32[]{:S(2)}) async-start(f32[64,12,128]{2,1,0:T(8,128)} %reshape.99), calls=%async_computation.5 | async-start | bytes 1048576 | tf_op jit(solution)/shard_map/all_to_all | solution.py:313
  155.5 5.2 %collective-permute-start.11 = (bf16[4,1,32,96]{3,2,1,0:T(8,128)(2,1)S(1)}, bf16[4,1,32,96]{3,2,1,0:T(8,128)(2,1)S(1)}, u32[]{:S(2)}, u32[]{:S(2)}) collective-permute-start(bf16[4,1,32,96]{3,2,1,0:T(8,128)(2,1)S(1)} %get-tuple-element.77), channel_id=1, source_target_pairs={{0,1},{1,2},{2,3},{3,4},{4,5},{5,6},{6,7},{7,8},{8,9},{9,10},{10,1... | collective-permute-start | bytes 73736 | tf_op jit(solution)/shard_map/ppermute | solution.py:32
  158.7 5.5 %collective-permute-start.12 = (bf16[4,1,32,96]{3,2,1,0:T(8,128)(2,1)S(1)}, bf16[4,1,32,96]{3,2,1,0:T(8,128)(2,1)S(1)}, u32[]{:S(2)}, u32[]{:S(2)}) collective-permute-start(bf16[4,1,32,96]{3,2,1,0:T(8,128)(2,1)S(1)} %get-tuple-element.78), channel_id=1, source_target_pairs={{1,0},{2,1},{3,2},{4,3},{5,4},{6,5},{7,6},{8,7},{9,8},{10,9},{11,1... | collective-permute-start | bytes 73736 | tf_op jit(solution)/shard_map/ppermute | solution.py:32
  173.8 19.3 %all-to-all-start.6 = ((bf16[64,12,128]{2,1,0:T(8,128)(2,1)}), bf16[64,12,128]{2,1,0:T(8,128)(2,1)S(1)}, u32[]{:S(2)}, u32[]{:S(2)}) async-start(bf16[64,12,128]{2,1,0:T(8,128)(2,1)} %broadcast_in_dim.30), calls=%async_computation.6 | async-start | bytes 524288 | tf_op jit(solution)/shard_map/all_to_all | solution.py:316
  194.1 17.8 %all-to-all-start.7 = ((bf16[4,768,128]{2,1,0:T(8,128)(2,1)}), bf16[4,768,128]{2,1,0:T(8,128)(2,1)S(1)}, u32[]{:S(2)}, u32[]{:S(2)}) async-start(bf16[4,768,128]{2,1,0:T(8,128)(2,1)} %broadcast_in_dim.32), calls=%async_computation.7 | async-start | bytes 1572864 | tf_op jit(solution)/shard_map/all_to_all | solution.py:319
  211.9 5.6 %collective-permute-start.13 = (bf16[3072,128]{1,0:T(8,128)(2,1)S(1)}, bf16[3072,128]{1,0:T(8,128)(2,1)S(1)}, u32[]{:S(2)}, u32[]{:S(2)}) collective-permute-start(bf16[3072,128]{1,0:T(8,128)(2,1)S(1)} %bitcast.56), channel_id=1, source_target_pairs={{0,1},{1,0},{2,3},{3,2},{4,5},{5,4},{6,7},{7,6},{8,9},{9,8},{10,11... | collective-permute-start | bytes 2359304 | tf_op jit(solution)/shard_map/ppermute | solution.py:322

commit v3 on v2

v3 whole, which is shorter than its diff:
```python
import functools

import jax
import jax.numpy as jnp
from jax import lax
from jax.experimental import pallas as pl
from jax.experimental.pallas import tpu as pltpu
from jax.sharding import Mesh
from jax.sharding import PartitionSpec as P

GROUPS = 32
EPSILON = 1e-05

TM = ("zh", "y")
HEIGHT = ("zl", "x", "c")
REST = ("zh", "y", "zl")

VMEM_LIMIT = 32 * 2**20


def fine_mesh(mesh):
    tm, height = mesh.shape["tm"], mesh.shape["height"]
    zh = 2 if tm % 2 == 0 else 1
    core = 2
    x = 4 if height % 8 == 0 else height // 2
    return Mesh(mesh.devices.reshape(zh, tm // zh, height // (core * x), x, core), TM + HEIGHT)


def neighbour(value, axis, steps):
    count = lax.axis_size(axis)
    first, last = max(0, -steps), min(count, count - steps)
    return lax.ppermute(value, axis, [(i, i + steps) for i in range(first, last)])


def conv(padded, weight):
    return lax.conv_general_dilated(
        padded[None],
        weight,
        (1, 1, 1),
        "VALID",
        dimension_numbers=("NDHWC", "DHWIO", "NDHWC"),
        preferred_element_type=jnp.float32,
    )[0]


def whole(count=1, space=pltpu.VMEM):
    return [pl.BlockSpec(memory_space=space)] * count


def group_sums(first, second, outs):
    member = lax.broadcasted_iota(jnp.int32, (2, outs, outs), 1) // (outs // GROUPS)
    other = lax.broadcasted_iota(jnp.int32, (2, outs, outs), 2) // (outs // GROUPS)
    same = (member[0] == other[0]).astype(jnp.float32)
    both = jnp.concatenate([first, second, jnp.zeros((6, outs), jnp.float32)], 0)
    return jnp.dot(both, same, precision=lax.Precision.HIGHEST, preferred_element_type=jnp.float32)[:2]


def cell_sums(field):
    return jnp.sum(field.reshape(-1, field.shape[-1]), 0, keepdims=True)


def inside(where, field):
    row = lax.broadcasted_iota(jnp.int32, field.shape, 1)
    last = field.shape[1] - 1
    out = ((row == 0) & (where[1] == 1)) | ((row == last) & (where[2] == 1))
    return jnp.where(out, 0.0, field)


def conv_one_kernel(cache, features, above, below, weight, pre_norm, sums, wide):
    frames, rows, cols, outs = pre_norm.shape
    cells_in, half, ins = features.shape[1], cols // 2, features.shape[-1]
    timed = jnp.concatenate([cache[...], features[...]], 0)
    rowed = jnp.concatenate([above[:, :half][:, None], timed, below[:, :half][:, None]], 1)
    by_tap = []
    for e in range(3):
        total = jnp.zeros((frames, rows, half, outs), jnp.float32)
        for b in range(3):
            product = sum(
                jnp.dot(
                    rowed[a : a + frames].reshape(-1, ins),
                    weight[a, b, e],
                    preferred_element_type=jnp.float32,
                )
                for a in range(3)
            ).reshape(frames, cells_in + 2, half, outs)
            total += jnp.stack([product[:, (r + b) // 2] for r in range(rows)], 1)
        by_tap.append(total.reshape(frames * rows, half, outs))
    wide[...] = jnp.zeros_like(wide)
    wide[:, 8 : 8 + half, :outs] = by_tap[0]
    even = wide[:, 7 : 7 + half, :outs] + by_tap[1] + by_tap[2]
    wide[:, 8 : 8 + half, :outs] = by_tap[2]
    odd = by_tap[0] + by_tap[1] + wide[:, 9 : 9 + half, :outs]
    wide[:, pl.ds(0, half, stride=2), :outs] = even
    wide[:, pl.ds(1, half, stride=2), :outs] = odd
    pre = wide[:, :cols, :outs].reshape(pre_norm.shape)
    pre_norm[...] = pre
    own = pre[:, 1:-1]
    both = group_sums(cell_sums(own), cell_sums(own * own), outs)
    sums[...] = jnp.broadcast_to(both[None], sums.shape)


def conv_one(cache, features, above, below, weight, copies):
    frames, cells_in, half, _ = features.shape
    outs = weight.shape[-1]
    rows, cols = 2 * cells_in + 2, 2 * half
    return pl.pallas_call(
        conv_one_kernel,
        out_shape=(
            jax.ShapeDtypeStruct((frames, rows, cols, outs), jnp.float32),
            jax.ShapeDtypeStruct((copies, 2, outs), jnp.float32),
        ),
        in_specs=whole(5),
        out_specs=whole(2),
        scratch_shapes=[pltpu.VMEM((frames * rows, cols + 16, 128), jnp.float32)],
        compiler_params=pltpu.CompilerParams(vmem_limit_bytes=VMEM_LIMIT),
        name="conv_one",
    )(cache, features, above, below, weight)


def grad_hidden_kernel(cot, later, above, below, weight, grad_hidden, shifted, wide):
    frames, rows, cols, ins = grad_hidden.shape
    outs = cot.shape[-1]
    half = cols // 2
    timed = jnp.concatenate([cot[...], later[...]], 0)
    pair = lambda part: jnp.stack([part[:, half:, :outs], part[:, half:, outs:]], 1)
    rowed = jnp.concatenate([pair(above), timed, pair(below)], 1).astype(jnp.float32)
    wide[...] = jnp.zeros_like(wide)
    wide[:, 8 : 8 + cols, :outs] = rowed.reshape(-1, cols, outs)
    total = jnp.zeros((frames * rows * cols, ins), jnp.float32)
    for e in range(3):
        part = wide[:, 9 - e : 9 - e + cols, :outs].astype(jnp.bfloat16)
        part = part.reshape(2 * frames, rows + 2, cols, outs)
        shifted[e] = part
        for a in range(3):
            for b in range(3):
                total += lax.dot_general(
                    part[2 - a : 2 - a + frames, 2 - b : 2 - b + rows].reshape(-1, outs),
                    weight[a, b, e],
                    (((1,), (1,)), ((), ())),
                    preferred_element_type=jnp.float32,
                )
    grad_hidden[...] = total.reshape(grad_hidden.shape)


def hidden_grads(cot, later, above, below, weight):
    frames, rows, cols, outs = cot.shape
    return pl.pallas_call(
        grad_hidden_kernel,
        out_shape=(
            jax.ShapeDtypeStruct((frames, rows + 2, cols, weight.shape[-2]), jnp.float32),
            jax.ShapeDtypeStruct((3, 2 * frames, rows + 4, cols, outs), jnp.bfloat16),
        ),
        in_specs=whole(5),
        out_specs=whole(2),
        scratch_shapes=[pltpu.VMEM((2 * frames * (rows + 4), cols + 16, 128), jnp.float32)],
        compiler_params=pltpu.CompilerParams(vmem_limit_bytes=VMEM_LIMIT),
        cost_estimate=pl.CostEstimate(flops=2**30, bytes_accessed=2**21, transcendentals=0),
        name="grad_hidden",
    )(cot, later, above, below, weight)


def middle_kernel(count, where, came, pre_norm, grad_hidden, gain, shift, hidden, grad_normed, normed, rstd, sums):
    outs = pre_norm.shape[-1]
    total = jnp.sum(came[...], 0)
    mean = total[:1] / count
    scaled = lax.rsqrt(total[1:2] / count - mean * mean + EPSILON)
    rstd[...] = scaled
    flat = (pre_norm[...].reshape(-1, outs) - mean) * scaled
    shifted = flat * gain[...] + shift[...]
    sigma = 1.0 / (1.0 + jnp.exp(-shifted))
    hidden[...] = inside(where, (shifted * sigma).reshape(pre_norm.shape)).astype(jnp.bfloat16)
    grad = grad_hidden[...].reshape(-1, outs) * sigma * (1.0 + shifted * (1.0 - sigma)) * gain[...]
    grad, flat = grad.reshape(pre_norm.shape), flat.reshape(pre_norm.shape)
    grad_normed[...] = grad
    normed[...] = flat
    own = grad[:, 1:-1]
    both = group_sums(cell_sums(own), cell_sums(own * flat[:, 1:-1]), outs)
    sums[...] = jnp.broadcast_to(both[None], sums.shape)


def middle(count, where, came, pre_norm, grad_hidden, gain, shift, copies):
    shape, outs = pre_norm.shape, pre_norm.shape[-1]
    return pl.pallas_call(
        functools.partial(middle_kernel, count),
        out_shape=(
            jax.ShapeDtypeStruct(shape, jnp.bfloat16),
            jax.ShapeDtypeStruct(shape, jnp.float32),
            jax.ShapeDtypeStruct(shape, jnp.float32),
            jax.ShapeDtypeStruct((1, outs), jnp.float32),
            jax.ShapeDtypeStruct((copies, 2, outs), jnp.float32),
        ),
        in_specs=whole(1, pltpu.SMEM) + whole(5),
        out_specs=whole(5),
        compiler_params=pltpu.CompilerParams(vmem_limit_bytes=VMEM_LIMIT),
        name="middle",
    )(where, came, pre_norm, grad_hidden, gain[None], shift[None])


def second_weight_kernel(hidden, shifted, out):
    frames, rows, cols, ins = hidden.shape
    outs = shifted.shape[-1]
    own = hidden[:, 1:-1].reshape(-1, ins).astype(jnp.float32).T.astype(jnp.bfloat16)
    for a in range(3):
        pieces = [
            shifted[e, 2 - a : 2 - a + frames, 3 - b : 3 - b + rows - 2].reshape(-1, outs)
            for b in range(3)
            for e in range(3)
        ]
        pieces.append(jnp.zeros((pieces[0].shape[0], 32), jnp.bfloat16))
        out[a] = jnp.dot(own, jnp.concatenate(pieces, 1), preferred_element_type=jnp.float32)


def second_weight(hidden, shifted):
    return pl.pallas_call(
        second_weight_kernel,
        out_shape=jax.ShapeDtypeStruct((3, hidden.shape[-1], 896), jnp.float32),
        in_specs=whole(2),
        out_specs=whole()[0],
        compiler_params=pltpu.CompilerParams(vmem_limit_bytes=VMEM_LIMIT),
        cost_estimate=pl.CostEstimate(flops=2**29, bytes_accessed=2**21, transcendentals=0),
        name="second_weight",
    )(hidden, shifted)


def col_sums(wide, cells):
    half = cells.shape[1] // 2
    wide[...] = jnp.zeros_like(wide)
    wide[:, 8 : 8 + cells.shape[1], : cells.shape[2]] = cells

    def every_second(start):
        return wide[:, pl.ds(start, half, stride=2), : cells.shape[2]]

    before, even, odd, after = (every_second(7 + k) for k in range(4))
    return odd + after, even + odd, before + even


def weight_grads_kernel(
    count, where, cache, features, above, below, came, grad_normed, normed, rstd, two, grad_pre, away, kept, wide
):
    frames, rows, cols, outs = grad_normed.shape
    ins, mids = features.shape[-1], two.shape[1]
    total = jnp.sum(came[...], 0) / count
    timed = jnp.concatenate([cache[...], features[...]], 0)
    rows_in = jnp.concatenate([above[:, : cols // 2][:, None], timed, below[:, : cols // 2][:, None]], 1)
    merged = (frames * rows * cols, outs)
    grad = grad_normed[...].reshape(merged) - total[:1] - normed[...].reshape(merged) * total[1:2]
    grad = inside(where, (grad * rstd[...]).reshape(grad_normed.shape)).astype(jnp.bfloat16)
    grad_pre[...] = grad
    grad = grad[:, 1:-1].astype(jnp.float32)
    rows = rows - 2
    by_tap = col_sums(wide, grad.reshape(frames * rows, cols, outs))
    pieces = []
    for b in range(3):
        for e in range(3):
            part = by_tap[e].reshape(frames, rows, cols // 2, outs)
            none = jnp.zeros_like(part[:, 0])
            r = [part[:, k] for k in range(rows)]
            stacked = (
                [r[0], r[1] + r[2], r[3], none],
                [none, r[0] + r[1], r[2] + r[3], none],
                [none, r[0], r[1] + r[2], r[3]],
            )[b]
            cells = jnp.stack(stacked, 1).astype(jnp.bfloat16)
            pieces.append(cells.reshape(-1, outs))
    pieces.append(jnp.zeros((pieces[0].shape[0], 32), jnp.bfloat16))
    cells = jnp.concatenate(pieces, 1)
    lower = where[0] == 0

    def write(at, low, high):
        away[at : at + low.shape[0]] = jnp.where(lower, high, low).astype(jnp.bfloat16)
        kept[at : at + low.shape[0]] = jnp.where(lower, low, high)

    at = 0
    for a in range(3):
        product = lax.dot_general(
            rows_in[a : a + frames].reshape(-1, ins),
            cells,
            (((0,), (0,)), ((), ())),
            preferred_element_type=jnp.float32,
        )
        for j in range(7):
            block = product[:, 128 * j : 128 * j + 128]
            write(at, block[: ins // 2], block[ins // 2 :])
            at += ins // 2
    for a in range(3):
        product = two[a]
        for j in range(7):
            block = product[:, 128 * j : 128 * j + 128]
            write(at, block[: mids // 2], block[mids // 2 :])
            at += mids // 2
    if at < kept.shape[0]:
        tail = jnp.zeros((kept.shape[0] - at, 128), jnp.float32)
        away[at:] = tail.astype(jnp.bfloat16)
        kept[at:] = tail


def weight_grads(count, where, cache, features, above, below, came, grad_normed, normed, rstd, two, half_rows):
    frames, rows, cols, outs = grad_normed.shape
    return pl.pallas_call(
        functools.partial(weight_grads_kernel, count),
        out_shape=(
            jax.ShapeDtypeStruct(grad_normed.shape, jnp.bfloat16),
            jax.ShapeDtypeStruct((half_rows, 128), jnp.bfloat16),
            jax.ShapeDtypeStruct((half_rows, 128), jnp.float32),
        ),
        in_specs=whole(1, pltpu.SMEM) + whole(9),
        out_specs=whole(3),
        scratch_shapes=[pltpu.VMEM((frames * (rows - 2), cols + 16, 128), jnp.float32)],
        compiler_params=pltpu.CompilerParams(vmem_limit_bytes=VMEM_LIMIT),
        name="weight_grads",
    )(where, cache, features, above, below, came, grad_normed, normed, rstd, two)


def unpack_kernel(scale, where, mine_one, other_one, mine_two, other_two, one, two):
    lower = where[0] == 0
    for mine, other, out in ((mine_one, other_one, one), (mine_two, other_two, two)):
        taps, rows, outs = out.shape
        half = rows // 2
        own = jnp.concatenate([mine[half * j : half * j + half] for j in range(7)], 1)
        far = jnp.concatenate([other[half * j : half * j + half] for j in range(7)], 1)
        own, far = own.astype(jnp.float32) * scale, far.astype(jnp.float32) * scale
        low, high = jnp.where(lower, own, far), jnp.where(lower, far, own)
        for k in range(taps):
            out[k, :half] = low[:, outs * k : outs * k + outs]
            out[k, half:] = high[:, outs * k : outs * k + outs]


def unpack(where, mine, other, ins, mids, scale):
    half_one, half_two = 7 * ins // 2, 7 * mids // 2
    skip = 3 * half_one // half_two
    block_one = pl.BlockSpec((half_one, 128), lambda a: (a, 0))
    block_two = pl.BlockSpec((half_two, 128), lambda a: (a + skip, 0))
    return pl.pallas_call(
        functools.partial(unpack_kernel, scale),
        grid=(3,),
        out_shape=(
            jax.ShapeDtypeStruct((27, ins, mids), jnp.float32),
            jax.ShapeDtypeStruct((27, mids, mids), jnp.float32),
        ),
        in_specs=[pl.BlockSpec(memory_space=pltpu.SMEM), block_one, block_one, block_two, block_two],
        out_specs=[
            pl.BlockSpec((9, ins, mids), lambda a: (a, 0, 0)),
            pl.BlockSpec((9, mids, mids), lambda a: (a, 0, 0)),
        ],
        compiler_params=pltpu.CompilerParams(vmem_limit_bytes=VMEM_LIMIT),
        name="unpack",
    )(where, mine, other, mine, other)


def feature_grads_kernel(grad_pre, weight, out, wide):
    frames, rows, cols, outs = grad_pre.shape
    own, cells_in, cols_in, ins = out.shape
    by_tap = col_sums(wide, grad_pre[...].astype(jnp.float32).reshape(frames * rows, cols, outs))
    total = jnp.zeros((own * cells_in * cols_in, ins), jnp.float32)
    for b in range(3):
        for e in range(3):
            part = by_tap[e].reshape(frames, rows, cols // 2, outs)
            cells = jnp.stack(
                [part[:, 2 * k + 2 - b] + part[:, 2 * k + 3 - b] for k in range(cells_in)], 1
            ).astype(jnp.bfloat16)
            for a in range(3):
                total += lax.dot_general(
                    cells[2 - a : 2 - a + own].reshape(-1, outs),
                    weight[a, b, e],
                    (((1,), (1,)), ((), ())),
                    preferred_element_type=jnp.float32,
                )
    out[...] = total.reshape(out.shape)


def feature_grads(grad_rowed, weight, shape):
    frames, rows, cols, _ = grad_rowed.shape
    return pl.pallas_call(
        feature_grads_kernel,
        out_shape=jax.ShapeDtypeStruct(shape, jnp.float32),
        in_specs=whole(2),
        out_specs=whole()[0],
        scratch_shapes=[pltpu.VMEM((frames * rows, cols + 16, 128), jnp.float32)],
        compiler_params=pltpu.CompilerParams(vmem_limit_bytes=VMEM_LIMIT),
        cost_estimate=pl.CostEstimate(flops=2**28, bytes_accessed=2**21, transcendentals=0),
        name="feature_grads",
    )(grad_rowed, weight)


def half_rows(ins, mids):
    unit = lax.axis_size("x") * lax.axis_size(REST)
    return -(-(21 * (ins + mids) // 2) // unit) * unit


SWAP = [(0, 1), (1, 0)]


def body(features, cotangent, weight_one, weight_two, norm_gain, norm_shift):
    frames, ins = features.shape[0], features.shape[-1]
    rows, cols, mids = cotangent.shape[1:]
    xs, rest, height = lax.axis_size("x"), lax.axis_size(REST), lax.axis_size(HEIGHT)
    cells = frames * rows * cols * 2 * xs * rest
    count = cells * (mids // GROUPS)
    at_row = lax.axis_index(HEIGHT)
    where = jnp.stack([lax.axis_index("c"), at_row == 0, at_row == height - 1]).astype(jnp.int32)
    barrier = lax.optimization_barrier

    def exchange(copies, axes):
        return lax.all_to_all(copies, axes, 0, 0)

    def spread(value, copies):
        return jnp.broadcast_to(value[None], (copies,) + value.shape)

    cache = neighbour(features, TM, 1)
    later = neighbour(cotangent, TM, -1)

    def edge(cell_row, cot_row):
        feature = jnp.concatenate([cache[:, cell_row], features[:, cell_row]], 0)
        pair = [jnp.concatenate([cotangent[:, k], later[:, k]], 0) for k in (cot_row, cot_row + 1)]
        return jnp.concatenate([feature, jnp.concatenate(pair, -1)], 1)

    above = neighbour(edge(-1, rows - 2), HEIGHT, 1)
    below = neighbour(edge(0, 0), HEIGHT, -1)
    pre_norm, sums = conv_one(cache, features, above, below, weight_one, height)
    came = exchange(sums, HEIGHT)
    grad_hidden, shifted_cot = hidden_grads(cotangent, later, above, below, weight_two)
    sums, grad_hidden, shifted_cot = barrier((came.sum(0), grad_hidden, shifted_cot))
    came = exchange(spread(sums, lax.axis_size(TM)), TM)
    pair, others = ("y", "c"), ("zh", "zl", "x")
    hidden, grad_normed, normed, rstd, sums = middle(
        count, where, came, pre_norm, grad_hidden, norm_gain, norm_shift, lax.axis_size(pair)
    )
    sums, hidden = barrier((sums, hidden))
    sums = exchange(sums, pair).sum(0)
    local_two = second_weight(hidden, shifted_cot)
    before = neighbour(hidden, TM, 1)
    sums, local_two, before = barrier((sums, local_two, before))
    came = exchange(spread(sums, lax.axis_size(others)), others)
    decoded = conv(
        jnp.pad(jnp.concatenate([before, hidden], 0), ((0, 0), (0, 0), (1, 1), (0, 0))), weight_two
    ).astype(jnp.bfloat16)
    came, decoded = barrier((came, decoded))

    scale = 1.0 / cells**0.5
    grad_pre, away, kept = weight_grads(
        count, where, cache, features, above, below, came, grad_normed, normed, rstd, local_two, half_rows(ins, mids)
    )

    part = kept + lax.ppermute(away, "c", SWAP).astype(jnp.float32)
    part = part.astype(jnp.bfloat16).reshape(xs, -1, 128)
    part, grad_pre = barrier((part, grad_pre))
    part = exchange(part, "x").astype(jnp.float32).sum(0)
    after = neighbour(grad_pre, TM, -1)
    part, after = barrier((part, after))
    part = exchange(part.reshape(rest, -1, 128), REST).sum(0).astype(jnp.bfloat16)
    grad_features = feature_grads(jnp.concatenate([grad_pre, after], 0), weight_one, features.shape)
    part, grad_features = barrier((part, grad_features))
    part = exchange(spread(part, rest), REST).reshape(-1, 128)
    part = exchange(spread(part, xs), "x").reshape(-1, 128)
    grad_one, grad_two = unpack(where, part, lax.ppermute(part, "c", SWAP), ins, mids, scale)
    return decoded, grad_features, grad_one.reshape(weight_one.shape), grad_two.reshape(weight_two.shape)


def solution(mesh):
    split = P(TM, HEIGHT, None, None)
    return jax.shard_map(
        body,
        mesh=fine_mesh(mesh),
        in_specs=(split, split, P(), P(), P(), P()),
        out_specs=(split, split, P(), P()),
        check_vma=False,
    )
```

time: 222 us -> 191 us (0.86)
  blocking collectives: 45.2 us -> 30.3 us
  matrix products: 11.3 us -> 1.56 us
  other arithmetic: 8.27 us -> 1.7 us
  Pallas kernels: 5.07 us -> 10.8 us
  local copies, waits for them, and re-layouts: 13.4 us -> 8.23 us
  starting transfers between devices: 74.5 us -> 71 us
  waiting for transfers between devices: 61.6 us -> 65.1 us
    ppermute x12 -> x6, starting transfers between devices: 33.4 us -> 17.4 us  [neighbour(): lax.ppermute(value, axis, [(i, i + steps) for i in range(first, last)])]
    all_to_all x2, blocking collectives: 45.2 us -> 30.3 us  [exchange(): return lax.all_to_all(copies, axes, 0, 0)]
    all_to_all x6, starting transfers between devices: 32.5 us -> 43.4 us  [exchange(): return lax.all_to_all(copies, axes, 0, 0)]
    all_to_all x6, waiting for transfers between devices: 47.1 us -> 56.6 us  [exchange(): return lax.all_to_all(copies, axes, 0, 0)]
    conv_general_dilated x3 -> x1, matrix products: 7.99 us -> 1.56 us  [conv(): lax.conv_general_dilated(padded[None], weight, (1, 1, 1), 'VALID', dimens...]
    ppermute x12 -> x6, waiting for transfers between devices: 10.8 us -> 4.69 us  [neighbour(): lax.ppermute(value, axis, [(i, i + steps) for i in range(first, last)])]
    pallas_call x1 -> x5, Pallas kernels: 0.56 us -> 5.71 us  [the longest x1 1.54 us: conv_one(): pl.pallas_call(conv_one_kernel, out_shape=(jax.ShapeDtypeStruct((frames,...]
    dot_general x5 -> x0, matrix products: 3.3 us -> none  [the longest x3 2.91 us: body(): lax.dot_general(flat_hidden, shifted_cot[2 - a:2 - a + frames].reshape(-1...]
  transfers between devices with their start and end apart: 20 -> 14, of which waited for: 12 -> 10; matrix products, arithmetic and copies ran while one was open for 5% -> 3% of each run, Pallas kernels for 1% -> 2%
where the time goes in v3:
time: 191 us; the launch traced here: 190 us
  starting transfers between devices  71 us (37%)
  waiting for transfers between devices  65.1 us (34%)
  blocking collectives  30.3 us (16%)
  Pallas kernels  10.8 us (6%)
  local copies, waits for them, and re-layouts  8.23 us (4%)
    all_to_all x6, waiting for transfers between devices, exchange(): return lax.all_to_all(copies, axes, 0, 0)  56.6 us
    all_to_all x6, starting transfers between devices, exchange(): return lax.all_to_all(copies, axes, 0, 0)  43.4 us
    all_to_all x2, blocking collectives, exchange(): return lax.all_to_all(copies, axes, 0, 0)  30.3 us
    ppermute x6, starting transfers between devices, neighbour(): lax.ppermute(value, axis, [(i, i + steps) for i in range(first, last)])  17.4 us
    ppermute x1, starting transfers between devices, body(): lax.ppermute(part, 'c', SWAP)  6.77 us
    ppermute x6, waiting for transfers between devices, neighbour(): lax.ppermute(value, axis, [(i, i + steps) for i in range(first, last)])  4.69 us
    unnamed x19, local copies, waits for them, and re-layouts  4.43 us
  transfers between devices with their start and end apart: 14, of which 10 were waited for; matrix products, arithmetic and copies ran while one was open for 3% of the time, Pallas kernels for 2%

profile of v3, /device:TPU:1, one launch (start us, length us, event | category | flops | bytes accessed | tf_op | source)
XLA Modules:
  0.0 189.5 jit_solution(4946346055153057326)
XLA Ops:
  1.5 4.0 %collective-permute-start = (bf16[2,2,16,192]{3,2,0,1:T(8,128)(2,1)S(1)}, bf16[2,2,16,192]{3,2,0,1:T(8,128)(2,1)S(1)}, u32[]{:S(2)}, u32[]{:S(2)}) collective-permute-start(bf16[2,2,16,192]{3,2,0,1:T(8,128)(2,1)S(1)} %copy.22), channel_id=1, source_target_pairs={{0,32},{32,64},{64,96},{96,128},{128,160},{160,192},{192,224},{224... | collective-permute-start | bytes 73736 | tf_op jit(solution)/shard_map/ppermute | solution.py:32
  6.4 1.3 collective-permute-start.1
  9.2 2.2 %collective-permute-done.1 = bf16[2,4,32,96]{3,2,0,1:T(8,128)(2,1)S(1)} collective-permute-done((bf16[2,4,32,96]{3,2,0,1:T(8,128)(2,1)S(1)}, bf16[2,4,32,96]{3,2,0,1:T(8,128)(2,1)S(1)}, u32[]{:S(2)}, u32[]{:S(2)}) %collective-permute-start.1) | collective-permute-done | bytes 49184 | tf_op jit(solution)/shard_map/ppermute | solution.py:32
  11.5 5.1 %collective-permute-start.2 = (bf16[4,48,192]{2,1,0:T(8,128)(2,1)S(1)}, bf16[4,48,192]{2,1,0:T(8,128)(2,1)S(1)}, u32[]{:S(2)}, u32[]{:S(2)}) collective-permute-start(bf16[4,48,192]{2,1,0:T(8,128)(2,1)S(1)} %maximum_maximum_fusion), channel_id=1, source_target_pairs={{0,1},{1,2},{2,3},{3,4},{4,5},{5,6},{6,7},{7,8},{8,9},{9,10},{10,1... | collective-permute-start | bytes 221192 | tf_op jit(solution)/shard_map/ppermute | solution.py:32
  16.7 3.4 %collective-permute-start.3 = (bf16[4,48,192]{2,1,0:T(8,128)(2,1)S(1)}, bf16[4,48,192]{2,1,0:T(8,128)(2,1)S(1)}, u32[]{:S(2)}, u32[]{:S(2)}) collective-permute-start(bf16[4,48,192]{2,1,0:T(8,128)(2,1)S(1)} %maximum_maximum_fusion.1), channel_id=1, source_target_pairs={{1,0},{2,1},{3,2},{4,3},{5,4},{6,5},{7,6},{8,7},{9,8},{10,9},{11,1... | collective-permute-start | bytes 221192 | tf_op jit(solution)/shard_map/ppermute | solution.py:32
  20.1 2.5 %collective-permute-done.3.below = bf16[4,48,192]{2,1,0:T(8,128)(2,1)S(1)} collective-permute-done((bf16[4,48,192]{2,1,0:T(8,128)(2,1)S(1)}, bf16[4,48,192]{2,1,0:T(8,128)(2,1)S(1)}, u32[]{:S(2)}, u32[]{:S(2)}) %collective-permute-start.3) | collective-permute-done | bytes 73760 | tf_op jit(solution)/shard_map/ppermute | solution.py:32
  22.6 1.3 copy-done
  24.7 1.5 conv_one.1
  26.2 10.8 %all-to-all-start = ((f32[32,2,96]{2,1,0:T(2,128)}), f32[32,2,96]{2,1,0:T(2,128)S(1)}, u32[]{:S(2)}, u32[]{:S(2)}) async-start(f32[32,2,96]{2,1,0:T(2,128)} %get-tuple-element.34), calls=%async_computation | async-start | bytes 65536 | tf_op jit(solution)/shard_map/all_to_all | solution.py:404
  38.1 6.6 %all-to-all-done = f32[32,2,96]{2,1,0:T(2,128)S(1)} async-done(((f32[32,2,96]{2,1,0:T(2,128)}), f32[32,2,96]{2,1,0:T(2,128)S(1)}, u32[]{:S(2)}, u32[]{:S(2)}) %all-to-all-start) | async-done | bytes 24608 | tf_op jit(solution)/shard_map/all_to_all | solution.py:404
  45.4 14.5 %all-to-all-start.1 = ((f32[16,2,96]{2,1,0:T(2,128)}), f32[16,2,96]{2,1,0:T(2,128)S(1)}, u32[]{:S(2)}, u32[]{:S(2)}) async-start(f32[16,2,96]{2,1,0:T(2,128)} %broadcast_in_dim.16), calls=%async_computation.1 | async-start | bytes 32768 | tf_op jit(solution)/shard_map/all_to_all | solution.py:404
  60.0 11.2 %all-to-all-done.1.came = f32[16,2,96]{2,1,0:T(2,128)S(1)} async-done(((f32[16,2,96]{2,1,0:T(2,128)}), f32[16,2,96]{2,1,0:T(2,128)S(1)}, u32[]{:S(2)}, u32[]{:S(2)}) %all-to-all-start.1) | async-done | bytes 12320 | tf_op jit(solution)/shard_map/all_to_all | solution.py:404
  71.1 1.5 middle.1
  72.6 2.2 %collective-permute-start.4 = (bf16[2,6,32,96]{3,2,1,0:T(8,128)(2,1)S(1)}, bf16[2,6,32,96]{3,2,1,0:T(8,128)(2,1)S(1)}, u32[]{:S(2)}, u32[]{:S(2)}) collective-permute-start(bf16[2,6,32,96]{3,2,1,0:T(8,128)(2,1)S(1)} %get-tuple-element.43.hidden), channel_id=1, source_target_pairs={{0,32},{32,64},{64,96},{96,128},{128,160},{160,192},{192,224},{224... | collective-permute-start | bytes 221192 | tf_op jit(solution)/shard_map/ppermute | solution.py:32
  74.9 6.1 %all-to-all-start.2 = ((f32[16,2,96]{2,1,0:T(2,128)}), f32[16,2,96]{2,1,0:T(2,128)S(1)}, u32[]{:S(2)}, u32[]{:S(2)}) async-start(f32[16,2,96]{2,1,0:T(2,128)} %get-tuple-element.42), calls=%async_computation.2 | async-start | bytes 32768 | tf_op jit(solution)/shard_map/all_to_all | solution.py:404
  81.5 6.7 %all-to-all-done.2 = f32[16,2,96]{2,1,0:T(2,128)S(1)} async-done(((f32[16,2,96]{2,1,0:T(2,128)}), f32[16,2,96]{2,1,0:T(2,128)S(1)}, u32[]{:S(2)}, u32[]{:S(2)}) %all-to-all-start.2) | async-done | bytes 12320 | tf_op jit(solution)/shard_map/all_to_all | solution.py:404
  88.9 3.9 %all-to-all-start.3 = ((f32[32,2,96]{2,1,0:T(2,128)}), f32[32,2,96]{2,1,0:T(2,128)S(1)}, u32[]{:S(2)}, u32[]{:S(2)}) async-start(f32[32,2,96]{2,1,0:T(2,128)} %broadcast_in_dim.37), calls=%async_computation.3 | async-start | bytes 65536 | tf_op jit(solution)/shard_map/all_to_all | solution.py:404
  92.9 1.6 convolution_convert_fusion
  95.1 6.4 %all-to-all-done.3.came = f32[32,2,96]{2,1,0:T(2,128)S(1)} async-done(((f32[32,2,96]{2,1,0:T(2,128)}), f32[32,2,96]{2,1,0:T(2,128)S(1)}, u32[]{:S(2)}, u32[]{:S(2)}) %all-to-all-start.3) | async-done | bytes 24608 | tf_op jit(solution)/shard_map/all_to_all | solution.py:404
  102.7 3.4 %collective-permute-start.5 = (bf16[3072,128]{1,0:T(8,128)(2,1)S(1)}, bf16[3072,128]{1,0:T(8,128)(2,1)S(1)}, u32[]{:S(2)}, u32[]{:S(2)}) collective-permute-start(bf16[3072,128]{1,0:T(8,128)(2,1)S(1)} %get-tuple-element.54), channel_id=1, source_target_pairs={{0,1},{1,0},{2,3},{3,2},{4,5},{5,4},{6,7},{7,6},{8,9},{9,8},{10,11... | collective-permute-start | bytes 2359304 | tf_op jit(solution)/shard_map/ppermute | solution.py:444
  106.0 1.9 collective-permute-done.5
  109.0 3.5 %all-to-all-start.4 = ((bf16[4,768,128]{2,1,0:T(8,128)(2,1)}), bf16[4,768,128]{2,1,0:T(8,128)(2,1)S(1)}, u32[]{:S(2)}, u32[]{:S(2)}) async-start(bf16[4,768,128]{2,1,0:T(8,128)(2,1)} %bitcast.18), calls=%async_computation.4 | async-start | bytes 1572864 | tf_op jit(solution)/shard_map/all_to_all | solution.py:404
  112.5 1.4 collective-permute-start.6
  113.9 10.6 %all-to-all-done.4 = bf16[4,768,128]{2,1,0:T(8,128)(2,1)S(1)} async-done(((bf16[4,768,128]{2,1,0:T(8,128)(2,1)}), bf16[4,768,128]{2,1,0:T(8,128)(2,1)S(1)}, u32[]{:S(2)}, u32[]{:S(2)}) %all-to-all-start.4) | async-done | bytes 786464 | tf_op jit(solution)/shard_map/all_to_all | solution.py:404
  125.4 4.6 %all-to-all-start.5 = ((f32[64,12,128]{2,1,0:T(8,128)}), f32[64,12,128]{2,1,0:T(8,128)S(1)}, u32[]{:S(2)}, u32[]{:S(2)}) async-start(f32[64,12,128]{2,1,0:T(8,128)} %reshape.29), calls=%async_computation.5 | async-start | bytes 1048576 | tf_op jit(solution)/shard_map/all_to_all | solution.py:404
  130.1 1.6 feature_grads.1
  131.8 15.1 %all-to-all-done.5 = f32[64,12,128]{2,1,0:T(8,128)S(1)} async-done(((f32[64,12,128]{2,1,0:T(8,128)}), f32[64,12,128]{2,1,0:T(8,128)S(1)}, u32[]{:S(2)}, u32[]{:S(2)}) %all-to-all-start.5) | async-done | bytes 393248 | tf_op jit(solution)/shard_map/all_to_all | solution.py:404
  147.0 19.5 %all_to_all.40 = bf16[64,12,128]{2,1,0:T(8,128)(2,1)S(1)} all-to-all(bf16[64,12,128]{2,1,0:T(8,128)(2,1)S(1)} %broadcast_in_dim.39), channel_id=1, replica_groups=mesh['zh'=2,'y'=8,'zl'=4,'x'=4,'c'=2] {'zh','y','zl'}, dimensions={0} | all-to-all | bytes 393216 | tf_op jit(solution)/shard_map/all_to_all | solution.py:404
  166.7 10.8 %all_to_all.41 = bf16[4,768,128]{2,1,0:T(8,128)(2,1)S(1)} all-to-all(bf16[4,768,128]{2,1,0:T(8,128)(2,1)S(1)} %broadcast_in_dim.41), channel_id=1, replica_groups=mesh['zh'=2,'y'=8,'zl'=4,'x'=4,'c'=2] {'x'}, dimensions={0} | all-to-all | bytes 1572864 | tf_op jit(solution)/shard_map/all_to_all | solution.py:404
  177.4 6.8 %collective-permute-start.7 = (bf16[3072,128]{1,0:T(8,128)(2,1)S(1)}, bf16[3072,128]{1,0:T(8,128)(2,1)S(1)}, u32[]{:S(2)}, u32[]{:S(2)}) collective-permute-start(bf16[3072,128]{1,0:T(8,128)(2,1)S(1)} %bitcast.39), channel_id=1, source_target_pairs={{0,1},{1,0},{2,3},{3,2},{4,5},{5,4},{6,7},{7,6},{8,9},{9,8},{10,11... | collective-permute-start | bytes 2359304 | tf_op jit(solution)/shard_map/ppermute | solution.py:455
  184.2 1.9 collective-permute-done.7.other_one.other_two
  186.1 3.4 %unpack.1 = (f32[27,192,96]{2,1,0:T(8,128)}, f32[27,96,96]{2,1,0:T(8,128)}) custom-call(s32[3]{0:T(128)S(1)} %pad_add_fusion.where, bf16[3072,128]{1,0:T(8,128)(2,1)S(1)} %bitcast.40, bf16[3072,128]{1,0:T(8,128)(2,1)S(1)} %collective-permute-done.7.other_one.other_two, bf16[3072,128]{1,0:T(8,128)(2,1)S(1)} %bitcast.41, ...), custom_call_target="tpu_custom_call" | custom-call | tf_op jit(solution)/shard_map/unpack/pallas_call | solution.py:333
  (47 shorter events, 11.3 us)
Async XLA Ops:
  0.6 36.4 %copy-start.4 = (bf16[2,4,32,96]{3,2,1,0:T(8,128)(2,1)S(1)}, bf16[2,4,32,96]{3,2,1,0:T(8,128)(2,1)}, u32[]{:S(2)}) copy-start(bf16[2,4,32,96]{3,2,1,0:T(8,128)(2,1)} %cot.1) | copy-start | bytes 147460
  0.6 36.4 %copy-start.7 = (bf16[3,3,3,96,96]{4,3,2,1,0:T(8,128)(2,1)S(1)}, bf16[3,3,3,96,96]{4,3,2,1,0:T(8,128)(2,1)}, u32[]{:S(2)}) copy-start(bf16[3,3,3,96,96]{4,3,2,1,0:T(8,128)(2,1)} %weight.4) | copy-start | bytes 1492996
  1.5 7.7 %collective-permute-start = (bf16[2,2,16,192]{3,2,0,1:T(8,128)(2,1)S(1)}, bf16[2,2,16,192]{3,2,0,1:T(8,128)(2,1)S(1)}, u32[]{:S(2)}, u32[]{:S(2)}) collective-permute-start(bf16[2,2,16,192]{3,2,0,1:T(8,128)(2,1)S(1)} %copy.22), channel_id=1, source_target_pairs={{0,32},{32,64},{64,96},{96,128},{128,160},{160,192},{192,224},{224... | collective-permute-start | bytes 73736 | tf_op jit(solution)/shard_map/ppermute | solution.py:32
  6.4 5.0 %collective-permute-start.1 = (bf16[2,4,32,96]{3,2,0,1:T(8,128)(2,1)S(1)}, bf16[2,4,32,96]{3,2,0,1:T(8,128)(2,1)S(1)}, u32[]{:S(2)}, u32[]{:S(2)}) collective-permute-start(bf16[2,4,32,96]{3,2,0,1:T(8,128)(2,1)S(1)} %copy.24), channel_id=1, source_target_pairs={{32,0},{64,32},{96,64},{128,96},{160,128},{192,160},{224,192},{256... | collective-permute-start | bytes 147464 | tf_op jit(solution)/shard_map/ppermute | solution.py:32
  11.5 8.7 %collective-permute-start.2 = (bf16[4,48,192]{2,1,0:T(8,128)(2,1)S(1)}, bf16[4,48,192]{2,1,0:T(8,128)(2,1)S(1)}, u32[]{:S(2)}, u32[]{:S(2)}) collective-permute-start(bf16[4,48,192]{2,1,0:T(8,128)(2,1)S(1)} %maximum_maximum_fusion), channel_id=1, source_target_pairs={{0,1},{1,2},{2,3},{3,4},{4,5},{5,6},{6,7},{7,8},{8,9},{9,10},{10,1... | collective-permute-start | bytes 221192 | tf_op jit(solution)/shard_map/ppermute | solution.py:32
  16.7 5.9 %collective-permute-start.3 = (bf16[4,48,192]{2,1,0:T(8,128)(2,1)S(1)}, bf16[4,48,192]{2,1,0:T(8,128)(2,1)S(1)}, u32[]{:S(2)}, u32[]{:S(2)}) collective-permute-start(bf16[4,48,192]{2,1,0:T(8,128)(2,1)S(1)} %maximum_maximum_fusion.1), channel_id=1, source_target_pairs={{1,0},{2,1},{3,2},{4,3},{5,4},{6,5},{7,6},{8,7},{9,8},{10,9},{11,1... | collective-permute-start | bytes 221192 | tf_op jit(solution)/shard_map/ppermute | solution.py:32
  22.6 1.3 copy-start
  23.9 0.8 copy-start.2
  26.2 18.5 %all-to-all-start = ((f32[32,2,96]{2,1,0:T(2,128)}), f32[32,2,96]{2,1,0:T(2,128)S(1)}, u32[]{:S(2)}, u32[]{:S(2)}) async-start(f32[32,2,96]{2,1,0:T(2,128)} %get-tuple-element.34), calls=%async_computation | async-start | bytes 65536 | tf_op jit(solution)/shard_map/all_to_all | solution.py:404
  37.1 34.0 %copy-start.5 = (f32[96]{0:T(128)S(1)}, f32[96]{0:T(128)}, u32[]{:S(2)}) copy-start(f32[96]{0:T(128)} %param.10) | copy-start | bytes 1156
  37.1 34.0 %copy-start.6 = (f32[96]{0:T(128)S(1)}, f32[96]{0:T(128)}, u32[]{:S(2)}) copy-start(f32[96]{0:T(128)} %param.11) | copy-start | bytes 1156
  45.4 25.8 %all-to-all-start.1 = ((f32[16,2,96]{2,1,0:T(2,128)}), f32[16,2,96]{2,1,0:T(2,128)S(1)}, u32[]{:S(2)}, u32[]{:S(2)}) async-start(f32[16,2,96]{2,1,0:T(2,128)} %broadcast_in_dim.16), calls=%async_computation.1 | async-start | bytes 32768 | tf_op jit(solution)/shard_map/all_to_all | solution.py:404
  72.6 15.7 %collective-permute-start.4 = (bf16[2,6,32,96]{3,2,1,0:T(8,128)(2,1)S(1)}, bf16[2,6,32,96]{3,2,1,0:T(8,128)(2,1)S(1)}, u32[]{:S(2)}, u32[]{:S(2)}) collective-permute-start(bf16[2,6,32,96]{3,2,1,0:T(8,128)(2,1)S(1)} %get-tuple-element.43.hidden), channel_id=1, source_target_pairs={{0,32},{32,64},{64,96},{96,128},{128,160},{160,192},{192,224},{224... | collective-permute-start | bytes 221192 | tf_op jit(solution)/shard_map/ppermute | solution.py:32
  74.9 13.4 %all-to-all-start.2 = ((f32[16,2,96]{2,1,0:T(2,128)}), f32[16,2,96]{2,1,0:T(2,128)S(1)}, u32[]{:S(2)}, u32[]{:S(2)}) async-start(f32[16,2,96]{2,1,0:T(2,128)} %get-tuple-element.42), calls=%async_computation.2 | async-start | bytes 32768 | tf_op jit(solution)/shard_map/all_to_all | solution.py:404
  88.9 12.6 %all-to-all-start.3 = ((f32[32,2,96]{2,1,0:T(2,128)}), f32[32,2,96]{2,1,0:T(2,128)S(1)}, u32[]{:S(2)}, u32[]{:S(2)}) async-start(f32[32,2,96]{2,1,0:T(2,128)} %broadcast_in_dim.37), calls=%async_computation.3 | async-start | bytes 65536 | tf_op jit(solution)/shard_map/all_to_all | solution.py:404
  92.9 8.6 %copy-start.3 = (bf16[2,2,16,192]{3,2,1,0:T(8,128)(2,1)S(1)}, bf16[2,2,16,192]{3,2,1,0:T(8,128)(2,1)}, u32[]{:S(2)}) copy-start(bf16[2,2,16,192]{3,2,1,0:T(8,128)(2,1)} %features.3) | copy-start | bytes 73732
  102.7 5.3 %collective-permute-start.5 = (bf16[3072,128]{1,0:T(8,128)(2,1)S(1)}, bf16[3072,128]{1,0:T(8,128)(2,1)S(1)}, u32[]{:S(2)}, u32[]{:S(2)}) collective-permute-start(bf16[3072,128]{1,0:T(8,128)(2,1)S(1)} %get-tuple-element.54), channel_id=1, source_target_pairs={{0,1},{1,0},{2,3},{3,2},{4,5},{5,4},{6,7},{7,6},{8,9},{9,8},{10,11... | collective-permute-start | bytes 2359304 | tf_op jit(solution)/shard_map/ppermute | solution.py:444
  109.0 15.5 %all-to-all-start.4 = ((bf16[4,768,128]{2,1,0:T(8,128)(2,1)}), bf16[4,768,128]{2,1,0:T(8,128)(2,1)S(1)}, u32[]{:S(2)}, u32[]{:S(2)}) async-start(bf16[4,768,128]{2,1,0:T(8,128)(2,1)} %bitcast.18), calls=%async_computation.4 | async-start | bytes 1572864 | tf_op jit(solution)/shard_map/all_to_all | solution.py:404
  112.5 17.6 %copy-start.1 = (bf16[3,3,3,192,96]{4,3,2,1,0:T(8,128)(2,1)S(1)}, bf16[3,3,3,192,96]{4,3,2,1,0:T(8,128)(2,1)}, u32[]{:S(2)}) copy-start(bf16[3,3,3,192,96]{4,3,2,1,0:T(8,128)(2,1)} %weight.5) | copy-start | bytes 2985988
  112.5 12.1 %collective-permute-start.6 = (bf16[2,6,32,96]{3,2,1,0:T(8,128)(2,1)S(1)}, bf16[2,6,32,96]{3,2,1,0:T(8,128)(2,1)S(1)}, u32[]{:S(2)}, u32[]{:S(2)}) collective-permute-start(bf16[2,6,32,96]{3,2,1,0:T(8,128)(2,1)S(1)} %get-tuple-element.57), channel_id=1, source_target_pairs={{32,0},{64,32},{96,64},{128,96},{160,128},{192,160},{224,192},{256... | collective-permute-start | bytes 221192 | tf_op jit(solution)/shard_map/ppermute | solution.py:32
  125.4 21.4 %all-to-all-start.5 = ((f32[64,12,128]{2,1,0:T(8,128)}), f32[64,12,128]{2,1,0:T(8,128)S(1)}, u32[]{:S(2)}, u32[]{:S(2)}) async-start(f32[64,12,128]{2,1,0:T(8,128)} %reshape.29), calls=%async_computation.5 | async-start | bytes 1048576 | tf_op jit(solution)/shard_map/all_to_all | solution.py:404
  177.4 8.7 %collective-permute-start.7 = (bf16[3072,128]{1,0:T(8,128)(2,1)S(1)}, bf16[3072,128]{1,0:T(8,128)(2,1)S(1)}, u32[]{:S(2)}, u32[]{:S(2)}) collective-permute-start(bf16[3072,128]{1,0:T(8,128)(2,1)S(1)} %bitcast.39), channel_id=1, source_target_pairs={{0,1},{1,0},{2,3},{3,2},{4,5},{5,4},{6,7},{7,6},{8,9},{9,8},{10,11... | collective-permute-start | bytes 2359304 | tf_op jit(solution)/shard_map/ppermute | solution.py:455

commit v4 on v3

--- a/solution.py
+++ b/solution.py
@@ -64,6 +64,42 @@
     last = field.shape[1] - 1
     out = ((row == 0) & (where[1] == 1)) | ((row == last) & (where[2] == 1))
     return jnp.where(out, 0.0, field)
+
+
+def edges_kernel(cache, features, cot, later, downward, upward):
+    cells, rows = features.shape[1], cot.shape[1]
+    half = features.shape[2]
+    for out, cell, row in ((downward, cells - 1, rows - 2), (upward, 0, 0)):
+        out[:, :half] = jnp.concatenate([cache[:, cell], features[:, cell]], 0)
+        pair = [jnp.concatenate([cot[:, k], later[:, k]], 0) for k in (row, row + 1)]
+        out[:, half:] = jnp.concatenate(pair, 2)
+
+
+def edges(cache, features, cot, later):
+    frames, _, half, ins = features.shape
+    shape = jax.ShapeDtypeStruct((2 * frames, half + cot.shape[2], ins), jnp.bfloat16)
+    return pl.pallas_call(
+        edges_kernel,
+        out_shape=(shape, shape),
+        in_specs=whole(4),
+        out_specs=whole(2),
+        compiler_params=pltpu.CompilerParams(vmem_limit_bytes=VMEM_LIMIT),
+        name="edges",
+    )(cache, features, cot, later)
+
+
+def relay_kernel(came, out):
+    out[...] = jnp.broadcast_to(jnp.sum(came[...], 0, keepdims=True), out.shape)
+
+
+def relay(came, copies):
+    return pl.pallas_call(
+        relay_kernel,
+        out_shape=jax.ShapeDtypeStruct((copies,) + came.shape[1:], came.dtype),
+        in_specs=whole(1),
+        out_specs=whole()[0],
+        name="relay",
+    )(came)
 
 
 def conv_one_kernel(cache, features, above, below, weight, pre_norm, sums, wide):
@@ -311,40 +347,43 @@
     )(where, cache, features, above, below, came, grad_normed, normed, rstd, two)
 
 
-def unpack_kernel(scale, where, mine_one, other_one, mine_two, other_two, one, two):
-    lower = where[0] == 0
-    for mine, other, out in ((mine_one, other_one, one), (mine_two, other_two, two)):
+def unpack_kernel(scale, half, part_one, part_two, *rest):
+    one, two = rest[-2:]
+    for part, out in ((part_one, one), (part_two, two)):
         taps, rows, outs = out.shape
-        half = rows // 2
-        own = jnp.concatenate([mine[half * j : half * j + half] for j in range(7)], 1)
-        far = jnp.concatenate([other[half * j : half * j + half] for j in range(7)], 1)
-        own, far = own.astype(jnp.float32) * scale, far.astype(jnp.float32) * scale
-        low, high = jnp.where(lower, own, far), jnp.where(lower, far, own)
+        lanes = jnp.concatenate([part[rows * j : rows * j + rows] for j in range(7)], 1)
+        lanes = lanes.astype(jnp.float32) * scale
         for k in range(taps):
-            out[k, :half] = low[:, outs * k : outs * k + outs]
-            out[k, half:] = high[:, outs * k : outs * k + outs]
-
-
-def unpack(where, mine, other, ins, mids, scale):
+            out[k] = lanes[:, outs * k : outs * k + outs]
+
+
+def unpack(half, part, ins, mids, scale, begun=()):
     half_one, half_two = 7 * ins // 2, 7 * mids // 2
     skip = 3 * half_one // half_two
-    block_one = pl.BlockSpec((half_one, 128), lambda a: (a, 0))
-    block_two = pl.BlockSpec((half_two, 128), lambda a: (a + skip, 0))
     return pl.pallas_call(
         functools.partial(unpack_kernel, scale),
-        grid=(3,),
+        grid_spec=pltpu.PrefetchScalarGridSpec(
+            num_scalar_prefetch=1,
+            grid=(3,),
+            in_specs=[
+                pl.BlockSpec((half_one, 128), lambda a, half: (a, 0)),
+                pl.BlockSpec((half_two, 128), lambda a, half: (a + skip, 0)),
+            ]
+            + whole(len(begun), pl.ANY),
+            out_specs=[
+                pl.BlockSpec((9, ins // 2, mids), lambda a, half: (a, half[0], 0)),
+                pl.BlockSpec((9, mids // 2, mids), lambda a, half: (a, half[0], 0)),
+            ],
+        ),
         out_shape=(
             jax.ShapeDtypeStruct((27, ins, mids), jnp.float32),
             jax.ShapeDtypeStruct((27, mids, mids), jnp.float32),
         ),
-        in_specs=[pl.BlockSpec(memory_space=pltpu.SMEM), block_one, block_one, block_two, block_two],
-        out_specs=[
-            pl.BlockSpec((9, ins, mids), lambda a: (a, 0, 0)),
-            pl.BlockSpec((9, mids, mids), lambda a: (a, 0, 0)),
-        ],
-        compiler_params=pltpu.CompilerParams(vmem_limit_bytes=VMEM_LIMIT),
+        input_output_aliases={3 + k: k for k in range(len(begun))},
+        compiler_params=pltpu.CompilerParams(vmem_limit_bytes=VMEM_LIMIT),
+        cost_estimate=pl.CostEstimate(flops=2**20, bytes_accessed=2**22, transcendentals=0),
         name="unpack",
-    )(where, mine, other, mine, other)
+    )(half, part, part, *begun)
 
 
 def feature_grads_kernel(grad_pre, weight, out, wide):
@@ -409,28 +448,24 @@
     cache = neighbour(features, TM, 1)
     later = neighbour(cotangent, TM, -1)
 
-    def edge(cell_row, cot_row):
-        feature = jnp.concatenate([cache[:, cell_row], features[:, cell_row]], 0)
-        pair = [jnp.concatenate([cotangent[:, k], later[:, k]], 0) for k in (cot_row, cot_row + 1)]
-        return jnp.concatenate([feature, jnp.concatenate(pair, -1)], 1)
-
-    above = neighbour(edge(-1, rows - 2), HEIGHT, 1)
-    below = neighbour(edge(0, 0), HEIGHT, -1)
+    downward, upward = edges(cache, features, cotangent, later)
+    above = neighbour(downward, HEIGHT, 1)
+    below = neighbour(upward, HEIGHT, -1)
     pre_norm, sums = conv_one(cache, features, above, below, weight_one, height)
     came = exchange(sums, HEIGHT)
     grad_hidden, shifted_cot = hidden_grads(cotangent, later, above, below, weight_two)
-    sums, grad_hidden, shifted_cot = barrier((came.sum(0), grad_hidden, shifted_cot))
-    came = exchange(spread(sums, lax.axis_size(TM)), TM)
+    came, grad_hidden, shifted_cot = barrier((came, grad_hidden, shifted_cot))
+    came = exchange(relay(came, lax.axis_size(TM)), TM)
     pair, others = ("y", "c"), ("zh", "zl", "x")
     hidden, grad_normed, normed, rstd, sums = middle(
         count, where, came, pre_norm, grad_hidden, norm_gain, norm_shift, lax.axis_size(pair)
     )
     sums, hidden = barrier((sums, hidden))
-    sums = exchange(sums, pair).sum(0)
+    came = exchange(sums, pair)
     local_two = second_weight(hidden, shifted_cot)
     before = neighbour(hidden, TM, 1)
-    sums, local_two, before = barrier((sums, local_two, before))
-    came = exchange(spread(sums, lax.axis_size(others)), others)
+    came, local_two, before = barrier((came, local_two, before))
+    came = exchange(relay(came, lax.axis_size(others)), others)
     decoded = conv(
         jnp.pad(jnp.concatenate([before, hidden], 0), ((0, 0), (0, 0), (1, 1), (0, 0))), weight_two
     ).astype(jnp.bfloat16)
@@ -444,15 +479,18 @@
     part = kept + lax.ppermute(away, "c", SWAP).astype(jnp.float32)
     part = part.astype(jnp.bfloat16).reshape(xs, -1, 128)
     part, grad_pre = barrier((part, grad_pre))
-    part = exchange(part, "x").astype(jnp.float32).sum(0)
+    part = exchange(part, "x").astype(jnp.float32).sum(0).astype(jnp.bfloat16)
     after = neighbour(grad_pre, TM, -1)
     part, after = barrier((part, after))
-    part = exchange(part.reshape(rest, -1, 128), REST).sum(0).astype(jnp.bfloat16)
+    part = exchange(part.reshape(rest, -1, 128), REST).astype(jnp.float32).sum(0).astype(jnp.bfloat16)
     grad_features = feature_grads(jnp.concatenate([grad_pre, after], 0), weight_one, features.shape)
     part, grad_features = barrier((part, grad_features))
     part = exchange(spread(part, rest), REST).reshape(-1, 128)
     part = exchange(spread(part, xs), "x").reshape(-1, 128)
-    grad_one, grad_two = unpack(where, part, lax.ppermute(part, "c", SWAP), ins, mids, scale)
+    other = lax.ppermute(part, "c", SWAP)
+    core = where[:1]
+    begun = unpack(core, part, ins, mids, scale)
+    grad_one, grad_two = unpack(1 - core, other, ins, mids, scale, begun)
     return decoded, grad_features, grad_one.reshape(weight_one.shape), grad_two.reshape(weight_two.shape)
 
 

time: 191 us -> 187 us (0.979)
  waiting for transfers between devices: 65.1 us -> 56.5 us
  Pallas kernels: 10.8 us -> 14.6 us
  starting transfers between devices: 71 us -> 74.7 us
    all_to_all x6, waiting for transfers between devices: 56.6 us -> 52.4 us  [exchange(): return lax.all_to_all(copies, axes, 0, 0)]
    pallas_call x1 -> x5, Pallas kernels: 3.43 us -> 7.24 us  [the longest x2 4.4 us: unpack(): pl.pallas_call(functools.partial(unpack_kernel, scale), grid_spec=pltpu.P...]
    ppermute x6, starting transfers between devices: 17.4 us -> 20.1 us  [neighbour(): lax.ppermute(value, axis, [(i, i + steps) for i in range(first, last)])]
    ppermute x6, waiting for transfers between devices: 4.69 us -> 2.23 us  [neighbour(): lax.ppermute(value, axis, [(i, i + steps) for i in range(first, last)])]
    unnamed x19 -> x25, local copies, waits for them, and re-layouts: 4.43 us -> 5.57 us
  transfers between devices with their start and end apart: 14 -> 14, of which waited for: 10 -> 9; matrix products, arithmetic and copies ran while one was open for 3% -> 1% of each run, Pallas kernels for 2% -> 3%
where the time goes in v4:
time: 187 us; the launch traced here: 186 us
  starting transfers between devices  74.7 us (40%)
  waiting for transfers between devices  56.5 us (30%)
  blocking collectives  29.3 us (16%)
  Pallas kernels  14.6 us (8%)
  local copies, waits for them, and re-layouts  6.5 us (3%)
    all_to_all x6, waiting for transfers between devices, exchange(): return lax.all_to_all(copies, axes, 0, 0)  52.4 us
    all_to_all x6, starting transfers between devices, exchange(): return lax.all_to_all(copies, axes, 0, 0)  44.4 us
    all_to_all x2, blocking collectives, exchange(): return lax.all_to_all(copies, axes, 0, 0)  29.3 us
    ppermute x6, starting transfers between devices, neighbour(): lax.ppermute(value, axis, [(i, i + steps) for i in range(first, last)])  20.1 us
    ppermute x1, starting transfers between devices, body(): other = lax.ppermute(part, 'c', SWAP)  6.77 us
    unnamed x25, local copies, waits for them, and re-layouts  5.57 us
    pallas_call x2, Pallas kernels, unpack(): pl.pallas_call(functools.partial(unpack_kernel, scale), grid_spec=pltpu.P...  4.4 us
  transfers between devices with their start and end apart: 14, of which 9 were waited for; matrix products, arithmetic and copies ran while one was open for 1% of the time, Pallas kernels for 3%

profile of v4, /device:TPU:1, one launch (start us, length us, event | category | flops | bytes accessed | tf_op | source)
XLA Modules:
  0.0 185.6 jit_solution(11045072612865133998)
XLA Ops:
  1.9 4.7 %collective-permute-start = (bf16[2,2,16,192]{3,2,1,0:T(8,128)(2,1)}, bf16[2,2,16,192]{3,2,1,0:T(8,128)(2,1)S(1)}, u32[]{:S(2)}, u32[]{:S(2)}) collective-permute-start(bf16[2,2,16,192]{3,2,1,0:T(8,128)(2,1)} %features.5), channel_id=1, source_target_pairs={{0,32},{32,64},{64,96},{96,128},{128,160},{160,192},{192,224},{224... | collective-permute-start | bytes 73736 | tf_op jit(solution)/shard_map/ppermute | solution.py:32
  6.6 1.3 collective-permute-done.cache
  9.6 5.0 %collective-permute-start.2 = (bf16[4,48,192]{2,1,0:T(8,128)(2,1)S(1)}, bf16[4,48,192]{2,1,0:T(8,128)(2,1)S(1)}, u32[]{:S(2)}, u32[]{:S(2)}) collective-permute-start(bf16[4,48,192]{2,1,0:T(8,128)(2,1)S(1)} %get-tuple-element.38), channel_id=1, source_target_pairs={{0,1},{1,2},{2,3},{3,4},{4,5},{5,6},{6,7},{7,8},{8,9},{9,10},{10,1... | collective-permute-start | bytes 221192 | tf_op jit(solution)/shard_map/ppermute | solution.py:32
  14.6 5.6 %collective-permute-start.3 = (bf16[4,48,192]{2,1,0:T(8,128)(2,1)S(1)}, bf16[4,48,192]{2,1,0:T(8,128)(2,1)S(1)}, u32[]{:S(2)}, u32[]{:S(2)}) collective-permute-start(bf16[4,48,192]{2,1,0:T(8,128)(2,1)S(1)} %get-tuple-element.39), channel_id=1, source_target_pairs={{1,0},{2,1},{3,2},{4,3},{5,4},{6,5},{7,6},{8,7},{9,8},{10,9},{11,1... | collective-permute-start | bytes 221192 | tf_op jit(solution)/shard_map/ppermute | solution.py:32
  21.1 1.3 copy-done
  23.2 1.5 conv_one.1
  24.7 10.3 %all-to-all-start = ((f32[32,2,96]{2,1,0:T(2,128)}), f32[32,2,96]{2,1,0:T(2,128)S(1)}, u32[]{:S(2)}, u32[]{:S(2)}) async-start(f32[32,2,96]{2,1,0:T(2,128)} %get-tuple-element.40), calls=%async_computation | async-start | bytes 65536 | tf_op jit(solution)/shard_map/all_to_all | solution.py:443
  36.0 6.6 %all-to-all-done.came = f32[32,2,96]{2,1,0:T(2,128)S(1)} async-done(((f32[32,2,96]{2,1,0:T(2,128)}), f32[32,2,96]{2,1,0:T(2,128)S(1)}, u32[]{:S(2)}, u32[]{:S(2)}) %all-to-all-start) | async-done | bytes 24608 | tf_op jit(solution)/shard_map/all_to_all | solution.py:443
  43.2 1.4 relay.2
  44.6 16.1 %all-to-all-start.1 = ((f32[16,2,96]{2,1,0:T(2,128)}), f32[16,2,96]{2,1,0:T(2,128)S(1)}, u32[]{:S(2)}, u32[]{:S(2)}) async-start(f32[16,2,96]{2,1,0:T(2,128)} %relay.2), calls=%async_computation.1 | async-start | bytes 32768 | tf_op jit(solution)/shard_map/all_to_all | solution.py:443
  60.9 11.2 %all-to-all-done.1.came = f32[16,2,96]{2,1,0:T(2,128)S(1)} async-done(((f32[16,2,96]{2,1,0:T(2,128)}), f32[16,2,96]{2,1,0:T(2,128)S(1)}, u32[]{:S(2)}, u32[]{:S(2)}) %all-to-all-start.1) | async-done | bytes 12320 | tf_op jit(solution)/shard_map/all_to_all | solution.py:443
  72.0 1.5 middle.1
  73.5 2.2 %collective-permute-start.4 = (bf16[2,6,32,96]{3,2,1,0:T(8,128)(2,1)S(1)}, bf16[2,6,32,96]{3,2,1,0:T(8,128)(2,1)S(1)}, u32[]{:S(2)}, u32[]{:S(2)}) collective-permute-start(bf16[2,6,32,96]{3,2,1,0:T(8,128)(2,1)S(1)} %get-tuple-element.49.hidden), channel_id=1, source_target_pairs={{0,32},{32,64},{64,96},{96,128},{128,160},{160,192},{192,224},{224... | collective-permute-start | bytes 221192 | tf_op jit(solution)/shard_map/ppermute | solution.py:32
  75.8 6.1 %all-to-all-start.2 = ((f32[16,2,96]{2,1,0:T(2,128)}), f32[16,2,96]{2,1,0:T(2,128)S(1)}, u32[]{:S(2)}, u32[]{:S(2)}) async-start(f32[16,2,96]{2,1,0:T(2,128)} %get-tuple-element.48), calls=%async_computation.2 | async-start | bytes 32768 | tf_op jit(solution)/shard_map/all_to_all | solution.py:443
  82.4 6.7 %all-to-all-done.2.came = f32[16,2,96]{2,1,0:T(2,128)S(1)} async-done(((f32[16,2,96]{2,1,0:T(2,128)}), f32[16,2,96]{2,1,0:T(2,128)S(1)}, u32[]{:S(2)}, u32[]{:S(2)}) %all-to-all-start.2) | async-done | bytes 12320 | tf_op jit(solution)/shard_map/all_to_all | solution.py:443
  89.8 1.4 relay.3
  91.1 3.9 %all-to-all-start.3 = ((f32[32,2,96]{2,1,0:T(2,128)}), f32[32,2,96]{2,1,0:T(2,128)S(1)}, u32[]{:S(2)}, u32[]{:S(2)}) async-start(f32[32,2,96]{2,1,0:T(2,128)} %relay.3), calls=%async_computation.3 | async-start | bytes 65536 | tf_op jit(solution)/shard_map/all_to_all | solution.py:443
  95.1 1.5 convolution_convert_fusion
  97.2 6.5 %all-to-all-done.3.came = f32[32,2,96]{2,1,0:T(2,128)S(1)} async-done(((f32[32,2,96]{2,1,0:T(2,128)}), f32[32,2,96]{2,1,0:T(2,128)S(1)}, u32[]{:S(2)}, u32[]{:S(2)}) %all-to-all-start.3) | async-done | bytes 24608 | tf_op jit(solution)/shard_map/all_to_all | solution.py:443
  104.9 3.4 %collective-permute-start.5 = (bf16[3072,128]{1,0:T(8,128)(2,1)S(1)}, bf16[3072,128]{1,0:T(8,128)(2,1)S(1)}, u32[]{:S(2)}, u32[]{:S(2)}) collective-permute-start(bf16[3072,128]{1,0:T(8,128)(2,1)S(1)} %get-tuple-element.60), channel_id=1, source_target_pairs={{0,1},{1,0},{2,3},{3,2},{4,5},{5,4},{6,7},{7,6},{8,9},{9,8},{10,11... | collective-permute-start | bytes 2359304 | tf_op jit(solution)/shard_map/ppermute | solution.py:479
  108.2 1.9 %collective-permute-done.5 = bf16[3072,128]{1,0:T(8,128)(2,1)S(1)} collective-permute-done((bf16[3072,128]{1,0:T(8,128)(2,1)S(1)}, bf16[3072,128]{1,0:T(8,128)(2,1)S(1)}, u32[]{:S(2)}, u32[]{:S(2)}) %collective-permute-start.5) | collective-permute-done | bytes 786464 | tf_op jit(solution)/shard_map/ppermute | solution.py:479
  111.2 3.5 %all-to-all-start.4 = ((bf16[4,768,128]{2,1,0:T(8,128)(2,1)}), bf16[4,768,128]{2,1,0:T(8,128)(2,1)S(1)}, u32[]{:S(2)}, u32[]{:S(2)}) async-start(bf16[4,768,128]{2,1,0:T(8,128)(2,1)} %bitcast.6), calls=%async_computation.4 | async-start | bytes 1572864 | tf_op jit(solution)/shard_map/all_to_all | solution.py:443
  114.7 1.4 collective-permute-start.6
  116.1 10.6 %all-to-all-done.4 = bf16[4,768,128]{2,1,0:T(8,128)(2,1)S(1)} async-done(((bf16[4,768,128]{2,1,0:T(8,128)(2,1)}), bf16[4,768,128]{2,1,0:T(8,128)(2,1)S(1)}, u32[]{:S(2)}, u32[]{:S(2)}) %all-to-all-start.4) | async-done | bytes 786464 | tf_op jit(solution)/shard_map/all_to_all | solution.py:443
  127.6 4.6 %all-to-all-start.5 = ((bf16[64,12,128]{2,1,0:T(8,128)(2,1)}), bf16[64,12,128]{2,1,0:T(8,128)(2,1)S(1)}, u32[]{:S(2)}, u32[]{:S(2)}) async-start(bf16[64,12,128]{2,1,0:T(8,128)(2,1)} %reshape.27), calls=%async_computation.5 | async-start | bytes 524288 | tf_op jit(solution)/shard_map/all_to_all | solution.py:443
  132.3 1.6 feature_grads.1
  134.0 10.8 %all-to-all-done.5 = bf16[64,12,128]{2,1,0:T(8,128)(2,1)S(1)} async-done(((bf16[64,12,128]{2,1,0:T(8,128)(2,1)}), bf16[64,12,128]{2,1,0:T(8,128)(2,1)S(1)}, u32[]{:S(2)}, u32[]{:S(2)}) %all-to-all-start.5) | async-done | bytes 196640 | tf_op jit(solution)/shard_map/all_to_all | solution.py:443
  144.9 18.5 %all_to_all.40 = bf16[64,12,128]{2,1,0:T(8,128)(2,1)S(1)} all-to-all(bf16[64,12,128]{2,1,0:T(8,128)(2,1)S(1)} %broadcast_in_dim.25), channel_id=1, replica_groups=mesh['zh'=2,'y'=8,'zl'=4,'x'=4,'c'=2] {'zh','y','zl'}, dimensions={0} | all-to-all | bytes 393216 | tf_op jit(solution)/shard_map/all_to_all | solution.py:443
  163.6 10.8 %all_to_all.41 = bf16[4,768,128]{2,1,0:T(8,128)(2,1)S(1)} all-to-all(bf16[4,768,128]{2,1,0:T(8,128)(2,1)S(1)} %broadcast_in_dim.27), channel_id=1, replica_groups=mesh['zh'=2,'y'=8,'zl'=4,'x'=4,'c'=2] {'x'}, dimensions={0} | all-to-all | bytes 1572864 | tf_op jit(solution)/shard_map/all_to_all | solution.py:443
  174.4 6.8 %collective-permute-start.7 = (bf16[3072,128]{1,0:T(8,128)(2,1)S(1)}, bf16[3072,128]{1,0:T(8,128)(2,1)S(1)}, u32[]{:S(2)}, u32[]{:S(2)}) collective-permute-start(bf16[3072,128]{1,0:T(8,128)(2,1)S(1)} %bitcast.15), channel_id=1, source_target_pairs={{0,1},{1,0},{2,3},{3,2},{4,5},{5,4},{6,7},{7,6},{8,9},{9,8},{10,11... | collective-permute-start | bytes 2359304 | tf_op jit(solution)/shard_map/ppermute | solution.py:490
  181.2 2.2 %unpack.2 = (f32[27,192,96]{2,1,0:T(8,128)}, f32[27,96,96]{2,1,0:T(8,128)}) custom-call(s32[1]{0:T(128)} %bitcast.half, bf16[3072,128]{1,0:T(8,128)(2,1)S(1)} %bitcast.16, bf16[3072,128]{1,0:T(8,128)(2,1)S(1)} %bitcast.17), custom_call_target="tpu_custom_call" | custom-call | flops 1048576 | bytes 4194304 | tf_op jit(solution)/shard_map/unpack/pallas_call | solution.py:363
  183.4 2.2 %unpack.3 = (f32[27,192,96]{2,1,0:T(8,128)}, f32[27,96,96]{2,1,0:T(8,128)}) custom-call(s32[1]{0:T(128)S(6)} %sub.3.half, bf16[3072,128]{1,0:T(8,128)(2,1)S(1)} %collective-permute-done.7.part_one.part_two, bf16[3072,128]{1,0:T(8,128)(2,1)S(1)} %collective-permute-done.7.part_one.part_two, ...), custom_call_target="tpu_custom_call", output_to_operand_aliasing={{0}: (3, {}), {1}: (4, {})} | custom-call | flops 1048576 | bytes 4194304 | tf_op jit(solution)/shard_map/unpack/pallas_call | solution.py:363
  (45 shorter events, 11.7 us)
Async XLA Ops:
  0.6 7.3 %collective-permute-start.1 = (bf16[2,4,32,96]{3,2,1,0:T(8,128)(2,1)}, bf16[2,4,32,96]{3,2,1,0:T(8,128)(2,1)S(1)}, u32[]{:S(2)}, u32[]{:S(2)}) collective-permute-start(bf16[2,4,32,96]{3,2,1,0:T(8,128)(2,1)} %cot.3), channel_id=1, source_target_pairs={{32,0},{64,32},{96,64},{128,96},{160,128},{192,160},{224,192},{256... | collective-permute-start | bytes 147464 | tf_op jit(solution)/shard_map/ppermute | solution.py:32
  1.9 6.0 %collective-permute-start = (bf16[2,2,16,192]{3,2,1,0:T(8,128)(2,1)}, bf16[2,2,16,192]{3,2,1,0:T(8,128)(2,1)S(1)}, u32[]{:S(2)}, u32[]{:S(2)}) collective-permute-start(bf16[2,2,16,192]{3,2,1,0:T(8,128)(2,1)} %features.5), channel_id=1, source_target_pairs={{0,32},{32,64},{64,96},{96,128},{128,160},{160,192},{192,224},{224... | collective-permute-start | bytes 73736 | tf_op jit(solution)/shard_map/ppermute | solution.py:32
  7.9 0.8 copy-start.2
  8.7 0.8 copy-start.5
  9.5 25.5 %copy-start.6 = (bf16[2,4,32,96]{3,2,1,0:T(8,128)(2,1)S(1)}, bf16[2,4,32,96]{3,2,1,0:T(8,128)(2,1)}, u32[]{:S(2)}) copy-start(bf16[2,4,32,96]{3,2,1,0:T(8,128)(2,1)} %cot.3) | copy-start | bytes 147460
  9.6 10.6 %collective-permute-start.2 = (bf16[4,48,192]{2,1,0:T(8,128)(2,1)S(1)}, bf16[4,48,192]{2,1,0:T(8,128)(2,1)S(1)}, u32[]{:S(2)}, u32[]{:S(2)}) collective-permute-start(bf16[4,48,192]{2,1,0:T(8,128)(2,1)S(1)} %get-tuple-element.38), channel_id=1, source_target_pairs={{0,1},{1,2},{2,3},{3,4},{4,5},{5,6},{6,7},{7,8},{8,9},{9,10},{10,1... | collective-permute-start | bytes 221192 | tf_op jit(solution)/shard_map/ppermute | solution.py:32
  14.6 6.5 %collective-permute-start.3 = (bf16[4,48,192]{2,1,0:T(8,128)(2,1)S(1)}, bf16[4,48,192]{2,1,0:T(8,128)(2,1)S(1)}, u32[]{:S(2)}, u32[]{:S(2)}) collective-permute-start(bf16[4,48,192]{2,1,0:T(8,128)(2,1)S(1)} %get-tuple-element.39), channel_id=1, source_target_pairs={{1,0},{2,1},{3,2},{4,3},{5,4},{6,5},{7,6},{8,7},{9,8},{10,9},{11,1... | collective-permute-start | bytes 221192 | tf_op jit(solution)/shard_map/ppermute | solution.py:32
  21.1 1.3 copy-start
  22.4 0.8 copy-start.3
  23.2 11.8 %copy-start.9 = (bf16[3,3,3,96,96]{4,3,2,1,0:T(8,128)(2,1)S(1)}, bf16[3,3,3,96,96]{4,3,2,1,0:T(8,128)(2,1)}, u32[]{:S(2)}) copy-start(bf16[3,3,3,96,96]{4,3,2,1,0:T(8,128)(2,1)} %weight.4) | copy-start | bytes 1492996
  24.7 17.9 %all-to-all-start = ((f32[32,2,96]{2,1,0:T(2,128)}), f32[32,2,96]{2,1,0:T(2,128)S(1)}, u32[]{:S(2)}, u32[]{:S(2)}) async-start(f32[32,2,96]{2,1,0:T(2,128)} %get-tuple-element.40), calls=%async_computation | async-start | bytes 65536 | tf_op jit(solution)/shard_map/all_to_all | solution.py:443
  35.0 37.0 %copy-start.7 = (f32[96]{0:T(128)S(1)}, f32[96]{0:T(128)}, u32[]{:S(2)}) copy-start(f32[96]{0:T(128)} %param.10) | copy-start | bytes 1156
  35.0 37.0 %copy-start.8 = (f32[96]{0:T(128)S(1)}, f32[96]{0:T(128)}, u32[]{:S(2)}) copy-start(f32[96]{0:T(128)} %param.11) | copy-start | bytes 1156
  42.6 0.6 copy-start.10
  44.6 27.4 %all-to-all-start.1 = ((f32[16,2,96]{2,1,0:T(2,128)}), f32[16,2,96]{2,1,0:T(2,128)S(1)}, u32[]{:S(2)}, u32[]{:S(2)}) async-start(f32[16,2,96]{2,1,0:T(2,128)} %relay.2), calls=%async_computation.1 | async-start | bytes 32768 | tf_op jit(solution)/shard_map/all_to_all | solution.py:443
  73.5 15.6 %collective-permute-start.4 = (bf16[2,6,32,96]{3,2,1,0:T(8,128)(2,1)S(1)}, bf16[2,6,32,96]{3,2,1,0:T(8,128)(2,1)S(1)}, u32[]{:S(2)}, u32[]{:S(2)}) collective-permute-start(bf16[2,6,32,96]{3,2,1,0:T(8,128)(2,1)S(1)} %get-tuple-element.49.hidden), channel_id=1, source_target_pairs={{0,32},{32,64},{64,96},{96,128},{128,160},{160,192},{192,224},{224... | collective-permute-start | bytes 221192 | tf_op jit(solution)/shard_map/ppermute | solution.py:32
  75.8 13.4 %all-to-all-start.2 = ((f32[16,2,96]{2,1,0:T(2,128)}), f32[16,2,96]{2,1,0:T(2,128)S(1)}, u32[]{:S(2)}, u32[]{:S(2)}) async-start(f32[16,2,96]{2,1,0:T(2,128)} %get-tuple-element.48), calls=%async_computation.2 | async-start | bytes 32768 | tf_op jit(solution)/shard_map/all_to_all | solution.py:443
  89.2 0.6 copy-start.11
  91.1 12.6 %all-to-all-start.3 = ((f32[32,2,96]{2,1,0:T(2,128)}), f32[32,2,96]{2,1,0:T(2,128)S(1)}, u32[]{:S(2)}, u32[]{:S(2)}) async-start(f32[32,2,96]{2,1,0:T(2,128)} %relay.3), calls=%async_computation.3 | async-start | bytes 65536 | tf_op jit(solution)/shard_map/all_to_all | solution.py:443
  95.1 8.6 %copy-start.4 = (bf16[2,2,16,192]{3,2,1,0:T(8,128)(2,1)S(1)}, bf16[2,2,16,192]{3,2,1,0:T(8,128)(2,1)}, u32[]{:S(2)}) copy-start(bf16[2,2,16,192]{3,2,1,0:T(8,128)(2,1)} %features.5) | copy-start | bytes 73732
  104.9 5.3 %collective-permute-start.5 = (bf16[3072,128]{1,0:T(8,128)(2,1)S(1)}, bf16[3072,128]{1,0:T(8,128)(2,1)S(1)}, u32[]{:S(2)}, u32[]{:S(2)}) collective-permute-start(bf16[3072,128]{1,0:T(8,128)(2,1)S(1)} %get-tuple-element.60), channel_id=1, source_target_pairs={{0,1},{1,0},{2,3},{3,2},{4,5},{5,4},{6,7},{7,6},{8,9},{9,8},{10,11... | collective-permute-start | bytes 2359304 | tf_op jit(solution)/shard_map/ppermute | solution.py:479
  111.2 15.5 %all-to-all-start.4 = ((bf16[4,768,128]{2,1,0:T(8,128)(2,1)}), bf16[4,768,128]{2,1,0:T(8,128)(2,1)S(1)}, u32[]{:S(2)}, u32[]{:S(2)}) async-start(bf16[4,768,128]{2,1,0:T(8,128)(2,1)} %bitcast.6), calls=%async_computation.4 | async-start | bytes 1572864 | tf_op jit(solution)/shard_map/all_to_all | solution.py:443
  114.7 17.6 %copy-start.1 = (bf16[3,3,3,192,96]{4,3,2,1,0:T(8,128)(2,1)S(1)}, bf16[3,3,3,192,96]{4,3,2,1,0:T(8,128)(2,1)}, u32[]{:S(2)}) copy-start(bf16[3,3,3,192,96]{4,3,2,1,0:T(8,128)(2,1)} %weight.5) | copy-start | bytes 2985988
  114.7 12.2 %collective-permute-start.6 = (bf16[2,6,32,96]{3,2,1,0:T(8,128)(2,1)S(1)}, bf16[2,6,32,96]{3,2,1,0:T(8,128)(2,1)S(1)}, u32[]{:S(2)}, u32[]{:S(2)}) collective-permute-start(bf16[2,6,32,96]{3,2,1,0:T(8,128)(2,1)S(1)} %get-tuple-element.63), channel_id=1, source_target_pairs={{32,0},{64,32},{96,64},{128,96},{160,128},{192,160},{224,192},{256... | collective-permute-start | bytes 221192 | tf_op jit(solution)/shard_map/ppermute | solution.py:32
  127.6 17.2 %all-to-all-start.5 = ((bf16[64,12,128]{2,1,0:T(8,128)(2,1)}), bf16[64,12,128]{2,1,0:T(8,128)(2,1)S(1)}, u32[]{:S(2)}, u32[]{:S(2)}) async-start(bf16[64,12,128]{2,1,0:T(8,128)(2,1)} %reshape.27), calls=%async_computation.5 | async-start | bytes 524288 | tf_op jit(solution)/shard_map/all_to_all | solution.py:443
  174.4 9.0 %collective-permute-start.7 = (bf16[3072,128]{1,0:T(8,128)(2,1)S(1)}, bf16[3072,128]{1,0:T(8,128)(2,1)S(1)}, u32[]{:S(2)}, u32[]{:S(2)}) collective-permute-start(bf16[3072,128]{1,0:T(8,128)(2,1)S(1)} %bitcast.15), channel_id=1, source_target_pairs={{0,1},{1,0},{2,3},{3,2},{4,5},{5,4},{6,7},{7,6},{8,9},{9,8},{10,11... | collective-permute-start | bytes 2359304 | tf_op jit(solution)/shard_map/ppermute | solution.py:490

commit v5 on v4

--- a/solution.py
+++ b/solution.py
@@ -88,21 +88,7 @@
     )(cache, features, cot, later)
 
 
-def relay_kernel(came, out):
-    out[...] = jnp.broadcast_to(jnp.sum(came[...], 0, keepdims=True), out.shape)
-
-
-def relay(came, copies):
-    return pl.pallas_call(
-        relay_kernel,
-        out_shape=jax.ShapeDtypeStruct((copies,) + came.shape[1:], came.dtype),
-        in_specs=whole(1),
-        out_specs=whole()[0],
-        name="relay",
-    )(came)
-
-
-def conv_one_kernel(cache, features, above, below, weight, pre_norm, sums, wide):
+def conv_one_kernel(cache, features, above, below, weight, cot, pre_norm, sums, wide):
     frames, rows, cols, outs = pre_norm.shape
     cells_in, half, ins = features.shape[1], cols // 2, features.shape[-1]
     timed = jnp.concatenate([cache[...], features[...]], 0)
@@ -132,10 +118,11 @@
     pre_norm[...] = pre
     own = pre[:, 1:-1]
     both = group_sums(cell_sums(own), cell_sums(own * own), outs)
+    both = jnp.concatenate([both, cell_sums(cot[...].astype(jnp.float32)), jnp.zeros((1, outs), jnp.float32)], 0)
     sums[...] = jnp.broadcast_to(both[None], sums.shape)
 
 
-def conv_one(cache, features, above, below, weight, copies):
+def conv_one(cache, features, above, below, weight, cot, copies):
     frames, cells_in, half, _ = features.shape
     outs = weight.shape[-1]
     rows, cols = 2 * cells_in + 2, 2 * half
@@ -143,17 +130,17 @@
         conv_one_kernel,
         out_shape=(
             jax.ShapeDtypeStruct((frames, rows, cols, outs), jnp.float32),
-            jax.ShapeDtypeStruct((copies, 2, outs), jnp.float32),
+            jax.ShapeDtypeStruct((copies, 4, outs), jnp.float32),
         ),
-        in_specs=whole(5),
+        in_specs=whole(6),
         out_specs=whole(2),
         scratch_shapes=[pltpu.VMEM((frames * rows, cols + 16, 128), jnp.float32)],
         compiler_params=pltpu.CompilerParams(vmem_limit_bytes=VMEM_LIMIT),
         name="conv_one",
-    )(cache, features, above, below, weight)
-
-
-def grad_hidden_kernel(cot, later, above, below, weight, grad_hidden, shifted, wide):
+    )(cache, features, above, below, weight, cot)
+
+
+def grad_hidden_kernel(cot, later, above, below, weight, grad_hidden, shifted, all_taps, wide):
     frames, rows, cols, ins = grad_hidden.shape
     outs = cot.shape[-1]
     half = cols // 2
@@ -176,6 +163,9 @@
                     preferred_element_type=jnp.float32,
                 )
     grad_hidden[...] = total.reshape(grad_hidden.shape)
+    all_taps[...] = sum(
+        weight[a, b, e].astype(jnp.float32) for a in range(3) for b in range(3) for e in range(3)
+    )
 
 
 def hidden_grads(cot, later, above, below, weight):
@@ -185,9 +175,10 @@
         out_shape=(
             jax.ShapeDtypeStruct((frames, rows + 2, cols, weight.shape[-2]), jnp.float32),
             jax.ShapeDtypeStruct((3, 2 * frames, rows + 4, cols, outs), jnp.bfloat16),
+            jax.ShapeDtypeStruct(weight.shape[-2:], jnp.float32),
         ),
         in_specs=whole(5),
-        out_specs=whole(2),
+        out_specs=whole(3),
         scratch_shapes=[pltpu.VMEM((2 * frames * (rows + 4), cols + 16, 128), jnp.float32)],
         compiler_params=pltpu.CompilerParams(vmem_limit_bytes=VMEM_LIMIT),
         cost_estimate=pl.CostEstimate(flops=2**30, bytes_accessed=2**21, transcendentals=0),
@@ -195,12 +186,11 @@
     )(cot, later, above, below, weight)
 
 
-def middle_kernel(count, where, came, pre_norm, grad_hidden, gain, shift, hidden, grad_normed, normed, rstd, sums):
+def middle_kernel(count, where, came, pre_norm, grad_hidden, all_taps, gain, shift, hidden, grad_normed, normed, vectors):
     outs = pre_norm.shape[-1]
     total = jnp.sum(came[...], 0)
     mean = total[:1] / count
     scaled = lax.rsqrt(total[1:2] / count - mean * mean + EPSILON)
-    rstd[...] = scaled
     flat = (pre_norm[...].reshape(-1, outs) - mean) * scaled
     shifted = flat * gain[...] + shift[...]
     sigma = 1.0 / (1.0 + jnp.exp(-shifted))
@@ -210,11 +200,30 @@
     grad_normed[...] = grad
     normed[...] = flat
     own = grad[:, 1:-1]
-    both = group_sums(cell_sums(own), cell_sums(own * flat[:, 1:-1]), outs)
-    sums[...] = jnp.broadcast_to(both[None], sums.shape)
-
-
-def middle(count, where, came, pre_norm, grad_hidden, gain, shift, copies):
+
+    cells = count / (outs // GROUPS)
+    level = lax.dot_general(
+        total[2:3] / cells,
+        all_taps[...],
+        (((1,), (1,)), ((), ())),
+        precision=lax.Precision.HIGHEST,
+        preferred_element_type=jnp.float32,
+    )
+    at = lax.broadcasted_iota(jnp.int32, (16, outs), 0).astype(jnp.float32) * 0.45 - 3.375
+    share = jnp.exp(-0.5 * at * at)
+    share = share / jnp.sum(share, 0, keepdims=True)
+    point = at * gain[...] + shift[...]
+    slope = 1.0 / (1.0 + jnp.exp(-point))
+    slope = slope * (1.0 + point * (1.0 - slope)) * share
+    level = level * gain[...] * (cells / count)
+    offsets = group_sums(
+        level * jnp.sum(slope, 0, keepdims=True), level * jnp.sum(slope * at, 0, keepdims=True), outs
+    )
+    rows = [scaled, offsets, cell_sums(own), cell_sums(own * flat[:, 1:-1])]
+    vectors[...] = jnp.concatenate(rows + [jnp.zeros((3, outs), jnp.float32)], 0)
+
+
+def middle(count, where, came, pre_norm, grad_hidden, all_taps, gain, shift):
     shape, outs = pre_norm.shape, pre_norm.shape[-1]
     return pl.pallas_call(
         functools.partial(middle_kernel, count),
@@ -222,14 +231,13 @@
             jax.ShapeDtypeStruct(shape, jnp.bfloat16),
             jax.ShapeDtypeStruct(shape, jnp.float32),
             jax.ShapeDtypeStruct(shape, jnp.float32),
-            jax.ShapeDtypeStruct((1, outs), jnp.float32),
-            jax.ShapeDtypeStruct((copies, 2, outs), jnp.float32),
+            jax.ShapeDtypeStruct((8, outs), jnp.float32),
         ),
-        in_specs=whole(1, pltpu.SMEM) + whole(5),
-        out_specs=whole(5),
+        in_specs=whole(1, pltpu.SMEM) + whole(6),
+        out_specs=whole(4),
         compiler_params=pltpu.CompilerParams(vmem_limit_bytes=VMEM_LIMIT),
         name="middle",
-    )(where, came, pre_norm, grad_hidden, gain[None], shift[None])
+    )(where, came, pre_norm, grad_hidden, all_taps, gain[None], shift[None])
 
 
 def second_weight_kernel(hidden, shifted, out):
@@ -270,110 +278,251 @@
     return odd + after, even + odd, before + even
 
 
-def weight_grads_kernel(
-    count, where, cache, features, above, below, came, grad_normed, normed, rstd, two, grad_pre, away, kept, wide
-):
+def group_lanes(outs, first):
+    lane = lax.broadcasted_iota(jnp.int32, (outs, 128), 1)
+    group = lax.broadcasted_iota(jnp.int32, (outs, 128), 0) // (outs // GROUPS)
+    return (lane == group + (64 if first else 64 + GROUPS)).astype(jnp.float32)
+
+
+def exact(left, right, dims):
+    return lax.dot_general(
+        left, right, (dims, ((), ())), precision=lax.Precision.HIGHEST, preferred_element_type=jnp.float32
+    )
+
+
+def with_sums(tiles, sums):
+    high = sums.astype(jnp.bfloat16).astype(jnp.float32)
+    middle = (sums - high).astype(jnp.bfloat16).astype(jnp.float32)
+    low = sums - high - middle
+    row = lax.broadcasted_iota(jnp.int32, (8, 128), 0)
+    lane = lax.broadcasted_iota(jnp.int32, (8, 128), 1)
+    parts = jnp.where(row == 0, high, jnp.where(row == 1, middle, jnp.where(row == 2, low, 0.0)))
+    return jnp.where((lane < 64)[None], tiles, parts[None])
+
+
+def weight_grads_kernel(where, cache, features, above, below, grad_normed, normed, vectors, two, away, kept, wide):
     frames, rows, cols, outs = grad_normed.shape
-    ins, mids = features.shape[-1], two.shape[1]
-    total = jnp.sum(came[...], 0) / count
+    rows, half = rows - 2, cols // 2
+    ins, mids, pieces, part_rows = features.shape[-1], two.shape[1], kept.shape[0], kept.shape[2]
     timed = jnp.concatenate([cache[...], features[...]], 0)
-    rows_in = jnp.concatenate([above[:, : cols // 2][:, None], timed, below[:, : cols // 2][:, None]], 1)
-    merged = (frames * rows * cols, outs)
-    grad = grad_normed[...].reshape(merged) - total[:1] - normed[...].reshape(merged) * total[1:2]
-    grad = inside(where, (grad * rstd[...]).reshape(grad_normed.shape)).astype(jnp.bfloat16)
-    grad_pre[...] = grad
-    grad = grad[:, 1:-1].astype(jnp.float32)
-    rows = rows - 2
-    by_tap = col_sums(wide, grad.reshape(frames * rows, cols, outs))
-    pieces = []
-    for b in range(3):
-        for e in range(3):
-            part = by_tap[e].reshape(frames, rows, cols // 2, outs)
-            none = jnp.zeros_like(part[:, 0])
-            r = [part[:, k] for k in range(rows)]
-            stacked = (
-                [r[0], r[1] + r[2], r[3], none],
-                [none, r[0] + r[1], r[2] + r[3], none],
-                [none, r[0], r[1] + r[2], r[3]],
-            )[b]
-            cells = jnp.stack(stacked, 1).astype(jnp.bfloat16)
-            pieces.append(cells.reshape(-1, outs))
-    pieces.append(jnp.zeros((pieces[0].shape[0], 32), jnp.bfloat16))
-    cells = jnp.concatenate(pieces, 1)
+    rows_in = jnp.concatenate([above[:, :half][:, None], timed, below[:, :half][:, None]], 1)
+    rstd, f0, s0 = (vectors[k : k + 1] for k in range(3))
+    own = normed[:, 1:-1].reshape(-1, outs)
+    grad = (grad_normed[:, 1:-1].reshape(-1, outs) - f0 - own * s0) * rstd
     lower = where[0] == 0
 
-    def write(at, low, high):
-        away[at : at + low.shape[0]] = jnp.where(lower, high, low).astype(jnp.bfloat16)
-        kept[at : at + low.shape[0]] = jnp.where(lower, low, high)
-
+    def pool(field, last):
+        by_tap = col_sums(wide, field.reshape(frames * rows, cols, outs))
+        taps = []
+        for b in range(3):
+            for e in range(3):
+                part = by_tap[e].reshape(frames, rows, half, outs)
+                none = jnp.zeros_like(part[:, 0])
+                r = [part[:, k] for k in range(rows)]
+                stacked = (
+                    [r[0], r[1] + r[2], r[3], none],
+                    [none, r[0] + r[1], r[2] + r[3], none],
+                    [none, r[0], r[1] + r[2], r[3]],
+                )[b]
+                taps.append(jnp.stack(stacked, 1).astype(jnp.bfloat16).reshape(-1, outs))
+        return jnp.concatenate(taps + [last], 1)
+
+    at = lax.broadcasted_iota(jnp.int32, (frames * 4 * half, 32), 0)
+    tap = lax.broadcasted_iota(jnp.int32, (frames * 4 * half, 32), 1)
+    b, e, row, col = tap // 3, tap % 3, at // half % 4, at % half
+    two_rows = (row == 1) & (b < 2) | (row == 2) & (b > 0)
+    one_row = (row == 0) & (b == 0) | (row == 2) & (b == 0) | (row == 1) & (b == 2) | (row == 3) & (b == 2)
+    in_rows = jnp.where(two_rows, 2.0, jnp.where(one_row, 1.0, 0.0))
+    in_cols = jnp.where((e == 0) & (col == half - 1) | (e == 2) & (col == 0), 1.0, 2.0)
+    counts = jnp.where(tap < 9, in_rows * in_cols, 0.0).astype(jnp.bfloat16)
+
+    def write(part, at, low, high):
+        while low.shape[0]:
+            x, row = at // part_rows, at % part_rows
+            n = min(low.shape[0], part_rows - row)
+            away[x, part, row : row + n] = jnp.where(lower, high[:n], low[:n]).astype(jnp.bfloat16)
+            kept[x, part, row : row + n] = jnp.where(lower, low[:n], high[:n])
+            low, high, at = low[n:], high[n:], at + n
+
+    for part, field, last in ((0, grad, counts), (1, own * rstd, jnp.zeros_like(counts))):
+        cells = pool(field, last)
+        at = 0
+        for a in range(3):
+            product = lax.dot_general(
+                rows_in[a : a + frames].reshape(-1, ins),
+                cells,
+                (((0,), (0,)), ((), ())),
+                preferred_element_type=jnp.float32,
+            )
+            for j in range(7):
+                block = product[:, 128 * j : 128 * j + 128]
+                write(part, at, block[: ins // 2], block[ins // 2 :])
+                at += ins // 2
+        nothing = jnp.zeros((pieces * part_rows - at, 128), jnp.float32)
+        write(part, at, nothing, nothing)
+
+    sums = exact(vectors[3:4], group_lanes(outs, True), ((1,), (0,)))
+    sums += exact(vectors[4:5], group_lanes(outs, False), ((1,), (0,)))
+    blocks = [two[a, :, 128 * j : 128 * j + 128] for a in range(3) for j in range(7)]
+    nothing = [jnp.zeros((pieces * part_rows // 2 - 21 * mids // 2, 128), jnp.float32)]
+    halves = [jnp.concatenate([k[i : i + mids // 2] for k in blocks] + nothing, 0) for i in (0, mids // 2)]
+    row = lax.broadcasted_iota(jnp.int32, (1, 8, 128), 1)
+    tiled = []
+    for half_rows in halves:
+        tiles = half_rows.reshape(-1, 8, 128)
+        turned = jnp.concatenate([tiles[:, 4:], tiles[:, :4]], 1)
+        swap = lambda k: jnp.concatenate([k[..., 64:], k[..., :64]], 2)
+        even = jnp.where(row < 4, tiles, swap(turned))
+        odd = jnp.where(row < 4, turned, swap(tiles))
+        tiled.append(with_sums(jnp.stack([even, odd], 1).reshape(-1, 8, 128), sums).reshape(-1, 128))
+    write(2, 0, *tiled)
+
+
+def weight_grads(where, cache, features, above, below, grad_normed, normed, vectors, two, pieces, part_rows):
+    frames, rows, cols, _ = grad_normed.shape
+    shape = (pieces, 3, part_rows, 128)
+    return pl.pallas_call(
+        weight_grads_kernel,
+        out_shape=(jax.ShapeDtypeStruct(shape, jnp.bfloat16), jax.ShapeDtypeStruct(shape, jnp.float32)),
+        in_specs=whole(1, pltpu.SMEM) + whole(8),
+        out_specs=whole(2),
+        scratch_shapes=[pltpu.VMEM((frames * (rows - 2), cols + 16, 128), jnp.float32)],
+        compiler_params=pltpu.CompilerParams(vmem_limit_bytes=VMEM_LIMIT),
+        name="weight_grads",
+    )(where, cache, features, above, below, grad_normed, normed, vectors, two)
+
+
+def sums_of(tile):
+    return tile[0:1] + tile[1:2] + tile[2:3]
+
+
+def add_pair_kernel(kept, came, out):
+    total = kept[...] + came[...].astype(jnp.float32)
+    out[:, :2] = total[:, :2].astype(jnp.bfloat16)
+    tiles = total[:, 2].reshape(-1, 8, 128)
+    tiles = with_sums(tiles, sums_of(tiles[0]))
+    out[:, 2] = tiles.astype(jnp.bfloat16).reshape(out.shape[0], -1, 128)
+
+
+def add_pair(kept, came):
+    return pl.pallas_call(
+        add_pair_kernel,
+        out_shape=jax.ShapeDtypeStruct(kept.shape, jnp.bfloat16),
+        in_specs=whole(2),
+        out_specs=whole()[0],
+        compiler_params=pltpu.CompilerParams(vmem_limit_bytes=VMEM_LIMIT),
+        name="add_pair",
+    )(kept, came)
+
+
+def add_row_kernel(came, out):
+    total = jnp.sum(came[...].astype(jnp.float32), 0)
+    for part in range(3):
+        tiles = total[part].reshape(-1, 8, 128)
+        if part == 2:
+            tiles = with_sums(tiles, sums_of(tiles[0]))
+        out[:, part] = tiles.astype(jnp.bfloat16)
+
+
+def add_row(came):
+    return pl.pallas_call(
+        add_row_kernel,
+        out_shape=jax.ShapeDtypeStruct((came.shape[2] // 8, 3, 8, 128), jnp.bfloat16),
+        in_specs=whole(1),
+        out_specs=whole()[0],
+        compiler_params=pltpu.CompilerParams(vmem_limit_bytes=VMEM_LIMIT),
+        name="add_row",
+    )(came)
+
+
+def combine_kernel(count, tiles_per_block, where, came, vectors, piece, final, lanes):
+    outs = vectors.shape[1]
+    total = jnp.sum(came[...].astype(jnp.float32), 0)
+    sums = sums_of(total[0, 2]) / count
+    first = exact(sums, group_lanes(outs, True), ((1,), (1,)))
+    second = exact(sums, group_lanes(outs, False), ((1,), (1,)))
+    rest = (first - vectors[1:2]) * vectors[0:1]
+    final[...] = jnp.concatenate([first, second, rest, jnp.zeros((5, outs), jnp.float32)], 0)
+    lane = lax.broadcasted_iota(jnp.int32, (outs, 896), 1)
+    channel = lax.broadcasted_iota(jnp.int32, (outs, 896), 0)
+    spread = ((lane % outs == channel) & (lane < 9 * outs)).astype(jnp.float32)
+    lanes[...] = jnp.broadcast_to(exact(second - vectors[2:3], spread, ((1,), (0,))), lanes.shape)
+    for k in range(piece.shape[0]):
+        block = (where[3] * piece.shape[0] + k) // tiles_per_block % 7
+        change = lanes[0:1, pl.ds(pl.multiple_of(block * 128, 128), 128)]
+        upper = jnp.concatenate([total[k, 2, :4, :64], total[k, 2, 4:, :64]], 1)
+        grad = total[k, 0] - change * total[k, 1]
+        piece[k] = jnp.concatenate([grad, upper], 0).astype(jnp.bfloat16)
+
+
+def combine(count, ins, where, came, vectors):
+    return pl.pallas_call(
+        functools.partial(combine_kernel, count, ins // 16),
+        out_shape=(
+            jax.ShapeDtypeStruct((came.shape[1], 12, 128), jnp.bfloat16),
+            jax.ShapeDtypeStruct(vectors.shape, jnp.float32),
+        ),
+        in_specs=whole(1, pltpu.SMEM) + whole(2),
+        out_specs=whole(2),
+        scratch_shapes=[pltpu.VMEM((8, 896), jnp.float32)],
+        compiler_params=pltpu.CompilerParams(vmem_limit_bytes=VMEM_LIMIT),
+        name="combine",
+    )(where, came, vectors)
+
+
+def grad_pre_kernel(where, grad_normed, normed, vectors, final, out):
+    shape = grad_normed.shape
+    flat = (-1, shape[-1])
+    grad = grad_normed[...].reshape(flat) - final[:1] - normed[...].reshape(flat) * final[1:2]
+    out[...] = inside(where, (grad * vectors[:1]).reshape(shape)).astype(jnp.bfloat16)
+
+
+def grad_before_norm(where, grad_normed, normed, vectors, final):
+    return pl.pallas_call(
+        grad_pre_kernel,
+        out_shape=jax.ShapeDtypeStruct(grad_normed.shape, jnp.bfloat16),
+        in_specs=whole(1, pltpu.SMEM) + whole(4),
+        out_specs=whole()[0],
+        compiler_params=pltpu.CompilerParams(vmem_limit_bytes=VMEM_LIMIT),
+        cost_estimate=pl.CostEstimate(flops=2**20, bytes_accessed=2**20, transcendentals=0),
+        name="grad_pre",
+    )(where, grad_normed, normed, vectors, final)
+
+
+def unpack_kernel(scale, half, part, final, *rest):
+    one, two, flat = rest[-3:]
+    pieces, rows = part.shape[0], part.shape[1]
+    for x in range(pieces):
+        flat[rows * 2 // 3 * x : rows * 2 // 3 * (x + 1)] = part[x, : rows * 2 // 3]
+        at = pieces * (rows * 2 // 3) + rows // 3 * x
+        flat[at : at + rows // 3] = part[x, rows * 2 // 3 :]
     at = 0
-    for a in range(3):
-        product = lax.dot_general(
-            rows_in[a : a + frames].reshape(-1, ins),
-            cells,
-            (((0,), (0,)), ((), ())),
-            preferred_element_type=jnp.float32,
-        )
-        for j in range(7):
-            block = product[:, 128 * j : 128 * j + 128]
-            write(at, block[: ins // 2], block[ins // 2 :])
-            at += ins // 2
-    for a in range(3):
-        product = two[a]
-        for j in range(7):
-            block = product[:, 128 * j : 128 * j + 128]
-            write(at, block[: mids // 2], block[mids // 2 :])
-            at += mids // 2
-    if at < kept.shape[0]:
-        tail = jnp.zeros((kept.shape[0] - at, 128), jnp.float32)
-        away[at:] = tail.astype(jnp.bfloat16)
-        kept[at:] = tail
-
-
-def weight_grads(count, where, cache, features, above, below, came, grad_normed, normed, rstd, two, half_rows):
-    frames, rows, cols, outs = grad_normed.shape
-    return pl.pallas_call(
-        functools.partial(weight_grads_kernel, count),
-        out_shape=(
-            jax.ShapeDtypeStruct(grad_normed.shape, jnp.bfloat16),
-            jax.ShapeDtypeStruct((half_rows, 128), jnp.bfloat16),
-            jax.ShapeDtypeStruct((half_rows, 128), jnp.float32),
-        ),
-        in_specs=whole(1, pltpu.SMEM) + whole(9),
-        out_specs=whole(3),
-        scratch_shapes=[pltpu.VMEM((frames * (rows - 2), cols + 16, 128), jnp.float32)],
-        compiler_params=pltpu.CompilerParams(vmem_limit_bytes=VMEM_LIMIT),
-        name="weight_grads",
-    )(where, cache, features, above, below, came, grad_normed, normed, rstd, two)
-
-
-def unpack_kernel(scale, half, part_one, part_two, *rest):
-    one, two = rest[-2:]
-    for part, out in ((part_one, one), (part_two, two)):
-        taps, rows, outs = out.shape
-        lanes = jnp.concatenate([part[rows * j : rows * j + rows] for j in range(7)], 1)
-        lanes = lanes.astype(jnp.float32) * scale
-        for k in range(taps):
-            out[k] = lanes[:, outs * k : outs * k + outs]
-
-
-def unpack(half, part, ins, mids, scale, begun=()):
-    half_one, half_two = 7 * ins // 2, 7 * mids // 2
-    skip = 3 * half_one // half_two
+    for out in (one, two):
+        taps, channels, outs = out.shape
+        for a in range(3):
+            blocks = [flat[at + channels * j : at + channels * j + channels] for j in range(7)]
+            lanes = jnp.concatenate(blocks, 1).astype(jnp.float32) * scale
+            for k in range(9):
+                grad = lanes[:, outs * k : outs * k + outs]
+                if out is one:
+                    grad = grad - lanes[:, 9 * outs + k : 9 * outs + k + 1] * final[2:3]
+                out[9 * a + k] = grad
+            at += 7 * channels
+        at = pieces * (rows * 2 // 3)
+
+
+def unpack(half, part, final, ins, mids, scale, begun=()):
     return pl.pallas_call(
         functools.partial(unpack_kernel, scale),
         grid_spec=pltpu.PrefetchScalarGridSpec(
             num_scalar_prefetch=1,
-            grid=(3,),
-            in_specs=[
-                pl.BlockSpec((half_one, 128), lambda a, half: (a, 0)),
-                pl.BlockSpec((half_two, 128), lambda a, half: (a + skip, 0)),
-            ]
-            + whole(len(begun), pl.ANY),
+            grid=(1,),
+            in_specs=whole(2) + whole(len(begun), pl.ANY),
             out_specs=[
-                pl.BlockSpec((9, ins // 2, mids), lambda a, half: (a, half[0], 0)),
-                pl.BlockSpec((9, mids // 2, mids), lambda a, half: (a, half[0], 0)),
+                pl.BlockSpec((27, ins // 2, mids), lambda a, half: (0, half[0], 0)),
+                pl.BlockSpec((27, mids // 2, mids), lambda a, half: (0, half[0], 0)),
             ],
+            scratch_shapes=[pltpu.VMEM((part.shape[0] * part.shape[1], 128), jnp.bfloat16)],
         ),
         out_shape=(
             jax.ShapeDtypeStruct((27, ins, mids), jnp.float32),
@@ -383,7 +532,7 @@
         compiler_params=pltpu.CompilerParams(vmem_limit_bytes=VMEM_LIMIT),
         cost_estimate=pl.CostEstimate(flops=2**20, bytes_accessed=2**22, transcendentals=0),
         name="unpack",
-    )(half, part, part, *begun)
+    )(half, part, final, *begun)
 
 
 def feature_grads_kernel(grad_pre, weight, out, wide):
@@ -421,11 +570,6 @@
     )(grad_rowed, weight)
 
 
-def half_rows(ins, mids):
-    unit = lax.axis_size("x") * lax.axis_size(REST)
-    return -(-(21 * (ins + mids) // 2) // unit) * unit
-
-
 SWAP = [(0, 1), (1, 0)]
 
 
@@ -436,7 +580,8 @@
     cells = frames * rows * cols * 2 * xs * rest
     count = cells * (mids // GROUPS)
     at_row = lax.axis_index(HEIGHT)
-    where = jnp.stack([lax.axis_index("c"), at_row == 0, at_row == height - 1]).astype(jnp.int32)
+    owned = lax.axis_index("x") * rest + lax.axis_index(REST)
+    where = jnp.stack([lax.axis_index("c"), at_row == 0, at_row == height - 1, owned]).astype(jnp.int32)
     barrier = lax.optimization_barrier
 
     def exchange(copies, axes):
@@ -451,46 +596,44 @@
     downward, upward = edges(cache, features, cotangent, later)
     above = neighbour(downward, HEIGHT, 1)
     below = neighbour(upward, HEIGHT, -1)
-    pre_norm, sums = conv_one(cache, features, above, below, weight_one, height)
+    pre_norm, sums = conv_one(cache, features, above, below, weight_one, cotangent, height)
     came = exchange(sums, HEIGHT)
-    grad_hidden, shifted_cot = hidden_grads(cotangent, later, above, below, weight_two)
-    came, grad_hidden, shifted_cot = barrier((came, grad_hidden, shifted_cot))
-    came = exchange(relay(came, lax.axis_size(TM)), TM)
-    pair, others = ("y", "c"), ("zh", "zl", "x")
-    hidden, grad_normed, normed, rstd, sums = middle(
-        count, where, came, pre_norm, grad_hidden, norm_gain, norm_shift, lax.axis_size(pair)
+    grad_hidden, shifted_cot, all_taps = hidden_grads(cotangent, later, above, below, weight_two)
+    sums, grad_hidden, shifted_cot = barrier((came.sum(0), grad_hidden, shifted_cot))
+    came = exchange(spread(sums, lax.axis_size(TM)), TM)
+    hidden, grad_normed, normed, vectors = middle(
+        count, where, came, pre_norm, grad_hidden, all_taps, norm_gain, norm_shift
     )
-    sums, hidden = barrier((sums, hidden))
-    came = exchange(sums, pair)
     local_two = second_weight(hidden, shifted_cot)
+
+    scale = 1.0 / cells**0.5
+    part_rows = -(-21 * ins // (2 * 8 * xs * rest)) * 8 * rest
+    away, kept = weight_grads(
+        where, cache, features, above, below, grad_normed, normed, vectors, local_two, xs, part_rows
+    )
+    part = add_pair(kept, lax.ppermute(away, "c", SWAP))
+    part, hidden = barrier((part, hidden))
+    part = add_row(exchange(part, "x"))
     before = neighbour(hidden, TM, 1)
-    came, local_two, before = barrier((came, local_two, before))
-    came = exchange(relay(came, lax.axis_size(others)), others)
+    part, before = barrier((part, before))
+    came = exchange(part.reshape(rest, -1, 3, 8, 128), REST)
     decoded = conv(
         jnp.pad(jnp.concatenate([before, hidden], 0), ((0, 0), (0, 0), (1, 1), (0, 0))), weight_two
     ).astype(jnp.bfloat16)
     came, decoded = barrier((came, decoded))
-
-    scale = 1.0 / cells**0.5
-    grad_pre, away, kept = weight_grads(
-        count, where, cache, features, above, below, came, grad_normed, normed, rstd, local_two, half_rows(ins, mids)
-    )
-
-    part = kept + lax.ppermute(away, "c", SWAP).astype(jnp.float32)
-    part = part.astype(jnp.bfloat16).reshape(xs, -1, 128)
-    part, grad_pre = barrier((part, grad_pre))
-    part = exchange(part, "x").astype(jnp.float32).sum(0).astype(jnp.bfloat16)
+    part, final = combine(count, ins, where, came, vectors)
+    grad_pre = grad_before_norm(where, grad_normed, normed, vectors, final)
+    part = exchange(spread(part, rest), REST)
     after = neighbour(grad_pre, TM, -1)
     part, after = barrier((part, after))
-    part = exchange(part.reshape(rest, -1, 128), REST).astype(jnp.float32).sum(0).astype(jnp.bfloat16)
+    part = jnp.concatenate([part[:, :, :8].reshape(-1, 128), part[:, :, 8:].reshape(-1, 128)], 0)
+    part = exchange(spread(part, xs), "x")
     grad_features = feature_grads(jnp.concatenate([grad_pre, after], 0), weight_one, features.shape)
     part, grad_features = barrier((part, grad_features))
-    part = exchange(spread(part, rest), REST).reshape(-1, 128)
-    part = exchange(spread(part, xs), "x").reshape(-1, 128)
     other = lax.ppermute(part, "c", SWAP)
     core = where[:1]
-    begun = unpack(core, part, ins, mids, scale)
-    grad_one, grad_two = unpack(1 - core, other, ins, mids, scale, begun)
+    begun = unpack(core, part, final, ins, mids, scale)
+    grad_one, grad_two = unpack(1 - core, other, final, ins, mids, scale, begun)
     return decoded, grad_features, grad_one.reshape(weight_one.shape), grad_two.reshape(weight_two.shape)
 
 

time: 187 us -> 178 us (0.952)
  blocking collectives: 29.3 us -> 0 us
  waiting for transfers between devices: 56.5 us -> 70.9 us
  Pallas kernels: 14.6 us -> 20.5 us
    all_to_all x2 -> x0, blocking collectives: 29.3 us -> none  [exchange(): return lax.all_to_all(copies, axes, 0, 0)]
    all_to_all x6, waiting for transfers between devices: 52.4 us -> 59.3 us  [exchange(): return lax.all_to_all(copies, axes, 0, 0)]
    ppermute x6, waiting for transfers between devices: 2.23 us -> 8.66 us  [neighbour(): lax.ppermute(value, axis, [(i, i + steps) for i in range(first, last)])]
    pallas_call x2, Pallas kernels: 4.4 us -> 8.52 us  [unpack(): pl.pallas_call(functools.partial(unpack_kernel, scale), grid_spec=pltpu.P...]
    pallas_call x3 -> x5, Pallas kernels: 3.9 us -> 6.12 us  [the longest x1 1.99 us: weight_grads(): pl.pallas_call(weight_grads_kernel, out_shape=(jax.ShapeDtypeStruct(shape...]
    broadcast_in_dim x3, local copies, waits for them, and re-layouts: 0.19 us -> 2.35 us  [spread(): return jnp.broadcast_to(value[None], (copies,) + value.shape)]
    unnamed x25 -> x23, local copies, waits for them, and re-layouts: 5.57 us -> 5.19 us
  transfers between devices with their start and end apart: 14 -> 14, of which waited for: 9 -> 10; matrix products, arithmetic and copies ran while one was open for 1% -> 1% of each run, Pallas kernels for 3% -> 5%
where the time goes in v5:
time: 178 us; the launch traced here: 177 us
  starting transfers between devices  75.6 us (42%)
  waiting for transfers between devices  70.9 us (40%)
  Pallas kernels  20.5 us (12%)
  local copies, waits for them, and re-layouts  7.57 us (4%)
    all_to_all x6, waiting for transfers between devices, exchange(): return lax.all_to_all(copies, axes, 0, 0)  59.3 us
    all_to_all x6, starting transfers between devices, exchange(): return lax.all_to_all(copies, axes, 0, 0)  44.7 us
    ppermute x6, starting transfers between devices, neighbour(): lax.ppermute(value, axis, [(i, i + steps) for i in range(first, last)])  20.2 us
    ppermute x6, waiting for transfers between devices, neighbour(): lax.ppermute(value, axis, [(i, i + steps) for i in range(first, last)])  8.66 us
    pallas_call x2, Pallas kernels, unpack(): pl.pallas_call(functools.partial(unpack_kernel, scale), grid_spec=pltpu.P...  8.52 us
    ppermute x1, starting transfers between devices, body(): other = lax.ppermute(part, 'c', SWAP)  6.86 us
    unnamed x23, local copies, waits for them, and re-layouts  5.19 us
    ppermute x1, starting transfers between devices, body(): part = add_pair(kept, lax.ppermute(away, 'c', SWAP))  3.73 us
  transfers between devices with their start and end apart: 14, of which 10 were waited for; matrix products, arithmetic and copies ran while one was open for 1% of the time, Pallas kernels for 5%

profile of v5, /device:TPU:1, one launch (start us, length us, event | category | flops | bytes accessed | tf_op | source)
XLA Modules:
  0.0 177.3 jit_solution(16543539166908705606)
XLA Ops:
  0.6 1.3 collective-permute-start.1
  1.9 4.7 %collective-permute-start = (bf16[2,2,16,192]{3,2,1,0:T(8,128)(2,1)}, bf16[2,2,16,192]{3,2,1,0:T(8,128)(2,1)S(1)}, u32[]{:S(2)}, u32[]{:S(2)}) collective-permute-start(bf16[2,2,16,192]{3,2,1,0:T(8,128)(2,1)} %features.5), channel_id=1, source_target_pairs={{0,32},{32,64},{64,96},{96,128},{128,160},{160,192},{192,224},{224... | collective-permute-start | bytes 73736 | tf_op jit(solution)/shard_map/ppermute | solution.py:32
  6.6 1.3 collective-permute-done.cache
  9.6 5.0 %collective-permute-start.2 = (bf16[4,48,192]{2,1,0:T(8,128)(2,1)S(1)}, bf16[4,48,192]{2,1,0:T(8,128)(2,1)S(1)}, u32[]{:S(2)}, u32[]{:S(2)}) collective-permute-start(bf16[4,48,192]{2,1,0:T(8,128)(2,1)S(1)} %get-tuple-element.36), channel_id=1, source_target_pairs={{0,1},{1,2},{2,3},{3,4},{4,5},{5,6},{6,7},{7,8},{8,9},{9,10},{10,1... | collective-permute-start | bytes 221192 | tf_op jit(solution)/shard_map/ppermute | solution.py:32
  14.6 5.6 %collective-permute-start.3 = (bf16[4,48,192]{2,1,0:T(8,128)(2,1)S(1)}, bf16[4,48,192]{2,1,0:T(8,128)(2,1)S(1)}, u32[]{:S(2)}, u32[]{:S(2)}) collective-permute-start(bf16[4,48,192]{2,1,0:T(8,128)(2,1)S(1)} %get-tuple-element.37), channel_id=1, source_target_pairs={{1,0},{2,1},{3,2},{4,3},{5,4},{6,5},{7,6},{8,7},{9,8},{10,9},{11,1... | collective-permute-start | bytes 221192 | tf_op jit(solution)/shard_map/ppermute | solution.py:32
  21.1 1.3 copy-done
  24.0 1.6 conv_one.1
  25.6 10.3 %all-to-all-start = ((f32[32,4,96]{2,1,0:T(4,128)}), f32[32,4,96]{2,1,0:T(4,128)S(1)}, u32[]{:S(2)}, u32[]{:S(2)}) async-start(f32[32,4,96]{2,1,0:T(4,128)} %get-tuple-element.38), calls=%async_computation | async-start | bytes 131072 | tf_op jit(solution)/shard_map/all_to_all | solution.py:588
  36.9 6.7 %all-to-all-done = f32[32,4,96]{2,1,0:T(4,128)S(1)} async-done(((f32[32,4,96]{2,1,0:T(4,128)}), f32[32,4,96]{2,1,0:T(4,128)S(1)}, u32[]{:S(2)}, u32[]{:S(2)}) %all-to-all-start) | async-done | bytes 49184 | tf_op jit(solution)/shard_map/all_to_all | solution.py:588
  44.3 16.1 %all-to-all-start.1 = ((f32[16,4,96]{2,1,0:T(4,128)}), f32[16,4,96]{2,1,0:T(4,128)S(1)}, u32[]{:S(2)}, u32[]{:S(2)}) async-start(f32[16,4,96]{2,1,0:T(4,128)} %broadcast_in_dim.14), calls=%async_computation.1 | async-start | bytes 65536 | tf_op jit(solution)/shard_map/all_to_all | solution.py:588
  60.5 11.2 %all-to-all-done.1.came = f32[16,4,96]{2,1,0:T(4,128)S(1)} async-done(((f32[16,4,96]{2,1,0:T(4,128)}), f32[16,4,96]{2,1,0:T(4,128)S(1)}, u32[]{:S(2)}, u32[]{:S(2)}) %all-to-all-start.1) | async-done | bytes 24608 | tf_op jit(solution)/shard_map/all_to_all | solution.py:588
  73.2 2.0 %weight_grads.1 = (bf16[4,3,512,128]{3,2,1,0:T(8,128)(2,1)S(1)}, f32[4,3,512,128]{3,2,1,0:T(8,128)S(1)}) custom-call(s32[4]{0:T(128)S(1)} %pad_add_fusion.where, bf16[2,2,16,192]{3,2,1,0:T(8,128)(2,1)S(1)} %collective-permute-done.cache, bf16[2,2,16,192]{3,2,1,0:T(8,128)(2,1)S(1)} %copy-done.4, bf16[4,48,192]{2,1,0:T(8,128)(2,1)S(1)} %collective-permute-done.2.above, ...), custom_call_target="tpu_custom_call" | custom-call | tf_op jit(solution)/shard_map/weight_grads/pallas_call | solution.py:384
  75.2 3.7 %collective-permute-start.4 = (bf16[4,3,512,128]{3,2,1,0:T(8,128)(2,1)S(1)}, bf16[4,3,512,128]{3,2,1,0:T(8,128)(2,1)S(1)}, u32[]{:S(2)}, u32[]{:S(2)}) collective-permute-start(bf16[4,3,512,128]{3,2,1,0:T(8,128)(2,1)S(1)} %get-tuple-element.51), channel_id=1, source_target_pairs={{0,1},{1,0},{2,3},{3,2},{4,5},{5,4},{6,7},{7,6},{8,9},{9,8},{10,11... | collective-permute-start | bytes 4718600 | tf_op jit(solution)/shard_map/ppermute | solution.py:614
  79.0 3.0 %collective-permute-done.4.came = bf16[4,3,512,128]{3,2,1,0:T(8,128)(2,1)S(1)} collective-permute-done((bf16[4,3,512,128]{3,2,1,0:T(8,128)(2,1)S(1)}, bf16[4,3,512,128]{3,2,1,0:T(8,128)(2,1)S(1)}, u32[]{:S(2)}, u32[]{:S(2)}) %collective-permute-start.4) | collective-permute-done | bytes 1572896 | tf_op jit(solution)/shard_map/ppermute | solution.py:614
  82.0 1.4 add_pair.1
  83.4 3.6 %all-to-all-start.2 = ((bf16[4,3,512,128]{3,2,1,0:T(8,128)(2,1)}), bf16[4,3,512,128]{3,2,1,0:T(8,128)(2,1)S(1)}, u32[]{:S(2)}, u32[]{:S(2)}) async-start(bf16[4,3,512,128]{3,2,1,0:T(8,128)(2,1)} %add_pair.1), calls=%async_computation.2 | async-start | bytes 3145728 | tf_op jit(solution)/shard_map/all_to_all | solution.py:588
  87.0 2.4 %collective-permute-start.5 = (bf16[2,6,32,96]{3,2,1,0:T(8,128)(2,1)S(1)}, bf16[2,6,32,96]{3,2,1,0:T(8,128)(2,1)S(1)}, u32[]{:S(2)}, u32[]{:S(2)}) collective-permute-start(bf16[2,6,32,96]{3,2,1,0:T(8,128)(2,1)S(1)} %get-tuple-element.53.hidden), channel_id=1, source_target_pairs={{0,32},{32,64},{64,96},{96,128},{128,160},{160,192},{192,224},{224... | collective-permute-start | bytes 221192 | tf_op jit(solution)/shard_map/ppermute | solution.py:32
  89.4 18.0 %all-to-all-done.2.came = bf16[4,3,512,128]{3,2,1,0:T(8,128)(2,1)S(1)} async-done(((bf16[4,3,512,128]{3,2,1,0:T(8,128)(2,1)}), bf16[4,3,512,128]{3,2,1,0:T(8,128)(2,1)S(1)}, u32[]{:S(2)}, u32[]{:S(2)}) %all-to-all-start.2) | async-done | bytes 1572896 | tf_op jit(solution)/shard_map/all_to_all | solution.py:588
  108.4 4.6 %all-to-all-start.3 = ((bf16[64,1,3,8,128]{4,3,2,1,0:T(8,128)(2,1)}), bf16[64,1,3,8,128]{4,3,2,1,0:T(8,128)(2,1)S(1)}, u32[]{:S(2)}, u32[]{:S(2)}) async-start(bf16[64,1,3,8,128]{4,3,2,1,0:T(8,128)(2,1)} %bitcast.6), calls=%async_computation.3 | async-start | bytes 786432 | tf_op jit(solution)/shard_map/all_to_all | solution.py:588
  113.1 1.5 convolution_convert_fusion
  115.3 12.5 %all-to-all-done.3.came = bf16[64,1,3,8,128]{4,3,2,1,0:T(8,128)(2,1)S(1)} async-done(((bf16[64,1,3,8,128]{4,3,2,1,0:T(8,128)(2,1)}), bf16[64,1,3,8,128]{4,3,2,1,0:T(8,128)(2,1)S(1)}, u32[]{:S(2)}, u32[]{:S(2)}) %all-to-all-start.3) | async-done | bytes 393248 | tf_op jit(solution)/shard_map/all_to_all | solution.py:588
  127.8 1.1 combine.1
  129.7 6.7 %all-to-all-start.4 = ((bf16[64,1,12,128]{3,2,1,0:T(8,128)(2,1)}), bf16[64,1,12,128]{3,2,1,0:T(8,128)(2,1)S(1)}, u32[]{:S(2)}, u32[]{:S(2)}) async-start(bf16[64,1,12,128]{3,2,1,0:T(8,128)(2,1)} %broadcast_in_dim.34), calls=%async_computation.4 | async-start | bytes 524288 | tf_op jit(solution)/shard_map/all_to_all | solution.py:588
  136.9 1.3 collective-permute-start.6
  138.2 6.4 %collective-permute-done.6 = bf16[2,6,32,96]{3,2,1,0:T(8,128)(2,1)S(1)} collective-permute-done((bf16[2,6,32,96]{3,2,1,0:T(8,128)(2,1)S(1)}, bf16[2,6,32,96]{3,2,1,0:T(8,128)(2,1)S(1)}, u32[]{:S(2)}, u32[]{:S(2)}) %collective-permute-start.6) | collective-permute-done | bytes 73760 | tf_op jit(solution)/shard_map/ppermute | solution.py:32
  144.7 4.2 %all-to-all-done.4 = bf16[64,1,12,128]{3,2,1,0:T(8,128)(2,1)S(1)} async-done(((bf16[64,1,12,128]{3,2,1,0:T(8,128)(2,1)}), bf16[64,1,12,128]{3,2,1,0:T(8,128)(2,1)S(1)}, u32[]{:S(2)}, u32[]{:S(2)}) %all-to-all-start.4) | async-done | bytes 196640 | tf_op jit(solution)/shard_map/all_to_all | solution.py:588
  149.9 3.5 %all-to-all-start.5 = ((bf16[4,768,128]{2,1,0:T(8,128)(2,1)}), bf16[4,768,128]{2,1,0:T(8,128)(2,1)S(1)}, u32[]{:S(2)}, u32[]{:S(2)}) async-start(bf16[4,768,128]{2,1,0:T(8,128)(2,1)} %broadcast_in_dim.35), calls=%async_computation.5 | async-start | bytes 1572864 | tf_op jit(solution)/shard_map/all_to_all | solution.py:588
  153.5 1.6 feature_grads.1
  155.1 6.7 %all-to-all-done.5.part = bf16[4,768,128]{2,1,0:T(8,128)(2,1)S(1)} async-done(((bf16[4,768,128]{2,1,0:T(8,128)(2,1)}), bf16[4,768,128]{2,1,0:T(8,128)(2,1)S(1)}, u32[]{:S(2)}, u32[]{:S(2)}) %all-to-all-start.5) | async-done | bytes 786464 | tf_op jit(solution)/shard_map/all_to_all | solution.py:588
  161.9 6.9 %collective-permute-start.7 = (bf16[4,768,128]{2,1,0:T(8,128)(2,1)S(1)}, bf16[4,768,128]{2,1,0:T(8,128)(2,1)S(1)}, u32[]{:S(2)}, u32[]{:S(2)}) collective-permute-start(bf16[4,768,128]{2,1,0:T(8,128)(2,1)S(1)} %all-to-all-done.5.part), channel_id=1, source_target_pairs={{0,1},{1,0},{2,3},{3,2},{4,5},{5,4},{6,7},{7,6},{8,9},{9,8},{10,11... | collective-permute-start | bytes 2359304 | tf_op jit(solution)/shard_map/ppermute | solution.py:633
  168.7 4.3 %unpack.2 = (f32[27,192,96]{2,1,0:T(8,128)}, f32[27,96,96]{2,1,0:T(8,128)}) custom-call(s32[1]{0:T(128)} %bitcast.half, bf16[4,768,128]{2,1,0:T(8,128)(2,1)S(1)} %all-to-all-done.5.part, f32[8,96]{1,0:T(8,128)S(1)} %get-tuple-element.59.final), custom_call_target="tpu_custom_call" | custom-call | flops 1048576 | bytes 4194304 | tf_op jit(solution)/shard_map/unpack/pallas_call | solution.py:515
  173.0 4.3 %unpack.3 = (f32[27,192,96]{2,1,0:T(8,128)}, f32[27,96,96]{2,1,0:T(8,128)}) custom-call(s32[1]{0:T(128)S(6)} %sub.3.half, bf16[4,768,128]{2,1,0:T(8,128)(2,1)S(1)} %collective-permute-done.7.part, f32[8,96]{1,0:T(8,128)S(1)} %get-tuple-element.59.final, f32[27,192,96]{2,1,0:T(8,128)} %get-tuple-element.64.rest_0_, ...), custom_call_target="tpu_custom_call", output_to_operand_aliasing={{0}: (3, {}), {1}: (4, {})} | custom-call | flops 1048576 | bytes 4194304 | tf_op jit(solution)/shard_map/unpack/pallas_call | solution.py:515
  (43 shorter events, 11.6 us)
Async XLA Ops:
  0.6 7.3 %collective-permute-start.1 = (bf16[2,4,32,96]{3,2,1,0:T(8,128)(2,1)}, bf16[2,4,32,96]{3,2,1,0:T(8,128)(2,1)S(1)}, u32[]{:S(2)}, u32[]{:S(2)}) collective-permute-start(bf16[2,4,32,96]{3,2,1,0:T(8,128)(2,1)} %cot.5), channel_id=1, source_target_pairs={{32,0},{64,32},{96,64},{128,96},{160,128},{192,160},{224,192},{256... | collective-permute-start | bytes 147464 | tf_op jit(solution)/shard_map/ppermute | solution.py:32
  1.9 6.0 %collective-permute-start = (bf16[2,2,16,192]{3,2,1,0:T(8,128)(2,1)}, bf16[2,2,16,192]{3,2,1,0:T(8,128)(2,1)S(1)}, u32[]{:S(2)}, u32[]{:S(2)}) collective-permute-start(bf16[2,2,16,192]{3,2,1,0:T(8,128)(2,1)} %features.5), channel_id=1, source_target_pairs={{0,32},{32,64},{64,96},{96,128},{128,160},{160,192},{192,224},{224... | collective-permute-start | bytes 73736 | tf_op jit(solution)/shard_map/ppermute | solution.py:32
  7.9 0.8 copy-start.2
  8.7 0.8 copy-start.5
  9.5 26.3 %copy-start.7 = (bf16[2,4,32,96]{3,2,1,0:T(8,128)(2,1)S(1)}, bf16[2,4,32,96]{3,2,1,0:T(8,128)(2,1)}, u32[]{:S(2)}) copy-start(bf16[2,4,32,96]{3,2,1,0:T(8,128)(2,1)} %cot.5) | copy-start | bytes 147460
  9.6 10.6 %collective-permute-start.2 = (bf16[4,48,192]{2,1,0:T(8,128)(2,1)S(1)}, bf16[4,48,192]{2,1,0:T(8,128)(2,1)S(1)}, u32[]{:S(2)}, u32[]{:S(2)}) collective-permute-start(bf16[4,48,192]{2,1,0:T(8,128)(2,1)S(1)} %get-tuple-element.36), channel_id=1, source_target_pairs={{0,1},{1,2},{2,3},{3,4},{4,5},{5,6},{6,7},{7,8},{8,9},{9,10},{10,1... | collective-permute-start | bytes 221192 | tf_op jit(solution)/shard_map/ppermute | solution.py:32
  14.6 6.5 %collective-permute-start.3 = (bf16[4,48,192]{2,1,0:T(8,128)(2,1)S(1)}, bf16[4,48,192]{2,1,0:T(8,128)(2,1)S(1)}, u32[]{:S(2)}, u32[]{:S(2)}) collective-permute-start(bf16[4,48,192]{2,1,0:T(8,128)(2,1)S(1)} %get-tuple-element.37), channel_id=1, source_target_pairs={{1,0},{2,1},{3,2},{4,3},{5,4},{6,5},{7,6},{8,7},{9,8},{10,9},{11,1... | collective-permute-start | bytes 221192 | tf_op jit(solution)/shard_map/ppermute | solution.py:32
  21.1 1.3 copy-start
  22.4 0.8 copy-start.3
  23.2 0.8 copy-start.6
  24.0 11.8 %copy-start.10 = (bf16[3,3,3,96,96]{4,3,2,1,0:T(8,128)(2,1)S(1)}, bf16[3,3,3,96,96]{4,3,2,1,0:T(8,128)(2,1)}, u32[]{:S(2)}) copy-start(bf16[3,3,3,96,96]{4,3,2,1,0:T(8,128)(2,1)} %weight.4) | copy-start | bytes 1492996
  25.6 18.0 %all-to-all-start = ((f32[32,4,96]{2,1,0:T(4,128)}), f32[32,4,96]{2,1,0:T(4,128)S(1)}, u32[]{:S(2)}, u32[]{:S(2)}) async-start(f32[32,4,96]{2,1,0:T(4,128)} %get-tuple-element.38), calls=%async_computation | async-start | bytes 131072 | tf_op jit(solution)/shard_map/all_to_all | solution.py:588
  35.9 35.8 %copy-start.8 = (f32[96]{0:T(128)S(1)}, f32[96]{0:T(128)}, u32[]{:S(2)}) copy-start(f32[96]{0:T(128)} %param.10) | copy-start | bytes 1156
  35.9 35.8 %copy-start.9 = (f32[96]{0:T(128)S(1)}, f32[96]{0:T(128)}, u32[]{:S(2)}) copy-start(f32[96]{0:T(128)} %param.11) | copy-start | bytes 1156
  36.9 36.4 %copy-start.4 = (bf16[2,2,16,192]{3,2,1,0:T(8,128)(2,1)S(1)}, bf16[2,2,16,192]{3,2,1,0:T(8,128)(2,1)}, u32[]{:S(2)}) copy-start(bf16[2,2,16,192]{3,2,1,0:T(8,128)(2,1)} %features.5) | copy-start | bytes 73732
  44.3 27.4 %all-to-all-start.1 = ((f32[16,4,96]{2,1,0:T(4,128)}), f32[16,4,96]{2,1,0:T(4,128)S(1)}, u32[]{:S(2)}, u32[]{:S(2)}) async-start(f32[16,4,96]{2,1,0:T(4,128)} %broadcast_in_dim.14), calls=%async_computation.1 | async-start | bytes 65536 | tf_op jit(solution)/shard_map/all_to_all | solution.py:588
  75.2 6.8 %collective-permute-start.4 = (bf16[4,3,512,128]{3,2,1,0:T(8,128)(2,1)S(1)}, bf16[4,3,512,128]{3,2,1,0:T(8,128)(2,1)S(1)}, u32[]{:S(2)}, u32[]{:S(2)}) collective-permute-start(bf16[4,3,512,128]{3,2,1,0:T(8,128)(2,1)S(1)} %get-tuple-element.51), channel_id=1, source_target_pairs={{0,1},{1,0},{2,3},{3,2},{4,5},{5,4},{6,7},{7,6},{8,9},{9,8},{10,11... | collective-permute-start | bytes 4718600 | tf_op jit(solution)/shard_map/ppermute | solution.py:614
  83.4 24.0 %all-to-all-start.2 = ((bf16[4,3,512,128]{3,2,1,0:T(8,128)(2,1)}), bf16[4,3,512,128]{3,2,1,0:T(8,128)(2,1)S(1)}, u32[]{:S(2)}, u32[]{:S(2)}) async-start(bf16[4,3,512,128]{3,2,1,0:T(8,128)(2,1)} %add_pair.1), calls=%async_computation.2 | async-start | bytes 3145728 | tf_op jit(solution)/shard_map/all_to_all | solution.py:588
  87.0 21.4 %collective-permute-start.5 = (bf16[2,6,32,96]{3,2,1,0:T(8,128)(2,1)S(1)}, bf16[2,6,32,96]{3,2,1,0:T(8,128)(2,1)S(1)}, u32[]{:S(2)}, u32[]{:S(2)}) collective-permute-start(bf16[2,6,32,96]{3,2,1,0:T(8,128)(2,1)S(1)} %get-tuple-element.53.hidden), channel_id=1, source_target_pairs={{0,32},{32,64},{64,96},{96,128},{128,160},{160,192},{192,224},{224... | collective-permute-start | bytes 221192 | tf_op jit(solution)/shard_map/ppermute | solution.py:32
  108.4 19.4 %all-to-all-start.3 = ((bf16[64,1,3,8,128]{4,3,2,1,0:T(8,128)(2,1)}), bf16[64,1,3,8,128]{4,3,2,1,0:T(8,128)(2,1)S(1)}, u32[]{:S(2)}, u32[]{:S(2)}) async-start(bf16[64,1,3,8,128]{4,3,2,1,0:T(8,128)(2,1)} %bitcast.6), calls=%async_computation.3 | async-start | bytes 786432 | tf_op jit(solution)/shard_map/all_to_all | solution.py:588
  129.7 19.2 %all-to-all-start.4 = ((bf16[64,1,12,128]{3,2,1,0:T(8,128)(2,1)}), bf16[64,1,12,128]{3,2,1,0:T(8,128)(2,1)S(1)}, u32[]{:S(2)}, u32[]{:S(2)}) async-start(bf16[64,1,12,128]{3,2,1,0:T(8,128)(2,1)} %broadcast_in_dim.34), calls=%async_computation.4 | async-start | bytes 524288 | tf_op jit(solution)/shard_map/all_to_all | solution.py:588
  136.9 7.7 %collective-permute-start.6 = (bf16[2,6,32,96]{3,2,1,0:T(8,128)(2,1)S(1)}, bf16[2,6,32,96]{3,2,1,0:T(8,128)(2,1)S(1)}, u32[]{:S(2)}, u32[]{:S(2)}) collective-permute-start(bf16[2,6,32,96]{3,2,1,0:T(8,128)(2,1)S(1)} %grad_pre.1), channel_id=1, source_target_pairs={{32,0},{64,32},{96,64},{128,96},{160,128},{192,160},{224,192},{256... | collective-permute-start | bytes 221192 | tf_op jit(solution)/shard_map/ppermute | solution.py:32
  148.9 4.5 %copy-start.1 = (bf16[3,3,3,192,96]{4,3,2,1,0:T(8,128)(2,1)S(1)}, bf16[3,3,3,192,96]{4,3,2,1,0:T(8,128)(2,1)}, u32[]{:S(2)}) copy-start(bf16[3,3,3,192,96]{4,3,2,1,0:T(8,128)(2,1)} %weight.5) | copy-start | bytes 2985988
  149.9 11.9 %all-to-all-start.5 = ((bf16[4,768,128]{2,1,0:T(8,128)(2,1)}), bf16[4,768,128]{2,1,0:T(8,128)(2,1)S(1)}, u32[]{:S(2)}, u32[]{:S(2)}) async-start(bf16[4,768,128]{2,1,0:T(8,128)(2,1)} %broadcast_in_dim.35), calls=%async_computation.5 | async-start | bytes 1572864 | tf_op jit(solution)/shard_map/all_to_all | solution.py:588
  161.9 11.1 %collective-permute-start.7 = (bf16[4,768,128]{2,1,0:T(8,128)(2,1)S(1)}, bf16[4,768,128]{2,1,0:T(8,128)(2,1)S(1)}, u32[]{:S(2)}, u32[]{:S(2)}) collective-permute-start(bf16[4,768,128]{2,1,0:T(8,128)(2,1)S(1)} %all-to-all-done.5.part), channel_id=1, source_target_pairs={{0,1},{1,0},{2,3},{3,2},{4,5},{5,4},{6,7},{7,6},{8,9},{9,8},{10,11... | collective-permute-start | bytes 2359304 | tf_op jit(solution)/shard_map/ppermute | solution.py:633

commit v6 on v5

--- a/solution.py
+++ b/solution.py
@@ -64,6 +64,28 @@
     last = field.shape[1] - 1
     out = ((row == 0) & (where[1] == 1)) | ((row == last) & (where[2] == 1))
     return jnp.where(out, 0.0, field)
+
+
+def resident_kernel(*refs):
+    sources, copies, sems = refs[:4], refs[4:8], refs[8]
+    moves = [pltpu.make_async_copy(sources[k], copies[k], sems.at[k]) for k in range(4)]
+    for move in moves:
+        move.start()
+    for move in moves:
+        move.wait()
+
+
+def resident(*arrays):
+    return pl.pallas_call(
+        resident_kernel,
+        out_shape=[jax.ShapeDtypeStruct(k.shape, k.dtype) for k in arrays],
+        in_specs=whole(4, pltpu.HBM),
+        out_specs=whole(4),
+        scratch_shapes=[pltpu.SemaphoreType.DMA((4,))],
+        compiler_params=pltpu.CompilerParams(vmem_limit_bytes=VMEM_LIMIT),
+        cost_estimate=pl.CostEstimate(flops=0, bytes_accessed=2**22, transcendentals=0),
+        name="resident",
+    )(*arrays)
 
 
 def edges_kernel(cache, features, cot, later, downward, upward):
@@ -290,20 +312,22 @@
     )
 
 
-def with_sums(tiles, sums):
+def in_parts(sums, rows):
     high = sums.astype(jnp.bfloat16).astype(jnp.float32)
     middle = (sums - high).astype(jnp.bfloat16).astype(jnp.float32)
     low = sums - high - middle
-    row = lax.broadcasted_iota(jnp.int32, (8, 128), 0)
-    lane = lax.broadcasted_iota(jnp.int32, (8, 128), 1)
-    parts = jnp.where(row == 0, high, jnp.where(row == 1, middle, jnp.where(row == 2, low, 0.0)))
-    return jnp.where((lane < 64)[None], tiles, parts[None])
+    row = lax.broadcasted_iota(jnp.int32, (rows, 128), 0)
+    return jnp.where(row == 0, high, jnp.where(row == 1, middle, jnp.where(row == 2, low, 0.0)))
+
+
+def sums_of(tile):
+    return tile[0:1] + tile[1:2] + tile[2:3]
 
 
 def weight_grads_kernel(where, cache, features, above, below, grad_normed, normed, vectors, two, away, kept, wide):
     frames, rows, cols, outs = grad_normed.shape
     rows, half = rows - 2, cols // 2
-    ins, mids, pieces, part_rows = features.shape[-1], two.shape[1], kept.shape[0], kept.shape[2]
+    ins, mids, pieces, part_rows = features.shape[-1], two.shape[1], kept.shape[0], (kept.shape[1] - 16) * 2 // 5
     timed = jnp.concatenate([cache[...], features[...]], 0)
     rows_in = jnp.concatenate([above[:, :half][:, None], timed, below[:, :half][:, None]], 1)
     rstd, f0, s0 = (vectors[k : k + 1] for k in range(3))
@@ -337,11 +361,12 @@
     counts = jnp.where(tap < 9, in_rows * in_cols, 0.0).astype(jnp.bfloat16)
 
     def write(part, at, low, high):
+        deep = part_rows if part < 2 else part_rows // 2
         while low.shape[0]:
-            x, row = at // part_rows, at % part_rows
-            n = min(low.shape[0], part_rows - row)
-            away[x, part, row : row + n] = jnp.where(lower, high[:n], low[:n]).astype(jnp.bfloat16)
-            kept[x, part, row : row + n] = jnp.where(lower, low[:n], high[:n])
+            x, row = at // deep, part_rows * part + at % deep
+            n = min(low.shape[0], deep - at % deep)
+            away[x, row : row + n] = jnp.where(lower, high[:n], low[:n]).astype(jnp.bfloat16)
+            kept[x, row : row + n] = jnp.where(lower, low[:n], high[:n])
             low, high, at = low[n:], high[n:], at + n
 
     for part, field, last in ((0, grad, counts), (1, own * rstd, jnp.zeros_like(counts))):
@@ -363,24 +388,23 @@
 
     sums = exact(vectors[3:4], group_lanes(outs, True), ((1,), (0,)))
     sums += exact(vectors[4:5], group_lanes(outs, False), ((1,), (0,)))
-    blocks = [two[a, :, 128 * j : 128 * j + 128] for a in range(3) for j in range(7)]
-    nothing = [jnp.zeros((pieces * part_rows // 2 - 21 * mids // 2, 128), jnp.float32)]
-    halves = [jnp.concatenate([k[i : i + mids // 2] for k in blocks] + nothing, 0) for i in (0, mids // 2)]
-    row = lax.broadcasted_iota(jnp.int32, (1, 8, 128), 1)
-    tiled = []
-    for half_rows in halves:
-        tiles = half_rows.reshape(-1, 8, 128)
-        turned = jnp.concatenate([tiles[:, 4:], tiles[:, :4]], 1)
-        swap = lambda k: jnp.concatenate([k[..., 64:], k[..., :64]], 2)
-        even = jnp.where(row < 4, tiles, swap(turned))
-        odd = jnp.where(row < 4, turned, swap(tiles))
-        tiled.append(with_sums(jnp.stack([even, odd], 1).reshape(-1, 8, 128), sums).reshape(-1, 128))
-    write(2, 0, *tiled)
+    sums = in_parts(sums, 16)
+    at = 0
+    for a in range(3):
+        for j in range(7):
+            block = two[a, :, 128 * j : 128 * j + 128]
+            write(2, at, block[: mids // 2], block[mids // 2 :])
+            at += mids // 2
+    nothing = jnp.zeros((pieces * part_rows // 2 - at, 128), jnp.float32)
+    write(2, at, nothing, nothing)
+    for x in range(pieces):
+        away[x, part_rows * 5 // 2 :] = sums.astype(jnp.bfloat16)
+        kept[x, part_rows * 5 // 2 :] = sums
 
 
 def weight_grads(where, cache, features, above, below, grad_normed, normed, vectors, two, pieces, part_rows):
     frames, rows, cols, _ = grad_normed.shape
-    shape = (pieces, 3, part_rows, 128)
+    shape = (pieces, part_rows * 5 // 2 + 16, 128)
     return pl.pallas_call(
         weight_grads_kernel,
         out_shape=(jax.ShapeDtypeStruct(shape, jnp.bfloat16), jax.ShapeDtypeStruct(shape, jnp.float32)),
@@ -392,16 +416,12 @@
     )(where, cache, features, above, below, grad_normed, normed, vectors, two)
 
 
-def sums_of(tile):
-    return tile[0:1] + tile[1:2] + tile[2:3]
-
-
 def add_pair_kernel(kept, came, out):
     total = kept[...] + came[...].astype(jnp.float32)
-    out[:, :2] = total[:, :2].astype(jnp.bfloat16)
-    tiles = total[:, 2].reshape(-1, 8, 128)
-    tiles = with_sums(tiles, sums_of(tiles[0]))
-    out[:, 2] = tiles.astype(jnp.bfloat16).reshape(out.shape[0], -1, 128)
+    out[...] = total.astype(jnp.bfloat16)
+    sums = in_parts(sums_of(total[0, -16:]), 16).astype(jnp.bfloat16)
+    for x in range(out.shape[0]):
+        out[x, out.shape[1] - 16 :] = sums
 
 
 def add_pair(kept, came):
@@ -417,17 +437,26 @@
 
 def add_row_kernel(came, out):
     total = jnp.sum(came[...].astype(jnp.float32), 0)
-    for part in range(3):
-        tiles = total[part].reshape(-1, 8, 128)
-        if part == 2:
-            tiles = with_sums(tiles, sums_of(tiles[0]))
-        out[:, part] = tiles.astype(jnp.bfloat16)
+    n = out.shape[0] * 8
+    out[:, 0] = total[:n].astype(jnp.bfloat16).reshape(-1, 8, 128)
+    out[:, 1] = total[n : 2 * n].astype(jnp.bfloat16).reshape(-1, 8, 128)
+    tiles = total[2 * n : n * 5 // 2].reshape(-1, 8, 128)
+    row = lax.broadcasted_iota(jnp.int32, (1, 8, 128), 1)
+    lane = lax.broadcasted_iota(jnp.int32, (1, 8, 128), 2)
+    turned = jnp.concatenate([tiles[:, 4:], tiles[:, :4]], 1)
+    swap = lambda k: jnp.concatenate([k[..., 64:], k[..., :64]], 2)
+    even = jnp.where(row < 4, tiles, swap(turned))
+    odd = jnp.where(row < 4, turned, swap(tiles))
+    both = jnp.stack([even, odd], 1).reshape(-1, 8, 128)
+    sums = in_parts(sums_of(total[n * 5 // 2 :]), 8)
+    out[:, 2] = jnp.where(lane < 64, both, sums[None]).astype(jnp.bfloat16)
 
 
 def add_row(came):
+    tiles = (came.shape[1] - 16) // 20
     return pl.pallas_call(
         add_row_kernel,
-        out_shape=jax.ShapeDtypeStruct((came.shape[2] // 8, 3, 8, 128), jnp.bfloat16),
+        out_shape=jax.ShapeDtypeStruct((tiles, 3, 8, 128), jnp.bfloat16),
         in_specs=whole(1),
         out_specs=whole()[0],
         compiler_params=pltpu.CompilerParams(vmem_limit_bytes=VMEM_LIMIT),
@@ -492,23 +521,31 @@
 def unpack_kernel(scale, half, part, final, *rest):
     one, two, flat = rest[-3:]
     pieces, rows = part.shape[0], part.shape[1]
-    for x in range(pieces):
-        flat[rows * 2 // 3 * x : rows * 2 // 3 * (x + 1)] = part[x, : rows * 2 // 3]
-        at = pieces * (rows * 2 // 3) + rows // 3 * x
-        flat[at : at + rows // 3] = part[x, rows * 2 // 3 :]
-    at = 0
-    for out in (one, two):
+    split = rows * 2 // 3
+    step = pl.program_id(0)
+
+    @pl.when(step == 0)
+    def _():
+        for x in range(pieces):
+            flat[split * x : split * (x + 1)] = part[x, :split]
+            at = pieces * split + (rows - split) * x
+            flat[at : at + rows - split] = part[x, split:]
+
+    for out, begin in ((one, 0), (two, pieces * split)):
         taps, channels, outs = out.shape
-        for a in range(3):
-            blocks = [flat[at + channels * j : at + channels * j + channels] for j in range(7)]
-            lanes = jnp.concatenate(blocks, 1).astype(jnp.float32) * scale
-            for k in range(9):
-                grad = lanes[:, outs * k : outs * k + outs]
-                if out is one:
-                    grad = grad - lanes[:, 9 * outs + k : 9 * outs + k + 1] * final[2:3]
-                out[9 * a + k] = grad
-            at += 7 * channels
-        at = pieces * (rows * 2 // 3)
+        blocks = []
+        for j in range(7):
+            at = pl.multiple_of(begin + (step * 7 + j) * channels, 16)
+            blocks.append(flat[pl.ds(at, channels)].astype(jnp.float32))
+        lanes = jnp.concatenate(blocks, 1) * scale
+        if out is one:
+            change = jnp.concatenate([final[2:3]] * taps + [jnp.zeros((1, 32), jnp.float32)], 1)
+            tap = lax.broadcasted_iota(jnp.int32, (32, change.shape[1]), 0)
+            lane = lax.broadcasted_iota(jnp.int32, (32, change.shape[1]), 1)
+            change = jnp.where(lane // outs == tap, change, 0.0)
+            lanes -= exact(lanes[:, outs * taps :], change, ((1,), (0,)))
+        for k in range(taps):
+            out[k] = lanes[:, outs * k : outs * k + outs]
 
 
 def unpack(half, part, final, ins, mids, scale, begun=()):
@@ -516,11 +553,11 @@
         functools.partial(unpack_kernel, scale),
         grid_spec=pltpu.PrefetchScalarGridSpec(
             num_scalar_prefetch=1,
-            grid=(1,),
+            grid=(3,),
             in_specs=whole(2) + whole(len(begun), pl.ANY),
             out_specs=[
-                pl.BlockSpec((27, ins // 2, mids), lambda a, half: (0, half[0], 0)),
-                pl.BlockSpec((27, mids // 2, mids), lambda a, half: (0, half[0], 0)),
+                pl.BlockSpec((9, ins // 2, mids), lambda a, half: (a, half[0], 0)),
+                pl.BlockSpec((9, mids // 2, mids), lambda a, half: (a, half[0], 0)),
             ],
             scratch_shapes=[pltpu.VMEM((part.shape[0] * part.shape[1], 128), jnp.bfloat16)],
         ),
@@ -593,6 +630,7 @@
     cache = neighbour(features, TM, 1)
     later = neighbour(cotangent, TM, -1)
 
+    features, cotangent, weight_one, weight_two = resident(features, cotangent, weight_one, weight_two)
     downward, upward = edges(cache, features, cotangent, later)
     above = neighbour(downward, HEIGHT, 1)
     below = neighbour(upward, HEIGHT, -1)

time: 178 us -> 168 us (0.944)
  waiting for transfers between devices: 70.9 us -> 64.7 us
  Pallas kernels: 20.5 us -> 16.6 us
  starting transfers between devices: 75.6 us -> 72.3 us
  local copies, waits for them, and re-layouts: 7.57 us -> 10.1 us
    all_to_all x6, waiting for transfers between devices: 59.3 us -> 54.7 us  [exchange(): return lax.all_to_all(copies, axes, 0, 0)]
    pallas_call x2, Pallas kernels: 8.52 us -> 5.86 us  [unpack(): pl.pallas_call(functools.partial(unpack_kernel, scale), grid_spec=pltpu.P...]
    all_to_all x6, starting transfers between devices: 44.7 us -> 42.2 us  [exchange(): return lax.all_to_all(copies, axes, 0, 0)]
    unnamed x23 -> x21, local copies, waits for them, and re-layouts: 5.19 us -> 7.72 us
  transfers between devices with their start and end apart: 14 -> 14, of which waited for: 10 -> 9; matrix products, arithmetic and copies ran while one was open for 1% -> 2% of each run, Pallas kernels for 5% -> 5%
where the time goes in v6:
time: 168 us; the launch traced here: 167 us
  starting transfers between devices  72.3 us (43%)
  waiting for transfers between devices  64.7 us (39%)
  Pallas kernels  16.6 us (10%)
  local copies, waits for them, and re-layouts  10.1 us (6%)
  matrix products  2.6 us (2%)
    all_to_all x6, waiting for transfers between devices, exchange(): return lax.all_to_all(copies, axes, 0, 0)  54.7 us
    all_to_all x6, starting transfers between devices, exchange(): return lax.all_to_all(copies, axes, 0, 0)  42.2 us
    ppermute x6, starting transfers between devices, neighbour(): lax.ppermute(value, axis, [(i, i + steps) for i in range(first, last)])  19.7 us
    unnamed x21, local copies, waits for them, and re-layouts  7.72 us
    ppermute x6, waiting for transfers between devices, neighbour(): lax.ppermute(value, axis, [(i, i + steps) for i in range(first, last)])  7.34 us
    ppermute x1, starting transfers between devices, body(): other = lax.ppermute(part, 'c', SWAP)  6.68 us
    pallas_call x2, Pallas kernels, unpack(): pl.pallas_call(functools.partial(unpack_kernel, scale), grid_spec=pltpu.P...  5.86 us
    ppermute x1, starting transfers between devices, body(): part = add_pair(kept, lax.ppermute(away, 'c', SWAP))  3.73 us
  transfers between devices with their start and end apart: 14, of which 9 were waited for; matrix products, arithmetic and copies ran while one was open for 2% of the time, Pallas kernels for 5%

profile of v6, /device:TPU:1, one launch (start us, length us, event | category | flops | bytes accessed | tf_op | source)
XLA Modules:
  0.0 167.5 jit_solution(17785034607339135550)
XLA Ops:
  0.6 1.3 collective-permute-start.1
  1.9 4.7 %collective-permute-start = (bf16[2,2,16,192]{3,2,1,0:T(8,128)(2,1)}, bf16[2,2,16,192]{3,2,1,0:T(8,128)(2,1)S(1)}, u32[]{:S(2)}, u32[]{:S(2)}) collective-permute-start(bf16[2,2,16,192]{3,2,1,0:T(8,128)(2,1)} %refs_0_.1), channel_id=1, source_target_pairs={{0,32},{32,64},{64,96},{96,128},{128,160},{160,192},{192,224},{224... | collective-permute-start | bytes 73736 | tf_op jit(solution)/shard_map/ppermute | solution.py:32
  6.6 1.3 copy-done.1
  7.9 1.1 copy-done.2
  11.2 4.4 %collective-permute-start.2 = (bf16[4,48,192]{2,1,0:T(8,128)(2,1)S(1)}, bf16[4,48,192]{2,1,0:T(8,128)(2,1)S(1)}, u32[]{:S(2)}, u32[]{:S(2)}) collective-permute-start(bf16[4,48,192]{2,1,0:T(8,128)(2,1)S(1)} %get-tuple-element.42), channel_id=1, source_target_pairs={{0,1},{1,2},{2,3},{3,4},{4,5},{5,6},{6,7},{7,8},{8,9},{9,10},{10,1... | collective-permute-start | bytes 221192 | tf_op jit(solution)/shard_map/ppermute | solution.py:32
  15.6 5.6 %collective-permute-start.3 = (bf16[4,48,192]{2,1,0:T(8,128)(2,1)S(1)}, bf16[4,48,192]{2,1,0:T(8,128)(2,1)S(1)}, u32[]{:S(2)}, u32[]{:S(2)}) collective-permute-start(bf16[4,48,192]{2,1,0:T(8,128)(2,1)S(1)} %get-tuple-element.43), channel_id=1, source_target_pairs={{1,0},{2,1},{3,2},{4,3},{5,4},{6,5},{7,6},{8,7},{9,8},{10,9},{11,1... | collective-permute-start | bytes 221192 | tf_op jit(solution)/shard_map/ppermute | solution.py:32
  22.1 1.6 conv_one.1
  23.7 10.3 %all-to-all-start = ((f32[32,4,96]{2,1,0:T(4,128)}), f32[32,4,96]{2,1,0:T(4,128)S(1)}, u32[]{:S(2)}, u32[]{:S(2)}) async-start(f32[32,4,96]{2,1,0:T(4,128)} %get-tuple-element.45), calls=%async_computation | async-start | bytes 131072 | tf_op jit(solution)/shard_map/all_to_all | solution.py:625
  35.8 5.8 %all-to-all-done = f32[32,4,96]{2,1,0:T(4,128)S(1)} async-done(((f32[32,4,96]{2,1,0:T(4,128)}), f32[32,4,96]{2,1,0:T(4,128)S(1)}, u32[]{:S(2)}, u32[]{:S(2)}) %all-to-all-start) | async-done | bytes 49184 | tf_op jit(solution)/shard_map/all_to_all | solution.py:625
  42.3 13.6 %all-to-all-start.1 = ((f32[16,4,96]{2,1,0:T(4,128)}), f32[16,4,96]{2,1,0:T(4,128)S(1)}, u32[]{:S(2)}, u32[]{:S(2)}) async-start(f32[16,4,96]{2,1,0:T(4,128)} %broadcast_in_dim.14), calls=%async_computation.1 | async-start | bytes 65536 | tf_op jit(solution)/shard_map/all_to_all | solution.py:625
  56.0 11.2 %all-to-all-done.1.came = f32[16,4,96]{2,1,0:T(4,128)S(1)} async-done(((f32[16,4,96]{2,1,0:T(4,128)}), f32[16,4,96]{2,1,0:T(4,128)S(1)}, u32[]{:S(2)}, u32[]{:S(2)}) %all-to-all-start.1) | async-done | bytes 24608 | tf_op jit(solution)/shard_map/all_to_all | solution.py:625
  68.2 1.1 copy-done.9
  69.9 1.5 weight_grads.1
  71.4 3.7 %collective-permute-start.4 = (bf16[4,1296,128]{2,1,0:T(8,128)(2,1)S(1)}, bf16[4,1296,128]{2,1,0:T(8,128)(2,1)S(1)}, u32[]{:S(2)}, u32[]{:S(2)}) collective-permute-start(bf16[4,1296,128]{2,1,0:T(8,128)(2,1)S(1)} %get-tuple-element.59), channel_id=1, source_target_pairs={{0,1},{1,0},{2,3},{3,2},{4,5},{5,4},{6,7},{7,6},{8,9},{9,8},{10,11... | collective-permute-start | bytes 3981320 | tf_op jit(solution)/shard_map/ppermute | solution.py:652
  75.1 2.7 %collective-permute-done.4.came = bf16[4,1296,128]{2,1,0:T(8,128)(2,1)S(1)} collective-permute-done((bf16[4,1296,128]{2,1,0:T(8,128)(2,1)S(1)}, bf16[4,1296,128]{2,1,0:T(8,128)(2,1)S(1)}, u32[]{:S(2)}, u32[]{:S(2)}) %collective-permute-start.4) | collective-permute-done | bytes 1327136 | tf_op jit(solution)/shard_map/ppermute | solution.py:652
  79.1 3.5 %all-to-all-start.2 = ((bf16[4,1296,128]{2,1,0:T(8,128)(2,1)}), bf16[4,1296,128]{2,1,0:T(8,128)(2,1)S(1)}, u32[]{:S(2)}, u32[]{:S(2)}) async-start(bf16[4,1296,128]{2,1,0:T(8,128)(2,1)} %copy-done), calls=%async_computation.2 | async-start | bytes 2654208 | tf_op jit(solution)/shard_map/all_to_all | solution.py:625
  82.6 2.4 %collective-permute-start.5 = (bf16[2,6,32,96]{3,2,1,0:T(8,128)(2,1)S(1)}, bf16[2,6,32,96]{3,2,1,0:T(8,128)(2,1)S(1)}, u32[]{:S(2)}, u32[]{:S(2)}) collective-permute-start(bf16[2,6,32,96]{3,2,1,0:T(8,128)(2,1)S(1)} %get-tuple-element.61.hidden), channel_id=1, source_target_pairs={{0,32},{32,64},{64,96},{96,128},{128,160},{160,192},{192,224},{224... | collective-permute-start | bytes 221192 | tf_op jit(solution)/shard_map/ppermute | solution.py:32
  85.1 15.4 %all-to-all-done.2.came = bf16[4,1296,128]{2,1,0:T(8,128)(2,1)S(1)} async-done(((bf16[4,1296,128]{2,1,0:T(8,128)(2,1)}), bf16[4,1296,128]{2,1,0:T(8,128)(2,1)S(1)}, u32[]{:S(2)}, u32[]{:S(2)}) %all-to-all-start.2) | async-done | bytes 1327136 | tf_op jit(solution)/shard_map/all_to_all | solution.py:625
  101.5 4.6 %all-to-all-start.3 = ((bf16[64,1,3,8,128]{4,3,2,1,0:T(8,128)(2,1)}), bf16[64,1,3,8,128]{4,3,2,1,0:T(8,128)(2,1)S(1)}, u32[]{:S(2)}, u32[]{:S(2)}) async-start(bf16[64,1,3,8,128]{4,3,2,1,0:T(8,128)(2,1)} %bitcast.6), calls=%async_computation.3 | async-start | bytes 786432 | tf_op jit(solution)/shard_map/all_to_all | solution.py:625
  106.2 2.6 %convolution_convert_fusion = bf16[1,2,4,32,96]{4,0,3,2,1:T(2,128)(2,1)S(1)} fusion(bf16[3,3,3,96,96]{4,3,2,1,0:T(8,128)(2,1)} %copy-done.7, bf16[1,4,6,34,96]{4,3,2,1,0:T(8,128)(2,1)S(1)} %fusion.5), kind=kOutput, calls=%fused_computation | convolution fusion | flops 127426560 | bytes 703488 | tf_op jit(solution)/shard_map/conv_general_dilated | solution.py:36
  109.5 11.4 %all-to-all-done.3.came = bf16[64,1,3,8,128]{4,3,2,1,0:T(8,128)(2,1)S(1)} async-done(((bf16[64,1,3,8,128]{4,3,2,1,0:T(8,128)(2,1)}), bf16[64,1,3,8,128]{4,3,2,1,0:T(8,128)(2,1)S(1)}, u32[]{:S(2)}, u32[]{:S(2)}) %all-to-all-start.3) | async-done | bytes 393248 | tf_op jit(solution)/shard_map/all_to_all | solution.py:625
  120.9 1.1 combine.1
  122.8 6.7 %all-to-all-start.4 = ((bf16[64,1,12,128]{3,2,1,0:T(8,128)(2,1)}), bf16[64,1,12,128]{3,2,1,0:T(8,128)(2,1)S(1)}, u32[]{:S(2)}, u32[]{:S(2)}) async-start(bf16[64,1,12,128]{3,2,1,0:T(8,128)(2,1)} %broadcast_in_dim.34), calls=%async_computation.4 | async-start | bytes 524288 | tf_op jit(solution)/shard_map/all_to_all | solution.py:625
  130.0 1.3 collective-permute-start.6
  131.3 6.4 %collective-permute-done.6 = bf16[2,6,32,96]{3,2,1,0:T(8,128)(2,1)S(1)} collective-permute-done((bf16[2,6,32,96]{3,2,1,0:T(8,128)(2,1)S(1)}, bf16[2,6,32,96]{3,2,1,0:T(8,128)(2,1)S(1)}, u32[]{:S(2)}, u32[]{:S(2)}) %collective-permute-start.6) | collective-permute-done | bytes 73760 | tf_op jit(solution)/shard_map/ppermute | solution.py:32
  137.8 4.2 %all-to-all-done.4 = bf16[64,1,12,128]{3,2,1,0:T(8,128)(2,1)S(1)} async-done(((bf16[64,1,12,128]{3,2,1,0:T(8,128)(2,1)}), bf16[64,1,12,128]{3,2,1,0:T(8,128)(2,1)S(1)}, u32[]{:S(2)}, u32[]{:S(2)}) %all-to-all-start.4) | async-done | bytes 196640 | tf_op jit(solution)/shard_map/all_to_all | solution.py:625
  143.0 3.5 %all-to-all-start.5 = ((bf16[4,768,128]{2,1,0:T(8,128)(2,1)}), bf16[4,768,128]{2,1,0:T(8,128)(2,1)S(1)}, u32[]{:S(2)}, u32[]{:S(2)}) async-start(bf16[4,768,128]{2,1,0:T(8,128)(2,1)} %broadcast_in_dim.35), calls=%async_computation.5 | async-start | bytes 1572864 | tf_op jit(solution)/shard_map/all_to_all | solution.py:625
  146.6 1.6 feature_grads.1
  148.2 6.7 %all-to-all-done.5.part = bf16[4,768,128]{2,1,0:T(8,128)(2,1)S(1)} async-done(((bf16[4,768,128]{2,1,0:T(8,128)(2,1)}), bf16[4,768,128]{2,1,0:T(8,128)(2,1)S(1)}, u32[]{:S(2)}, u32[]{:S(2)}) %all-to-all-start.5) | async-done | bytes 786464 | tf_op jit(solution)/shard_map/all_to_all | solution.py:625
  154.9 6.7 %collective-permute-start.7 = (bf16[4,768,128]{2,1,0:T(8,128)(2,1)S(1)}, bf16[4,768,128]{2,1,0:T(8,128)(2,1)S(1)}, u32[]{:S(2)}, u32[]{:S(2)}) collective-permute-start(bf16[4,768,128]{2,1,0:T(8,128)(2,1)S(1)} %all-to-all-done.5.part), channel_id=1, source_target_pairs={{0,1},{1,0},{2,3},{3,2},{4,5},{5,4},{6,7},{7,6},{8,9},{9,8},{10,11... | collective-permute-start | bytes 2359304 | tf_op jit(solution)/shard_map/ppermute | solution.py:671
  161.6 2.9 %unpack.2 = (f32[27,192,96]{2,1,0:T(8,128)}, f32[27,96,96]{2,1,0:T(8,128)}) custom-call(s32[1]{0:T(128)} %bitcast.half, bf16[4,768,128]{2,1,0:T(8,128)(2,1)S(1)} %all-to-all-done.5.part, f32[8,96]{1,0:T(8,128)S(1)} %get-tuple-element.67.final), custom_call_target="tpu_custom_call" | custom-call | flops 1048576 | bytes 4194304 | tf_op jit(solution)/shard_map/unpack/pallas_call | solution.py:552
  164.6 2.9 %unpack.3 = (f32[27,192,96]{2,1,0:T(8,128)}, f32[27,96,96]{2,1,0:T(8,128)}) custom-call(s32[1]{0:T(128)S(6)} %sub.3.half, bf16[4,768,128]{2,1,0:T(8,128)(2,1)S(1)} %collective-permute-done.7.part, f32[8,96]{1,0:T(8,128)S(1)} %get-tuple-element.67.final, f32[27,192,96]{2,1,0:T(8,128)} %get-tuple-element.72.rest_0_, ...), custom_call_target="tpu_custom_call", output_to_operand_aliasing={{0}: (3, {}), {1}: (4, {})} | custom-call | flops 1048576 | bytes 4194304 | tf_op jit(solution)/shard_map/unpack/pallas_call | solution.py:552
  (42 shorter events, 12.7 us)
Async XLA Ops:
  0.6 10.5 %collective-permute-start.1 = (bf16[2,4,32,96]{3,2,1,0:T(8,128)(2,1)}, bf16[2,4,32,96]{3,2,1,0:T(8,128)(2,1)S(1)}, u32[]{:S(2)}, u32[]{:S(2)}) collective-permute-start(bf16[2,4,32,96]{3,2,1,0:T(8,128)(2,1)} %refs_1_.1), channel_id=1, source_target_pairs={{32,0},{64,32},{96,64},{128,96},{160,128},{192,160},{224,192},{256... | collective-permute-start | bytes 147464 | tf_op jit(solution)/shard_map/ppermute | solution.py:32
  1.9 9.2 %collective-permute-start = (bf16[2,2,16,192]{3,2,1,0:T(8,128)(2,1)}, bf16[2,2,16,192]{3,2,1,0:T(8,128)(2,1)S(1)}, u32[]{:S(2)}, u32[]{:S(2)}) collective-permute-start(bf16[2,2,16,192]{3,2,1,0:T(8,128)(2,1)} %refs_0_.1), channel_id=1, source_target_pairs={{0,32},{32,64},{64,96},{96,128},{128,160},{160,192},{192,224},{224... | collective-permute-start | bytes 73736 | tf_op jit(solution)/shard_map/ppermute | solution.py:32
  6.6 1.3 copy-start.1
  7.9 1.1 copy-start.2
  9.0 0.8 copy-start.3
  9.9 0.8 copy-start.4
  11.1 56.2 %copy-start.7 = (bf16[3,3,3,96,96]{4,3,2,1,0:T(8,128)(2,1)}, bf16[3,3,3,96,96]{4,3,2,1,0:T(8,128)(2,1)S(1)}, u32[]{:S(2)}) copy-start(bf16[3,3,3,96,96]{4,3,2,1,0:T(8,128)(2,1)S(1)} %get-tuple-element.46.weight) | copy-start | bytes 1492996
  11.2 10.0 %collective-permute-start.2 = (bf16[4,48,192]{2,1,0:T(8,128)(2,1)S(1)}, bf16[4,48,192]{2,1,0:T(8,128)(2,1)S(1)}, u32[]{:S(2)}, u32[]{:S(2)}) collective-permute-start(bf16[4,48,192]{2,1,0:T(8,128)(2,1)S(1)} %get-tuple-element.42), channel_id=1, source_target_pairs={{0,1},{1,2},{2,3},{3,4},{4,5},{5,6},{6,7},{7,8},{8,9},{9,10},{10,1... | collective-permute-start | bytes 221192 | tf_op jit(solution)/shard_map/ppermute | solution.py:32
  15.6 6.5 %collective-permute-start.3 = (bf16[4,48,192]{2,1,0:T(8,128)(2,1)S(1)}, bf16[4,48,192]{2,1,0:T(8,128)(2,1)S(1)}, u32[]{:S(2)}, u32[]{:S(2)}) collective-permute-start(bf16[4,48,192]{2,1,0:T(8,128)(2,1)S(1)} %get-tuple-element.43), channel_id=1, source_target_pairs={{1,0},{2,1},{3,2},{4,3},{5,4},{6,5},{7,6},{8,7},{9,8},{10,9},{11,1... | collective-permute-start | bytes 221192 | tf_op jit(solution)/shard_map/ppermute | solution.py:32
  23.7 18.0 %all-to-all-start = ((f32[32,4,96]{2,1,0:T(4,128)}), f32[32,4,96]{2,1,0:T(4,128)S(1)}, u32[]{:S(2)}, u32[]{:S(2)}) async-start(f32[32,4,96]{2,1,0:T(4,128)} %get-tuple-element.45), calls=%async_computation | async-start | bytes 131072 | tf_op jit(solution)/shard_map/all_to_all | solution.py:625
  33.9 33.3 %copy-start.5 = (f32[96]{0:T(128)S(1)}, f32[96]{0:T(128)}, u32[]{:S(2)}) copy-start(f32[96]{0:T(128)} %param.10) | copy-start | bytes 1156
  33.9 33.3 %copy-start.6 = (f32[96]{0:T(128)S(1)}, f32[96]{0:T(128)}, u32[]{:S(2)}) copy-start(f32[96]{0:T(128)} %param.11) | copy-start | bytes 1156
  34.9 0.9 copy-start.8
  42.3 24.9 %all-to-all-start.1 = ((f32[16,4,96]{2,1,0:T(4,128)}), f32[16,4,96]{2,1,0:T(4,128)S(1)}, u32[]{:S(2)}, u32[]{:S(2)}) async-start(f32[16,4,96]{2,1,0:T(4,128)} %broadcast_in_dim.14), calls=%async_computation.1 | async-start | bytes 65536 | tf_op jit(solution)/shard_map/all_to_all | solution.py:625
  68.2 1.1 copy-start.9
  71.4 6.4 %collective-permute-start.4 = (bf16[4,1296,128]{2,1,0:T(8,128)(2,1)S(1)}, bf16[4,1296,128]{2,1,0:T(8,128)(2,1)S(1)}, u32[]{:S(2)}, u32[]{:S(2)}) collective-permute-start(bf16[4,1296,128]{2,1,0:T(8,128)(2,1)S(1)} %get-tuple-element.59), channel_id=1, source_target_pairs={{0,1},{1,0},{2,3},{3,2},{4,5},{5,4},{6,7},{7,6},{8,9},{9,8},{10,11... | collective-permute-start | bytes 3981320 | tf_op jit(solution)/shard_map/ppermute | solution.py:652
  78.0 1.1 copy-start
  79.1 21.3 %all-to-all-start.2 = ((bf16[4,1296,128]{2,1,0:T(8,128)(2,1)}), bf16[4,1296,128]{2,1,0:T(8,128)(2,1)S(1)}, u32[]{:S(2)}, u32[]{:S(2)}) async-start(bf16[4,1296,128]{2,1,0:T(8,128)(2,1)} %copy-done), calls=%async_computation.2 | async-start | bytes 2654208 | tf_op jit(solution)/shard_map/all_to_all | solution.py:625
  82.6 18.8 %collective-permute-start.5 = (bf16[2,6,32,96]{3,2,1,0:T(8,128)(2,1)S(1)}, bf16[2,6,32,96]{3,2,1,0:T(8,128)(2,1)S(1)}, u32[]{:S(2)}, u32[]{:S(2)}) collective-permute-start(bf16[2,6,32,96]{3,2,1,0:T(8,128)(2,1)S(1)} %get-tuple-element.61.hidden), channel_id=1, source_target_pairs={{0,32},{32,64},{64,96},{96,128},{128,160},{160,192},{192,224},{224... | collective-permute-start | bytes 221192 | tf_op jit(solution)/shard_map/ppermute | solution.py:32
  101.5 19.4 %all-to-all-start.3 = ((bf16[64,1,3,8,128]{4,3,2,1,0:T(8,128)(2,1)}), bf16[64,1,3,8,128]{4,3,2,1,0:T(8,128)(2,1)S(1)}, u32[]{:S(2)}, u32[]{:S(2)}) async-start(bf16[64,1,3,8,128]{4,3,2,1,0:T(8,128)(2,1)} %bitcast.6), calls=%async_computation.3 | async-start | bytes 786432 | tf_op jit(solution)/shard_map/all_to_all | solution.py:625
  122.8 19.2 %all-to-all-start.4 = ((bf16[64,1,12,128]{3,2,1,0:T(8,128)(2,1)}), bf16[64,1,12,128]{3,2,1,0:T(8,128)(2,1)S(1)}, u32[]{:S(2)}, u32[]{:S(2)}) async-start(bf16[64,1,12,128]{3,2,1,0:T(8,128)(2,1)} %broadcast_in_dim.34), calls=%async_computation.4 | async-start | bytes 524288 | tf_op jit(solution)/shard_map/all_to_all | solution.py:625
  130.0 7.7 %collective-permute-start.6 = (bf16[2,6,32,96]{3,2,1,0:T(8,128)(2,1)S(1)}, bf16[2,6,32,96]{3,2,1,0:T(8,128)(2,1)S(1)}, u32[]{:S(2)}, u32[]{:S(2)}) collective-permute-start(bf16[2,6,32,96]{3,2,1,0:T(8,128)(2,1)S(1)} %grad_pre.1), channel_id=1, source_target_pairs={{32,0},{64,32},{96,64},{128,96},{160,128},{192,160},{224,192},{256... | collective-permute-start | bytes 221192 | tf_op jit(solution)/shard_map/ppermute | solution.py:32
  143.0 11.9 %all-to-all-start.5 = ((bf16[4,768,128]{2,1,0:T(8,128)(2,1)}), bf16[4,768,128]{2,1,0:T(8,128)(2,1)S(1)}, u32[]{:S(2)}, u32[]{:S(2)}) async-start(bf16[4,768,128]{2,1,0:T(8,128)(2,1)} %broadcast_in_dim.35), calls=%async_computation.5 | async-start | bytes 1572864 | tf_op jit(solution)/shard_map/all_to_all | solution.py:625
  154.9 9.6 %collective-permute-start.7 = (bf16[4,768,128]{2,1,0:T(8,128)(2,1)S(1)}, bf16[4,768,128]{2,1,0:T(8,128)(2,1)S(1)}, u32[]{:S(2)}, u32[]{:S(2)}) collective-permute-start(bf16[4,768,128]{2,1,0:T(8,128)(2,1)S(1)} %all-to-all-done.5.part), channel_id=1, source_target_pairs={{0,1},{1,0},{2,3},{3,2},{4,5},{5,4},{6,7},{7,6},{8,9},{9,8},{10,11... | collective-permute-start | bytes 2359304 | tf_op jit(solution)/shard_map/ppermute | solution.py:671

commit v7 on v6

--- a/solution.py
+++ b/solution.py
@@ -67,8 +67,9 @@
 
 
 def resident_kernel(*refs):
-    sources, copies, sems = refs[:4], refs[4:8], refs[8]
-    moves = [pltpu.make_async_copy(sources[k], copies[k], sems.at[k]) for k in range(4)]
+    count = len(refs) // 2
+    sems = refs[-1]
+    moves = [pltpu.make_async_copy(refs[k], refs[count + k], sems.at[k]) for k in range(count)]
     for move in moves:
         move.start()
     for move in moves:
@@ -76,12 +77,13 @@
 
 
 def resident(*arrays):
+    count = len(arrays)
     return pl.pallas_call(
         resident_kernel,
         out_shape=[jax.ShapeDtypeStruct(k.shape, k.dtype) for k in arrays],
-        in_specs=whole(4, pltpu.HBM),
-        out_specs=whole(4),
-        scratch_shapes=[pltpu.SemaphoreType.DMA((4,))],
+        in_specs=whole(count, pltpu.HBM),
+        out_specs=whole(count),
+        scratch_shapes=[pltpu.SemaphoreType.DMA((count,))],
         compiler_params=pltpu.CompilerParams(vmem_limit_bytes=VMEM_LIMIT),
         cost_estimate=pl.CostEstimate(flops=0, bytes_accessed=2**22, transcendentals=0),
         name="resident",
@@ -162,20 +164,28 @@
     )(cache, features, above, below, weight, cot)
 
 
-def grad_hidden_kernel(cot, later, above, below, weight, grad_hidden, shifted, all_taps, wide):
-    frames, rows, cols, ins = grad_hidden.shape
-    outs = cot.shape[-1]
+def fill_cot(wide, cot, later, above, below):
+    cols, outs = cot.shape[2:]
     half = cols // 2
     timed = jnp.concatenate([cot[...], later[...]], 0)
     pair = lambda part: jnp.stack([part[:, half:, :outs], part[:, half:, outs:]], 1)
     rowed = jnp.concatenate([pair(above), timed, pair(below)], 1).astype(jnp.float32)
     wide[...] = jnp.zeros_like(wide)
     wide[:, 8 : 8 + cols, :outs] = rowed.reshape(-1, cols, outs)
+
+
+def col_tap(wide, e, shape):
+    part = wide[:, 9 - e : 9 - e + shape[2], : shape[3]].astype(jnp.bfloat16)
+    return part.reshape(2 * shape[0], shape[1] + 4, shape[2], shape[3])
+
+
+def grad_hidden_kernel(cot, later, above, below, weight, grad_hidden, all_taps, wide):
+    frames, rows, cols, ins = grad_hidden.shape
+    outs = cot.shape[-1]
+    fill_cot(wide, cot, later, above, below)
     total = jnp.zeros((frames * rows * cols, ins), jnp.float32)
     for e in range(3):
-        part = wide[:, 9 - e : 9 - e + cols, :outs].astype(jnp.bfloat16)
-        part = part.reshape(2 * frames, rows + 2, cols, outs)
-        shifted[e] = part
+        part = col_tap(wide, e, cot.shape)
         for a in range(3):
             for b in range(3):
                 total += lax.dot_general(
@@ -196,11 +206,10 @@
         grad_hidden_kernel,
         out_shape=(
             jax.ShapeDtypeStruct((frames, rows + 2, cols, weight.shape[-2]), jnp.float32),
-            jax.ShapeDtypeStruct((3, 2 * frames, rows + 4, cols, outs), jnp.bfloat16),
             jax.ShapeDtypeStruct(weight.shape[-2:], jnp.float32),
         ),
         in_specs=whole(5),
-        out_specs=whole(3),
+        out_specs=whole(2),
         scratch_shapes=[pltpu.VMEM((2 * frames * (rows + 4), cols + 16, 128), jnp.float32)],
         compiler_params=pltpu.CompilerParams(vmem_limit_bytes=VMEM_LIMIT),
         cost_estimate=pl.CostEstimate(flops=2**30, bytes_accessed=2**21, transcendentals=0),
@@ -262,13 +271,15 @@
     )(where, came, pre_norm, grad_hidden, all_taps, gain[None], shift[None])
 
 
-def second_weight_kernel(hidden, shifted, out):
+def second_weight_kernel(hidden, cot, later, above, below, out, wide):
     frames, rows, cols, ins = hidden.shape
-    outs = shifted.shape[-1]
+    outs = cot.shape[-1]
     own = hidden[:, 1:-1].reshape(-1, ins).astype(jnp.float32).T.astype(jnp.bfloat16)
+    fill_cot(wide, cot, later, above, below)
+    shifted = [col_tap(wide, e, cot.shape) for e in range(3)]
     for a in range(3):
         pieces = [
-            shifted[e, 2 - a : 2 - a + frames, 3 - b : 3 - b + rows - 2].reshape(-1, outs)
+            shifted[e][2 - a : 2 - a + frames, 3 - b : 3 - b + rows - 2].reshape(-1, outs)
             for b in range(3)
             for e in range(3)
         ]
@@ -276,16 +287,17 @@
         out[a] = jnp.dot(own, jnp.concatenate(pieces, 1), preferred_element_type=jnp.float32)
 
 
-def second_weight(hidden, shifted):
+def second_weight(hidden, cot, later, above, below):
+    frames, rows, cols, _ = cot.shape
     return pl.pallas_call(
         second_weight_kernel,
         out_shape=jax.ShapeDtypeStruct((3, hidden.shape[-1], 896), jnp.float32),
-        in_specs=whole(2),
+        in_specs=whole(5),
         out_specs=whole()[0],
-        compiler_params=pltpu.CompilerParams(vmem_limit_bytes=VMEM_LIMIT),
-        cost_estimate=pl.CostEstimate(flops=2**29, bytes_accessed=2**21, transcendentals=0),
+        scratch_shapes=[pltpu.VMEM((2 * frames * (rows + 4), cols + 16, 128), jnp.float32)],
+        compiler_params=pltpu.CompilerParams(vmem_limit_bytes=VMEM_LIMIT),
         name="second_weight",
-    )(hidden, shifted)
+    )(hidden, cot, later, above, below)
 
 
 def col_sums(wide, cells):
@@ -416,12 +428,17 @@
     )(where, cache, features, above, below, grad_normed, normed, vectors, two)
 
 
-def add_pair_kernel(kept, came, out):
-    total = kept[...] + came[...].astype(jnp.float32)
-    out[...] = total.astype(jnp.bfloat16)
-    sums = in_parts(sums_of(total[0, -16:]), 16).astype(jnp.bfloat16)
-    for x in range(out.shape[0]):
-        out[x, out.shape[1] - 16 :] = sums
+def add_pair_kernel(kept, came, out, total, sems):
+    deep = kept.shape[1] - 16
+    sums = in_parts(sums_of(kept[0, deep:] + came[0, deep:].astype(jnp.float32)), 16).astype(jnp.bfloat16)
+    moves = []
+    for x in range(kept.shape[0]):
+        total[x, :deep] = (kept[x, :deep] + came[x, :deep].astype(jnp.float32)).astype(jnp.bfloat16)
+        total[x, deep:] = sums
+        moves.append(pltpu.make_async_copy(total.at[x], out.at[x], sems.at[x]))
+        moves[x].start()
+    for move in moves:
+        move.wait()
 
 
 def add_pair(kept, came):
@@ -429,7 +446,8 @@
         add_pair_kernel,
         out_shape=jax.ShapeDtypeStruct(kept.shape, jnp.bfloat16),
         in_specs=whole(2),
-        out_specs=whole()[0],
+        out_specs=whole(1, pltpu.HBM)[0],
+        scratch_shapes=[pltpu.VMEM(kept.shape, jnp.bfloat16), pltpu.SemaphoreType.DMA((kept.shape[0],))],
         compiler_params=pltpu.CompilerParams(vmem_limit_bytes=VMEM_LIMIT),
         name="add_pair",
     )(kept, came)
@@ -543,7 +561,11 @@
             tap = lax.broadcasted_iota(jnp.int32, (32, change.shape[1]), 0)
             lane = lax.broadcasted_iota(jnp.int32, (32, change.shape[1]), 1)
             change = jnp.where(lane // outs == tap, change, 0.0)
-            lanes -= exact(lanes[:, outs * taps :], change, ((1,), (0,)))
+            high = change.astype(jnp.bfloat16)
+            low = (change - high.astype(jnp.float32)).astype(jnp.bfloat16)
+            met = jnp.concatenate([blocks[-1][:, 96:]] * 2, 1).astype(jnp.bfloat16)
+            change = jnp.concatenate([high, low], 0)
+            lanes -= jnp.dot(met, change, preferred_element_type=jnp.float32) * scale
         for k in range(taps):
             out[k] = lanes[:, outs * k : outs * k + outs]
 
@@ -630,19 +652,21 @@
     cache = neighbour(features, TM, 1)
     later = neighbour(cotangent, TM, -1)
 
-    features, cotangent, weight_one, weight_two = resident(features, cotangent, weight_one, weight_two)
+    features, cotangent = resident(features, cotangent)
     downward, upward = edges(cache, features, cotangent, later)
+    downward, upward, weight_one, weight_two = barrier((downward, upward, weight_one, weight_two))
+    weight_one, weight_two = resident(weight_one, weight_two)
     above = neighbour(downward, HEIGHT, 1)
     below = neighbour(upward, HEIGHT, -1)
     pre_norm, sums = conv_one(cache, features, above, below, weight_one, cotangent, height)
     came = exchange(sums, HEIGHT)
-    grad_hidden, shifted_cot, all_taps = hidden_grads(cotangent, later, above, below, weight_two)
-    sums, grad_hidden, shifted_cot = barrier((came.sum(0), grad_hidden, shifted_cot))
+    grad_hidden, all_taps = hidden_grads(cotangent, later, above, below, weight_two)
+    sums, grad_hidden = barrier((came.sum(0), grad_hidden))
     came = exchange(spread(sums, lax.axis_size(TM)), TM)
     hidden, grad_normed, normed, vectors = middle(
         count, where, came, pre_norm, grad_hidden, all_taps, norm_gain, norm_shift
     )
-    local_two = second_weight(hidden, shifted_cot)
+    local_two = second_weight(hidden, cotangent, later, above, below)
 
     scale = 1.0 / cells**0.5
     part_rows = -(-21 * ins // (2 * 8 * xs * rest)) * 8 * rest

time: 168 us -> 167 us (level)
  local copies, waits for them, and re-layouts: 10.1 us -> 8.09 us
    unnamed x21 -> x17, local copies, waits for them, and re-layouts: 7.72 us -> 5.71 us
  transfers between devices with their start and end apart: 14 -> 14, of which waited for: 9 -> 8; matrix products, arithmetic and copies ran while one was open for 2% -> 2% of each run, Pallas kernels for 5% -> 4%
where the time goes in v7:
time: 167 us; the launch traced here: 166 us
  starting transfers between devices  73 us (44%)
  waiting for transfers between devices  64.8 us (39%)
  Pallas kernels  16.3 us (10%)
  local copies, waits for them, and re-layouts  8.09 us (5%)
  matrix products  2.6 us (2%)
    all_to_all x6, waiting for transfers between devices, exchange(): return lax.all_to_all(copies, axes, 0, 0)  55.7 us
    all_to_all x6, starting transfers between devices, exchange(): return lax.all_to_all(copies, axes, 0, 0)  42.8 us
    ppermute x6, starting transfers between devices, neighbour(): lax.ppermute(value, axis, [(i, i + steps) for i in range(first, last)])  19.8 us
    ppermute x1, starting transfers between devices, body(): other = lax.ppermute(part, 'c', SWAP)  6.68 us
    ppermute x6, waiting for transfers between devices, neighbour(): lax.ppermute(value, axis, [(i, i + steps) for i in range(first, last)])  6.46 us
    unnamed x17, local copies, waits for them, and re-layouts  5.71 us
    pallas_call x2, Pallas kernels, unpack(): pl.pallas_call(functools.partial(unpack_kernel, scale), grid_spec=pltpu.P...  5.17 us
    ppermute x1, starting transfers between devices, body(): part = add_pair(kept, lax.ppermute(away, 'c', SWAP))  3.74 us
  transfers between devices with their start and end apart: 14, of which 8 were waited for; matrix products, arithmetic and copies ran while one was open for 2% of the time, Pallas kernels for 4%

profile of v7, /device:TPU:1, one launch (start us, length us, event | category | flops | bytes accessed | tf_op | source)
XLA Modules:
  0.0 166.1 jit_solution(10857684624152258238)
XLA Ops:
  0.6 1.3 collective-permute-start.1
  1.9 4.7 %collective-permute-start = (bf16[2,2,16,192]{3,2,1,0:T(8,128)(2,1)}, bf16[2,2,16,192]{3,2,1,0:T(8,128)(2,1)S(1)}, u32[]{:S(2)}, u32[]{:S(2)}) collective-permute-start(bf16[2,2,16,192]{3,2,1,0:T(8,128)(2,1)} %refs_0_.1), channel_id=1, source_target_pairs={{0,32},{32,64},{64,96},{96,128},{128,160},{160,192},{192,224},{224... | collective-permute-start | bytes 73736 | tf_op jit(solution)/shard_map/ppermute | solution.py:32
  8.4 4.6 %collective-permute-start.2 = (bf16[4,48,192]{2,1,0:T(8,128)(2,1)S(1)}, bf16[4,48,192]{2,1,0:T(8,128)(2,1)S(1)}, u32[]{:S(2)}, u32[]{:S(2)}) collective-permute-start(bf16[4,48,192]{2,1,0:T(8,128)(2,1)S(1)} %get-tuple-element.46), channel_id=1, source_target_pairs={{0,1},{1,2},{2,3},{3,4},{4,5},{5,6},{6,7},{7,8},{8,9},{9,10},{10,1... | collective-permute-start | bytes 221192 | tf_op jit(solution)/shard_map/ppermute | solution.py:32
  13.0 5.6 %collective-permute-start.3 = (bf16[4,48,192]{2,1,0:T(8,128)(2,1)S(1)}, bf16[4,48,192]{2,1,0:T(8,128)(2,1)S(1)}, u32[]{:S(2)}, u32[]{:S(2)}) collective-permute-start(bf16[4,48,192]{2,1,0:T(8,128)(2,1)S(1)} %get-tuple-element.47), channel_id=1, source_target_pairs={{1,0},{2,1},{3,2},{4,3},{5,4},{6,5},{7,6},{8,7},{9,8},{10,9},{11,1... | collective-permute-start | bytes 221192 | tf_op jit(solution)/shard_map/ppermute | solution.py:32
  18.6 1.3 copy-done.1
  19.9 1.1 copy-done.2
  21.4 1.6 conv_one.1
  22.9 8.4 %all-to-all-start = ((f32[32,4,96]{2,1,0:T(4,128)}), f32[32,4,96]{2,1,0:T(4,128)S(1)}, u32[]{:S(2)}, u32[]{:S(2)}) async-start(f32[32,4,96]{2,1,0:T(4,128)} %get-tuple-element.51), calls=%async_computation | async-start | bytes 131072 | tf_op jit(solution)/shard_map/all_to_all | solution.py:647
  32.3 6.8 %all-to-all-done = f32[32,4,96]{2,1,0:T(4,128)S(1)} async-done(((f32[32,4,96]{2,1,0:T(4,128)}), f32[32,4,96]{2,1,0:T(4,128)S(1)}, u32[]{:S(2)}, u32[]{:S(2)}) %all-to-all-start) | async-done | bytes 49184 | tf_op jit(solution)/shard_map/all_to_all | solution.py:647
  39.7 16.1 %all-to-all-start.1 = ((f32[16,4,96]{2,1,0:T(4,128)}), f32[16,4,96]{2,1,0:T(4,128)S(1)}, u32[]{:S(2)}, u32[]{:S(2)}) async-start(f32[16,4,96]{2,1,0:T(4,128)} %broadcast_in_dim.14), calls=%async_computation.1 | async-start | bytes 65536 | tf_op jit(solution)/shard_map/all_to_all | solution.py:647
  55.9 11.2 %all-to-all-done.1.came = f32[16,4,96]{2,1,0:T(4,128)S(1)} async-done(((f32[16,4,96]{2,1,0:T(4,128)}), f32[16,4,96]{2,1,0:T(4,128)S(1)}, u32[]{:S(2)}, u32[]{:S(2)}) %all-to-all-start.1) | async-done | bytes 24608 | tf_op jit(solution)/shard_map/all_to_all | solution.py:647
  68.7 1.5 weight_grads.1
  70.2 3.7 %collective-permute-start.4 = (bf16[4,1296,128]{2,1,0:T(8,128)(2,1)S(1)}, bf16[4,1296,128]{2,1,0:T(8,128)(2,1)S(1)}, u32[]{:S(2)}, u32[]{:S(2)}) collective-permute-start(bf16[4,1296,128]{2,1,0:T(8,128)(2,1)S(1)} %get-tuple-element.63), channel_id=1, source_target_pairs={{0,1},{1,0},{2,3},{3,2},{4,5},{5,4},{6,7},{7,6},{8,9},{9,8},{10,11... | collective-permute-start | bytes 3981320 | tf_op jit(solution)/shard_map/ppermute | solution.py:676
  74.0 2.7 %collective-permute-done.4.came = bf16[4,1296,128]{2,1,0:T(8,128)(2,1)S(1)} collective-permute-done((bf16[4,1296,128]{2,1,0:T(8,128)(2,1)S(1)}, bf16[4,1296,128]{2,1,0:T(8,128)(2,1)S(1)}, u32[]{:S(2)}, u32[]{:S(2)}) %collective-permute-start.4) | collective-permute-done | bytes 1327136 | tf_op jit(solution)/shard_map/ppermute | solution.py:676
  77.3 1.1 copy-done
  78.4 3.5 %all-to-all-start.2 = ((bf16[4,1296,128]{2,1,0:T(8,128)(2,1)}), bf16[4,1296,128]{2,1,0:T(8,128)(2,1)S(1)}, u32[]{:S(2)}, u32[]{:S(2)}) async-start(bf16[4,1296,128]{2,1,0:T(8,128)(2,1)} %copy-done), calls=%async_computation.2 | async-start | bytes 2654208 | tf_op jit(solution)/shard_map/all_to_all | solution.py:647
  81.9 2.4 %collective-permute-start.5 = (bf16[2,6,32,96]{3,2,1,0:T(8,128)(2,1)S(1)}, bf16[2,6,32,96]{3,2,1,0:T(8,128)(2,1)S(1)}, u32[]{:S(2)}, u32[]{:S(2)}) collective-permute-start(bf16[2,6,32,96]{3,2,1,0:T(8,128)(2,1)S(1)} %get-tuple-element.65.hidden), channel_id=1, source_target_pairs={{0,32},{32,64},{64,96},{96,128},{128,160},{160,192},{192,224},{224... | collective-permute-start | bytes 221192 | tf_op jit(solution)/shard_map/ppermute | solution.py:32
  84.4 15.4 %all-to-all-done.2.came = bf16[4,1296,128]{2,1,0:T(8,128)(2,1)S(1)} async-done(((bf16[4,1296,128]{2,1,0:T(8,128)(2,1)}), bf16[4,1296,128]{2,1,0:T(8,128)(2,1)S(1)}, u32[]{:S(2)}, u32[]{:S(2)}) %all-to-all-start.2) | async-done | bytes 1327136 | tf_op jit(solution)/shard_map/all_to_all | solution.py:647
  100.8 4.6 %all-to-all-start.3 = ((bf16[64,1,3,8,128]{4,3,2,1,0:T(8,128)(2,1)}), bf16[64,1,3,8,128]{4,3,2,1,0:T(8,128)(2,1)S(1)}, u32[]{:S(2)}, u32[]{:S(2)}) async-start(bf16[64,1,3,8,128]{4,3,2,1,0:T(8,128)(2,1)} %bitcast.6), calls=%async_computation.3 | async-start | bytes 786432 | tf_op jit(solution)/shard_map/all_to_all | solution.py:647
  105.5 2.6 %convolution_convert_fusion = bf16[1,2,4,32,96]{4,0,3,2,1:T(2,128)(2,1)S(1)} fusion(bf16[3,3,3,96,96]{4,3,2,1,0:T(8,128)(2,1)} %copy-done.7, bf16[1,4,6,34,96]{4,3,2,1,0:T(8,128)(2,1)S(1)} %fusion.5), kind=kOutput, calls=%fused_computation | convolution fusion | flops 127426560 | bytes 703488 | tf_op jit(solution)/shard_map/conv_general_dilated | solution.py:36
  108.8 11.4 %all-to-all-done.3.came = bf16[64,1,3,8,128]{4,3,2,1,0:T(8,128)(2,1)S(1)} async-done(((bf16[64,1,3,8,128]{4,3,2,1,0:T(8,128)(2,1)}), bf16[64,1,3,8,128]{4,3,2,1,0:T(8,128)(2,1)S(1)}, u32[]{:S(2)}, u32[]{:S(2)}) %all-to-all-start.3) | async-done | bytes 393248 | tf_op jit(solution)/shard_map/all_to_all | solution.py:647
  120.2 1.1 combine.1
  122.1 6.7 %all-to-all-start.4 = ((bf16[64,1,12,128]{3,2,1,0:T(8,128)(2,1)}), bf16[64,1,12,128]{3,2,1,0:T(8,128)(2,1)S(1)}, u32[]{:S(2)}, u32[]{:S(2)}) async-start(bf16[64,1,12,128]{3,2,1,0:T(8,128)(2,1)} %broadcast_in_dim.34), calls=%async_computation.4 | async-start | bytes 524288 | tf_op jit(solution)/shard_map/all_to_all | solution.py:647
  129.3 1.3 collective-permute-start.6
  130.6 6.4 %collective-permute-done.6 = bf16[2,6,32,96]{3,2,1,0:T(8,128)(2,1)S(1)} collective-permute-done((bf16[2,6,32,96]{3,2,1,0:T(8,128)(2,1)S(1)}, bf16[2,6,32,96]{3,2,1,0:T(8,128)(2,1)S(1)}, u32[]{:S(2)}, u32[]{:S(2)}) %collective-permute-start.6) | collective-permute-done | bytes 73760 | tf_op jit(solution)/shard_map/ppermute | solution.py:32
  137.1 4.2 %all-to-all-done.4 = bf16[64,1,12,128]{3,2,1,0:T(8,128)(2,1)S(1)} async-done(((bf16[64,1,12,128]{3,2,1,0:T(8,128)(2,1)}), bf16[64,1,12,128]{3,2,1,0:T(8,128)(2,1)S(1)}, u32[]{:S(2)}, u32[]{:S(2)}) %all-to-all-start.4) | async-done | bytes 196640 | tf_op jit(solution)/shard_map/all_to_all | solution.py:647
  142.3 3.5 %all-to-all-start.5 = ((bf16[4,768,128]{2,1,0:T(8,128)(2,1)}), bf16[4,768,128]{2,1,0:T(8,128)(2,1)S(1)}, u32[]{:S(2)}, u32[]{:S(2)}) async-start(bf16[4,768,128]{2,1,0:T(8,128)(2,1)} %broadcast_in_dim.35), calls=%async_computation.5 | async-start | bytes 1572864 | tf_op jit(solution)/shard_map/all_to_all | solution.py:647
  145.9 1.6 feature_grads.1
  147.5 6.7 %all-to-all-done.5.part = bf16[4,768,128]{2,1,0:T(8,128)(2,1)S(1)} async-done(((bf16[4,768,128]{2,1,0:T(8,128)(2,1)}), bf16[4,768,128]{2,1,0:T(8,128)(2,1)S(1)}, u32[]{:S(2)}, u32[]{:S(2)}) %all-to-all-start.5) | async-done | bytes 786464 | tf_op jit(solution)/shard_map/all_to_all | solution.py:647
  154.2 6.7 %collective-permute-start.7 = (bf16[4,768,128]{2,1,0:T(8,128)(2,1)S(1)}, bf16[4,768,128]{2,1,0:T(8,128)(2,1)S(1)}, u32[]{:S(2)}, u32[]{:S(2)}) collective-permute-start(bf16[4,768,128]{2,1,0:T(8,128)(2,1)S(1)} %all-to-all-done.5.part), channel_id=1, source_target_pairs={{0,1},{1,0},{2,3},{3,2},{4,5},{5,4},{6,7},{7,6},{8,9},{9,8},{10,11... | collective-permute-start | bytes 2359304 | tf_op jit(solution)/shard_map/ppermute | solution.py:695
  160.9 2.6 %unpack.2 = (f32[27,192,96]{2,1,0:T(8,128)}, f32[27,96,96]{2,1,0:T(8,128)}) custom-call(s32[1]{0:T(128)} %bitcast.half, bf16[4,768,128]{2,1,0:T(8,128)(2,1)S(1)} %all-to-all-done.5.part, f32[8,96]{1,0:T(8,128)S(1)} %get-tuple-element.71.final), custom_call_target="tpu_custom_call" | custom-call | flops 1048576 | bytes 4194304 | tf_op jit(solution)/shard_map/unpack/pallas_call | solution.py:574
  163.5 2.6 %unpack.3 = (f32[27,192,96]{2,1,0:T(8,128)}, f32[27,96,96]{2,1,0:T(8,128)}) custom-call(s32[1]{0:T(128)S(6)} %sub.3.half, bf16[4,768,128]{2,1,0:T(8,128)(2,1)S(1)} %collective-permute-done.7.part, f32[8,96]{1,0:T(8,128)S(1)} %get-tuple-element.71.final, f32[27,192,96]{2,1,0:T(8,128)} %get-tuple-element.76.rest_0_, ...), custom_call_target="tpu_custom_call", output_to_operand_aliasing={{0}: (3, {}), {1}: (4, {})} | custom-call | flops 1048576 | bytes 4194304 | tf_op jit(solution)/shard_map/unpack/pallas_call | solution.py:574
  (39 shorter events, 10.3 us)
Async XLA Ops:
  0.6 7.7 %collective-permute-start.1 = (bf16[2,4,32,96]{3,2,1,0:T(8,128)(2,1)}, bf16[2,4,32,96]{3,2,1,0:T(8,128)(2,1)S(1)}, u32[]{:S(2)}, u32[]{:S(2)}) collective-permute-start(bf16[2,4,32,96]{3,2,1,0:T(8,128)(2,1)} %refs_1_.1), channel_id=1, source_target_pairs={{32,0},{64,32},{96,64},{128,96},{160,128},{192,160},{224,192},{256... | collective-permute-start | bytes 147464 | tf_op jit(solution)/shard_map/ppermute | solution.py:32
  1.9 6.4 %collective-permute-start = (bf16[2,2,16,192]{3,2,1,0:T(8,128)(2,1)}, bf16[2,2,16,192]{3,2,1,0:T(8,128)(2,1)S(1)}, u32[]{:S(2)}, u32[]{:S(2)}) collective-permute-start(bf16[2,2,16,192]{3,2,1,0:T(8,128)(2,1)} %refs_0_.1), channel_id=1, source_target_pairs={{0,32},{32,64},{64,96},{96,128},{128,160},{160,192},{192,224},{224... | collective-permute-start | bytes 73736 | tf_op jit(solution)/shard_map/ppermute | solution.py:32
  6.6 0.8 copy-start.3
  7.4 0.8 copy-start.4
  8.4 12.9 %collective-permute-start.2 = (bf16[4,48,192]{2,1,0:T(8,128)(2,1)S(1)}, bf16[4,48,192]{2,1,0:T(8,128)(2,1)S(1)}, u32[]{:S(2)}, u32[]{:S(2)}) collective-permute-start(bf16[4,48,192]{2,1,0:T(8,128)(2,1)S(1)} %get-tuple-element.46), channel_id=1, source_target_pairs={{0,1},{1,2},{2,3},{3,4},{4,5},{5,6},{6,7},{7,8},{8,9},{9,10},{10,1... | collective-permute-start | bytes 221192 | tf_op jit(solution)/shard_map/ppermute | solution.py:32
  13.0 8.4 %collective-permute-start.3 = (bf16[4,48,192]{2,1,0:T(8,128)(2,1)S(1)}, bf16[4,48,192]{2,1,0:T(8,128)(2,1)S(1)}, u32[]{:S(2)}, u32[]{:S(2)}) collective-permute-start(bf16[4,48,192]{2,1,0:T(8,128)(2,1)S(1)} %get-tuple-element.47), channel_id=1, source_target_pairs={{1,0},{2,1},{3,2},{4,3},{5,4},{6,5},{7,6},{8,7},{9,8},{10,9},{11,1... | collective-permute-start | bytes 221192 | tf_op jit(solution)/shard_map/ppermute | solution.py:32
  18.6 1.3 copy-start.1
  19.9 1.1 copy-start.2
  21.4 45.8 %copy-start.7 = (bf16[3,3,3,96,96]{4,3,2,1,0:T(8,128)(2,1)}, bf16[3,3,3,96,96]{4,3,2,1,0:T(8,128)(2,1)S(1)}, u32[]{:S(2)}) copy-start(bf16[3,3,3,96,96]{4,3,2,1,0:T(8,128)(2,1)S(1)} %get-tuple-element.52.weight) | copy-start | bytes 1492996
  22.9 16.1 %all-to-all-start = ((f32[32,4,96]{2,1,0:T(4,128)}), f32[32,4,96]{2,1,0:T(4,128)S(1)}, u32[]{:S(2)}, u32[]{:S(2)}) async-start(f32[32,4,96]{2,1,0:T(4,128)} %get-tuple-element.51), calls=%async_computation | async-start | bytes 131072 | tf_op jit(solution)/shard_map/all_to_all | solution.py:647
  31.3 35.8 %copy-start.5 = (f32[96]{0:T(128)S(1)}, f32[96]{0:T(128)}, u32[]{:S(2)}) copy-start(f32[96]{0:T(128)} %param.10) | copy-start | bytes 1156
  31.3 35.8 %copy-start.6 = (f32[96]{0:T(128)S(1)}, f32[96]{0:T(128)}, u32[]{:S(2)}) copy-start(f32[96]{0:T(128)} %param.11) | copy-start | bytes 1156
  39.7 27.4 %all-to-all-start.1 = ((f32[16,4,96]{2,1,0:T(4,128)}), f32[16,4,96]{2,1,0:T(4,128)S(1)}, u32[]{:S(2)}, u32[]{:S(2)}) async-start(f32[16,4,96]{2,1,0:T(4,128)} %broadcast_in_dim.14), calls=%async_computation.1 | async-start | bytes 65536 | tf_op jit(solution)/shard_map/all_to_all | solution.py:647
  70.2 6.4 %collective-permute-start.4 = (bf16[4,1296,128]{2,1,0:T(8,128)(2,1)S(1)}, bf16[4,1296,128]{2,1,0:T(8,128)(2,1)S(1)}, u32[]{:S(2)}, u32[]{:S(2)}) collective-permute-start(bf16[4,1296,128]{2,1,0:T(8,128)(2,1)S(1)} %get-tuple-element.63), channel_id=1, source_target_pairs={{0,1},{1,0},{2,3},{3,2},{4,5},{5,4},{6,7},{7,6},{8,9},{9,8},{10,11... | collective-permute-start | bytes 3981320 | tf_op jit(solution)/shard_map/ppermute | solution.py:676
  77.3 1.1 copy-start
  78.4 21.3 %all-to-all-start.2 = ((bf16[4,1296,128]{2,1,0:T(8,128)(2,1)}), bf16[4,1296,128]{2,1,0:T(8,128)(2,1)S(1)}, u32[]{:S(2)}, u32[]{:S(2)}) async-start(bf16[4,1296,128]{2,1,0:T(8,128)(2,1)} %copy-done), calls=%async_computation.2 | async-start | bytes 2654208 | tf_op jit(solution)/shard_map/all_to_all | solution.py:647
  81.9 18.8 %collective-permute-start.5 = (bf16[2,6,32,96]{3,2,1,0:T(8,128)(2,1)S(1)}, bf16[2,6,32,96]{3,2,1,0:T(8,128)(2,1)S(1)}, u32[]{:S(2)}, u32[]{:S(2)}) collective-permute-start(bf16[2,6,32,96]{3,2,1,0:T(8,128)(2,1)S(1)} %get-tuple-element.65.hidden), channel_id=1, source_target_pairs={{0,32},{32,64},{64,96},{96,128},{128,160},{160,192},{192,224},{224... | collective-permute-start | bytes 221192 | tf_op jit(solution)/shard_map/ppermute | solution.py:32
  100.8 19.4 %all-to-all-start.3 = ((bf16[64,1,3,8,128]{4,3,2,1,0:T(8,128)(2,1)}), bf16[64,1,3,8,128]{4,3,2,1,0:T(8,128)(2,1)S(1)}, u32[]{:S(2)}, u32[]{:S(2)}) async-start(bf16[64,1,3,8,128]{4,3,2,1,0:T(8,128)(2,1)} %bitcast.6), calls=%async_computation.3 | async-start | bytes 786432 | tf_op jit(solution)/shard_map/all_to_all | solution.py:647
  122.1 19.2 %all-to-all-start.4 = ((bf16[64,1,12,128]{3,2,1,0:T(8,128)(2,1)}), bf16[64,1,12,128]{3,2,1,0:T(8,128)(2,1)S(1)}, u32[]{:S(2)}, u32[]{:S(2)}) async-start(bf16[64,1,12,128]{3,2,1,0:T(8,128)(2,1)} %broadcast_in_dim.34), calls=%async_computation.4 | async-start | bytes 524288 | tf_op jit(solution)/shard_map/all_to_all | solution.py:647
  129.3 7.7 %collective-permute-start.6 = (bf16[2,6,32,96]{3,2,1,0:T(8,128)(2,1)S(1)}, bf16[2,6,32,96]{3,2,1,0:T(8,128)(2,1)S(1)}, u32[]{:S(2)}, u32[]{:S(2)}) collective-permute-start(bf16[2,6,32,96]{3,2,1,0:T(8,128)(2,1)S(1)} %grad_pre.1), channel_id=1, source_target_pairs={{32,0},{64,32},{96,64},{128,96},{160,128},{192,160},{224,192},{256... | collective-permute-start | bytes 221192 | tf_op jit(solution)/shard_map/ppermute | solution.py:32
  142.3 11.9 %all-to-all-start.5 = ((bf16[4,768,128]{2,1,0:T(8,128)(2,1)}), bf16[4,768,128]{2,1,0:T(8,128)(2,1)S(1)}, u32[]{:S(2)}, u32[]{:S(2)}) async-start(bf16[4,768,128]{2,1,0:T(8,128)(2,1)} %broadcast_in_dim.35), calls=%async_computation.5 | async-start | bytes 1572864 | tf_op jit(solution)/shard_map/all_to_all | solution.py:647
  154.2 9.3 %collective-permute-start.7 = (bf16[4,768,128]{2,1,0:T(8,128)(2,1)S(1)}, bf16[4,768,128]{2,1,0:T(8,128)(2,1)S(1)}, u32[]{:S(2)}, u32[]{:S(2)}) collective-permute-start(bf16[4,768,128]{2,1,0:T(8,128)(2,1)S(1)} %all-to-all-done.5.part), channel_id=1, source_target_pairs={{0,1},{1,0},{2,3},{3,2},{4,5},{5,4},{6,7},{7,6},{8,9},{9,8},{10,11... | collective-permute-start | bytes 2359304 | tf_op jit(solution)/shard_map/ppermute | solution.py:695

commit v8 on v7

--- a/solution.py
+++ b/solution.py
@@ -142,11 +142,10 @@
     pre_norm[...] = pre
     own = pre[:, 1:-1]
     both = group_sums(cell_sums(own), cell_sums(own * own), outs)
-    both = jnp.concatenate([both, cell_sums(cot[...].astype(jnp.float32)), jnp.zeros((1, outs), jnp.float32)], 0)
-    sums[...] = jnp.broadcast_to(both[None], sums.shape)
-
-
-def conv_one(cache, features, above, below, weight, cot, copies):
+    sums[...] = jnp.concatenate([both, cell_sums(cot[...].astype(jnp.float32)), jnp.zeros((5, outs), jnp.float32)], 0)
+
+
+def conv_one(cache, features, above, below, weight, cot):
     frames, cells_in, half, _ = features.shape
     outs = weight.shape[-1]
     rows, cols = 2 * cells_in + 2, 2 * half
@@ -154,7 +153,7 @@
         conv_one_kernel,
         out_shape=(
             jax.ShapeDtypeStruct((frames, rows, cols, outs), jnp.float32),
-            jax.ShapeDtypeStruct((copies, 4, outs), jnp.float32),
+            jax.ShapeDtypeStruct((8, outs), jnp.float32),
         ),
         in_specs=whole(6),
         out_specs=whole(2),
@@ -217,16 +216,16 @@
     )(cot, later, above, below, weight)
 
 
-def middle_kernel(count, where, came, pre_norm, grad_hidden, all_taps, gain, shift, hidden, grad_normed, normed, vectors):
+def middle_kernel(count, where, known, pre_norm, grad_hidden, all_taps, hidden, grad_normed, normed, vectors):
     outs = pre_norm.shape[-1]
-    total = jnp.sum(came[...], 0)
+    total, gain, shift = known[:3], known[4:5], known[5:6]
     mean = total[:1] / count
     scaled = lax.rsqrt(total[1:2] / count - mean * mean + EPSILON)
     flat = (pre_norm[...].reshape(-1, outs) - mean) * scaled
-    shifted = flat * gain[...] + shift[...]
+    shifted = flat * gain + shift
     sigma = 1.0 / (1.0 + jnp.exp(-shifted))
     hidden[...] = inside(where, (shifted * sigma).reshape(pre_norm.shape)).astype(jnp.bfloat16)
-    grad = grad_hidden[...].reshape(-1, outs) * sigma * (1.0 + shifted * (1.0 - sigma)) * gain[...]
+    grad = grad_hidden[...].reshape(-1, outs) * sigma * (1.0 + shifted * (1.0 - sigma)) * gain
     grad, flat = grad.reshape(pre_norm.shape), flat.reshape(pre_norm.shape)
     grad_normed[...] = grad
     normed[...] = flat
@@ -243,10 +242,10 @@
     at = lax.broadcasted_iota(jnp.int32, (16, outs), 0).astype(jnp.float32) * 0.45 - 3.375
     share = jnp.exp(-0.5 * at * at)
     share = share / jnp.sum(share, 0, keepdims=True)
-    point = at * gain[...] + shift[...]
+    point = at * gain + shift
     slope = 1.0 / (1.0 + jnp.exp(-point))
     slope = slope * (1.0 + point * (1.0 - slope)) * share
-    level = level * gain[...] * (cells / count)
+    level = level * gain * (cells / count)
     offsets = group_sums(
         level * jnp.sum(slope, 0, keepdims=True), level * jnp.sum(slope * at, 0, keepdims=True), outs
     )
@@ -254,7 +253,7 @@
     vectors[...] = jnp.concatenate(rows + [jnp.zeros((3, outs), jnp.float32)], 0)
 
 
-def middle(count, where, came, pre_norm, grad_hidden, all_taps, gain, shift):
+def middle(count, where, known, pre_norm, grad_hidden, all_taps):
     shape, outs = pre_norm.shape, pre_norm.shape[-1]
     return pl.pallas_call(
         functools.partial(middle_kernel, count),
@@ -264,11 +263,11 @@
             jax.ShapeDtypeStruct(shape, jnp.float32),
             jax.ShapeDtypeStruct((8, outs), jnp.float32),
         ),
-        in_specs=whole(1, pltpu.SMEM) + whole(6),
+        in_specs=whole(1, pltpu.SMEM) + whole(4),
         out_specs=whole(4),
         compiler_params=pltpu.CompilerParams(vmem_limit_bytes=VMEM_LIMIT),
         name="middle",
-    )(where, came, pre_norm, grad_hidden, all_taps, gain[None], shift[None])
+    )(where, known, pre_norm, grad_hidden, all_taps)
 
 
 def second_weight_kernel(hidden, cot, later, above, below, out, wide):
@@ -456,8 +455,6 @@
 def add_row_kernel(came, out):
     total = jnp.sum(came[...].astype(jnp.float32), 0)
     n = out.shape[0] * 8
-    out[:, 0] = total[:n].astype(jnp.bfloat16).reshape(-1, 8, 128)
-    out[:, 1] = total[n : 2 * n].astype(jnp.bfloat16).reshape(-1, 8, 128)
     tiles = total[2 * n : n * 5 // 2].reshape(-1, 8, 128)
     row = lax.broadcasted_iota(jnp.int32, (1, 8, 128), 1)
     lane = lax.broadcasted_iota(jnp.int32, (1, 8, 128), 2)
@@ -467,14 +464,16 @@
     odd = jnp.where(row < 4, turned, swap(tiles))
     both = jnp.stack([even, odd], 1).reshape(-1, 8, 128)
     sums = in_parts(sums_of(total[n * 5 // 2 :]), 8)
-    out[:, 2] = jnp.where(lane < 64, both, sums[None]).astype(jnp.bfloat16)
+    both = jnp.where(lane < 64, both, sums[None])
+    parts = [total[:n].reshape(-1, 8, 128), total[n : 2 * n].reshape(-1, 8, 128), both, jnp.zeros_like(both)]
+    out[...] = jnp.concatenate(parts, 1).astype(jnp.bfloat16)
 
 
 def add_row(came):
     tiles = (came.shape[1] - 16) // 20
     return pl.pallas_call(
         add_row_kernel,
-        out_shape=jax.ShapeDtypeStruct((tiles, 3, 8, 128), jnp.bfloat16),
+        out_shape=jax.ShapeDtypeStruct((tiles, 32, 128), jnp.bfloat16),
         in_specs=whole(1),
         out_specs=whole()[0],
         compiler_params=pltpu.CompilerParams(vmem_limit_bytes=VMEM_LIMIT),
@@ -485,7 +484,7 @@
 def combine_kernel(count, tiles_per_block, where, came, vectors, piece, final, lanes):
     outs = vectors.shape[1]
     total = jnp.sum(came[...].astype(jnp.float32), 0)
-    sums = sums_of(total[0, 2]) / count
+    sums = sums_of(total[0, 16:]) / count
     first = exact(sums, group_lanes(outs, True), ((1,), (1,)))
     second = exact(sums, group_lanes(outs, False), ((1,), (1,)))
     rest = (first - vectors[1:2]) * vectors[0:1]
@@ -497,16 +496,16 @@
     for k in range(piece.shape[0]):
         block = (where[3] * piece.shape[0] + k) // tiles_per_block % 7
         change = lanes[0:1, pl.ds(pl.multiple_of(block * 128, 128), 128)]
-        upper = jnp.concatenate([total[k, 2, :4, :64], total[k, 2, 4:, :64]], 1)
-        grad = total[k, 0] - change * total[k, 1]
-        piece[k] = jnp.concatenate([grad, upper], 0).astype(jnp.bfloat16)
+        upper = jnp.concatenate([total[k, 16:20, :64], total[k, 20:24, :64]], 1)
+        grad = total[k, :8] - change * total[k, 8:16]
+        piece[k] = jnp.concatenate([grad, upper, jnp.zeros_like(upper)], 0).astype(jnp.bfloat16)
 
 
 def combine(count, ins, where, came, vectors):
     return pl.pallas_call(
         functools.partial(combine_kernel, count, ins // 16),
         out_shape=(
-            jax.ShapeDtypeStruct((came.shape[1], 12, 128), jnp.bfloat16),
+            jax.ShapeDtypeStruct((came.shape[1], 16, 128), jnp.bfloat16),
             jax.ShapeDtypeStruct(vectors.shape, jnp.float32),
         ),
         in_specs=whole(1, pltpu.SMEM) + whole(2),
@@ -658,14 +657,13 @@
     weight_one, weight_two = resident(weight_one, weight_two)
     above = neighbour(downward, HEIGHT, 1)
     below = neighbour(upward, HEIGHT, -1)
-    pre_norm, sums = conv_one(cache, features, above, below, weight_one, cotangent, height)
-    came = exchange(sums, HEIGHT)
+    pre_norm, sums = conv_one(cache, features, above, below, weight_one, cotangent)
+    came = exchange(spread(sums[:4], height), HEIGHT)
     grad_hidden, all_taps = hidden_grads(cotangent, later, above, below, weight_two)
     sums, grad_hidden = barrier((came.sum(0), grad_hidden))
     came = exchange(spread(sums, lax.axis_size(TM)), TM)
-    hidden, grad_normed, normed, vectors = middle(
-        count, where, came, pre_norm, grad_hidden, all_taps, norm_gain, norm_shift
-    )
+    known = jnp.concatenate([came.sum(0), norm_gain[None], norm_shift[None], jnp.zeros((2, mids), jnp.float32)], 0)
+    hidden, grad_normed, normed, vectors = middle(count, where, known, pre_norm, grad_hidden, all_taps)
     local_two = second_weight(hidden, cotangent, later, above, below)
 
     scale = 1.0 / cells**0.5
@@ -678,14 +676,14 @@
     part = add_row(exchange(part, "x"))
     before = neighbour(hidden, TM, 1)
     part, before = barrier((part, before))
-    came = exchange(part.reshape(rest, -1, 3, 8, 128), REST)
+    came = exchange(part.reshape(rest, -1, 32, 128), REST)
     decoded = conv(
         jnp.pad(jnp.concatenate([before, hidden], 0), ((0, 0), (0, 0), (1, 1), (0, 0))), weight_two
     ).astype(jnp.bfloat16)
     came, decoded = barrier((came, decoded))
     part, final = combine(count, ins, where, came, vectors)
     grad_pre = grad_before_norm(where, grad_normed, normed, vectors, final)
-    part = exchange(spread(part, rest), REST)
+    part = exchange(spread(part[:, :12], rest), REST)
     after = neighbour(grad_pre, TM, -1)
     part, after = barrier((part, after))
     part = jnp.concatenate([part[:, :, :8].reshape(-1, 128), part[:, :, 8:].reshape(-1, 128)], 0)

time: 167 us -> 170 us (1.018)
  waiting for transfers between devices: 64.8 us -> 68.9 us
    all_to_all x6, waiting for transfers between devices: 55.7 us -> 59.6 us  [exchange(): return lax.all_to_all(copies, axes, 0, 0)]
    unnamed x17 -> x19, local copies, waits for them, and re-layouts: 5.71 us -> 5.72 us
  transfers between devices with their start and end apart: 14 -> 14, of which waited for: 8 -> 8; matrix products, arithmetic and copies ran while one was open for 2% -> 1% of each run, Pallas kernels for 4% -> 4%
where the time goes in v8:
time: 170 us; the launch traced here: 169 us
  starting transfers between devices  73 us (43%)
  waiting for transfers between devices  68.9 us (41%)
  Pallas kernels  15.7 us (9%)
  local copies, waits for them, and re-layouts  8.83 us (5%)
    all_to_all x6, waiting for transfers between devices, exchange(): return lax.all_to_all(copies, axes, 0, 0)  59.6 us
    all_to_all x6, starting transfers between devices, exchange(): return lax.all_to_all(copies, axes, 0, 0)  43.1 us
    ppermute x6, starting transfers between devices, neighbour(): lax.ppermute(value, axis, [(i, i + steps) for i in range(first, last)])  19.8 us
    ppermute x6, waiting for transfers between devices, neighbour(): lax.ppermute(value, axis, [(i, i + steps) for i in range(first, last)])  6.56 us
    ppermute x1, starting transfers between devices, body(): other = lax.ppermute(part, 'c', SWAP)  6.42 us
    unnamed x19, local copies, waits for them, and re-layouts  5.72 us
    pallas_call x2, Pallas kernels, unpack(): pl.pallas_call(functools.partial(unpack_kernel, scale), grid_spec=pltpu.P...  5.17 us
    ppermute x1, starting transfers between devices, body(): part = add_pair(kept, lax.ppermute(away, 'c', SWAP))  3.74 us
  transfers between devices with their start and end apart: 14, of which 8 were waited for; matrix products, arithmetic and copies ran while one was open for 1% of the time, Pallas kernels for 4%

profile of v8, /device:TPU:1, one launch (start us, length us, event | category | flops | bytes accessed | tf_op | source)
XLA Modules:
  0.0 169.4 jit_solution(8928254604554224999)
XLA Ops:
  0.6 1.3 collective-permute-start.1
  1.9 4.7 %collective-permute-start = (bf16[2,2,16,192]{3,2,1,0:T(8,128)(2,1)}, bf16[2,2,16,192]{3,2,1,0:T(8,128)(2,1)S(1)}, u32[]{:S(2)}, u32[]{:S(2)}) collective-permute-start(bf16[2,2,16,192]{3,2,1,0:T(8,128)(2,1)} %refs_0_.1), channel_id=1, source_target_pairs={{0,32},{32,64},{64,96},{96,128},{128,160},{160,192},{192,224},{224... | collective-permute-start | bytes 73736 | tf_op jit(solution)/shard_map/ppermute | solution.py:32
  8.4 4.6 %collective-permute-start.2 = (bf16[4,48,192]{2,1,0:T(8,128)(2,1)S(1)}, bf16[4,48,192]{2,1,0:T(8,128)(2,1)S(1)}, u32[]{:S(2)}, u32[]{:S(2)}) collective-permute-start(bf16[4,48,192]{2,1,0:T(8,128)(2,1)S(1)} %get-tuple-element.46), channel_id=1, source_target_pairs={{0,1},{1,2},{2,3},{3,4},{4,5},{5,6},{6,7},{7,8},{8,9},{9,10},{10,1... | collective-permute-start | bytes 221192 | tf_op jit(solution)/shard_map/ppermute | solution.py:32
  13.0 5.6 %collective-permute-start.3 = (bf16[4,48,192]{2,1,0:T(8,128)(2,1)S(1)}, bf16[4,48,192]{2,1,0:T(8,128)(2,1)S(1)}, u32[]{:S(2)}, u32[]{:S(2)}) collective-permute-start(bf16[4,48,192]{2,1,0:T(8,128)(2,1)S(1)} %get-tuple-element.47), channel_id=1, source_target_pairs={{1,0},{2,1},{3,2},{4,3},{5,4},{6,5},{7,6},{8,7},{9,8},{10,9},{11,1... | collective-permute-start | bytes 221192 | tf_op jit(solution)/shard_map/ppermute | solution.py:32
  18.6 1.3 copy-done.1
  19.9 1.1 copy-done.2
  23.0 8.4 %all-to-all-start = ((f32[32,4,96]{2,1,0:T(4,128)}), f32[32,4,96]{2,1,0:T(4,128)S(1)}, u32[]{:S(2)}, u32[]{:S(2)}) async-start(f32[32,4,96]{2,1,0:T(4,128)} %broadcast_in_dim.18), calls=%async_computation | async-start | bytes 131072 | tf_op jit(solution)/shard_map/all_to_all | solution.py:646
  32.3 6.8 %all-to-all-done = f32[32,4,96]{2,1,0:T(4,128)S(1)} async-done(((f32[32,4,96]{2,1,0:T(4,128)}), f32[32,4,96]{2,1,0:T(4,128)S(1)}, u32[]{:S(2)}, u32[]{:S(2)}) %all-to-all-start) | async-done | bytes 49184 | tf_op jit(solution)/shard_map/all_to_all | solution.py:646
  39.7 16.1 %all-to-all-start.1 = ((f32[16,4,96]{2,1,0:T(4,128)}), f32[16,4,96]{2,1,0:T(4,128)S(1)}, u32[]{:S(2)}, u32[]{:S(2)}) async-start(f32[16,4,96]{2,1,0:T(4,128)} %broadcast_in_dim.19), calls=%async_computation.1 | async-start | bytes 65536 | tf_op jit(solution)/shard_map/all_to_all | solution.py:646
  56.0 11.1 %all-to-all-done.1 = f32[16,4,96]{2,1,0:T(4,128)S(1)} async-done(((f32[16,4,96]{2,1,0:T(4,128)}), f32[16,4,96]{2,1,0:T(4,128)S(1)}, u32[]{:S(2)}, u32[]{:S(2)}) %all-to-all-start.1) | async-done | bytes 24608 | tf_op jit(solution)/shard_map/all_to_all | solution.py:646
  68.9 1.5 weight_grads.1
  70.3 3.7 %collective-permute-start.4 = (bf16[4,1296,128]{2,1,0:T(8,128)(2,1)S(1)}, bf16[4,1296,128]{2,1,0:T(8,128)(2,1)S(1)}, u32[]{:S(2)}, u32[]{:S(2)}) collective-permute-start(bf16[4,1296,128]{2,1,0:T(8,128)(2,1)S(1)} %get-tuple-element.63), channel_id=1, source_target_pairs={{0,1},{1,0},{2,3},{3,2},{4,5},{5,4},{6,7},{7,6},{8,9},{9,8},{10,11... | collective-permute-start | bytes 3981320 | tf_op jit(solution)/shard_map/ppermute | solution.py:674
  74.1 2.7 %collective-permute-done.4.came = bf16[4,1296,128]{2,1,0:T(8,128)(2,1)S(1)} collective-permute-done((bf16[4,1296,128]{2,1,0:T(8,128)(2,1)S(1)}, bf16[4,1296,128]{2,1,0:T(8,128)(2,1)S(1)}, u32[]{:S(2)}, u32[]{:S(2)}) %collective-permute-start.4) | collective-permute-done | bytes 1327136 | tf_op jit(solution)/shard_map/ppermute | solution.py:674
  77.5 1.1 copy-done
  78.5 3.5 %all-to-all-start.2 = ((bf16[4,1296,128]{2,1,0:T(8,128)(2,1)}), bf16[4,1296,128]{2,1,0:T(8,128)(2,1)S(1)}, u32[]{:S(2)}, u32[]{:S(2)}) async-start(bf16[4,1296,128]{2,1,0:T(8,128)(2,1)} %copy-done), calls=%async_computation.2 | async-start | bytes 2654208 | tf_op jit(solution)/shard_map/all_to_all | solution.py:646
  82.1 2.4 %collective-permute-start.5 = (bf16[2,6,32,96]{3,2,1,0:T(8,128)(2,1)S(1)}, bf16[2,6,32,96]{3,2,1,0:T(8,128)(2,1)S(1)}, u32[]{:S(2)}, u32[]{:S(2)}) collective-permute-start(bf16[2,6,32,96]{3,2,1,0:T(8,128)(2,1)S(1)} %get-tuple-element.65.hidden), channel_id=1, source_target_pairs={{0,32},{32,64},{64,96},{96,128},{128,160},{160,192},{192,224},{224... | collective-permute-start | bytes 221192 | tf_op jit(solution)/shard_map/ppermute | solution.py:32
  84.5 15.4 %all-to-all-done.2.came = bf16[4,1296,128]{2,1,0:T(8,128)(2,1)S(1)} async-done(((bf16[4,1296,128]{2,1,0:T(8,128)(2,1)}), bf16[4,1296,128]{2,1,0:T(8,128)(2,1)S(1)}, u32[]{:S(2)}, u32[]{:S(2)}) %all-to-all-start.2) | async-done | bytes 1327136 | tf_op jit(solution)/shard_map/all_to_all | solution.py:646
  99.9 1.1 add_row.1
  100.9 4.8 %all-to-all-start.3 = ((bf16[64,1,32,128]{3,2,1,0:T(8,128)(2,1)}), bf16[64,1,32,128]{3,2,1,0:T(8,128)(2,1)S(1)}, u32[]{:S(2)}, u32[]{:S(2)}) async-start(bf16[64,1,32,128]{3,2,1,0:T(8,128)(2,1)} %bitcast.6), calls=%async_computation.3 | async-start | bytes 1048576 | tf_op jit(solution)/shard_map/all_to_all | solution.py:646
  105.8 1.5 convolution_convert_fusion
  108.0 15.2 %all-to-all-done.3.came = bf16[64,1,32,128]{3,2,1,0:T(8,128)(2,1)S(1)} async-done(((bf16[64,1,32,128]{3,2,1,0:T(8,128)(2,1)}), bf16[64,1,32,128]{3,2,1,0:T(8,128)(2,1)S(1)}, u32[]{:S(2)}, u32[]{:S(2)}) %all-to-all-start.3) | async-done | bytes 524320 | tf_op jit(solution)/shard_map/all_to_all | solution.py:646
  123.2 1.1 combine.1
  125.1 6.8 %all-to-all-start.4 = ((bf16[64,1,12,128]{3,2,1,0:T(8,128)(2,1)}), bf16[64,1,12,128]{3,2,1,0:T(8,128)(2,1)S(1)}, u32[]{:S(2)}, u32[]{:S(2)}) async-start(bf16[64,1,12,128]{3,2,1,0:T(8,128)(2,1)} %broadcast_in_dim.45), calls=%async_computation.4 | async-start | bytes 524288 | tf_op jit(solution)/shard_map/all_to_all | solution.py:646
  132.5 1.3 collective-permute-start.6
  133.8 6.5 %collective-permute-done.6 = bf16[2,6,32,96]{3,2,1,0:T(8,128)(2,1)S(1)} collective-permute-done((bf16[2,6,32,96]{3,2,1,0:T(8,128)(2,1)S(1)}, bf16[2,6,32,96]{3,2,1,0:T(8,128)(2,1)S(1)}, u32[]{:S(2)}, u32[]{:S(2)}) %collective-permute-start.6) | collective-permute-done | bytes 73760 | tf_op jit(solution)/shard_map/ppermute | solution.py:32
  140.4 4.2 %all-to-all-done.4 = bf16[64,1,12,128]{3,2,1,0:T(8,128)(2,1)S(1)} async-done(((bf16[64,1,12,128]{3,2,1,0:T(8,128)(2,1)}), bf16[64,1,12,128]{3,2,1,0:T(8,128)(2,1)S(1)}, u32[]{:S(2)}, u32[]{:S(2)}) %all-to-all-start.4) | async-done | bytes 196640 | tf_op jit(solution)/shard_map/all_to_all | solution.py:646
  145.6 3.5 %all-to-all-start.5 = ((bf16[4,768,128]{2,1,0:T(8,128)(2,1)}), bf16[4,768,128]{2,1,0:T(8,128)(2,1)S(1)}, u32[]{:S(2)}, u32[]{:S(2)}) async-start(bf16[4,768,128]{2,1,0:T(8,128)(2,1)} %broadcast_in_dim.46), calls=%async_computation.5 | async-start | bytes 1572864 | tf_op jit(solution)/shard_map/all_to_all | solution.py:646
  149.1 1.6 feature_grads.1
  150.8 7.0 %all-to-all-done.5.part = bf16[4,768,128]{2,1,0:T(8,128)(2,1)S(1)} async-done(((bf16[4,768,128]{2,1,0:T(8,128)(2,1)}), bf16[4,768,128]{2,1,0:T(8,128)(2,1)S(1)}, u32[]{:S(2)}, u32[]{:S(2)}) %all-to-all-start.5) | async-done | bytes 786464 | tf_op jit(solution)/shard_map/all_to_all | solution.py:646
  157.8 6.4 %collective-permute-start.7 = (bf16[4,768,128]{2,1,0:T(8,128)(2,1)S(1)}, bf16[4,768,128]{2,1,0:T(8,128)(2,1)S(1)}, u32[]{:S(2)}, u32[]{:S(2)}) collective-permute-start(bf16[4,768,128]{2,1,0:T(8,128)(2,1)S(1)} %all-to-all-done.5.part), channel_id=1, source_target_pairs={{0,1},{1,0},{2,3},{3,2},{4,5},{5,4},{6,7},{7,6},{8,9},{9,8},{10,11... | collective-permute-start | bytes 2359304 | tf_op jit(solution)/shard_map/ppermute | solution.py:693
  164.2 2.6 %unpack.2 = (f32[27,192,96]{2,1,0:T(8,128)}, f32[27,96,96]{2,1,0:T(8,128)}) custom-call(s32[1]{0:T(128)} %bitcast.half, bf16[4,768,128]{2,1,0:T(8,128)(2,1)S(1)} %all-to-all-done.5.part, f32[8,96]{1,0:T(8,128)S(1)} %get-tuple-element.71.final), custom_call_target="tpu_custom_call" | custom-call | flops 1048576 | bytes 4194304 | tf_op jit(solution)/shard_map/unpack/pallas_call | solution.py:573
  166.8 2.6 %unpack.3 = (f32[27,192,96]{2,1,0:T(8,128)}, f32[27,96,96]{2,1,0:T(8,128)}) custom-call(s32[1]{0:T(128)S(6)} %sub.3.half, bf16[4,768,128]{2,1,0:T(8,128)(2,1)S(1)} %collective-permute-done.7.part, f32[8,96]{1,0:T(8,128)S(1)} %get-tuple-element.71.final, f32[27,192,96]{2,1,0:T(8,128)} %get-tuple-element.76.rest_0_, ...), custom_call_target="tpu_custom_call", output_to_operand_aliasing={{0}: (3, {}), {1}: (4, {})} | custom-call | flops 1048576 | bytes 4194304 | tf_op jit(solution)/shard_map/unpack/pallas_call | solution.py:573
  (48 shorter events, 11.0 us)
Async XLA Ops:
  0.6 7.7 %collective-permute-start.1 = (bf16[2,4,32,96]{3,2,1,0:T(8,128)(2,1)}, bf16[2,4,32,96]{3,2,1,0:T(8,128)(2,1)S(1)}, u32[]{:S(2)}, u32[]{:S(2)}) collective-permute-start(bf16[2,4,32,96]{3,2,1,0:T(8,128)(2,1)} %refs_1_.1), channel_id=1, source_target_pairs={{32,0},{64,32},{96,64},{128,96},{160,128},{192,160},{224,192},{256... | collective-permute-start | bytes 147464 | tf_op jit(solution)/shard_map/ppermute | solution.py:32
  1.9 6.4 %collective-permute-start = (bf16[2,2,16,192]{3,2,1,0:T(8,128)(2,1)}, bf16[2,2,16,192]{3,2,1,0:T(8,128)(2,1)S(1)}, u32[]{:S(2)}, u32[]{:S(2)}) collective-permute-start(bf16[2,2,16,192]{3,2,1,0:T(8,128)(2,1)} %refs_0_.1), channel_id=1, source_target_pairs={{0,32},{32,64},{64,96},{96,128},{128,160},{160,192},{192,224},{224... | collective-permute-start | bytes 73736 | tf_op jit(solution)/shard_map/ppermute | solution.py:32
  6.6 0.8 copy-start.3
  7.4 0.8 copy-start.4
  8.4 12.9 %collective-permute-start.2 = (bf16[4,48,192]{2,1,0:T(8,128)(2,1)S(1)}, bf16[4,48,192]{2,1,0:T(8,128)(2,1)S(1)}, u32[]{:S(2)}, u32[]{:S(2)}) collective-permute-start(bf16[4,48,192]{2,1,0:T(8,128)(2,1)S(1)} %get-tuple-element.46), channel_id=1, source_target_pairs={{0,1},{1,2},{2,3},{3,4},{4,5},{5,6},{6,7},{7,8},{8,9},{9,10},{10,1... | collective-permute-start | bytes 221192 | tf_op jit(solution)/shard_map/ppermute | solution.py:32
  13.0 8.4 %collective-permute-start.3 = (bf16[4,48,192]{2,1,0:T(8,128)(2,1)S(1)}, bf16[4,48,192]{2,1,0:T(8,128)(2,1)S(1)}, u32[]{:S(2)}, u32[]{:S(2)}) collective-permute-start(bf16[4,48,192]{2,1,0:T(8,128)(2,1)S(1)} %get-tuple-element.47), channel_id=1, source_target_pairs={{1,0},{2,1},{3,2},{4,3},{5,4},{6,5},{7,6},{8,7},{9,8},{10,9},{11,1... | collective-permute-start | bytes 221192 | tf_op jit(solution)/shard_map/ppermute | solution.py:32
  18.6 1.3 copy-start.1
  19.9 1.1 copy-start.2
  21.4 10.9 %copy-start.5 = (bf16[3,3,3,96,96]{4,3,2,1,0:T(8,128)(2,1)}, bf16[3,3,3,96,96]{4,3,2,1,0:T(8,128)(2,1)S(1)}, u32[]{:S(2)}) copy-start(bf16[3,3,3,96,96]{4,3,2,1,0:T(8,128)(2,1)S(1)} %get-tuple-element.52.weight) | copy-start | bytes 1492996
  23.0 16.1 %all-to-all-start = ((f32[32,4,96]{2,1,0:T(4,128)}), f32[32,4,96]{2,1,0:T(4,128)S(1)}, u32[]{:S(2)}, u32[]{:S(2)}) async-start(f32[32,4,96]{2,1,0:T(4,128)} %broadcast_in_dim.18), calls=%async_computation | async-start | bytes 131072 | tf_op jit(solution)/shard_map/all_to_all | solution.py:646
  31.3 35.8 %copy-start.7 = (f32[96]{0:T(128)S(1)}, f32[96]{0:T(128)}, u32[]{:S(2)}) copy-start(f32[96]{0:T(128)} %param.11) | copy-start | bytes 1156
  31.3 35.8 %copy-start.8 = (f32[96]{0:T(128)S(1)}, f32[96]{0:T(128)}, u32[]{:S(2)}) copy-start(f32[96]{0:T(128)} %param.10) | copy-start | bytes 1156
  39.7 27.4 %all-to-all-start.1 = ((f32[16,4,96]{2,1,0:T(4,128)}), f32[16,4,96]{2,1,0:T(4,128)S(1)}, u32[]{:S(2)}, u32[]{:S(2)}) async-start(f32[16,4,96]{2,1,0:T(4,128)} %broadcast_in_dim.19), calls=%async_computation.1 | async-start | bytes 65536 | tf_op jit(solution)/shard_map/all_to_all | solution.py:646
  70.3 6.4 %collective-permute-start.4 = (bf16[4,1296,128]{2,1,0:T(8,128)(2,1)S(1)}, bf16[4,1296,128]{2,1,0:T(8,128)(2,1)S(1)}, u32[]{:S(2)}, u32[]{:S(2)}) collective-permute-start(bf16[4,1296,128]{2,1,0:T(8,128)(2,1)S(1)} %get-tuple-element.63), channel_id=1, source_target_pairs={{0,1},{1,0},{2,3},{3,2},{4,5},{5,4},{6,7},{7,6},{8,9},{9,8},{10,11... | collective-permute-start | bytes 3981320 | tf_op jit(solution)/shard_map/ppermute | solution.py:674
  77.4 1.1 copy-start
  78.5 21.3 %all-to-all-start.2 = ((bf16[4,1296,128]{2,1,0:T(8,128)(2,1)}), bf16[4,1296,128]{2,1,0:T(8,128)(2,1)S(1)}, u32[]{:S(2)}, u32[]{:S(2)}) async-start(bf16[4,1296,128]{2,1,0:T(8,128)(2,1)} %copy-done), calls=%async_computation.2 | async-start | bytes 2654208 | tf_op jit(solution)/shard_map/all_to_all | solution.py:646
  82.1 18.9 %collective-permute-start.5 = (bf16[2,6,32,96]{3,2,1,0:T(8,128)(2,1)S(1)}, bf16[2,6,32,96]{3,2,1,0:T(8,128)(2,1)S(1)}, u32[]{:S(2)}, u32[]{:S(2)}) collective-permute-start(bf16[2,6,32,96]{3,2,1,0:T(8,128)(2,1)S(1)} %get-tuple-element.65.hidden), channel_id=1, source_target_pairs={{0,32},{32,64},{64,96},{96,128},{128,160},{160,192},{192,224},{224... | collective-permute-start | bytes 221192 | tf_op jit(solution)/shard_map/ppermute | solution.py:32
  100.9 4.9 %copy-start.6 = (bf16[3,3,3,96,96]{4,3,2,1,0:T(8,128)(2,1)S(1)}, bf16[3,3,3,96,96]{4,3,2,1,0:T(8,128)(2,1)}, u32[]{:S(2)}) copy-start(bf16[3,3,3,96,96]{4,3,2,1,0:T(8,128)(2,1)} %copy-done.5) | copy-start | bytes 1492996
  100.9 22.3 %all-to-all-start.3 = ((bf16[64,1,32,128]{3,2,1,0:T(8,128)(2,1)}), bf16[64,1,32,128]{3,2,1,0:T(8,128)(2,1)S(1)}, u32[]{:S(2)}, u32[]{:S(2)}) async-start(bf16[64,1,32,128]{3,2,1,0:T(8,128)(2,1)} %bitcast.6), calls=%async_computation.3 | async-start | bytes 1048576 | tf_op jit(solution)/shard_map/all_to_all | solution.py:646
  125.1 19.4 %all-to-all-start.4 = ((bf16[64,1,12,128]{3,2,1,0:T(8,128)(2,1)}), bf16[64,1,12,128]{3,2,1,0:T(8,128)(2,1)S(1)}, u32[]{:S(2)}, u32[]{:S(2)}) async-start(bf16[64,1,12,128]{3,2,1,0:T(8,128)(2,1)} %broadcast_in_dim.45), calls=%async_computation.4 | async-start | bytes 524288 | tf_op jit(solution)/shard_map/all_to_all | solution.py:646
  132.5 7.8 %collective-permute-start.6 = (bf16[2,6,32,96]{3,2,1,0:T(8,128)(2,1)S(1)}, bf16[2,6,32,96]{3,2,1,0:T(8,128)(2,1)S(1)}, u32[]{:S(2)}, u32[]{:S(2)}) collective-permute-start(bf16[2,6,32,96]{3,2,1,0:T(8,128)(2,1)S(1)} %grad_pre.1), channel_id=1, source_target_pairs={{32,0},{64,32},{96,64},{128,96},{160,128},{192,160},{224,192},{256... | collective-permute-start | bytes 221192 | tf_op jit(solution)/shard_map/ppermute | solution.py:32
  145.6 12.2 %all-to-all-start.5 = ((bf16[4,768,128]{2,1,0:T(8,128)(2,1)}), bf16[4,768,128]{2,1,0:T(8,128)(2,1)S(1)}, u32[]{:S(2)}, u32[]{:S(2)}) async-start(bf16[4,768,128]{2,1,0:T(8,128)(2,1)} %broadcast_in_dim.46), calls=%async_computation.5 | async-start | bytes 1572864 | tf_op jit(solution)/shard_map/all_to_all | solution.py:646
  157.8 9.0 %collective-permute-start.7 = (bf16[4,768,128]{2,1,0:T(8,128)(2,1)S(1)}, bf16[4,768,128]{2,1,0:T(8,128)(2,1)S(1)}, u32[]{:S(2)}, u32[]{:S(2)}) collective-permute-start(bf16[4,768,128]{2,1,0:T(8,128)(2,1)S(1)} %all-to-all-done.5.part), channel_id=1, source_target_pairs={{0,1},{1,0},{2,3},{3,2},{4,5},{5,4},{6,7},{7,6},{8,9},{9,8},{10,11... | collective-permute-start | bytes 2359304 | tf_op jit(solution)/shard_map/ppermute | solution.py:693

commit v9 on v7

--- a/solution.py
+++ b/solution.py
@@ -490,10 +490,8 @@
     second = exact(sums, group_lanes(outs, False), ((1,), (1,)))
     rest = (first - vectors[1:2]) * vectors[0:1]
     final[...] = jnp.concatenate([first, second, rest, jnp.zeros((5, outs), jnp.float32)], 0)
-    lane = lax.broadcasted_iota(jnp.int32, (outs, 896), 1)
-    channel = lax.broadcasted_iota(jnp.int32, (outs, 896), 0)
-    spread = ((lane % outs == channel) & (lane < 9 * outs)).astype(jnp.float32)
-    lanes[...] = jnp.broadcast_to(exact(second - vectors[2:3], spread, ((1,), (0,))), lanes.shape)
+    spread = [second - vectors[2:3]] * 9 + [jnp.zeros((1, 32), jnp.float32)]
+    lanes[...] = jnp.broadcast_to(jnp.concatenate(spread, 1), lanes.shape)
     for k in range(piece.shape[0]):
         block = (where[3] * piece.shape[0] + k) // tiles_per_block % 7
         change = lanes[0:1, pl.ds(pl.multiple_of(block * 128, 128), 128)]
@@ -554,20 +552,24 @@
         blocks = []
         for j in range(7):
             at = pl.multiple_of(begin + (step * 7 + j) * channels, 16)
-            blocks.append(flat[pl.ds(at, channels)].astype(jnp.float32))
-        lanes = jnp.concatenate(blocks, 1) * scale
+            blocks.append(flat[pl.ds(at, channels)])
+        lanes = jnp.concatenate(blocks, 1)
         if out is one:
-            change = jnp.concatenate([final[2:3]] * taps + [jnp.zeros((1, 32), jnp.float32)], 1)
+            change = jnp.concatenate([final[2:3], jnp.zeros((1, 128 - outs), jnp.float32)], 1)
+            change = jnp.concatenate([change] * taps, 1)
             tap = lax.broadcasted_iota(jnp.int32, (32, change.shape[1]), 0)
             lane = lax.broadcasted_iota(jnp.int32, (32, change.shape[1]), 1)
-            change = jnp.where(lane // outs == tap, change, 0.0)
+            change = jnp.where(lane // 128 == tap, change, 0.0)
             high = change.astype(jnp.bfloat16)
             low = (change - high.astype(jnp.float32)).astype(jnp.bfloat16)
-            met = jnp.concatenate([blocks[-1][:, 96:]] * 2, 1).astype(jnp.bfloat16)
+            met = jnp.concatenate([blocks[-1].astype(jnp.float32)[:, 96:]] * 2, 1).astype(jnp.bfloat16)
             change = jnp.concatenate([high, low], 0)
-            lanes -= jnp.dot(met, change, preferred_element_type=jnp.float32) * scale
+            change = jnp.dot(met, change, preferred_element_type=jnp.float32)
         for k in range(taps):
-            out[k] = lanes[:, outs * k : outs * k + outs]
+            grad = lanes[:, outs * k : outs * k + outs].astype(jnp.float32)
+            if out is one:
+                grad = grad - change[:, 128 * k : 128 * k + outs]
+            out[k] = grad * scale
 
 
 def unpack(half, part, final, ins, mids, scale, begun=()):

time: 167 us -> 167 us (level)
  no operation moved by 1% of the time
where the time goes in v9:
time: 167 us; the launch traced here: 166 us
  starting transfers between devices  73 us (44%)
  waiting for transfers between devices  64.8 us (39%)
  Pallas kernels  16.4 us (10%)
  local copies, waits for them, and re-layouts  8.12 us (5%)
  matrix products  2.6 us (2%)
    all_to_all x6, waiting for transfers between devices, exchange(): return lax.all_to_all(copies, axes, 0, 0)  55.7 us
    all_to_all x6, starting transfers between devices, exchange(): return lax.all_to_all(copies, axes, 0, 0)  42.8 us
    ppermute x6, starting transfers between devices, neighbour(): lax.ppermute(value, axis, [(i, i + steps) for i in range(first, last)])  19.8 us
    ppermute x1, starting transfers between devices, body(): other = lax.ppermute(part, 'c', SWAP)  6.68 us
    ppermute x6, waiting for transfers between devices, neighbour(): lax.ppermute(value, axis, [(i, i + steps) for i in range(first, last)])  6.46 us
    unnamed x17, local copies, waits for them, and re-layouts  5.71 us
    pallas_call x2, Pallas kernels, unpack(): pl.pallas_call(functools.partial(unpack_kernel, scale), grid_spec=pltpu.P...  5.42 us
    ppermute x1, starting transfers between devices, body(): part = add_pair(kept, lax.ppermute(away, 'c', SWAP))  3.74 us
  transfers between devices with their start and end apart: 14, of which 8 were waited for; matrix products, arithmetic and copies ran while one was open for 2% of the time, Pallas kernels for 4%

profile of v9, /device:TPU:1, one launch (start us, length us, event | category | flops | bytes accessed | tf_op | source)
XLA Modules:
  0.0 166.2 jit_solution(13355477825275035018)
XLA Ops:
  0.6 1.3 collective-permute-start.1
  1.9 4.7 %collective-permute-start = (bf16[2,2,16,192]{3,2,1,0:T(8,128)(2,1)}, bf16[2,2,16,192]{3,2,1,0:T(8,128)(2,1)S(1)}, u32[]{:S(2)}, u32[]{:S(2)}) collective-permute-start(bf16[2,2,16,192]{3,2,1,0:T(8,128)(2,1)} %refs_0_.1), channel_id=1, source_target_pairs={{0,32},{32,64},{64,96},{96,128},{128,160},{160,192},{192,224},{224... | collective-permute-start | bytes 73736 | tf_op jit(solution)/shard_map/ppermute | solution.py:32
  8.4 4.6 %collective-permute-start.2 = (bf16[4,48,192]{2,1,0:T(8,128)(2,1)S(1)}, bf16[4,48,192]{2,1,0:T(8,128)(2,1)S(1)}, u32[]{:S(2)}, u32[]{:S(2)}) collective-permute-start(bf16[4,48,192]{2,1,0:T(8,128)(2,1)S(1)} %get-tuple-element.46), channel_id=1, source_target_pairs={{0,1},{1,2},{2,3},{3,4},{4,5},{5,6},{6,7},{7,8},{8,9},{9,10},{10,1... | collective-permute-start | bytes 221192 | tf_op jit(solution)/shard_map/ppermute | solution.py:32
  13.0 5.6 %collective-permute-start.3 = (bf16[4,48,192]{2,1,0:T(8,128)(2,1)S(1)}, bf16[4,48,192]{2,1,0:T(8,128)(2,1)S(1)}, u32[]{:S(2)}, u32[]{:S(2)}) collective-permute-start(bf16[4,48,192]{2,1,0:T(8,128)(2,1)S(1)} %get-tuple-element.47), channel_id=1, source_target_pairs={{1,0},{2,1},{3,2},{4,3},{5,4},{6,5},{7,6},{8,7},{9,8},{10,9},{11,1... | collective-permute-start | bytes 221192 | tf_op jit(solution)/shard_map/ppermute | solution.py:32
  18.6 1.3 copy-done.1
  19.9 1.1 copy-done.2
  21.4 1.6 conv_one.1
  22.9 8.4 %all-to-all-start = ((f32[32,4,96]{2,1,0:T(4,128)}), f32[32,4,96]{2,1,0:T(4,128)S(1)}, u32[]{:S(2)}, u32[]{:S(2)}) async-start(f32[32,4,96]{2,1,0:T(4,128)} %get-tuple-element.51), calls=%async_computation | async-start | bytes 131072 | tf_op jit(solution)/shard_map/all_to_all | solution.py:649
  32.3 6.8 %all-to-all-done = f32[32,4,96]{2,1,0:T(4,128)S(1)} async-done(((f32[32,4,96]{2,1,0:T(4,128)}), f32[32,4,96]{2,1,0:T(4,128)S(1)}, u32[]{:S(2)}, u32[]{:S(2)}) %all-to-all-start) | async-done | bytes 49184 | tf_op jit(solution)/shard_map/all_to_all | solution.py:649
  39.7 16.1 %all-to-all-start.1 = ((f32[16,4,96]{2,1,0:T(4,128)}), f32[16,4,96]{2,1,0:T(4,128)S(1)}, u32[]{:S(2)}, u32[]{:S(2)}) async-start(f32[16,4,96]{2,1,0:T(4,128)} %broadcast_in_dim.14), calls=%async_computation.1 | async-start | bytes 65536 | tf_op jit(solution)/shard_map/all_to_all | solution.py:649
  55.9 11.2 %all-to-all-done.1.came = f32[16,4,96]{2,1,0:T(4,128)S(1)} async-done(((f32[16,4,96]{2,1,0:T(4,128)}), f32[16,4,96]{2,1,0:T(4,128)S(1)}, u32[]{:S(2)}, u32[]{:S(2)}) %all-to-all-start.1) | async-done | bytes 24608 | tf_op jit(solution)/shard_map/all_to_all | solution.py:649
  68.7 1.5 weight_grads.1
  70.2 3.7 %collective-permute-start.4 = (bf16[4,1296,128]{2,1,0:T(8,128)(2,1)S(1)}, bf16[4,1296,128]{2,1,0:T(8,128)(2,1)S(1)}, u32[]{:S(2)}, u32[]{:S(2)}) collective-permute-start(bf16[4,1296,128]{2,1,0:T(8,128)(2,1)S(1)} %get-tuple-element.63), channel_id=1, source_target_pairs={{0,1},{1,0},{2,3},{3,2},{4,5},{5,4},{6,7},{7,6},{8,9},{9,8},{10,11... | collective-permute-start | bytes 3981320 | tf_op jit(solution)/shard_map/ppermute | solution.py:678
  74.0 2.7 %collective-permute-done.4.came = bf16[4,1296,128]{2,1,0:T(8,128)(2,1)S(1)} collective-permute-done((bf16[4,1296,128]{2,1,0:T(8,128)(2,1)S(1)}, bf16[4,1296,128]{2,1,0:T(8,128)(2,1)S(1)}, u32[]{:S(2)}, u32[]{:S(2)}) %collective-permute-start.4) | collective-permute-done | bytes 1327136 | tf_op jit(solution)/shard_map/ppermute | solution.py:678
  77.3 1.1 copy-done
  78.4 3.5 %all-to-all-start.2 = ((bf16[4,1296,128]{2,1,0:T(8,128)(2,1)}), bf16[4,1296,128]{2,1,0:T(8,128)(2,1)S(1)}, u32[]{:S(2)}, u32[]{:S(2)}) async-start(bf16[4,1296,128]{2,1,0:T(8,128)(2,1)} %copy-done), calls=%async_computation.2 | async-start | bytes 2654208 | tf_op jit(solution)/shard_map/all_to_all | solution.py:649
  81.9 2.4 %collective-permute-start.5 = (bf16[2,6,32,96]{3,2,1,0:T(8,128)(2,1)S(1)}, bf16[2,6,32,96]{3,2,1,0:T(8,128)(2,1)S(1)}, u32[]{:S(2)}, u32[]{:S(2)}) collective-permute-start(bf16[2,6,32,96]{3,2,1,0:T(8,128)(2,1)S(1)} %get-tuple-element.65.hidden), channel_id=1, source_target_pairs={{0,32},{32,64},{64,96},{96,128},{128,160},{160,192},{192,224},{224... | collective-permute-start | bytes 221192 | tf_op jit(solution)/shard_map/ppermute | solution.py:32
  84.4 15.4 %all-to-all-done.2.came = bf16[4,1296,128]{2,1,0:T(8,128)(2,1)S(1)} async-done(((bf16[4,1296,128]{2,1,0:T(8,128)(2,1)}), bf16[4,1296,128]{2,1,0:T(8,128)(2,1)S(1)}, u32[]{:S(2)}, u32[]{:S(2)}) %all-to-all-start.2) | async-done | bytes 1327136 | tf_op jit(solution)/shard_map/all_to_all | solution.py:649
  99.7 1.0 add_row.1
  100.8 4.6 %all-to-all-start.3 = ((bf16[64,1,3,8,128]{4,3,2,1,0:T(8,128)(2,1)}), bf16[64,1,3,8,128]{4,3,2,1,0:T(8,128)(2,1)S(1)}, u32[]{:S(2)}, u32[]{:S(2)}) async-start(bf16[64,1,3,8,128]{4,3,2,1,0:T(8,128)(2,1)} %bitcast.6), calls=%async_computation.3 | async-start | bytes 786432 | tf_op jit(solution)/shard_map/all_to_all | solution.py:649
  105.5 2.6 %convolution_convert_fusion = bf16[1,2,4,32,96]{4,0,3,2,1:T(2,128)(2,1)S(1)} fusion(bf16[3,3,3,96,96]{4,3,2,1,0:T(8,128)(2,1)} %copy-done.7, bf16[1,4,6,34,96]{4,3,2,1,0:T(8,128)(2,1)S(1)} %fusion.5), kind=kOutput, calls=%fused_computation | convolution fusion | flops 127426560 | bytes 703488 | tf_op jit(solution)/shard_map/conv_general_dilated | solution.py:36
  108.8 11.4 %all-to-all-done.3.came = bf16[64,1,3,8,128]{4,3,2,1,0:T(8,128)(2,1)S(1)} async-done(((bf16[64,1,3,8,128]{4,3,2,1,0:T(8,128)(2,1)}), bf16[64,1,3,8,128]{4,3,2,1,0:T(8,128)(2,1)S(1)}, u32[]{:S(2)}, u32[]{:S(2)}) %all-to-all-start.3) | async-done | bytes 393248 | tf_op jit(solution)/shard_map/all_to_all | solution.py:649
  121.9 6.7 %all-to-all-start.4 = ((bf16[64,1,12,128]{3,2,1,0:T(8,128)(2,1)}), bf16[64,1,12,128]{3,2,1,0:T(8,128)(2,1)S(1)}, u32[]{:S(2)}, u32[]{:S(2)}) async-start(bf16[64,1,12,128]{3,2,1,0:T(8,128)(2,1)} %broadcast_in_dim.34), calls=%async_computation.4 | async-start | bytes 524288 | tf_op jit(solution)/shard_map/all_to_all | solution.py:649
  129.1 1.3 collective-permute-start.6
  130.4 6.4 %collective-permute-done.6 = bf16[2,6,32,96]{3,2,1,0:T(8,128)(2,1)S(1)} collective-permute-done((bf16[2,6,32,96]{3,2,1,0:T(8,128)(2,1)S(1)}, bf16[2,6,32,96]{3,2,1,0:T(8,128)(2,1)S(1)}, u32[]{:S(2)}, u32[]{:S(2)}) %collective-permute-start.6) | collective-permute-done | bytes 73760 | tf_op jit(solution)/shard_map/ppermute | solution.py:32
  136.9 4.2 %all-to-all-done.4 = bf16[64,1,12,128]{3,2,1,0:T(8,128)(2,1)S(1)} async-done(((bf16[64,1,12,128]{3,2,1,0:T(8,128)(2,1)}), bf16[64,1,12,128]{3,2,1,0:T(8,128)(2,1)S(1)}, u32[]{:S(2)}, u32[]{:S(2)}) %all-to-all-start.4) | async-done | bytes 196640 | tf_op jit(solution)/shard_map/all_to_all | solution.py:649
  142.1 3.5 %all-to-all-start.5 = ((bf16[4,768,128]{2,1,0:T(8,128)(2,1)}), bf16[4,768,128]{2,1,0:T(8,128)(2,1)S(1)}, u32[]{:S(2)}, u32[]{:S(2)}) async-start(bf16[4,768,128]{2,1,0:T(8,128)(2,1)} %broadcast_in_dim.35), calls=%async_computation.5 | async-start | bytes 1572864 | tf_op jit(solution)/shard_map/all_to_all | solution.py:649
  145.7 1.6 feature_grads.1
  147.3 6.7 %all-to-all-done.5.part = bf16[4,768,128]{2,1,0:T(8,128)(2,1)S(1)} async-done(((bf16[4,768,128]{2,1,0:T(8,128)(2,1)}), bf16[4,768,128]{2,1,0:T(8,128)(2,1)S(1)}, u32[]{:S(2)}, u32[]{:S(2)}) %all-to-all-start.5) | async-done | bytes 786464 | tf_op jit(solution)/shard_map/all_to_all | solution.py:649
  154.1 6.7 %collective-permute-start.7 = (bf16[4,768,128]{2,1,0:T(8,128)(2,1)S(1)}, bf16[4,768,128]{2,1,0:T(8,128)(2,1)S(1)}, u32[]{:S(2)}, u32[]{:S(2)}) collective-permute-start(bf16[4,768,128]{2,1,0:T(8,128)(2,1)S(1)} %all-to-all-done.5.part), channel_id=1, source_target_pairs={{0,1},{1,0},{2,3},{3,2},{4,5},{5,4},{6,7},{7,6},{8,9},{9,8},{10,11... | collective-permute-start | bytes 2359304 | tf_op jit(solution)/shard_map/ppermute | solution.py:697
  160.7 2.7 %unpack.2 = (f32[27,192,96]{2,1,0:T(8,128)}, f32[27,96,96]{2,1,0:T(8,128)}) custom-call(s32[1]{0:T(128)} %bitcast.half, bf16[4,768,128]{2,1,0:T(8,128)(2,1)S(1)} %all-to-all-done.5.part, f32[8,96]{1,0:T(8,128)S(1)} %get-tuple-element.71.final), custom_call_target="tpu_custom_call" | custom-call | flops 1048576 | bytes 4194304 | tf_op jit(solution)/shard_map/unpack/pallas_call | solution.py:576
  163.5 2.7 %unpack.3 = (f32[27,192,96]{2,1,0:T(8,128)}, f32[27,96,96]{2,1,0:T(8,128)}) custom-call(s32[1]{0:T(128)S(6)} %sub.3.half, bf16[4,768,128]{2,1,0:T(8,128)(2,1)S(1)} %collective-permute-done.7.part, f32[8,96]{1,0:T(8,128)S(1)} %get-tuple-element.71.final, f32[27,192,96]{2,1,0:T(8,128)} %get-tuple-element.76.rest_0_, ...), custom_call_target="tpu_custom_call", output_to_operand_aliasing={{0}: (3, {}), {1}: (4, {})} | custom-call | flops 1048576 | bytes 4194304 | tf_op jit(solution)/shard_map/unpack/pallas_call | solution.py:576
  (39 shorter events, 10.2 us)
Async XLA Ops:
  0.6 7.7 %collective-permute-start.1 = (bf16[2,4,32,96]{3,2,1,0:T(8,128)(2,1)}, bf16[2,4,32,96]{3,2,1,0:T(8,128)(2,1)S(1)}, u32[]{:S(2)}, u32[]{:S(2)}) collective-permute-start(bf16[2,4,32,96]{3,2,1,0:T(8,128)(2,1)} %refs_1_.1), channel_id=1, source_target_pairs={{32,0},{64,32},{96,64},{128,96},{160,128},{192,160},{224,192},{256... | collective-permute-start | bytes 147464 | tf_op jit(solution)/shard_map/ppermute | solution.py:32
  1.9 6.4 %collective-permute-start = (bf16[2,2,16,192]{3,2,1,0:T(8,128)(2,1)}, bf16[2,2,16,192]{3,2,1,0:T(8,128)(2,1)S(1)}, u32[]{:S(2)}, u32[]{:S(2)}) collective-permute-start(bf16[2,2,16,192]{3,2,1,0:T(8,128)(2,1)} %refs_0_.1), channel_id=1, source_target_pairs={{0,32},{32,64},{64,96},{96,128},{128,160},{160,192},{192,224},{224... | collective-permute-start | bytes 73736 | tf_op jit(solution)/shard_map/ppermute | solution.py:32
  6.6 0.8 copy-start.3
  7.4 0.8 copy-start.4
  8.4 12.9 %collective-permute-start.2 = (bf16[4,48,192]{2,1,0:T(8,128)(2,1)S(1)}, bf16[4,48,192]{2,1,0:T(8,128)(2,1)S(1)}, u32[]{:S(2)}, u32[]{:S(2)}) collective-permute-start(bf16[4,48,192]{2,1,0:T(8,128)(2,1)S(1)} %get-tuple-element.46), channel_id=1, source_target_pairs={{0,1},{1,2},{2,3},{3,4},{4,5},{5,6},{6,7},{7,8},{8,9},{9,10},{10,1... | collective-permute-start | bytes 221192 | tf_op jit(solution)/shard_map/ppermute | solution.py:32
  13.0 8.4 %collective-permute-start.3 = (bf16[4,48,192]{2,1,0:T(8,128)(2,1)S(1)}, bf16[4,48,192]{2,1,0:T(8,128)(2,1)S(1)}, u32[]{:S(2)}, u32[]{:S(2)}) collective-permute-start(bf16[4,48,192]{2,1,0:T(8,128)(2,1)S(1)} %get-tuple-element.47), channel_id=1, source_target_pairs={{1,0},{2,1},{3,2},{4,3},{5,4},{6,5},{7,6},{8,7},{9,8},{10,9},{11,1... | collective-permute-start | bytes 221192 | tf_op jit(solution)/shard_map/ppermute | solution.py:32
  18.6 1.3 copy-start.1
  19.9 1.1 copy-start.2
  21.4 45.8 %copy-start.7 = (bf16[3,3,3,96,96]{4,3,2,1,0:T(8,128)(2,1)}, bf16[3,3,3,96,96]{4,3,2,1,0:T(8,128)(2,1)S(1)}, u32[]{:S(2)}) copy-start(bf16[3,3,3,96,96]{4,3,2,1,0:T(8,128)(2,1)S(1)} %get-tuple-element.52.weight) | copy-start | bytes 1492996
  22.9 16.1 %all-to-all-start = ((f32[32,4,96]{2,1,0:T(4,128)}), f32[32,4,96]{2,1,0:T(4,128)S(1)}, u32[]{:S(2)}, u32[]{:S(2)}) async-start(f32[32,4,96]{2,1,0:T(4,128)} %get-tuple-element.51), calls=%async_computation | async-start | bytes 131072 | tf_op jit(solution)/shard_map/all_to_all | solution.py:649
  31.3 35.8 %copy-start.5 = (f32[96]{0:T(128)S(1)}, f32[96]{0:T(128)}, u32[]{:S(2)}) copy-start(f32[96]{0:T(128)} %param.10) | copy-start | bytes 1156
  31.3 35.8 %copy-start.6 = (f32[96]{0:T(128)S(1)}, f32[96]{0:T(128)}, u32[]{:S(2)}) copy-start(f32[96]{0:T(128)} %param.11) | copy-start | bytes 1156
  39.7 27.4 %all-to-all-start.1 = ((f32[16,4,96]{2,1,0:T(4,128)}), f32[16,4,96]{2,1,0:T(4,128)S(1)}, u32[]{:S(2)}, u32[]{:S(2)}) async-start(f32[16,4,96]{2,1,0:T(4,128)} %broadcast_in_dim.14), calls=%async_computation.1 | async-start | bytes 65536 | tf_op jit(solution)/shard_map/all_to_all | solution.py:649
  70.2 6.4 %collective-permute-start.4 = (bf16[4,1296,128]{2,1,0:T(8,128)(2,1)S(1)}, bf16[4,1296,128]{2,1,0:T(8,128)(2,1)S(1)}, u32[]{:S(2)}, u32[]{:S(2)}) collective-permute-start(bf16[4,1296,128]{2,1,0:T(8,128)(2,1)S(1)} %get-tuple-element.63), channel_id=1, source_target_pairs={{0,1},{1,0},{2,3},{3,2},{4,5},{5,4},{6,7},{7,6},{8,9},{9,8},{10,11... | collective-permute-start | bytes 3981320 | tf_op jit(solution)/shard_map/ppermute | solution.py:678
  77.3 1.1 copy-start
  78.4 21.3 %all-to-all-start.2 = ((bf16[4,1296,128]{2,1,0:T(8,128)(2,1)}), bf16[4,1296,128]{2,1,0:T(8,128)(2,1)S(1)}, u32[]{:S(2)}, u32[]{:S(2)}) async-start(bf16[4,1296,128]{2,1,0:T(8,128)(2,1)} %copy-done), calls=%async_computation.2 | async-start | bytes 2654208 | tf_op jit(solution)/shard_map/all_to_all | solution.py:649
  81.9 18.8 %collective-permute-start.5 = (bf16[2,6,32,96]{3,2,1,0:T(8,128)(2,1)S(1)}, bf16[2,6,32,96]{3,2,1,0:T(8,128)(2,1)S(1)}, u32[]{:S(2)}, u32[]{:S(2)}) collective-permute-start(bf16[2,6,32,96]{3,2,1,0:T(8,128)(2,1)S(1)} %get-tuple-element.65.hidden), channel_id=1, source_target_pairs={{0,32},{32,64},{64,96},{96,128},{128,160},{160,192},{192,224},{224... | collective-permute-start | bytes 221192 | tf_op jit(solution)/shard_map/ppermute | solution.py:32
  100.8 19.4 %all-to-all-start.3 = ((bf16[64,1,3,8,128]{4,3,2,1,0:T(8,128)(2,1)}), bf16[64,1,3,8,128]{4,3,2,1,0:T(8,128)(2,1)S(1)}, u32[]{:S(2)}, u32[]{:S(2)}) async-start(bf16[64,1,3,8,128]{4,3,2,1,0:T(8,128)(2,1)} %bitcast.6), calls=%async_computation.3 | async-start | bytes 786432 | tf_op jit(solution)/shard_map/all_to_all | solution.py:649
  121.9 19.2 %all-to-all-start.4 = ((bf16[64,1,12,128]{3,2,1,0:T(8,128)(2,1)}), bf16[64,1,12,128]{3,2,1,0:T(8,128)(2,1)S(1)}, u32[]{:S(2)}, u32[]{:S(2)}) async-start(bf16[64,1,12,128]{3,2,1,0:T(8,128)(2,1)} %broadcast_in_dim.34), calls=%async_computation.4 | async-start | bytes 524288 | tf_op jit(solution)/shard_map/all_to_all | solution.py:649
  129.1 7.7 %collective-permute-start.6 = (bf16[2,6,32,96]{3,2,1,0:T(8,128)(2,1)S(1)}, bf16[2,6,32,96]{3,2,1,0:T(8,128)(2,1)S(1)}, u32[]{:S(2)}, u32[]{:S(2)}) collective-permute-start(bf16[2,6,32,96]{3,2,1,0:T(8,128)(2,1)S(1)} %grad_pre.1), channel_id=1, source_target_pairs={{32,0},{64,32},{96,64},{128,96},{160,128},{192,160},{224,192},{256... | collective-permute-start | bytes 221192 | tf_op jit(solution)/shard_map/ppermute | solution.py:32
  142.1 11.9 %all-to-all-start.5 = ((bf16[4,768,128]{2,1,0:T(8,128)(2,1)}), bf16[4,768,128]{2,1,0:T(8,128)(2,1)S(1)}, u32[]{:S(2)}, u32[]{:S(2)}) async-start(bf16[4,768,128]{2,1,0:T(8,128)(2,1)} %broadcast_in_dim.35), calls=%async_computation.5 | async-start | bytes 1572864 | tf_op jit(solution)/shard_map/all_to_all | solution.py:649
  154.1 9.4 %collective-permute-start.7 = (bf16[4,768,128]{2,1,0:T(8,128)(2,1)S(1)}, bf16[4,768,128]{2,1,0:T(8,128)(2,1)S(1)}, u32[]{:S(2)}, u32[]{:S(2)}) collective-permute-start(bf16[4,768,128]{2,1,0:T(8,128)(2,1)S(1)} %all-to-all-done.5.part), channel_id=1, source_target_pairs={{0,1},{1,0},{2,3},{3,2},{4,5},{5,4},{6,7},{7,6},{8,9},{9,8},{10,11... | collective-permute-start | bytes 2359304 | tf_op jit(solution)/shard_map/ppermute | solution.py:697

commit v10 on v7

--- a/solution.py
+++ b/solution.py
@@ -490,10 +490,8 @@
     second = exact(sums, group_lanes(outs, False), ((1,), (1,)))
     rest = (first - vectors[1:2]) * vectors[0:1]
     final[...] = jnp.concatenate([first, second, rest, jnp.zeros((5, outs), jnp.float32)], 0)
-    lane = lax.broadcasted_iota(jnp.int32, (outs, 896), 1)
-    channel = lax.broadcasted_iota(jnp.int32, (outs, 896), 0)
-    spread = ((lane % outs == channel) & (lane < 9 * outs)).astype(jnp.float32)
-    lanes[...] = jnp.broadcast_to(exact(second - vectors[2:3], spread, ((1,), (0,))), lanes.shape)
+    spread = [second - vectors[2:3]] * 9 + [jnp.zeros((1, 32), jnp.float32)]
+    lanes[...] = jnp.broadcast_to(jnp.concatenate(spread, 1), lanes.shape)
     for k in range(piece.shape[0]):
         block = (where[3] * piece.shape[0] + k) // tiles_per_block % 7
         change = lanes[0:1, pl.ds(pl.multiple_of(block * 128, 128), 128)]
@@ -674,20 +672,18 @@
         where, cache, features, above, below, grad_normed, normed, vectors, local_two, xs, part_rows
     )
     part = add_pair(kept, lax.ppermute(away, "c", SWAP))
-    part, hidden = barrier((part, hidden))
-    part = add_row(exchange(part, "x"))
+    part, hidden = barrier((add_row(exchange(part, "x")), hidden))
     before = neighbour(hidden, TM, 1)
-    part, before = barrier((part, before))
     came = exchange(part.reshape(rest, -1, 3, 8, 128), REST)
-    decoded = conv(
-        jnp.pad(jnp.concatenate([before, hidden], 0), ((0, 0), (0, 0), (1, 1), (0, 0))), weight_two
-    ).astype(jnp.bfloat16)
-    came, decoded = barrier((came, decoded))
+    came, before = barrier((came, before))
     part, final = combine(count, ins, where, came, vectors)
     grad_pre = grad_before_norm(where, grad_normed, normed, vectors, final)
     part = exchange(spread(part, rest), REST)
     after = neighbour(grad_pre, TM, -1)
-    part, after = barrier((part, after))
+    decoded = conv(
+        jnp.pad(jnp.concatenate([before, hidden], 0), ((0, 0), (0, 0), (1, 1), (0, 0))), weight_two
+    ).astype(jnp.bfloat16)
+    part, after, decoded = barrier((part, after, decoded))
     part = jnp.concatenate([part[:, :, :8].reshape(-1, 128), part[:, :, 8:].reshape(-1, 128)], 0)
     part = exchange(spread(part, xs), "x")
     grad_features = feature_grads(jnp.concatenate([grad_pre, after], 0), weight_one, features.shape)

time: 167 us -> 167 us (level)
  blocking collectives: 0 us -> 20.2 us
  waiting for transfers between devices: 64.8 us -> 47.9 us
    all_to_all x0 -> x1, blocking collectives: none -> 20.2 us  [exchange(): return lax.all_to_all(copies, axes, 0, 0)]
    all_to_all x6 -> x5, waiting for transfers between devices: 55.7 us -> 35.8 us  [exchange(): return lax.all_to_all(copies, axes, 0, 0)]
    ppermute x6, waiting for transfers between devices: 6.46 us -> 9.48 us  [neighbour(): lax.ppermute(value, axis, [(i, i + steps) for i in range(first, last)])]
    all_to_all x6 -> x5, starting transfers between devices: 42.8 us -> 41.2 us  [exchange(): return lax.all_to_all(copies, axes, 0, 0)]
    unnamed x17 -> x13, local copies, waits for them, and re-layouts: 5.71 us -> 4.65 us
  transfers between devices with their start and end apart: 14 -> 13, of which waited for: 8 -> 8; matrix products, arithmetic and copies ran while one was open for 2% -> 1% of each run, Pallas kernels for 4% -> 4%
where the time goes in v10:
time: 167 us; the launch traced here: 166 us
  starting transfers between devices  71.7 us (43%)
  waiting for transfers between devices  47.9 us (29%)
  blocking collectives  20.2 us (12%)
  Pallas kernels  16.1 us (10%)
  local copies, waits for them, and re-layouts  7.06 us (4%)
    all_to_all x5, starting transfers between devices, exchange(): return lax.all_to_all(copies, axes, 0, 0)  41.2 us
    all_to_all x5, waiting for transfers between devices, exchange(): return lax.all_to_all(copies, axes, 0, 0)  35.8 us
    all_to_all x1, blocking collectives, exchange(): return lax.all_to_all(copies, axes, 0, 0)  20.2 us
    ppermute x6, starting transfers between devices, neighbour(): lax.ppermute(value, axis, [(i, i + steps) for i in range(first, last)])  20.2 us
    ppermute x6, waiting for transfers between devices, neighbour(): lax.ppermute(value, axis, [(i, i + steps) for i in range(first, last)])  9.48 us
    ppermute x1, starting transfers between devices, body(): other = lax.ppermute(part, 'c', SWAP)  6.53 us
    pallas_call x2, Pallas kernels, unpack(): pl.pallas_call(functools.partial(unpack_kernel, scale), grid_spec=pltpu.P...  5.17 us
    unnamed x13, local copies, waits for them, and re-layouts  4.65 us
  transfers between devices with their start and end apart: 13, of which 8 were waited for; matrix products, arithmetic and copies ran while one was open for 1% of the time, Pallas kernels for 4%

profile of v10, /device:TPU:1, one launch (start us, length us, event | category | flops | bytes accessed | tf_op | source)
XLA Modules:
  0.0 165.8 jit_solution(2367533773949675742)
XLA Ops:
  0.6 1.3 collective-permute-start.1
  1.9 4.7 %collective-permute-start = (bf16[2,2,16,192]{3,2,1,0:T(8,128)(2,1)}, bf16[2,2,16,192]{3,2,1,0:T(8,128)(2,1)S(1)}, u32[]{:S(2)}, u32[]{:S(2)}) collective-permute-start(bf16[2,2,16,192]{3,2,1,0:T(8,128)(2,1)} %refs_0_.1), channel_id=1, source_target_pairs={{0,32},{32,64},{64,96},{96,128},{128,160},{160,192},{192,224},{224... | collective-permute-start | bytes 73736 | tf_op jit(solution)/shard_map/ppermute | solution.py:32
  8.4 4.6 %collective-permute-start.2 = (bf16[4,48,192]{2,1,0:T(8,128)(2,1)S(1)}, bf16[4,48,192]{2,1,0:T(8,128)(2,1)S(1)}, u32[]{:S(2)}, u32[]{:S(2)}) collective-permute-start(bf16[4,48,192]{2,1,0:T(8,128)(2,1)S(1)} %get-tuple-element.45), channel_id=1, source_target_pairs={{0,1},{1,2},{2,3},{3,4},{4,5},{5,6},{6,7},{7,8},{8,9},{9,10},{10,1... | collective-permute-start | bytes 221192 | tf_op jit(solution)/shard_map/ppermute | solution.py:32
  13.0 5.6 %collective-permute-start.3 = (bf16[4,48,192]{2,1,0:T(8,128)(2,1)S(1)}, bf16[4,48,192]{2,1,0:T(8,128)(2,1)S(1)}, u32[]{:S(2)}, u32[]{:S(2)}) collective-permute-start(bf16[4,48,192]{2,1,0:T(8,128)(2,1)S(1)} %get-tuple-element.46), channel_id=1, source_target_pairs={{1,0},{2,1},{3,2},{4,3},{5,4},{6,5},{7,6},{8,7},{9,8},{10,9},{11,1... | collective-permute-start | bytes 221192 | tf_op jit(solution)/shard_map/ppermute | solution.py:32
  18.6 1.3 copy-done
  19.9 1.1 copy-done.1
  21.4 1.6 conv_one.1
  22.9 8.4 %all-to-all-start = ((f32[32,4,96]{2,1,0:T(4,128)}), f32[32,4,96]{2,1,0:T(4,128)S(1)}, u32[]{:S(2)}, u32[]{:S(2)}) async-start(f32[32,4,96]{2,1,0:T(4,128)} %get-tuple-element.50), calls=%async_computation | async-start | bytes 131072 | tf_op jit(solution)/shard_map/all_to_all | solution.py:645
  32.3 6.8 %all-to-all-done = f32[32,4,96]{2,1,0:T(4,128)S(1)} async-done(((f32[32,4,96]{2,1,0:T(4,128)}), f32[32,4,96]{2,1,0:T(4,128)S(1)}, u32[]{:S(2)}, u32[]{:S(2)}) %all-to-all-start) | async-done | bytes 49184 | tf_op jit(solution)/shard_map/all_to_all | solution.py:645
  39.7 16.1 %all-to-all-start.1 = ((f32[16,4,96]{2,1,0:T(4,128)}), f32[16,4,96]{2,1,0:T(4,128)S(1)}, u32[]{:S(2)}, u32[]{:S(2)}) async-start(f32[16,4,96]{2,1,0:T(4,128)} %broadcast_in_dim.14), calls=%async_computation.1 | async-start | bytes 65536 | tf_op jit(solution)/shard_map/all_to_all | solution.py:645
  56.0 11.2 %all-to-all-done.1.came = f32[16,4,96]{2,1,0:T(4,128)S(1)} async-done(((f32[16,4,96]{2,1,0:T(4,128)}), f32[16,4,96]{2,1,0:T(4,128)S(1)}, u32[]{:S(2)}, u32[]{:S(2)}) %all-to-all-start.1) | async-done | bytes 24608 | tf_op jit(solution)/shard_map/all_to_all | solution.py:645
  68.7 1.5 weight_grads.1
  70.2 3.7 %collective-permute-start.4 = (bf16[4,1296,128]{2,1,0:T(8,128)(2,1)S(1)}, bf16[4,1296,128]{2,1,0:T(8,128)(2,1)S(1)}, u32[]{:S(2)}, u32[]{:S(2)}) collective-permute-start(bf16[4,1296,128]{2,1,0:T(8,128)(2,1)S(1)} %get-tuple-element.62), channel_id=1, source_target_pairs={{0,1},{1,0},{2,3},{3,2},{4,5},{5,4},{6,7},{7,6},{8,9},{9,8},{10,11... | collective-permute-start | bytes 3981320 | tf_op jit(solution)/shard_map/ppermute | solution.py:674
  73.9 2.7 %collective-permute-done.4.came = bf16[4,1296,128]{2,1,0:T(8,128)(2,1)S(1)} collective-permute-done((bf16[4,1296,128]{2,1,0:T(8,128)(2,1)S(1)}, bf16[4,1296,128]{2,1,0:T(8,128)(2,1)S(1)}, u32[]{:S(2)}, u32[]{:S(2)}) %collective-permute-start.4) | collective-permute-done | bytes 1327136 | tf_op jit(solution)/shard_map/ppermute | solution.py:674
  77.3 20.2 %all_to_all.30.came = bf16[4,1296,128]{2,1,0:T(8,128)(2,1)S(1)} all-to-all(bf16[4,1296,128]{2,1,0:T(8,128)(2,1)S(1)} %add_pair.1), channel_id=1, replica_groups=mesh['zh'=2,'y'=8,'zl'=4,'x'=4,'c'=2] {'x'}, dimensions={0} | all-to-all | bytes 2654208 | tf_op jit(solution)/shard_map/all_to_all | solution.py:645
  97.6 1.0 add_row.1
  98.6 4.6 %all-to-all-start.3 = ((bf16[64,1,3,8,128]{4,3,2,1,0:T(8,128)(2,1)}), bf16[64,1,3,8,128]{4,3,2,1,0:T(8,128)(2,1)S(1)}, u32[]{:S(2)}, u32[]{:S(2)}) async-start(bf16[64,1,3,8,128]{4,3,2,1,0:T(8,128)(2,1)} %bitcast.6), calls=%async_computation.3 | async-start | bytes 786432 | tf_op jit(solution)/shard_map/all_to_all | solution.py:645
  103.2 2.8 %collective-permute-start.5 = (bf16[2,6,32,96]{3,2,1,0:T(8,128)(2,1)S(1)}, bf16[2,6,32,96]{3,2,1,0:T(8,128)(2,1)S(1)}, u32[]{:S(2)}, u32[]{:S(2)}) collective-permute-start(bf16[2,6,32,96]{3,2,1,0:T(8,128)(2,1)S(1)} %get-tuple-element.64.hidden), channel_id=1, source_target_pairs={{0,32},{32,64},{64,96},{96,128},{128,160},{160,192},{192,224},{224... | collective-permute-start | bytes 221192 | tf_op jit(solution)/shard_map/ppermute | solution.py:32
  106.1 5.2 %collective-permute-done.5 = bf16[2,6,32,96]{3,2,1,0:T(8,128)(2,1)S(1)} collective-permute-done((bf16[2,6,32,96]{3,2,1,0:T(8,128)(2,1)S(1)}, bf16[2,6,32,96]{3,2,1,0:T(8,128)(2,1)S(1)}, u32[]{:S(2)}, u32[]{:S(2)}) %collective-permute-start.5) | collective-permute-done | bytes 73760 | tf_op jit(solution)/shard_map/ppermute | solution.py:32
  111.3 6.8 %all-to-all-done.3.came = bf16[64,1,3,8,128]{4,3,2,1,0:T(8,128)(2,1)S(1)} async-done(((bf16[64,1,3,8,128]{4,3,2,1,0:T(8,128)(2,1)}), bf16[64,1,3,8,128]{4,3,2,1,0:T(8,128)(2,1)S(1)}, u32[]{:S(2)}, u32[]{:S(2)}) %all-to-all-start.3) | async-done | bytes 393248 | tf_op jit(solution)/shard_map/all_to_all | solution.py:645
  119.8 8.6 %all-to-all-start.4 = ((bf16[64,1,12,128]{3,2,1,0:T(8,128)(2,1)}), bf16[64,1,12,128]{3,2,1,0:T(8,128)(2,1)S(1)}, u32[]{:S(2)}, u32[]{:S(2)}) async-start(bf16[64,1,12,128]{3,2,1,0:T(8,128)(2,1)} %broadcast_in_dim.33), calls=%async_computation.4 | async-start | bytes 524288 | tf_op jit(solution)/shard_map/all_to_all | solution.py:645
  129.0 1.3 collective-permute-start.6
  130.4 1.5 convolution_convert_fusion
  132.5 4.2 %collective-permute-done.6 = bf16[2,6,32,96]{3,2,1,0:T(8,128)(2,1)S(1)} collective-permute-done((bf16[2,6,32,96]{3,2,1,0:T(8,128)(2,1)S(1)}, bf16[2,6,32,96]{3,2,1,0:T(8,128)(2,1)S(1)}, u32[]{:S(2)}, u32[]{:S(2)}) %collective-permute-start.6) | collective-permute-done | bytes 73760 | tf_op jit(solution)/shard_map/ppermute | solution.py:32
  136.8 4.2 %all-to-all-done.4 = bf16[64,1,12,128]{3,2,1,0:T(8,128)(2,1)S(1)} async-done(((bf16[64,1,12,128]{3,2,1,0:T(8,128)(2,1)}), bf16[64,1,12,128]{3,2,1,0:T(8,128)(2,1)S(1)}, u32[]{:S(2)}, u32[]{:S(2)}) %all-to-all-start.4) | async-done | bytes 196640 | tf_op jit(solution)/shard_map/all_to_all | solution.py:645
  141.0 1.0 broadcast_in_dim.35
  142.0 3.5 %all-to-all-start.5 = ((bf16[4,768,128]{2,1,0:T(8,128)(2,1)}), bf16[4,768,128]{2,1,0:T(8,128)(2,1)S(1)}, u32[]{:S(2)}, u32[]{:S(2)}) async-start(bf16[4,768,128]{2,1,0:T(8,128)(2,1)} %broadcast_in_dim.35), calls=%async_computation.5 | async-start | bytes 1572864 | tf_op jit(solution)/shard_map/all_to_all | solution.py:645
  145.5 1.6 feature_grads.1
  147.2 6.9 %all-to-all-done.5.part = bf16[4,768,128]{2,1,0:T(8,128)(2,1)S(1)} async-done(((bf16[4,768,128]{2,1,0:T(8,128)(2,1)}), bf16[4,768,128]{2,1,0:T(8,128)(2,1)S(1)}, u32[]{:S(2)}, u32[]{:S(2)}) %all-to-all-start.5) | async-done | bytes 786464 | tf_op jit(solution)/shard_map/all_to_all | solution.py:645
  154.1 6.5 %collective-permute-start.7 = (bf16[4,768,128]{2,1,0:T(8,128)(2,1)S(1)}, bf16[4,768,128]{2,1,0:T(8,128)(2,1)S(1)}, u32[]{:S(2)}, u32[]{:S(2)}) collective-permute-start(bf16[4,768,128]{2,1,0:T(8,128)(2,1)S(1)} %all-to-all-done.5.part), channel_id=1, source_target_pairs={{0,1},{1,0},{2,3},{3,2},{4,5},{5,4},{6,7},{7,6},{8,9},{9,8},{10,11... | collective-permute-start | bytes 2359304 | tf_op jit(solution)/shard_map/ppermute | solution.py:691
  160.6 2.6 %unpack.2 = (f32[27,192,96]{2,1,0:T(8,128)}, f32[27,96,96]{2,1,0:T(8,128)}) custom-call(s32[1]{0:T(128)} %bitcast.half, bf16[4,768,128]{2,1,0:T(8,128)(2,1)S(1)} %all-to-all-done.5.part, f32[8,96]{1,0:T(8,128)S(1)} %get-tuple-element.67.final), custom_call_target="tpu_custom_call" | custom-call | flops 1048576 | bytes 4194304 | tf_op jit(solution)/shard_map/unpack/pallas_call | solution.py:572
  163.2 2.6 %unpack.3 = (f32[27,192,96]{2,1,0:T(8,128)}, f32[27,96,96]{2,1,0:T(8,128)}) custom-call(s32[1]{0:T(128)S(6)} %sub.3.half, bf16[4,768,128]{2,1,0:T(8,128)(2,1)S(1)} %collective-permute-done.7.part, f32[8,96]{1,0:T(8,128)S(1)} %get-tuple-element.67.final, f32[27,192,96]{2,1,0:T(8,128)} %get-tuple-element.74.rest_0_, ...), custom_call_target="tpu_custom_call", output_to_operand_aliasing={{0}: (3, {}), {1}: (4, {})} | custom-call | flops 1048576 | bytes 4194304 | tf_op jit(solution)/shard_map/unpack/pallas_call | solution.py:572
  (34 shorter events, 9.2 us)
Async XLA Ops:
  0.6 7.7 %collective-permute-start.1 = (bf16[2,4,32,96]{3,2,1,0:T(8,128)(2,1)}, bf16[2,4,32,96]{3,2,1,0:T(8,128)(2,1)S(1)}, u32[]{:S(2)}, u32[]{:S(2)}) collective-permute-start(bf16[2,4,32,96]{3,2,1,0:T(8,128)(2,1)} %refs_1_.1), channel_id=1, source_target_pairs={{32,0},{64,32},{96,64},{128,96},{160,128},{192,160},{224,192},{256... | collective-permute-start | bytes 147464 | tf_op jit(solution)/shard_map/ppermute | solution.py:32
  1.9 6.4 %collective-permute-start = (bf16[2,2,16,192]{3,2,1,0:T(8,128)(2,1)}, bf16[2,2,16,192]{3,2,1,0:T(8,128)(2,1)S(1)}, u32[]{:S(2)}, u32[]{:S(2)}) collective-permute-start(bf16[2,2,16,192]{3,2,1,0:T(8,128)(2,1)} %refs_0_.1), channel_id=1, source_target_pairs={{0,32},{32,64},{64,96},{96,128},{128,160},{160,192},{192,224},{224... | collective-permute-start | bytes 73736 | tf_op jit(solution)/shard_map/ppermute | solution.py:32
  6.6 0.8 copy-start.2
  7.4 0.8 copy-start.3
  8.4 12.9 %collective-permute-start.2 = (bf16[4,48,192]{2,1,0:T(8,128)(2,1)S(1)}, bf16[4,48,192]{2,1,0:T(8,128)(2,1)S(1)}, u32[]{:S(2)}, u32[]{:S(2)}) collective-permute-start(bf16[4,48,192]{2,1,0:T(8,128)(2,1)S(1)} %get-tuple-element.45), channel_id=1, source_target_pairs={{0,1},{1,2},{2,3},{3,4},{4,5},{5,6},{6,7},{7,8},{8,9},{9,10},{10,1... | collective-permute-start | bytes 221192 | tf_op jit(solution)/shard_map/ppermute | solution.py:32
  13.0 8.4 %collective-permute-start.3 = (bf16[4,48,192]{2,1,0:T(8,128)(2,1)S(1)}, bf16[4,48,192]{2,1,0:T(8,128)(2,1)S(1)}, u32[]{:S(2)}, u32[]{:S(2)}) collective-permute-start(bf16[4,48,192]{2,1,0:T(8,128)(2,1)S(1)} %get-tuple-element.46), channel_id=1, source_target_pairs={{1,0},{2,1},{3,2},{4,3},{5,4},{6,5},{7,6},{8,7},{9,8},{10,9},{11,1... | collective-permute-start | bytes 221192 | tf_op jit(solution)/shard_map/ppermute | solution.py:32
  18.6 1.3 copy-start
  19.9 1.1 copy-start.1
  22.9 16.1 %all-to-all-start = ((f32[32,4,96]{2,1,0:T(4,128)}), f32[32,4,96]{2,1,0:T(4,128)S(1)}, u32[]{:S(2)}, u32[]{:S(2)}) async-start(f32[32,4,96]{2,1,0:T(4,128)} %get-tuple-element.50), calls=%async_computation | async-start | bytes 131072 | tf_op jit(solution)/shard_map/all_to_all | solution.py:645
  31.3 35.8 %copy-start.4 = (f32[96]{0:T(128)S(1)}, f32[96]{0:T(128)}, u32[]{:S(2)}) copy-start(f32[96]{0:T(128)} %param.10) | copy-start | bytes 1156
  31.3 35.8 %copy-start.5 = (f32[96]{0:T(128)S(1)}, f32[96]{0:T(128)}, u32[]{:S(2)}) copy-start(f32[96]{0:T(128)} %param.11) | copy-start | bytes 1156
  39.7 27.4 %all-to-all-start.1 = ((f32[16,4,96]{2,1,0:T(4,128)}), f32[16,4,96]{2,1,0:T(4,128)S(1)}, u32[]{:S(2)}, u32[]{:S(2)}) async-start(f32[16,4,96]{2,1,0:T(4,128)} %broadcast_in_dim.14), calls=%async_computation.1 | async-start | bytes 65536 | tf_op jit(solution)/shard_map/all_to_all | solution.py:645
  70.2 6.4 %collective-permute-start.4 = (bf16[4,1296,128]{2,1,0:T(8,128)(2,1)S(1)}, bf16[4,1296,128]{2,1,0:T(8,128)(2,1)S(1)}, u32[]{:S(2)}, u32[]{:S(2)}) collective-permute-start(bf16[4,1296,128]{2,1,0:T(8,128)(2,1)S(1)} %get-tuple-element.62), channel_id=1, source_target_pairs={{0,1},{1,0},{2,3},{3,2},{4,5},{5,4},{6,7},{7,6},{8,9},{9,8},{10,11... | collective-permute-start | bytes 3981320 | tf_op jit(solution)/shard_map/ppermute | solution.py:674
  98.6 19.5 %all-to-all-start.3 = ((bf16[64,1,3,8,128]{4,3,2,1,0:T(8,128)(2,1)}), bf16[64,1,3,8,128]{4,3,2,1,0:T(8,128)(2,1)S(1)}, u32[]{:S(2)}, u32[]{:S(2)}) async-start(bf16[64,1,3,8,128]{4,3,2,1,0:T(8,128)(2,1)} %bitcast.6), calls=%async_computation.3 | async-start | bytes 786432 | tf_op jit(solution)/shard_map/all_to_all | solution.py:645
  103.2 8.1 %collective-permute-start.5 = (bf16[2,6,32,96]{3,2,1,0:T(8,128)(2,1)S(1)}, bf16[2,6,32,96]{3,2,1,0:T(8,128)(2,1)S(1)}, u32[]{:S(2)}, u32[]{:S(2)}) collective-permute-start(bf16[2,6,32,96]{3,2,1,0:T(8,128)(2,1)S(1)} %get-tuple-element.64.hidden), channel_id=1, source_target_pairs={{0,32},{32,64},{64,96},{96,128},{128,160},{160,192},{192,224},{224... | collective-permute-start | bytes 221192 | tf_op jit(solution)/shard_map/ppermute | solution.py:32
  119.8 21.1 %all-to-all-start.4 = ((bf16[64,1,12,128]{3,2,1,0:T(8,128)(2,1)}), bf16[64,1,12,128]{3,2,1,0:T(8,128)(2,1)S(1)}, u32[]{:S(2)}, u32[]{:S(2)}) async-start(bf16[64,1,12,128]{3,2,1,0:T(8,128)(2,1)} %broadcast_in_dim.33), calls=%async_computation.4 | async-start | bytes 524288 | tf_op jit(solution)/shard_map/all_to_all | solution.py:645
  129.0 7.8 %collective-permute-start.6 = (bf16[2,6,32,96]{3,2,1,0:T(8,128)(2,1)S(1)}, bf16[2,6,32,96]{3,2,1,0:T(8,128)(2,1)S(1)}, u32[]{:S(2)}, u32[]{:S(2)}) collective-permute-start(bf16[2,6,32,96]{3,2,1,0:T(8,128)(2,1)S(1)} %grad_pre.1), channel_id=1, source_target_pairs={{32,0},{64,32},{96,64},{128,96},{160,128},{192,160},{224,192},{256... | collective-permute-start | bytes 221192 | tf_op jit(solution)/shard_map/ppermute | solution.py:32
  142.0 12.1 %all-to-all-start.5 = ((bf16[4,768,128]{2,1,0:T(8,128)(2,1)}), bf16[4,768,128]{2,1,0:T(8,128)(2,1)S(1)}, u32[]{:S(2)}, u32[]{:S(2)}) async-start(bf16[4,768,128]{2,1,0:T(8,128)(2,1)} %broadcast_in_dim.35), calls=%async_computation.5 | async-start | bytes 1572864 | tf_op jit(solution)/shard_map/all_to_all | solution.py:645
  154.1 9.1 %collective-permute-start.7 = (bf16[4,768,128]{2,1,0:T(8,128)(2,1)S(1)}, bf16[4,768,128]{2,1,0:T(8,128)(2,1)S(1)}, u32[]{:S(2)}, u32[]{:S(2)}) collective-permute-start(bf16[4,768,128]{2,1,0:T(8,128)(2,1)S(1)} %all-to-all-done.5.part), channel_id=1, source_target_pairs={{0,1},{1,0},{2,3},{3,2},{4,5},{5,4},{6,7},{7,6},{8,9},{9,8},{10,11... | collective-permute-start | bytes 2359304 | tf_op jit(solution)/shard_map/ppermute | solution.py:691
